TPU v7x, 256 devices: a whole 4x4x8 slice. The times are simulated.
256 devices in a mesh: db: 16 (over y, x), head: 16 (over z, core).
Axes of the slice: x: 4, y: 4, z: 8, core: 2. Of those that a mesh axis runs over, the one named last changes fastest.
Arguments:
- tokens: bfloat16 [16384, 4096], P('db', 'head'), may hold values from -6 to 6
- query_weight: bfloat16 [4096, 4096], P(None, 'head'), may hold values from -0.09375 to 0.09375
- key_weight: bfloat16 [896, 4096], P(None, 'head'), may hold values from -0.1875 to 0.1875
- value_weight: bfloat16 [896, 4096], P(None, 'head'), may hold values from -0.1875 to 0.1875
- out_weight: bfloat16 [4096, 4096], P('head'), may hold values from -0.09375 to 0.09375
- codes: bfloat16 [128, 128, 896], P('db'), may hold values from -6 to 6
- scales: float32 [128, 7], P('db'), may hold values from 0.25 to 4
- block_len: int32 [128], P('db'), may hold values from 32 to 128
- nbr_owner: int32 [256, 2], P('db'), may hold values from 0 to 15, all different within a row; in each aligned block of 16 rows (0 to 15, 16 to 31, ...) at most 2 rows name the same one
- nbr_block: int32 [256, 2], P('db'), may hold values from 0 to 7
Outputs:
- cross_out: bfloat16 [16384, 4096], P('db', 'head')
Inputs may be any that keep to these rules, and one draw needn't show every extreme that they name: `nbr_owner`: the 2 neighbours of a span lie on different shards; among the spans of one index of db at most 2 neighbours lie on any one shard, and in some index of db exactly 2 do.
All inputs are finite; a program needn't handle non-finite values.
Results may differ from a plain program's by a relative error of at most 0.011.
Values may be sent and summed in bfloat16 or wider, within the bound.
No kernel may reach another device: no remote copies, remote signals or barrier semaphores. Data moves between devices by JAX's collectives and lax.ppermute only.
A program may use at most 128 MiB of HBM per device.

v0:
```python
import math

import jax
import jax.numpy as jnp
from jax import lax
from jax.sharding import PartitionSpec as P

HD = 128
ENC = 896
GROUP = 128
SPAN = 64
NBR_LEN = 128
NBRS = 2


def normalize(values):
    return values * lax.rsqrt(jnp.mean(values * values, axis=-1, keepdims=True) + 1e-06)


def local(
    tokens,
    query_weight,
    key_weight,
    value_weight,
    out_weight,
    codes,
    scales,
    block_len,
    nbr_owner,
    nbr_block,
):
    tok_rows = tokens.shape[0]
    local_width = query_weight.shape[1]
    heads_here = local_width // HD
    spans_here = tok_rows // SPAN
    factor = 2.0 / math.sqrt(HD)
    projected = jnp.dot(
        lax.all_gather(tokens, "head", axis=1, tiled=True),
        query_weight,
        preferred_element_type=jnp.float32,
    )
    queries = normalize(projected.reshape(spans_here, SPAN, heads_here, HD)).astype(jnp.bfloat16)
    shards = lax.axis_size("db")
    owners = nbr_owner.reshape(-1)
    wanted_blocks = nbr_block.reshape(-1)
    requests_here = owners.shape[0]
    capacity = max(2, -(-requests_here // shards))
    order_ids = jnp.arange(requests_here, dtype=jnp.int32)
    same_owner = (owners[:, None] == owners[None, :]) & (order_ids[:, None] > order_ids[None, :])
    slot_index = owners * capacity + jnp.sum(same_owner.astype(jnp.int32), axis=1)
    slot_table = (
        slot_index[:, None] == jnp.arange(shards * capacity, dtype=jnp.int32)[None, :]
    ).astype(jnp.int32)
    request_table = jnp.sum(slot_table * wanted_blocks[:, None], axis=0).reshape(shards, capacity)
    wanted = lax.all_to_all(request_table, "db", split_axis=0, concat_axis=0, tiled=True)
    item_count = wanted.shape[1]
    picked = codes[wanted]
    scale_rows = scales[wanted]
    lengths_here = block_len[wanted]
    grouped = picked.astype(jnp.float32).reshape(shards, item_count, NBR_LEN, ENC // GROUP, GROUP)
    encoded = (
        (grouped * scale_rows[:, :, None, :, None])
        .reshape(shards, item_count, NBR_LEN, ENC)
        .astype(jnp.bfloat16)
    )
    fetched = (
        lax.all_to_all(encoded, "db", split_axis=0, concat_axis=0, tiled=True),
        lax.all_to_all(lengths_here, "db", split_axis=0, concat_axis=0, tiled=True),
    )
    encoded_back, length_back = fetched
    chosen_rows = encoded_back.reshape(shards * capacity, NBR_LEN, ENC)[slot_index].reshape(-1, ENC)
    key_proj = jnp.dot(chosen_rows, key_weight, preferred_element_type=jnp.float32)
    key_part = (
        normalize(key_proj.reshape(-1, heads_here, HD))
        .astype(jnp.bfloat16)
        .reshape(-1, local_width)
    )
    value_part = jnp.dot(chosen_rows, value_weight, preferred_element_type=jnp.float32).astype(
        jnp.bfloat16
    )
    lengths_used = length_back.reshape(-1)[slot_index]
    key_grid = key_part.reshape(spans_here, NBRS * NBR_LEN, heads_here, HD)
    value_grid = value_part.reshape(spans_here, NBRS * NBR_LEN, heads_here, HD)
    positions = jnp.arange(NBR_LEN, dtype=jnp.int32)
    valid_keys = (positions[None, :] < lengths_used[:, None]).reshape(spans_here, NBRS * NBR_LEN)
    scores = (
        jnp.einsum("cthd,ckhd->chtk", queries, key_grid, preferred_element_type=jnp.float32)
        * factor
    )
    raised = jnp.where(valid_keys[:, None, None, :], jnp.exp(scores), 0.0)
    attn_weights = (raised / jnp.sum(raised, axis=-1, keepdims=True)).astype(jnp.bfloat16)
    attended = jnp.einsum(
        "chtk,ckhd->cthd", attn_weights, value_grid, preferred_element_type=jnp.float32
    )
    attended = attended.astype(jnp.bfloat16).reshape(tok_rows, local_width)
    partial_out = jnp.dot(attended, out_weight, preferred_element_type=jnp.float32)
    return lax.psum_scatter(partial_out, "head", scatter_dimension=1, tiled=True).astype(
        jnp.bfloat16
    )


def solution(mesh):
    placed = (
        P("db", "head"),
        P(None, "head"),
        P(None, "head"),
        P(None, "head"),
        P("head", None),
        P("db", None, None),
        P("db", None),
        P("db"),
        P("db", None),
        P("db", None),
    )
    return jax.shard_map(
        local, mesh=mesh, in_specs=placed, out_specs=P("db", "head"), check_vma=False
    )
```

profile of v0, /device:TPU:24, one launch (start us, length us, event | category | flops | bytes accessed | tf_op | source)
XLA Modules:
  0.0 319.6 jit_solution(6319229969004334110)
XLA Ops:
  6.5 0.7 all-gather.2.cloned.1.call-update
  7.3 0.8 copy.61
  8.0 0.1 mul.76
  8.1 0.8 copy.60
  8.9 0.1 reshape.134
  9.0 0.2 convert_reduce_fusion
  9.1 0.1 select_reduce_fusion
  9.2 0.1 all_to_all.17
  9.3 12.5 %all_to_all.26 = s32[16,1,2]{2,1,0:T(1,128)S(1)} all-to-all(s32[16,1,2]{2,1,0:T(1,128)S(1)} %bitcast.52), channel_id=1, replica_groups=mesh['db'=16,'head'=16] {'db'}, dimensions={0} | all-to-all | bytes 256 | tf_op jit(solution)/shard_map/all_to_all | solution.py:55
  21.9 0.1 copy.63
  22.0 0.1 copy.64
  22.0 0.1 reshape.143
  22.2 0.7 gather_fusion.3
  22.9 0.7 all_to_all.21
  23.6 5.4 %all-to-all-start.2 = ((s32[16,1,2]{2,1,0:T(1,128)}), s32[16,1,2]{2,1,0:T(1,128)S(1)}, u32[]{:S(2)}, u32[]{:S(2)}) async-start(s32[16,1,2]{2,1,0:T(1,128)} %bitcast.9), calls=%async_computation.2 | async-start | bytes 16384 | tf_op jit(solution)/shard_map/all_to_all | solution.py:68
  29.0 0.6 gather_fusion.1
  29.6 0.1 mul.79
  29.8 5.9 %gather_fusion = bf16[32,128,896]{2,1,0:T(8,128)(2,1)} fusion(bf16[8,128,896]{2,1,0:T(8,128)(2,1)} %param.15, s32[1024]{0:T(1024)S(1)} %pad_clamp_fusion.1), kind=kCustom, calls=%fused_computation | custom fusion | bytes 14680192 | tf_op jit(solution)/shard_map/gather | solution.py:57
  35.6 8.2 %fusion = bf16[16,2,128,896]{3,2,1,0:T(8,128)(2,1)} fusion(bf16[16,2,128,896]{3,2,1,0:T(8,128)(2,1)} %bitcast.43, f32[16,2,896]{2,1,0:T(2,128)S(1)} %copy.66), kind=kLoop, calls=%fused_computation.6 | loop fusion | flops 11010048 | bytes 14794752 | tf_op jit(solution)/shard_map/convert_element_type | solution.py:64
  43.8 7.4 %all-to-all-start.1 = ((bf16[16,2,128,896]{3,2,1,0:T(8,128)(2,1)}), bf16[16,2,128,896]{3,2,1,0:T(8,128)(2,1)}, u32[]{:S(2)}, u32[]{:S(2)}) async-start(bf16[16,2,128,896]{3,2,1,0:T(8,128)(2,1)} %fusion), calls=%async_computation.1 | async-start | bytes 14680064 | tf_op jit(solution)/shard_map/all_to_all | solution.py:67
  51.2 0.1 copy.67
  51.3 0.1 mul.85
  51.4 0.2 copy.76
  51.7 0.5 broadcast.116
  52.2 0.7 reduce.3
  52.9 0.1 reshape.138
  53.0 0.7 gather_fusion.4
  53.7 0.1 lt.53
  53.7 0.1 lt.54
  53.9 102.0 %all-to-all-done.1 = bf16[16,2,128,896]{3,2,1,0:T(8,128)(2,1)} async-done(((bf16[16,2,128,896]{3,2,1,0:T(8,128)(2,1)}), bf16[16,2,128,896]{3,2,1,0:T(8,128)(2,1)}, u32[]{:S(2)}, u32[]{:S(2)}) %all-to-all-start.1) | async-done | bytes 7340064 | tf_op jit(solution)/shard_map/all_to_all | solution.py:67
  155.8 7.5 %gather_fusion.2 = bf16[32,128,896]{2,1,0:T(8,128)(2,1)} fusion(bf16[32,128,896]{2,1,0:T(8,128)(2,1)} %bitcast.4, s32[1024]{0:T(1024)S(1)} %pad_clamp_fusion), kind=kCustom, calls=%fused_computation.2 | custom fusion | bytes 14680192 | tf_op jit(solution)/shard_map/gather | solution.py:71
  163.3 6.8 %convolution_convert_fusion = bf16[4096,256]{1,0:T(8,128)(2,1)} fusion(bf16[4096,896]{1,0:T(8,128)(2,1)} %bitcast.44, bf16[896,256]{1,0:T(8,128)(2,1)} %param.13), kind=kOutput, calls=%fused_computation.7 | convolution fusion | flops 1880096768 | bytes 9895936 | tf_op jit(solution)/shard_map/dot_general | solution.py:78
  170.1 4.0 %reshape.137 = bf16[16,256,2,128]{3,2,1,0:T(2,128)(2,1)} reshape(bf16[4096,256]{1,0:T(8,128)(2,1)} %convolution_convert_fusion) | data formatting | bytes 4194304 | tf_op jit(solution)/shard_map/reshape | solution.py:83
  174.1 4.9 %multiply_reduce_fusion = (f32[4096,2]{0,1:T(2,128)S(1)}, f32[4096,2,128]{2,0,1:T(8,128)S(1)}) fusion(bf16[4096,896,1]{1,0,2:T(8,128)(2,1)} %bitcast.45, bf16[2,128,896]{2,1,0:T(8,128)(2,1)S(1)} %bitcast.49), kind=kOutput, calls=%fused_computation.9 | convolution fusion | flops 1881137152 | bytes 12025856 | tf_op jit(solution)/shard_map/dot_general | solution.py:72
  179.0 2.3 multiply_convert_fusion
  181.3 7.3 %fusion.24 = f32[1024,256]{1,0:T(8,128)} fusion(bf16[1024,4096]{1,0:T(8,128)(2,1)} %all-gather.2.cloned.1.call-done, bf16[4096,256]{1,0:T(8,128)(2,1)} %param.11), kind=kOutput, calls=%fused_computation.48 | convolution fusion | flops 2147483648 | bytes 11534336 | tf_op jit(solution)/shard_map/dot_general | solution.py:37
  188.6 1.7 reshape.139
  190.3 2.0 multiply_reduce_fusion.1
  192.3 1.2 copy.69
  193.6 1.0 copy.70
  194.6 2.9 multiply_convert_fusion.1
  197.6 1.0 fusion.5
  198.6 0.6 copy-done.4
  199.2 0.8 fusion.9
  200.0 0.5 copy.75
  200.5 8.1 %fusion.16 = f32[1024,4096]{1,0:T(8,128)} fusion(bf16[256,4096]{1,0:T(8,128)(2,1)S(1)} %copy-done, bf16[128,8,2,128]{3,2,1,0:T(2,128)(2,1)S(1)} %bitcast.46), kind=kOutput, calls=%fused_computation.25 | convolution fusion | flops 2147483648 | bytes 19398656 | tf_op jit(solution)/shard_map/dot_general | solution.py:96
  208.6 102.1 %reduce-scatter.2.cloned.1.call-done = f32[1024,256]{1,0:T(8,128)} async-done(((f32[1024,4096]{1,0:T(8,128)}), f32[1024,256]{1,0:T(8,128)}) %reduce-scatter.2.cloned.1.call-update) | async-done | bytes 1048592 | tf_op jit(solution)/shard_map/reduce_scatter | solution.py:97
  310.7 2.1 convert_element_type.42
  (31 shorter events, 0.3 us)
Async XLA Ops:
  6.5 194.0 %copy-start = (bf16[256,4096]{1,0:T(8,128)(2,1)S(1)}, bf16[256,4096]{1,0:T(8,128)(2,1)}, u32[]{:S(2)}) copy-start(bf16[256,4096]{1,0:T(8,128)(2,1)} %param.14) | copy-start | bytes 6291460
  6.5 15.6 %copy-start.1 = (s32[8]{0:T(128)S(1)}, s32[8]{0:T(128)}, u32[]{:S(2)}) copy-start(s32[8]{0:T(128)} %param.17) | copy-start | bytes 100
  6.5 174.8 %all-gather.2.cloned.1.call-start = ((), (), s32[]{:S(2)}) async-start(), calls=%async_computation.4 | async-start | bytes 8912896 | tf_op jit(solution)/shard_map/all_gather | solution.py:38
  22.2 6.8 %copy-start.2 = (f32[8,7]{1,0:T(8,128)S(1)}, f32[8,7]{1,0:T(8,128)}, u32[]{:S(2)}) copy-start(f32[8,7]{1,0:T(8,128)} %param.16) | copy-start | bytes 676
  23.6 20.2 %all-to-all-start.2 = ((s32[16,1,2]{2,1,0:T(1,128)}), s32[16,1,2]{2,1,0:T(1,128)S(1)}, u32[]{:S(2)}, u32[]{:S(2)}) async-start(s32[16,1,2]{2,1,0:T(1,128)} %bitcast.9), calls=%async_computation.2 | async-start | bytes 16384 | tf_op jit(solution)/shard_map/all_to_all | solution.py:68
  43.8 7.4 %copy-start.6 = (s32[16,2]{0,1:T(2,128)S(1)}, s32[16,2]{0,1:T(2,128)}, u32[]{:S(2)}) copy-start(s32[16,2]{0,1:T(2,128)} %param.18) | copy-start | bytes 388
  43.8 7.6 %copy-start.5 = (bf16[896,256]{1,0:T(8,128)(2,1)S(1)}, bf16[896,256]{1,0:T(8,128)(2,1)}, u32[]{:S(2)}) copy-start(bf16[896,256]{1,0:T(8,128)(2,1)} %param.12) | copy-start | bytes 1376260
  43.8 112.0 %all-to-all-start.1 = ((bf16[16,2,128,896]{3,2,1,0:T(8,128)(2,1)}), bf16[16,2,128,896]{3,2,1,0:T(8,128)(2,1)}, u32[]{:S(2)}, u32[]{:S(2)}) async-start(bf16[16,2,128,896]{3,2,1,0:T(8,128)(2,1)} %fusion), calls=%async_computation.1 | async-start | bytes 14680064 | tf_op jit(solution)/shard_map/all_to_all | solution.py:67
  51.1 259.5 %reduce-scatter.2.cloned.1.call-start = ((), (), s32[]{:S(2)}) async-start(), calls=%async_computation.5 | async-start | bytes 17825792 | tf_op jit(solution)/shard_map/reduce_scatter | solution.py:97
  194.6 3.0 copy-start.3
  197.6 1.6 copy-start.4
Sparse Core Ops, SparseCore 0:
  9.1 66.7 all-gather.1
  208.8 101.8 reduce-scatter.1
where the time goes:
time: 321 us; the launch traced here: 320 us
  waiting for transfers between devices  205 us (64%)
  matrix products  28.9 us (9%)
  local copies, waits for them, and re-layouts  28.6 us (9%)
  other arithmetic  18.4 us (6%)
  between operations  13.6 us (4%)
  starting transfers between devices  12.8 us (4%)
  blocking collectives  12.5 us (4%)
    reduce_scatter x1, waiting for transfers between devices, local(): lax.psum_scatter(partial_out, 'head', scatter_dimension=1, tiled=True)  102 us
    all_to_all x1, waiting for transfers between devices, local(): lax.all_to_all(encoded, 'db', split_axis=0, concat_axis=0, tiled=True)  102 us
    all_to_all x1, blocking collectives, local(): lax.all_to_all(request_table, 'db', split_axis=0, concat_axis=0, tiled=True)  12.5 us
    convert_element_type x1, other arithmetic, local(): encoded = (grouped * scale_rows[:, :, None, :, None]).reshape(shards, ite...  8.17 us
    dot_general x1, matrix products, local(): jnp.dot(attended, out_weight, preferred_element_type=jnp.float32)  8.07 us
    gather x1, local copies, waits for them, and re-layouts, local(): encoded_back.reshape(shards * capacity, NBR_LEN, ENC)[slot_index]  7.47 us
    all_to_all x1, starting transfers between devices, local(): lax.all_to_all(encoded, 'db', split_axis=0, concat_axis=0, tiled=True)  7.35 us
    dot_general x1, matrix products, local(): jnp.dot(lax.all_gather(tokens, 'head', axis=1, tiled=True), query_weight,...  7.29 us
  transfers between devices with their start and end apart: 4, of which 2 were waited for; matrix products, arithmetic and copies ran while one was open for 14% of the time, Pallas kernels for 0%

commit v1 on v0

v1 whole, which is shorter than its diff:
```python
import math

import jax
import jax.numpy as jnp
from jax import lax
from jax.experimental import pallas as pl
from jax.experimental.pallas import tpu as pltpu
from jax.sharding import Mesh
from jax.sharding import PartitionSpec as P

HD = 128
ENC = 896
GROUP = 128
SPAN = 64
NBR_LEN = 128
NBRS = 2
DB = ("y", "x")
F32 = jnp.float32
BF16 = jnp.bfloat16
VMEM = pl.BlockSpec(memory_space=pltpu.VMEM)
SMEM = pl.BlockSpec(memory_space=pltpu.SMEM)
ANY = pl.BlockSpec(memory_space=pl.ANY)


def unit(values):
    return values * lax.rsqrt(jnp.mean(values * values, axis=-1, keepdims=True) + 1e-06)


def project_kernel(scales_ref, codes_ref, key_ref, value_ref, out_ref, enc_ref):
    step = pl.program_id(0)
    blocks = codes_ref.shape[0]
    for b in range(blocks):
        for g in range(ENC // GROUP):
            cols = slice(g * GROUP, (g + 1) * GROUP)
            scaled = codes_ref[b, :, cols].astype(F32) * scales_ref[step * blocks + b, g]
            enc_ref[b * NBR_LEN : (b + 1) * NBR_LEN, cols] = scaled.astype(BF16)
    enc = enc_ref[...]
    keys = jnp.dot(enc, key_ref[...], preferred_element_type=F32)
    values = jnp.dot(enc, value_ref[...], preferred_element_type=F32).astype(BF16)
    width = key_ref.shape[1]
    for b in range(blocks):
        rows = slice(b * NBR_LEN, (b + 1) * NBR_LEN)
        for h in range(width // HD):
            cols = slice(h * HD, (h + 1) * HD)
            out_ref[b, :, cols] = unit(keys[rows, cols]).astype(BF16)
        out_ref[b, :, width : 2 * width] = values[rows]


def project_blocks(codes, scales, key_weight, value_weight):
    count, width, per = codes.shape[0], key_weight.shape[1], 2
    return pl.pallas_call(
        project_kernel,
        grid=(count // per,),
        out_shape=jax.ShapeDtypeStruct((count, NBR_LEN, 2 * width), BF16),
        in_specs=[
            SMEM,
            pl.BlockSpec((per, NBR_LEN, ENC), lambda i: (i, 0, 0)),
            pl.BlockSpec((ENC, width), lambda i: (0, 0)),
            pl.BlockSpec((ENC, width), lambda i: (0, 0)),
        ],
        out_specs=pl.BlockSpec((per, NBR_LEN, 2 * width), lambda i: (i, 0, 0)),
        scratch_shapes=[pltpu.VMEM((per * NBR_LEN, ENC), BF16)],
        cost_estimate=pl.CostEstimate(
            flops=2 * count * NBR_LEN * ENC * 2 * width, bytes_accessed=5 << 20, transcendentals=0
        ),
        name="project_blocks",
    )(scales, codes, key_weight, value_weight)


def select_kernel(wanted_ref, rows_ref, out_ref, sems):
    shards, items = wanted_ref.shape
    copies = []
    for e in range(shards):
        for s in range(items):
            copy = pltpu.make_async_copy(
                rows_ref.at[wanted_ref[e, s]], out_ref.at[e, s], sems.at[e, s]
            )
            copy.start()
            copies.append(copy)
    for copy in copies:
        copy.wait()


def select_blocks(wanted, rows):
    shards, items = wanted.shape
    return pl.pallas_call(
        select_kernel,
        out_shape=jax.ShapeDtypeStruct((shards, items) + rows.shape[1:], BF16),
        in_specs=[SMEM, VMEM],
        out_specs=ANY,
        scratch_shapes=[pltpu.SemaphoreType.DMA((shards, items))],
        cost_estimate=pl.CostEstimate(flops=0, bytes_accessed=9 << 20, transcendentals=0),
        name="select_blocks",
    )(wanted, rows)


def query_kernel(tokens_ref, weight_ref, out_ref):
    projected = jnp.dot(tokens_ref[...], weight_ref[...], preferred_element_type=F32)
    for h in range(weight_ref.shape[1] // HD):
        cols = slice(h * HD, (h + 1) * HD)
        out_ref[:, cols] = unit(projected[:, cols]).astype(BF16)


def project_queries(tokens, weight):
    rows, depth = tokens.shape
    width, tile = weight.shape[1], 128
    return pl.pallas_call(
        query_kernel,
        grid=(rows // tile,),
        out_shape=jax.ShapeDtypeStruct((rows, width), BF16),
        in_specs=[
            pl.BlockSpec((tile, depth), lambda i: (i, 0)),
            pl.BlockSpec((depth, width), lambda i: (0, 0)),
        ],
        out_specs=pl.BlockSpec((tile, width), lambda i: (i, 0)),
        compiler_params=pltpu.CompilerParams(vmem_limit_bytes=24 << 20),
        cost_estimate=pl.CostEstimate(
            flops=2 * rows * depth * width, bytes_accessed=11 << 20, transcendentals=0
        ),
        name="project_queries",
    )(tokens, weight)


def attend_kernel(slot_ref, length_ref, query_ref, rows_ref, out_ref, held_ref, sems):
    requests = held_ref.shape[0]
    width = query_ref.shape[1]
    factor = 2.0 / math.sqrt(HD)
    copies = []
    for r in range(requests):
        copy = pltpu.make_async_copy(rows_ref.at[slot_ref[r]], held_ref.at[r], sems.at[r])
        copy.start()
        copies.append(copy)
    places = lax.broadcasted_iota(jnp.int32, (SPAN, NBR_LEN), 1)
    for c in range(requests // NBRS):
        for n in range(NBRS):
            copies[c * NBRS + n].wait()
        spans = slice(c * SPAN, (c + 1) * SPAN)
        for h in range(width // HD):
            cols = slice(h * HD, (h + 1) * HD)
            query = query_ref[spans, cols]
            raised = []
            for n in range(NBRS):
                scores = lax.dot_general(
                    query,
                    held_ref[c * NBRS + n, :, cols],
                    (((1,), (1,)), ((), ())),
                    preferred_element_type=F32,
                )
                raised.append(
                    jnp.where(
                        places < length_ref[c * NBRS + n], jnp.exp(scores * factor), 0.0
                    )
                )
            total = sum(jnp.sum(part, axis=-1, keepdims=True) for part in raised)
            scale = 1.0 / total
            result = jnp.zeros((SPAN, HD), F32)
            for n in range(NBRS):
                result += jnp.dot(
                    (raised[n] * scale).astype(BF16),
                    held_ref[c * NBRS + n, :, width + h * HD : width + (h + 1) * HD],
                    preferred_element_type=F32,
                )
            out_ref[spans, cols] = result.astype(BF16)


def attend(slot_index, lengths, queries, rows):
    requests = slot_index.shape[0]
    return pl.pallas_call(
        attend_kernel,
        out_shape=jax.ShapeDtypeStruct(queries.shape, BF16),
        in_specs=[SMEM, SMEM, VMEM, ANY],
        out_specs=VMEM,
        scratch_shapes=[
            pltpu.VMEM((requests,) + rows.shape[1:], BF16),
            pltpu.SemaphoreType.DMA((requests,)),
        ],
        compiler_params=pltpu.CompilerParams(vmem_limit_bytes=24 << 20),
        cost_estimate=pl.CostEstimate(
            flops=4 * queries.shape[0] * NBRS * NBR_LEN * queries.shape[1],
            bytes_accessed=6 << 20,
            transcendentals=0,
        ),
        name="attend",
    )(slot_index, lengths, queries, rows)


def reduce_ring(attended, own_weight, partner_attended, partner_weight, ring):
    rows = attended.shape[0] // 2
    stacked = jnp.concatenate([attended, partner_attended], axis=1)
    up = [(i, (i + 1) % ring) for i in range(ring)]
    down = [(i, (i - 1) % ring) for i in range(ring)]
    weight = jnp.concatenate([own_weight, partner_weight], axis=0)

    def share(half, step):
        return jnp.dot(
            stacked[half * rows : (half + 1) * rows],
            weight[:, step % ring],
            preferred_element_type=F32,
        )

    far = ring // 2
    chains = [(0, 1, far), (1, -1, far), (1, 1, far - 1), (0, -1, far - 1)]
    held = {}
    for distance in range(far, 0, -1):
        for half, way, first in chains:
            if distance > first:
                continue
            part = share(half, way * distance)
            if distance < first:
                part = part + held[half, way].astype(F32)
            held[half, way] = lax.ppermute(part.astype(BF16), "z", up if way == 1 else down)
    out = [
        (share(half, 0) + held[half, 1].astype(F32) + held[half, -1].astype(F32)).astype(BF16)
        for half in range(2)
    ]
    return jnp.concatenate(out, axis=0)


def local(
    tokens,
    query_weight,
    key_weight,
    value_weight,
    out_weight,
    codes,
    scales,
    block_len,
    nbr_owner,
    nbr_block,
):
    width = query_weight.shape[1]
    ring = lax.axis_size("z")
    cores = lax.axis_size("c")
    shards = lax.axis_size(DB)
    here, core = lax.axis_index("z"), lax.axis_index("c")
    swap = [(i, (i + 1) % cores) for i in range(cores)]

    gathered = lax.all_gather(tokens, ("z", "c"), axis=1, tiled=True)

    owners = nbr_owner.reshape(-1)
    wanted_blocks = nbr_block.reshape(-1)
    order = jnp.arange(owners.shape[0], dtype=jnp.int32)
    earlier = jnp.sum(
        ((owners[:, None] == owners[None, :]) & (order[:, None] > order[None, :])).astype(jnp.int32),
        axis=1,
    )
    slot_index = owners * NBRS + earlier
    slots = jnp.arange(shards * NBRS, dtype=jnp.int32)
    request_table = jnp.sum(
        jnp.where(slot_index[:, None] == slots[None, :], wanted_blocks[:, None], 0), axis=0
    ).reshape(shards, NBRS)
    notes = jnp.concatenate(
        [request_table, jnp.broadcast_to(block_len[None, :], (shards, block_len.shape[0]))], axis=1
    )
    heard = lax.all_to_all(notes, DB, split_axis=0, concat_axis=0, tiled=True)
    wanted = heard[:, :NBRS]
    all_lengths = heard[:, NBRS:].reshape(-1)
    block_ids = owners * block_len.shape[0] + wanted_blocks
    ids = jnp.arange(all_lengths.shape[0], dtype=jnp.int32)
    lengths = jnp.sum(
        jnp.where(block_ids[:, None] == ids[None, :], all_lengths[None, :], 0), axis=1
    )

    projected = project_blocks(codes, scales, key_weight, value_weight)
    sent = select_blocks(wanted, projected)
    rows = lax.all_to_all(sent, DB, split_axis=0, concat_axis=0, tiled=True)
    rows = rows.reshape(shards * NBRS, NBR_LEN, 2 * width)

    by_core = out_weight.reshape(width, ring, cores, width)
    own_weight = lax.dynamic_index_in_dim(by_core, core, 2, keepdims=False)
    lent_weight = lax.dynamic_index_in_dim(by_core, 1 - core, 2, keepdims=False)
    partner_weight = lax.ppermute(lent_weight, "c", swap)
    twice = jnp.concatenate([own_weight, own_weight], axis=1)
    own_weight = lax.dynamic_slice_in_dim(twice, here, ring, 1)
    twice = jnp.concatenate([partner_weight, partner_weight], axis=1)
    partner_weight = lax.dynamic_slice_in_dim(twice, here, ring, 1)

    queries = project_queries(gathered, query_weight)
    attended = attend(slot_index, lengths, queries, rows)
    partner_attended = lax.ppermute(attended, "c", swap)
    return reduce_ring(attended, own_weight, partner_attended, partner_weight, ring)


def solution(mesh):
    grid = Mesh(mesh.devices.reshape(4, 4, 8, 2), ("y", "x", "z", "c"))
    head = ("z", "c")
    placed = (
        P(DB, head),
        P(None, head),
        P(None, head),
        P(None, head),
        P(head, None),
        P(DB, None, None),
        P(DB, None),
        P(DB),
        P(DB, None),
        P(DB, None),
    )
    return jax.shard_map(
        local, mesh=grid, in_specs=placed, out_specs=P(DB, head), check_vma=False
    )
```

time: 321 us -> 179 us (0.56)
  waiting for transfers between devices: 205 us -> 62.3 us
  starting transfers between devices: 12.8 us -> 38.5 us
  Pallas kernels: 0 us -> 25.1 us
  matrix products: 28.9 us -> 4.75 us
  local copies, waits for them, and re-layouts: 28.6 us -> 15.5 us
  blocking collectives: 12.5 us -> 0 us
    reduce_scatter x1 -> x0, waiting for transfers between devices: 102 us -> none  [local(): lax.psum_scatter(partial_out, 'head', scatter_dimension=1, tiled=True)]
    all_to_all x2, waiting for transfers between devices: 102 us -> 11.8 us  [the longest x1 11.2 us: local(): rows = lax.all_to_all(sent, DB, split_axis=0, concat_axis=0, tiled=True)]
    all_gather x1, waiting for transfers between devices: 0.01 us -> 25.9 us  [local(): gathered = lax.all_gather(tokens, ('z', 'c'), axis=1, tiled=True)]
    pallas_call x0 -> x4, Pallas kernels: none -> 25.1 us  [the longest x1 12.3 us: attend(): pl.pallas_call(attend_kernel, out_shape=jax.ShapeDtypeStruct(queries.shap...]
    ppermute x0 -> x16, starting transfers between devices: none -> 24.7 us  [the longest x14 24.6 us: reduce_ring(): lax.ppermute(part.astype(BF16), 'z', up if way == 1 else down)]
    dot_general x6 -> x16, matrix products: 28.9 us -> 4.75 us  [share(): jnp.dot(stacked[half * rows:(half + 1) * rows], weight[:, step % ring], p...]
    ppermute x0 -> x16, waiting for transfers between devices: none -> 23.9 us  [the longest x14 23.9 us: reduce_ring(): lax.ppermute(part.astype(BF16), 'z', up if way == 1 else down)]
    concatenate x0 -> x6, other arithmetic: none -> 17.3 us  [the longest x1 9.09 us: reduce_ring(): weight = jnp.concatenate([own_weight, partner_weight], axis=0)]
  transfers between devices with their start and end apart: 4 -> 19, of which waited for: 2 -> 15; matrix products, arithmetic and copies ran while one was open for 14% -> 18% of each run, Pallas kernels for 0% -> 7%
where the time goes in v1:
time: 179 us; the launch traced here: 178 us
  waiting for transfers between devices  62.3 us (35%)
  starting transfers between devices  38.5 us (22%)
  Pallas kernels  25.1 us (14%)
  other arithmetic  17.8 us (10%)
  local copies, waits for them, and re-layouts  15.5 us (9%)
  between operations  13.7 us (8%)
  matrix products  4.75 us (3%)
    all_gather x1, waiting for transfers between devices, local(): gathered = lax.all_gather(tokens, ('z', 'c'), axis=1, tiled=True)  25.9 us
    ppermute x14, starting transfers between devices, reduce_ring(): lax.ppermute(part.astype(BF16), 'z', up if way == 1 else down)  24.6 us
    ppermute x14, waiting for transfers between devices, reduce_ring(): lax.ppermute(part.astype(BF16), 'z', up if way == 1 else down)  23.9 us
    pallas_call x1, Pallas kernels, attend(): pl.pallas_call(attend_kernel, out_shape=jax.ShapeDtypeStruct(queries.shap...  12.3 us
    all_to_all x1, waiting for transfers between devices, local(): rows = lax.all_to_all(sent, DB, split_axis=0, concat_axis=0, tiled=True)  11.2 us
    concatenate x1, other arithmetic, reduce_ring(): weight = jnp.concatenate([own_weight, partner_weight], axis=0)  9.09 us
    unnamed x15, local copies, waits for them, and re-layouts  8.8 us
    all_to_all x1, starting transfers between devices, local(): heard = lax.all_to_all(notes, DB, split_axis=0, concat_axis=0, tiled=True)  7.17 us
  transfers between devices with their start and end apart: 19, of which 15 were waited for; matrix products, arithmetic and copies ran while one was open for 18% of the time, Pallas kernels for 7%

profile of v1, /device:TPU:24, one launch (start us, length us, event | category | flops | bytes accessed | tf_op | source)
XLA Modules:
  0.0 177.7 jit_solution(2035114842356428611)
XLA Ops:
  6.5 0.7 all-gather.2.cloned.1.call-update
  7.3 0.8 copy.26
  8.1 0.8 copy.25
  9.3 0.7 pad.11.clone
  10.1 0.6 pad_add_fusion
  10.7 7.2 %all-to-all-start = ((s32[16,1,10]{2,1,0:T(1,128)}), s32[16,1,10]{2,1,0:T(1,128)S(1)}, u32[]{:S(2)}, u32[]{:S(2)}) async-start(s32[16,1,10]{2,1,0:T(1,128)} %bitcast), calls=%async_computation | async-start | bytes 16384 | tf_op jit(solution)/shard_map/all_to_all | solution.py:255
  17.8 4.9 %project_blocks.1.rows_ref = bf16[8,128,512]{2,1,0:T(8,128)(2,1)} custom-call(f32[8,7]{1,0:T(8,128)} %scales_ref.1, bf16[8,128,896]{2,1,0:T(8,128)(2,1)} %codes_ref.1, bf16[896,256]{1,0:T(8,128)(2,1)} %key_ref.1, bf16[896,256]{1,0:T(8,128)(2,1)} %value_ref.1), custom_call_target="tpu_custom_call" | custom-call | flops 939524096 | bytes 5242880 | tf_op jit(solution)/shard_map/project_blocks/pallas_call | solution.py:51
  22.7 0.6 all-to-all-done
  23.3 0.6 copy-done.4
  23.9 3.5 %select_blocks.1 = bf16[16,2,128,512]{3,2,1,0:T(8,128)(2,1)} custom-call(s32[16,2]{1,0:T(8,128)} %bitcast.65, bf16[8,128,512]{2,1,0:T(8,128)(2,1)} %project_blocks.1.rows_ref), custom_call_target="tpu_custom_call" | custom-call | bytes 9437184 | tf_op jit(solution)/shard_map/select_blocks/pallas_call | solution.py:86
  27.5 6.6 %all-to-all-start.1 = ((bf16[16,2,128,512]{3,2,1,0:T(8,128)(2,1)}), bf16[16,2,128,512]{3,2,1,0:T(8,128)(2,1)}, u32[]{:S(2)}, u32[]{:S(2)}) async-start(bf16[16,2,128,512]{3,2,1,0:T(8,128)(2,1)} %select_blocks.1), calls=%async_computation.1 | async-start | bytes 8388608 | tf_op jit(solution)/shard_map/all_to_all | solution.py:266
  34.1 3.3 %copy.27 = bf16[256,4096]{0,1:T(8,128)(2,1)S(1)} copy(bf16[256,4096]{1,0:T(8,128)(2,1)} %param.14) | data formatting | bytes 4194304 | tf_op args[4]
  37.4 1.2 constant_dynamic-slice_fusion
  38.6 2.6 %copy.29 = bf16[256,8,1,256]{3,1,0,2:T(8,128)(2,1)} copy(bf16[256,8,1,256]{0,3,2,1:T(8,128)(2,1)} %get-tuple-element.13) | data formatting | bytes 2097152 | tf_op jit(solution)/shard_map/jit(dynamic_index_in_dim)/dynamic_slice | solution.py:271
  41.2 1.8 %copy.28 = bf16[256,8,1,256]{3,1,0,2:T(8,128)(2,1)} copy(bf16[256,8,1,256]{0,3,2,1:T(8,128)(2,1)S(1)} %get-tuple-element.14) | data formatting | bytes 2097152 | tf_op jit(solution)/shard_map/jit(dynamic_index_in_dim)/dynamic_slice | solution.py:270
  43.0 3.4 %fusion.15 = bf16[256,8,256]{2,1,0:T(8,128)(2,1)} fusion(s32[]{:T(128)S(6)} %select_n.22, bf16[256,8,256]{2,1,0:T(8,128)(2,1)} %bitcast.64), kind=kLoop, calls=%fused_computation.49 | loop fusion | flops 2097152 | bytes 2097156 | tf_op jit(solution)/shard_map/concatenate | solution.py:273
  46.8 3.3 %fusion.14 = bf16[256,8,256]{2,1,0:T(8,128)(2,1)} fusion(s32[]{:T(128)S(6)} %select_n.22, bf16[256,8,256]{2,1,0:T(8,128)(2,1)} %collective-permute-done.1), kind=kLoop, calls=%fused_computation.48 | loop fusion | flops 2097152 | bytes 2097156 | tf_op jit(solution)/shard_map/concatenate | solution.py:275
  50.1 25.9 %all-gather.2.cloned.1.call-done.tokens_ref = bf16[1024,4096]{1,0:T(8,128)(2,1)} async-done(((bf16[1024,256]{1,0:T(8,128)(2,1)}), bf16[1024,4096]{1,0:T(8,128)(2,1)}) %all-gather.2.cloned.1.call-update) | async-done | bytes 8388624 | tf_op jit(solution)/shard_map/all_gather | solution.py:238
  76.0 3.4 %copy-done = bf16[1024,4096]{1,0:T(8,128)(2,1)S(1)} copy-done((bf16[1024,4096]{1,0:T(8,128)(2,1)S(1)}, bf16[1024,4096]{1,0:T(8,128)(2,1)}, u32[]{:S(2)}) %copy-start) | copy-done | bytes 8388632
  79.4 4.5 %project_queries.1.query_ref = bf16[1024,256]{1,0:T(8,128)(2,1)S(1)} custom-call(bf16[1024,4096]{1,0:T(8,128)(2,1)S(1)} %copy-done, bf16[4096,256]{1,0:T(8,128)(2,1)S(1)} %copy-done.1), custom_call_target="tpu_custom_call" | custom-call | flops 2147483648 | bytes 11534336 | tf_op jit(solution)/shard_map/project_queries/pallas_call | solution.py:107
  83.8 11.2 %all-to-all-done.1 = bf16[16,2,128,512]{3,2,1,0:T(8,128)(2,1)} async-done(((bf16[16,2,128,512]{3,2,1,0:T(8,128)(2,1)}), bf16[16,2,128,512]{3,2,1,0:T(8,128)(2,1)}, u32[]{:S(2)}, u32[]{:S(2)}) %all-to-all-start.1) | async-done | bytes 4194336 | tf_op jit(solution)/shard_map/all_to_all | solution.py:266
  95.0 12.3 %attend.1 = bf16[1024,256]{1,0:T(8,128)(2,1)S(1)} custom-call(s32[32]{0:T(128)S(1)} %get-tuple-element.18.slot_ref, s32[32]{0:T(128)S(1)} %select_reduce_fusion.length_ref, bf16[1024,256]{1,0:T(8,128)(2,1)S(1)} %project_queries.1.query_ref, bf16[32,128,512]{2,1,0:T(8,128)(2,1)} %bitcast.2.rows_ref), custom_call_target="tpu_custom_call" | custom-call | flops 268435456 | bytes 6291456 | tf_op jit(solution)/shard_map/attend/pallas_call | solution.py:168
  107.4 9.1 %fusion.18 = (bf16[512,1,256]{2,1,0:T(2,128)(2,1)S(1)}, bf16[512,1,256]{2,1,0:T(2,128)(2,1)S(1)}, bf16[512,1,256]{2,1,0:T(2,128)(2,1)S(1)}, bf16[512,1,256]{2,1,...) fusion(bf16[256,8,256]{2,1,0:T(8,128)(2,1)S(1)} %copy-done.2, ...), kind=kLoop, calls=%fused_computation.54 | loop fusion | flops 4194304 | bytes 4194304 | tf_op jit(solution)/shard_map/concatenate | solution.py:192
  116.6 0.3 convolution_convert_fusion
  116.9 5.5 %collective-permute-start.12 = (bf16[512,256]{1,0:T(8,128)(2,1)S(1)}, bf16[512,256]{1,0:T(8,128)(2,1)S(1)}, u32[]{:S(2)}, u32[]{:S(2)}) collective-permute-start(bf16[512,256]{1,0:T(8,128)(2,1)S(1)} %convolution_convert_fusion), channel_id=1, source_target_pairs={{0,14},{2,0},{4,2},{6,4},{8,6},{10,8},{12,10},{14,12},{1,15},{3,1}... | collective-permute-start | bytes 786440 | tf_op jit(solution)/shard_map/ppermute | solution.py:211
  122.4 0.3 convolution_convert_fusion.1
  123.3 0.3 convolution_convert_fusion.2
  123.6 3.3 %collective-permute-start.6 = (bf16[512,256]{1,0:T(8,128)(2,1)S(1)}, bf16[512,256]{1,0:T(8,128)(2,1)S(1)}, u32[]{:S(2)}, u32[]{:S(2)}) collective-permute-start(bf16[512,256]{1,0:T(8,128)(2,1)S(1)} %convolution_convert_fusion.2), channel_id=1, source_target_pairs={{0,14},{2,0},{4,2},{6,4},{8,6},{10,8},{12,10},{14,12},{1,15},{3,1}... | collective-permute-start | bytes 786440 | tf_op jit(solution)/shard_map/ppermute | solution.py:211
  126.9 2.1 %collective-permute-done.12 = bf16[512,256]{1,0:T(8,128)(2,1)S(1)} collective-permute-done((bf16[512,256]{1,0:T(8,128)(2,1)S(1)}, bf16[512,256]{1,0:T(8,128)(2,1)S(1)}, u32[]{:S(2)}, u32[]{:S(2)}) %collective-permute-start.12) | collective-permute-done | bytes 262176 | tf_op jit(solution)/shard_map/ppermute | solution.py:211
  129.3 3.8 %collective-permute-start.13 = (bf16[512,256]{1,0:T(8,128)(2,1)S(1)}, bf16[512,256]{1,0:T(8,128)(2,1)S(1)}, u32[]{:S(2)}, u32[]{:S(2)}) collective-permute-start(bf16[512,256]{1,0:T(8,128)(2,1)S(1)} %fusion.13), channel_id=1, source_target_pairs={{0,14},{2,0},{4,2},{6,4},{8,6},{10,8},{12,10},{14,12},{1,15},{3,1}... | collective-permute-start | bytes 786440 | tf_op jit(solution)/shard_map/ppermute | solution.py:211
  133.3 0.3 fusion.10
  133.7 0.9 collective-permute-done.6
  135.0 3.8 %collective-permute-start.7 = (bf16[512,256]{1,0:T(8,128)(2,1)S(1)}, bf16[512,256]{1,0:T(8,128)(2,1)S(1)}, u32[]{:S(2)}, u32[]{:S(2)}) collective-permute-start(bf16[512,256]{1,0:T(8,128)(2,1)S(1)} %fusion.8), channel_id=1, source_target_pairs={{0,14},{2,0},{4,2},{6,4},{8,6},{10,8},{12,10},{14,12},{1,15},{3,1}... | collective-permute-start | bytes 786440 | tf_op jit(solution)/shard_map/ppermute | solution.py:211
  138.9 0.3 fusion.6
  139.3 0.9 collective-permute-done.13
  140.3 0.3 fusion.12
  140.6 3.8 %collective-permute-start.14 = (bf16[512,256]{1,0:T(8,128)(2,1)S(1)}, bf16[512,256]{1,0:T(8,128)(2,1)S(1)}, u32[]{:S(2)}, u32[]{:S(2)}) collective-permute-start(bf16[512,256]{1,0:T(8,128)(2,1)S(1)} %fusion.12), channel_id=1, source_target_pairs={{0,14},{2,0},{4,2},{6,4},{8,6},{10,8},{12,10},{14,12},{1,15},{3,1}... | collective-permute-start | bytes 786440 | tf_op jit(solution)/shard_map/ppermute | solution.py:211
  145.0 5.2 %collective-permute-done.3 = bf16[512,256]{1,0:T(8,128)(2,1)S(1)} collective-permute-done((bf16[512,256]{1,0:T(8,128)(2,1)S(1)}, bf16[512,256]{1,0:T(8,128)(2,1)S(1)}, u32[]{:S(2)}, u32[]{:S(2)}) %collective-permute-start.3) | collective-permute-done | bytes 262176 | tf_op jit(solution)/shard_map/ppermute | solution.py:211
  150.6 0.5 collective-permute-done.14
  151.4 3.8 %collective-permute-start.15 = (bf16[512,256]{1,0:T(8,128)(2,1)S(1)}, bf16[512,256]{1,0:T(8,128)(2,1)S(1)}, u32[]{:S(2)}, u32[]{:S(2)}) collective-permute-start(bf16[512,256]{1,0:T(8,128)(2,1)S(1)} %fusion.11), channel_id=1, source_target_pairs={{0,14},{2,0},{4,2},{6,4},{8,6},{10,8},{12,10},{14,12},{1,15},{3,1}... | collective-permute-start | bytes 786440 | tf_op jit(solution)/shard_map/ppermute | solution.py:211
  155.1 0.3 fusion.7
  155.5 5.1 %collective-permute-done.4 = bf16[512,256]{1,0:T(8,128)(2,1)S(1)} collective-permute-done((bf16[512,256]{1,0:T(8,128)(2,1)S(1)}, bf16[512,256]{1,0:T(8,128)(2,1)S(1)}, u32[]{:S(2)}, u32[]{:S(2)}) %collective-permute-start.4) | collective-permute-done | bytes 262176 | tf_op jit(solution)/shard_map/ppermute | solution.py:211
  161.0 0.8 collective-permute-done.15
  161.9 0.3 fusion.3
  162.2 4.0 %collective-permute-done.8 = bf16[512,256]{1,0:T(8,128)(2,1)S(1)} collective-permute-done((bf16[512,256]{1,0:T(8,128)(2,1)S(1)}, bf16[512,256]{1,0:T(8,128)(2,1)S(1)}, u32[]{:S(2)}, u32[]{:S(2)}) %collective-permute-start.8) | collective-permute-done | bytes 262176 | tf_op jit(solution)/shard_map/ppermute | solution.py:211
  166.1 3.6 %collective-permute-done.5 = bf16[512,256]{1,0:T(8,128)(2,1)S(1)} collective-permute-done((bf16[512,256]{1,0:T(8,128)(2,1)S(1)}, bf16[512,256]{1,0:T(8,128)(2,1)S(1)}, u32[]{:S(2)}, u32[]{:S(2)}) %collective-permute-start.5) | collective-permute-done | bytes 262176 | tf_op jit(solution)/shard_map/ppermute | solution.py:211
  169.8 0.3 fusion.2
  170.1 0.8 pad_maximum_fusion.2
  (45 shorter events, 4.6 us)
Async XLA Ops:
  6.5 69.5 %all-gather.2.cloned.1.call-start = ((), (), s32[]{:S(2)}) async-start(), calls=%async_computation.2 | async-start | bytes 8912896 | tf_op jit(solution)/shard_map/all_gather | solution.py:238
  10.7 12.7 %all-to-all-start = ((s32[16,1,10]{2,1,0:T(1,128)}), s32[16,1,10]{2,1,0:T(1,128)S(1)}, u32[]{:S(2)}, u32[]{:S(2)}) async-start(s32[16,1,10]{2,1,0:T(1,128)} %bitcast), calls=%async_computation | async-start | bytes 16384 | tf_op jit(solution)/shard_map/all_to_all | solution.py:255
  23.3 0.6 copy-start.4
  27.5 67.5 %all-to-all-start.1 = ((bf16[16,2,128,512]{3,2,1,0:T(8,128)(2,1)}), bf16[16,2,128,512]{3,2,1,0:T(8,128)(2,1)}, u32[]{:S(2)}, u32[]{:S(2)}) async-start(bf16[16,2,128,512]{3,2,1,0:T(8,128)(2,1)} %select_blocks.1), calls=%async_computation.1 | async-start | bytes 8388608 | tf_op jit(solution)/shard_map/all_to_all | solution.py:266
  41.2 5.6 %collective-permute-start.1 = (bf16[256,8,256]{2,1,0:T(8,128)(2,1)}, bf16[256,8,256]{2,1,0:T(8,128)(2,1)}, u32[]{:S(2)}, u32[]{:S(2)}) collective-permute-start(bf16[256,8,256]{2,1,0:T(8,128)(2,1)} %bitcast.5), channel_id=1, source_target_pairs={{0,1},{1,0},{2,3},{3,2},{4,5},{5,4},{6,7},{7,6},{8,9},{9,8},{10,11... | collective-permute-start | bytes 3145736 | tf_op jit(solution)/shard_map/ppermute | solution.py:272
  41.2 5.2 %copy-start.5 = (s32[16,1,10]{2,1,0:T(1,128)S(1)}, s32[16,1,10]{2,1,0:T(1,128)}, u32[]{:S(2)}) copy-start(s32[16,1,10]{2,1,0:T(1,128)} %copy-done.4) | copy-start | bytes 1924
  43.0 33.0 %copy-start.1 = (bf16[4096,256]{1,0:T(8,128)(2,1)S(1)}, bf16[4096,256]{1,0:T(8,128)(2,1)}, u32[]{:S(2)}) copy-start(bf16[4096,256]{1,0:T(8,128)(2,1)} %weight_ref.1) | copy-start | bytes 6291460
  76.0 3.4 %copy-start = (bf16[1024,4096]{1,0:T(8,128)(2,1)S(1)}, bf16[1024,4096]{1,0:T(8,128)(2,1)}, u32[]{:S(2)}) copy-start(bf16[1024,4096]{1,0:T(8,128)(2,1)} %all-gather.2.cloned.1.call-done.tokens_ref) | copy-start | bytes 25165828
  95.0 12.4 %copy-start.2 = (bf16[256,8,256]{2,1,0:T(8,128)(2,1)S(1)}, bf16[256,8,256]{2,1,0:T(8,128)(2,1)}, u32[]{:S(2)}) copy-start(bf16[256,8,256]{2,1,0:T(8,128)(2,1)} %fusion.15) | copy-start | bytes 3145732
  95.0 12.4 %copy-start.3 = (bf16[256,8,256]{2,1,0:T(8,128)(2,1)S(1)}, bf16[256,8,256]{2,1,0:T(8,128)(2,1)}, u32[]{:S(2)}) copy-start(bf16[256,8,256]{2,1,0:T(8,128)(2,1)} %fusion.14) | copy-start | bytes 3145732
  107.3 9.2 %collective-permute-start = (bf16[1024,256]{1,0:T(8,128)(2,1)S(1)}, bf16[1024,256]{1,0:T(8,128)(2,1)S(1)}, u32[]{:S(2)}, u32[]{:S(2)}) collective-permute-start(bf16[1024,256]{1,0:T(8,128)(2,1)S(1)} %attend.1), channel_id=1, source_target_pairs={{0,1},{1,0},{2,3},{3,2},{4,5},{5,4},{6,7},{7,6},{8,9},{9,8},{10,11... | collective-permute-start | bytes 1572872 | tf_op jit(solution)/shard_map/ppermute | solution.py:280
  116.9 12.1 %collective-permute-start.12 = (bf16[512,256]{1,0:T(8,128)(2,1)S(1)}, bf16[512,256]{1,0:T(8,128)(2,1)S(1)}, u32[]{:S(2)}, u32[]{:S(2)}) collective-permute-start(bf16[512,256]{1,0:T(8,128)(2,1)S(1)} %convolution_convert_fusion), channel_id=1, source_target_pairs={{0,14},{2,0},{4,2},{6,4},{8,6},{10,8},{12,10},{14,12},{1,15},{3,1}... | collective-permute-start | bytes 786440 | tf_op jit(solution)/shard_map/ppermute | solution.py:211
  122.7 10.6 %collective-permute-start.9 = (bf16[512,256]{1,0:T(8,128)(2,1)S(1)}, bf16[512,256]{1,0:T(8,128)(2,1)S(1)}, u32[]{:S(2)}, u32[]{:S(2)}) collective-permute-start(bf16[512,256]{1,0:T(8,128)(2,1)S(1)} %convolution_convert_fusion.1), channel_id=1, source_target_pairs={{0,2},{2,4},{4,6},{6,8},{8,10},{10,12},{12,14},{14,0},{1,3},{3,5},... | collective-permute-start | bytes 786440 | tf_op jit(solution)/shard_map/ppermute | solution.py:211
  123.6 11.1 %collective-permute-start.6 = (bf16[512,256]{1,0:T(8,128)(2,1)S(1)}, bf16[512,256]{1,0:T(8,128)(2,1)S(1)}, u32[]{:S(2)}, u32[]{:S(2)}) collective-permute-start(bf16[512,256]{1,0:T(8,128)(2,1)S(1)} %convolution_convert_fusion.2), channel_id=1, source_target_pairs={{0,14},{2,0},{4,2},{6,4},{8,6},{10,8},{12,10},{14,12},{1,15},{3,1}... | collective-permute-start | bytes 786440 | tf_op jit(solution)/shard_map/ppermute | solution.py:211
  126.9 12.1 %collective-permute-start.2 = (bf16[512,256]{1,0:T(8,128)(2,1)S(1)}, bf16[512,256]{1,0:T(8,128)(2,1)S(1)}, u32[]{:S(2)}, u32[]{:S(2)}) collective-permute-start(bf16[512,256]{1,0:T(8,128)(2,1)S(1)} %convolution_convert_fusion.3), channel_id=1, source_target_pairs={{0,2},{2,4},{4,6},{6,8},{8,10},{10,12},{12,14},{14,0},{1,3},{3,5},... | collective-permute-start | bytes 786440 | tf_op jit(solution)/shard_map/ppermute | solution.py:211
  129.3 10.9 %collective-permute-start.13 = (bf16[512,256]{1,0:T(8,128)(2,1)S(1)}, bf16[512,256]{1,0:T(8,128)(2,1)S(1)}, u32[]{:S(2)}, u32[]{:S(2)}) collective-permute-start(bf16[512,256]{1,0:T(8,128)(2,1)S(1)} %fusion.13), channel_id=1, source_target_pairs={{0,14},{2,0},{4,2},{6,4},{8,6},{10,8},{12,10},{14,12},{1,15},{3,1}... | collective-permute-start | bytes 786440 | tf_op jit(solution)/shard_map/ppermute | solution.py:211
  133.6 10.9 %collective-permute-start.10 = (bf16[512,256]{1,0:T(8,128)(2,1)S(1)}, bf16[512,256]{1,0:T(8,128)(2,1)S(1)}, u32[]{:S(2)}, u32[]{:S(2)}) collective-permute-start(bf16[512,256]{1,0:T(8,128)(2,1)S(1)} %fusion.10), channel_id=1, source_target_pairs={{0,2},{2,4},{4,6},{6,8},{8,10},{10,12},{12,14},{14,0},{1,3},{3,5},... | collective-permute-start | bytes 786440 | tf_op jit(solution)/shard_map/ppermute | solution.py:211
  135.0 20.2 %collective-permute-start.7 = (bf16[512,256]{1,0:T(8,128)(2,1)S(1)}, bf16[512,256]{1,0:T(8,128)(2,1)S(1)}, u32[]{:S(2)}, u32[]{:S(2)}) collective-permute-start(bf16[512,256]{1,0:T(8,128)(2,1)S(1)} %fusion.8), channel_id=1, source_target_pairs={{0,14},{2,0},{4,2},{6,4},{8,6},{10,8},{12,10},{14,12},{1,15},{3,1}... | collective-permute-start | bytes 786440 | tf_op jit(solution)/shard_map/ppermute | solution.py:211
  139.3 10.9 %collective-permute-start.3 = (bf16[512,256]{1,0:T(8,128)(2,1)S(1)}, bf16[512,256]{1,0:T(8,128)(2,1)S(1)}, u32[]{:S(2)}, u32[]{:S(2)}) collective-permute-start(bf16[512,256]{1,0:T(8,128)(2,1)S(1)} %fusion.6), channel_id=1, source_target_pairs={{0,2},{2,4},{4,6},{6,8},{8,10},{10,12},{12,14},{14,0},{1,3},{3,5},... | collective-permute-start | bytes 786440 | tf_op jit(solution)/shard_map/ppermute | solution.py:211
  140.6 10.5 %collective-permute-start.14 = (bf16[512,256]{1,0:T(8,128)(2,1)S(1)}, bf16[512,256]{1,0:T(8,128)(2,1)S(1)}, u32[]{:S(2)}, u32[]{:S(2)}) collective-permute-start(bf16[512,256]{1,0:T(8,128)(2,1)S(1)} %fusion.12), channel_id=1, source_target_pairs={{0,14},{2,0},{4,2},{6,4},{8,6},{10,8},{12,10},{14,12},{1,15},{3,1}... | collective-permute-start | bytes 786440 | tf_op jit(solution)/shard_map/ppermute | solution.py:211
  144.9 16.2 %collective-permute-start.11 = (bf16[512,256]{1,0:T(8,128)(2,1)S(1)}, bf16[512,256]{1,0:T(8,128)(2,1)S(1)}, u32[]{:S(2)}, u32[]{:S(2)}) collective-permute-start(bf16[512,256]{1,0:T(8,128)(2,1)S(1)} %fusion.9), channel_id=1, source_target_pairs={{0,2},{2,4},{4,6},{6,8},{8,10},{10,12},{12,14},{14,0},{1,3},{3,5},... | collective-permute-start | bytes 786440 | tf_op jit(solution)/shard_map/ppermute | solution.py:211
  150.5 10.2 %collective-permute-start.4 = (bf16[512,256]{1,0:T(8,128)(2,1)S(1)}, bf16[512,256]{1,0:T(8,128)(2,1)S(1)}, u32[]{:S(2)}, u32[]{:S(2)}) collective-permute-start(bf16[512,256]{1,0:T(8,128)(2,1)S(1)} %fusion.5), channel_id=1, source_target_pairs={{0,2},{2,4},{4,6},{6,8},{8,10},{10,12},{12,14},{14,0},{1,3},{3,5},... | collective-permute-start | bytes 786440 | tf_op jit(solution)/shard_map/ppermute | solution.py:211
  151.4 10.5 %collective-permute-start.15 = (bf16[512,256]{1,0:T(8,128)(2,1)S(1)}, bf16[512,256]{1,0:T(8,128)(2,1)S(1)}, u32[]{:S(2)}, u32[]{:S(2)}) collective-permute-start(bf16[512,256]{1,0:T(8,128)(2,1)S(1)} %fusion.11), channel_id=1, source_target_pairs={{0,14},{2,0},{4,2},{6,4},{8,6},{10,8},{12,10},{14,12},{1,15},{3,1}... | collective-permute-start | bytes 786440 | tf_op jit(solution)/shard_map/ppermute | solution.py:211
  155.4 10.7 %collective-permute-start.8 = (bf16[512,256]{1,0:T(8,128)(2,1)S(1)}, bf16[512,256]{1,0:T(8,128)(2,1)S(1)}, u32[]{:S(2)}, u32[]{:S(2)}) collective-permute-start(bf16[512,256]{1,0:T(8,128)(2,1)S(1)} %fusion.7), channel_id=1, source_target_pairs={{0,14},{2,0},{4,2},{6,4},{8,6},{10,8},{12,10},{14,12},{1,15},{3,1}... | collective-permute-start | bytes 786440 | tf_op jit(solution)/shard_map/ppermute | solution.py:211
  160.9 8.8 %collective-permute-start.5 = (bf16[512,256]{1,0:T(8,128)(2,1)S(1)}, bf16[512,256]{1,0:T(8,128)(2,1)S(1)}, u32[]{:S(2)}, u32[]{:S(2)}) collective-permute-start(bf16[512,256]{1,0:T(8,128)(2,1)S(1)} %fusion.4), channel_id=1, source_target_pairs={{0,2},{2,4},{4,6},{6,8},{8,10},{10,12},{12,14},{14,0},{1,3},{3,5},... | collective-permute-start | bytes 786440 | tf_op jit(solution)/shard_map/ppermute | solution.py:211
Sparse Core Ops, SparseCore 0:
  9.1 66.8 all-gather.1

commit v2 on v1

v2 whole, which is shorter than its diff:
```python
import functools
import math

import jax
import jax.numpy as jnp
from jax import lax
from jax.experimental import pallas as pl
from jax.experimental.pallas import tpu as pltpu
from jax.sharding import Mesh
from jax.sharding import PartitionSpec as P

HD = 128
ENC = 896
GROUP = 128
SPAN = 64
NBR_LEN = 128
NBRS = 2
DB = ("y", "x")
F32 = jnp.float32
BF16 = jnp.bfloat16
VMEM = pl.BlockSpec(memory_space=pltpu.VMEM)
SMEM = pl.BlockSpec(memory_space=pltpu.SMEM)
ANY = pl.BlockSpec(memory_space=pl.ANY)


def unit(values):
    return values * lax.rsqrt(jnp.mean(values * values, axis=-1, keepdims=True) + 1e-06)


def project_kernel(scales_ref, codes_ref, key_ref, value_ref, out_ref, enc_ref):
    step = pl.program_id(0)
    blocks = codes_ref.shape[0]
    for b in range(blocks):
        for g in range(ENC // GROUP):
            cols = slice(g * GROUP, (g + 1) * GROUP)
            scaled = codes_ref[b, :, cols].astype(F32) * scales_ref[step * blocks + b, g]
            enc_ref[b * NBR_LEN : (b + 1) * NBR_LEN, cols] = scaled.astype(BF16)
    enc = enc_ref[...]
    keys = jnp.dot(enc, key_ref[...], preferred_element_type=F32)
    values = jnp.dot(enc, value_ref[...], preferred_element_type=F32).astype(BF16)
    width = key_ref.shape[1]
    for b in range(blocks):
        rows = slice(b * NBR_LEN, (b + 1) * NBR_LEN)
        for h in range(width // HD):
            cols = slice(h * HD, (h + 1) * HD)
            out_ref[b, :, cols] = unit(keys[rows, cols]).astype(BF16)
        out_ref[b, :, width : 2 * width] = values[rows]


def project_blocks(codes, scales, key_weight, value_weight):
    count, width, per = codes.shape[0], key_weight.shape[1], 2
    return pl.pallas_call(
        project_kernel,
        grid=(count // per,),
        out_shape=jax.ShapeDtypeStruct((count, NBR_LEN, 2 * width), BF16),
        in_specs=[
            SMEM,
            pl.BlockSpec((per, NBR_LEN, ENC), lambda i: (i, 0, 0)),
            pl.BlockSpec((ENC, width), lambda i: (0, 0)),
            pl.BlockSpec((ENC, width), lambda i: (0, 0)),
        ],
        out_specs=pl.BlockSpec((per, NBR_LEN, 2 * width), lambda i: (i, 0, 0)),
        scratch_shapes=[pltpu.VMEM((per * NBR_LEN, ENC), BF16)],
        cost_estimate=pl.CostEstimate(
            flops=2 * count * NBR_LEN * ENC * 2 * width, bytes_accessed=5 << 20, transcendentals=0
        ),
        name="project_blocks",
    )(scales, codes, key_weight, value_weight)


def select_kernel(place_ref, heard_ref, rows_ref, out_ref, sems):
    shards, requests = out_ref.shape[0], out_ref.shape[0] * NBRS
    here = place_ref[0]
    copies = []
    for e in range(shards):
        first, last = jnp.int32(-1), jnp.int32(0)
        for r in range(requests):
            mine = heard_ref[e, r] == here
            block = heard_ref[e, requests + r]
            first = jnp.where(mine & (first < 0), block, first)
            last = jnp.where(mine, block, last)
        for s, block in enumerate((jnp.maximum(first, 0), last)):
            copy = pltpu.make_async_copy(rows_ref.at[block], out_ref.at[e, s], sems.at[e, s])
            copy.start()
            copies.append(copy)
    for copy in copies:
        copy.wait()


def select_blocks(place, heard, rows):
    shards = heard.shape[0]
    return pl.pallas_call(
        select_kernel,
        out_shape=jax.ShapeDtypeStruct((shards, NBRS) + rows.shape[1:], BF16),
        in_specs=[SMEM, SMEM, VMEM],
        out_specs=ANY,
        scratch_shapes=[pltpu.SemaphoreType.DMA((shards, NBRS))],
        cost_estimate=pl.CostEstimate(flops=0, bytes_accessed=9 << 20, transcendentals=0),
        name="select_blocks",
    )(place, heard, rows)


def query_kernel(tokens_ref, weight_ref, out_ref):
    projected = jnp.dot(tokens_ref[...], weight_ref[...], preferred_element_type=F32)
    for h in range(weight_ref.shape[1] // HD):
        cols = slice(h * HD, (h + 1) * HD)
        out_ref[:, cols] = unit(projected[:, cols]).astype(BF16)


def project_queries(tokens, weight):
    rows, depth = tokens.shape
    width, tile = weight.shape[1], 128
    return pl.pallas_call(
        query_kernel,
        grid=(rows // tile,),
        out_shape=jax.ShapeDtypeStruct((rows, width), BF16),
        in_specs=[
            pl.BlockSpec((tile, depth), lambda i: (i, 0)),
            pl.BlockSpec((depth, width), lambda i: (0, 0)),
        ],
        out_specs=pl.BlockSpec((tile, width), lambda i: (i, 0)),
        compiler_params=pltpu.CompilerParams(vmem_limit_bytes=24 << 20),
        cost_estimate=pl.CostEstimate(
            flops=2 * rows * depth * width, bytes_accessed=11 << 20, transcendentals=0
        ),
        name="project_queries",
    )(tokens, weight)


def attend_kernel(first, slot_ref, length_ref, query_ref, rows_ref, out_ref, held_ref, sems):
    spans = slot_ref.shape[0] // NBRS
    count = sems.shape[0] // NBRS
    width = query_ref.shape[1]
    keys = NBRS * NBR_LEN
    factor = 2.0 / math.sqrt(HD)
    copies = []
    for c in range(count):
        for n in range(NBRS):
            copy = pltpu.make_async_copy(
                rows_ref.at[slot_ref[n * spans + first + c]],
                held_ref.at[pl.ds((c * NBRS + n) * NBR_LEN, NBR_LEN)],
                sems.at[c * NBRS + n],
            )
            copy.start()
            copies.append(copy)
    places = lax.broadcasted_iota(jnp.int32, (SPAN, keys), 1)
    group = 4
    for start in range(0, count, group):
        members = [(c, h) for c in range(start, start + group) for h in range(width // HD)]
        for copy in copies[start * NBRS : (start + group) * NBRS]:
            copy.wait()
        raised = []
        for c, h in members:
            scores = lax.dot_general(
                query_ref[c * SPAN : (c + 1) * SPAN, h * HD : (h + 1) * HD],
                held_ref[c * keys : (c + 1) * keys, h * HD : (h + 1) * HD],
                (((1,), (1,)), ((), ())),
                preferred_element_type=F32,
            )
            ends = [length_ref[n * spans + first + c] + n * NBR_LEN for n in range(NBRS)]
            valid = (places < ends[0]) | ((places >= NBR_LEN) & (places < ends[1]))
            raised.append(jnp.where(valid, jnp.exp(scores * factor), 0.0))
        weights = [
            (part * (1.0 / jnp.sum(part, axis=-1, keepdims=True))).astype(BF16) for part in raised
        ]
        for (c, h), part in zip(members, weights):
            cols = slice(width + h * HD, width + (h + 1) * HD)
            result = jnp.dot(
                part, held_ref[c * keys : (c + 1) * keys, cols], preferred_element_type=F32
            )
            out_ref[c * SPAN : (c + 1) * SPAN, h * HD : (h + 1) * HD] = result.astype(BF16)


def attend(part, parts, slot_index, lengths, queries, rows):
    tokens, width = queries.shape[0] // parts, queries.shape[1]
    count = tokens // SPAN
    requests = count * NBRS
    return pl.pallas_call(
        functools.partial(attend_kernel, part * count),
        grid=(1,),
        out_shape=jax.ShapeDtypeStruct((tokens, width), BF16),
        in_specs=[SMEM, SMEM, pl.BlockSpec((tokens, width), lambda i: (part, 0)), ANY],
        out_specs=pl.BlockSpec((tokens, width), lambda i: (0, 0)),
        scratch_shapes=[
            pltpu.VMEM((requests * NBR_LEN, rows.shape[2]), BF16),
            pltpu.SemaphoreType.DMA((requests,)),
        ],
        compiler_params=pltpu.CompilerParams(vmem_limit_bytes=24 << 20),
        cost_estimate=pl.CostEstimate(
            flops=4 * tokens * NBRS * NBR_LEN * width, bytes_accessed=3 << 20, transcendentals=0
        ),
        name="attend",
    )(slot_index, lengths, queries, rows)


def relay_kernel(place_ref, weight_ref, own_ref, lent_ref, sems):
    here, core = place_ref[0], place_ref[1]
    ring, _, width = own_ref.shape
    copies = []
    for k in range(ring):
        chip = lax.rem(here + k, ring)
        for i, (ref, which) in enumerate(((own_ref, core), (lent_ref, 1 - core))):
            cols = pl.ds(pl.multiple_of((chip * 2 + which) * width, width), width)
            copy = pltpu.make_async_copy(weight_ref.at[:, cols], ref.at[k], sems.at[i, k])
            copy.start()
            copies.append(copy)
    for copy in copies:
        copy.wait()


def relay(place, weight, ring):
    depth = weight.shape[0]
    shape = jax.ShapeDtypeStruct((ring, depth, weight.shape[1] // (2 * ring)), BF16)
    return pl.pallas_call(
        relay_kernel,
        out_shape=(shape, shape),
        in_specs=[SMEM, ANY],
        out_specs=(ANY, ANY),
        scratch_shapes=[pltpu.SemaphoreType.DMA((2, ring))],
        cost_estimate=pl.CostEstimate(flops=0, bytes_accessed=4 << 20, transcendentals=0),
        name="relay",
    )(place, weight)


def reduce_ring(attended, partner_attended, own_weight, partner_weight, ring):
    up = [(i, (i + 1) % ring) for i in range(ring)]
    down = [(i, (i - 1) % ring) for i in range(ring)]

    def share(half, step):
        return jnp.dot(
            attended[half], own_weight[step % ring], preferred_element_type=F32
        ) + jnp.dot(partner_attended[half], partner_weight[step % ring], preferred_element_type=F32)

    far = ring // 2
    chains = [(0, 1, far), (1, -1, far), (0, -1, far - 1), (1, 1, far - 1)]
    held = {}
    for distance in range(far, 0, -1):
        for half, way, first in chains:
            if distance > first:
                continue
            part = share(half, way * distance)
            if distance < first:
                part = part + held[half, way].astype(F32)
            held[half, way] = lax.ppermute(part.astype(BF16), "z", up if way == 1 else down)
    out = [
        (share(half, 0) + held[half, 1].astype(F32) + held[half, -1].astype(F32)).astype(BF16)
        for half in range(2)
    ]
    return jnp.concatenate(out, axis=0)


def local(
    tokens,
    query_weight,
    key_weight,
    value_weight,
    out_weight,
    codes,
    scales,
    block_len,
    nbr_owner,
    nbr_block,
):
    width = query_weight.shape[1]
    ring = lax.axis_size("z")
    cores = lax.axis_size("c")
    shards = lax.axis_size(DB)
    here, core = lax.axis_index("z"), lax.axis_index("c")
    swap = [(i, (i + 1) % cores) for i in range(cores)]

    gathered = lax.all_gather(tokens, ("z", "c"), axis=1, tiled=True)

    owners = nbr_owner.T.reshape(-1)
    wanted_blocks = nbr_block.T.reshape(-1)
    notes = jnp.concatenate([owners, wanted_blocks, block_len])
    notes = jnp.broadcast_to(notes[None, :], (shards, notes.shape[0]))
    heard = lax.all_to_all(notes, DB, split_axis=0, concat_axis=0, tiled=True)
    projected = project_blocks(codes, scales, key_weight, value_weight)
    sent = select_blocks(lax.axis_index(DB).astype(jnp.int32).reshape(1), heard, projected)
    rows = lax.all_to_all(sent, DB, split_axis=0, concat_axis=0, tiled=True)
    rows = rows.reshape(shards * NBRS, NBR_LEN, 2 * width)

    order = jnp.arange(owners.shape[0], dtype=jnp.int32)
    earlier = jnp.sum(
        ((owners[:, None] == owners[None, :]) & (order[:, None] > order[None, :])).astype(jnp.int32),
        axis=1,
    )
    slot_index = owners * NBRS + earlier
    all_lengths = heard[:, 2 * owners.shape[0] :].reshape(-1)
    block_ids = owners * block_len.shape[0] + wanted_blocks
    ids = jnp.arange(all_lengths.shape[0], dtype=jnp.int32)
    lengths = jnp.sum(
        jnp.where(block_ids[:, None] == ids[None, :], all_lengths[None, :], 0), axis=1
    )

    own_weight, lent_weight = relay(jnp.stack([here, core]).astype(jnp.int32), out_weight, ring)
    partner_weight = lax.ppermute(lent_weight, "c", swap)

    queries = project_queries(gathered, query_weight)
    attended = [attend(part, 2, slot_index, lengths, queries, rows) for part in range(2)]
    partner_attended = [lax.ppermute(part, "c", swap) for part in attended]
    return reduce_ring(attended, partner_attended, own_weight, partner_weight, ring)


def solution(mesh):
    grid = Mesh(mesh.devices.reshape(4, 4, 8, 2), ("y", "x", "z", "c"))
    head = ("z", "c")
    placed = (
        P(DB, head),
        P(None, head),
        P(None, head),
        P(None, head),
        P(head, None),
        P(DB, None, None),
        P(DB, None),
        P(DB),
        P(DB, None),
        P(DB, None),
    )
    return jax.shard_map(
        local, mesh=grid, in_specs=placed, out_specs=P(DB, head), check_vma=False
    )
```

time: 179 us -> 184 us (1.028)
  Pallas kernels: 25.1 us -> 87.3 us
  waiting for transfers between devices: 62.3 us -> 15.3 us
  matrix products: 4.75 us -> 21.7 us
  other arithmetic: 17.8 us -> 2.52 us
  local copies, waits for them, and re-layouts: 15.5 us -> 6.28 us
  starting transfers between devices: 38.5 us -> 36 us
    pallas_call x2 -> x4, Pallas kernels: 15.8 us -> 78.1 us  [the longest x1 68.2 us: relay(): pl.pallas_call(relay_kernel, out_shape=(shape, shape), in_specs=[SMEM, AN...]
    all_gather x1, waiting for transfers between devices: 25.9 us -> 0.02 us  [local(): gathered = lax.all_gather(tokens, ('z', 'c'), axis=1, tiled=True)]
    dot_general x16 -> x32, matrix products: 4.75 us -> 21.7 us  [the longest x16 18.1 us: share(): jnp.dot(partner_attended[half], partner_weight[step % ring], preferred_el...]
    concatenate x5 -> x1, other arithmetic: 16.5 us -> 0.73 us  [local(): notes = jnp.concatenate([owners, wanted_blocks, block_len])]
    all_to_all x1, waiting for transfers between devices: 11.2 us -> 0.01 us  [local(): rows = lax.all_to_all(sent, DB, split_axis=0, concat_axis=0, tiled=True)]
    ppermute x14, waiting for transfers between devices: 23.9 us -> 14 us  [reduce_ring(): lax.ppermute(part.astype(BF16), 'z', up if way == 1 else down)]
    dynamic_slice x3 -> x0, local copies, waits for them, and re-layouts: 5.59 us -> none  [the longest x2 3.8 us: local(): lent_weight = lax.dynamic_index_in_dim(by_core, 1 - core, 2, keepdims=False)]
    unnamed x15 -> x10, local copies, waits for them, and re-layouts: 8.8 us -> 3.99 us
  transfers between devices with their start and end apart: 19 -> 20, of which waited for: 15 -> 6; matrix products, arithmetic and copies ran while one was open for 18% -> 13% of each run, Pallas kernels for 7% -> 48%
where the time goes in v2:
time: 184 us; the launch traced here: 183 us
  Pallas kernels  87.3 us (47%)
  starting transfers between devices  36 us (20%)
  matrix products  21.7 us (12%)
  waiting for transfers between devices  15.3 us (8%)
  between operations  13.8 us (8%)
  local copies, waits for them, and re-layouts  6.28 us (3%)
  other arithmetic  2.52 us (1%)
    pallas_call x1, Pallas kernels, relay(): pl.pallas_call(relay_kernel, out_shape=(shape, shape), in_specs=[SMEM, AN...  68.2 us
    ppermute x14, starting transfers between devices, reduce_ring(): lax.ppermute(part.astype(BF16), 'z', up if way == 1 else down)  21.1 us
    dot_general x16, matrix products, share(): jnp.dot(partner_attended[half], partner_weight[step % ring], preferred_el...  18.1 us
    ppermute x14, waiting for transfers between devices, reduce_ring(): lax.ppermute(part.astype(BF16), 'z', up if way == 1 else down)  14 us
    all_to_all x1, starting transfers between devices, local(): heard = lax.all_to_all(notes, DB, split_axis=0, concat_axis=0, tiled=True)  7.17 us
    all_to_all x1, starting transfers between devices, local(): rows = lax.all_to_all(sent, DB, split_axis=0, concat_axis=0, tiled=True)  6.74 us
    pallas_call x2, Pallas kernels, attend(): pl.pallas_call(functools.partial(attend_kernel, part * count), grid=(1,),...  6.15 us
    pallas_call x1, Pallas kernels, project_blocks(): pl.pallas_call(project_kernel, grid=(count // per,), out_shape=jax.ShapeD...  4.87 us
  transfers between devices with their start and end apart: 20, of which 6 were waited for; matrix products, arithmetic and copies ran while one was open for 13% of the time, Pallas kernels for 48%

profile of v2, /device:TPU:24, one launch (start us, length us, event | category | flops | bytes accessed | tf_op | source)
XLA Modules:
  0.0 182.9 jit_solution(2469453748666356136)
XLA Ops:
  6.5 0.7 all-gather.2.cloned.1.call-update
  7.3 0.8 reshape.32
  8.0 0.8 reshape.31
  8.8 0.7 pad_add_fusion
  9.5 0.6 broadcast_in_dim.24
  10.1 7.2 %all-to-all-start = ((s32[16,1,72]{2,1,0:T(1,128)}), s32[16,1,72]{2,1,0:T(1,128)S(1)}, u32[]{:S(2)}, u32[]{:S(2)}) async-start(s32[16,1,72]{2,1,0:T(1,128)} %broadcast_in_dim.24), calls=%async_computation | async-start | bytes 16384 | tf_op jit(solution)/shard_map/all_to_all | solution.py:277
  17.3 4.9 %project_blocks.1.rows_ref = bf16[8,128,512]{2,1,0:T(8,128)(2,1)} custom-call(f32[8,7]{1,0:T(8,128)} %scales_ref.1, bf16[8,128,896]{2,1,0:T(8,128)(2,1)} %codes_ref.1, bf16[896,256]{1,0:T(8,128)(2,1)} %key_ref.1, bf16[896,256]{1,0:T(8,128)(2,1)} %value_ref.1), custom_call_target="tpu_custom_call" | custom-call | flops 939524096 | bytes 5242880 | tf_op jit(solution)/shard_map/project_blocks/pallas_call | solution.py:52
  22.2 0.6 all-to-all-done
  22.8 0.6 copy-done.3
  23.4 3.8 %select_blocks.1 = bf16[16,2,128,512]{3,2,1,0:T(8,128)(2,1)} custom-call(s32[1]{0:T(128)} %bitcast.3.place_ref, s32[16,72]{1,0:T(8,128)} %bitcast.111, bf16[8,128,512]{2,1,0:T(8,128)(2,1)} %project_blocks.1.rows_ref), custom_call_target="tpu_custom_call" | custom-call | bytes 9437184 | tf_op jit(solution)/shard_map/select_blocks/pallas_call | solution.py:92
  27.2 6.7 %all-to-all-start.1 = ((bf16[16,2,128,512]{3,2,1,0:T(8,128)(2,1)}), bf16[16,2,128,512]{3,2,1,0:T(8,128)(2,1)}, u32[]{:S(2)}, u32[]{:S(2)}) async-start(bf16[16,2,128,512]{3,2,1,0:T(8,128)(2,1)} %select_blocks.1), calls=%async_computation.1 | async-start | bytes 8388608 | tf_op jit(solution)/shard_map/all_to_all | solution.py:280
  34.0 0.6 pad_add_fusion.1.place_ref
  34.6 68.2 %relay.1 = (bf16[8,256,256]{2,1,0:T(8,128)(2,1)}, bf16[8,256,256]{2,1,0:T(8,128)(2,1)}) custom-call(s32[2]{0:T(128)} %pad_add_fusion.1.place_ref, bf16[256,4096]{1,0:T(8,128)(2,1)} %weight_ref.3), custom_call_target="tpu_custom_call" | custom-call | bytes 4194304 | tf_op jit(solution)/shard_map/relay/pallas_call | solution.py:214
  102.8 0.3 collective-permute-start.1
  103.6 3.4 %copy-done = bf16[1024,4096]{1,0:T(8,128)(2,1)S(1)} copy-done((bf16[1024,4096]{1,0:T(8,128)(2,1)S(1)}, bf16[1024,4096]{1,0:T(8,128)(2,1)}, u32[]{:S(2)}) %copy-start) | copy-done | bytes 8388632
  107.0 4.3 %project_queries.1.query_ref = bf16[1024,256]{1,0:T(8,128)(2,1)S(1)} custom-call(bf16[1024,4096]{1,0:T(8,128)(2,1)S(1)} %copy-done, bf16[4096,256]{1,0:T(8,128)(2,1)S(1)} %copy-done.1), custom_call_target="tpu_custom_call" | custom-call | flops 2147483648 | bytes 11534336 | tf_op jit(solution)/shard_map/project_queries/pallas_call | solution.py:113
  111.3 3.1 %attend.3 = bf16[512,256]{1,0:T(8,128)(2,1)S(1)} custom-call(s32[32]{0:T(128)S(1)} %get-tuple-element.10.slot_ref, s32[32]{0:T(128)S(1)} %select_reduce_fusion.length_ref, bf16[1024,256]{1,0:T(8,128)(2,1)S(1)} %project_queries.1.query_ref, bf16[32,128,512]{2,1,0:T(8,128)(2,1)} %bitcast.4.rows_ref), custom_call_target="tpu_custom_call" | custom-call | flops 134217728 | bytes 3145728 | tf_op jit(solution)/shard_map/attend/pallas_call | solution.py:178
  114.4 0.4 collective-permute-start.9
  116.6 3.1 %attend.2 = bf16[512,256]{1,0:T(8,128)(2,1)S(1)} custom-call(s32[32]{0:T(128)S(1)} %get-tuple-element.10.slot_ref, s32[32]{0:T(128)S(1)} %select_reduce_fusion.length_ref, bf16[1024,256]{1,0:T(8,128)(2,1)S(1)} %project_queries.1.query_ref, bf16[32,128,512]{2,1,0:T(8,128)(2,1)} %bitcast.4.rows_ref), custom_call_target="tpu_custom_call" | custom-call | flops 134217728 | bytes 3145728 | tf_op jit(solution)/shard_map/attend/pallas_call | solution.py:178
  120.0 0.3 collective-permute-start
  121.8 1.1 fusion.29
  123.0 3.4 %collective-permute-start.13 = (bf16[512,256]{1,0:T(8,128)(2,1)S(1)}, bf16[512,256]{1,0:T(8,128)(2,1)S(1)}, u32[]{:S(2)}, u32[]{:S(2)}) collective-permute-start(bf16[512,256]{1,0:T(8,128)(2,1)S(1)} %fusion.29), channel_id=1, source_target_pairs={{0,14},{2,0},{4,2},{6,4},{8,6},{10,8},{12,10},{14,12},{1,15},{3,1}... | collective-permute-start | bytes 786440 | tf_op jit(solution)/shard_map/ppermute | solution.py:244
  126.4 1.1 fusion.28
  127.6 1.1 fusion.27
  128.7 3.3 %collective-permute-start.6 = (bf16[512,256]{1,0:T(8,128)(2,1)S(1)}, bf16[512,256]{1,0:T(8,128)(2,1)S(1)}, u32[]{:S(2)}, u32[]{:S(2)}) collective-permute-start(bf16[512,256]{1,0:T(8,128)(2,1)S(1)} %fusion.27), channel_id=1, source_target_pairs={{0,14},{2,0},{4,2},{6,4},{8,6},{10,8},{12,10},{14,12},{1,15},{3,1}... | collective-permute-start | bytes 786440 | tf_op jit(solution)/shard_map/ppermute | solution.py:244
  132.0 1.1 fusion.26
  133.2 1.1 fusion.25
  134.4 3.6 %collective-permute-start.14 = (bf16[512,256]{1,0:T(8,128)(2,1)S(1)}, bf16[512,256]{1,0:T(8,128)(2,1)S(1)}, u32[]{:S(2)}, u32[]{:S(2)}) collective-permute-start(bf16[512,256]{1,0:T(8,128)(2,1)S(1)} %fusion.25), channel_id=1, source_target_pairs={{0,14},{2,0},{4,2},{6,4},{8,6},{10,8},{12,10},{14,12},{1,15},{3,1}... | collective-permute-start | bytes 786440 | tf_op jit(solution)/shard_map/ppermute | solution.py:244
  138.0 1.1 fusion.22
  139.2 1.1 fusion.20
  140.3 3.3 %collective-permute-start.7 = (bf16[512,256]{1,0:T(8,128)(2,1)S(1)}, bf16[512,256]{1,0:T(8,128)(2,1)S(1)}, u32[]{:S(2)}, u32[]{:S(2)}) collective-permute-start(bf16[512,256]{1,0:T(8,128)(2,1)S(1)} %fusion.20), channel_id=1, source_target_pairs={{0,14},{2,0},{4,2},{6,4},{8,6},{10,8},{12,10},{14,12},{1,15},{3,1}... | collective-permute-start | bytes 786440 | tf_op jit(solution)/shard_map/ppermute | solution.py:244
  143.6 1.1 fusion.18
  144.9 1.1 fusion.24
  146.0 3.6 %collective-permute-start.15 = (bf16[512,256]{1,0:T(8,128)(2,1)S(1)}, bf16[512,256]{1,0:T(8,128)(2,1)S(1)}, u32[]{:S(2)}, u32[]{:S(2)}) collective-permute-start(bf16[512,256]{1,0:T(8,128)(2,1)S(1)} %fusion.24), channel_id=1, source_target_pairs={{0,14},{2,0},{4,2},{6,4},{8,6},{10,8},{12,10},{14,12},{1,15},{3,1}... | collective-permute-start | bytes 786440 | tf_op jit(solution)/shard_map/ppermute | solution.py:244
  149.6 1.1 fusion.21
  150.9 4.4 %collective-permute-done.3 = bf16[512,256]{1,0:T(8,128)(2,1)S(1)} collective-permute-done((bf16[512,256]{1,0:T(8,128)(2,1)S(1)}, bf16[512,256]{1,0:T(8,128)(2,1)S(1)}, u32[]{:S(2)}, u32[]{:S(2)}) %collective-permute-start.3) | collective-permute-done | bytes 262176 | tf_op jit(solution)/shard_map/ppermute | solution.py:244
  155.3 1.1 fusion.17
  156.5 1.1 fusion.23
  157.7 3.3 %collective-permute-start.16 = (bf16[512,256]{1,0:T(8,128)(2,1)S(1)}, bf16[512,256]{1,0:T(8,128)(2,1)S(1)}, u32[]{:S(2)}, u32[]{:S(2)}) collective-permute-start(bf16[512,256]{1,0:T(8,128)(2,1)S(1)} %fusion.23), channel_id=1, source_target_pairs={{0,14},{2,0},{4,2},{6,4},{8,6},{10,8},{12,10},{14,12},{1,15},{3,1}... | collective-permute-start | bytes 786440 | tf_op jit(solution)/shard_map/ppermute | solution.py:244
  161.0 1.1 fusion.19
  162.2 2.9 %collective-permute-done.4 = bf16[512,256]{1,0:T(8,128)(2,1)S(1)} collective-permute-done((bf16[512,256]{1,0:T(8,128)(2,1)S(1)}, bf16[512,256]{1,0:T(8,128)(2,1)S(1)}, u32[]{:S(2)}, u32[]{:S(2)}) %collective-permute-start.4) | collective-permute-done | bytes 262176 | tf_op jit(solution)/shard_map/ppermute | solution.py:244
  165.1 1.1 fusion.16
  166.4 0.6 collective-permute-done.16
  167.0 1.1 fusion.15
  168.1 1.7 collective-permute-done.8
  169.8 4.3 %collective-permute-done.5 = bf16[512,256]{1,0:T(8,128)(2,1)S(1)} collective-permute-done((bf16[512,256]{1,0:T(8,128)(2,1)S(1)}, bf16[512,256]{1,0:T(8,128)(2,1)S(1)}, u32[]{:S(2)}, u32[]{:S(2)}) %collective-permute-start.5) | collective-permute-done | bytes 262176 | tf_op jit(solution)/shard_map/ppermute | solution.py:244
  174.1 1.1 fusion.14
  175.3 0.8 pad_maximum_fusion
  (52 shorter events, 4.8 us)
Async XLA Ops:
  6.5 97.1 %all-gather.2.cloned.1.call-start = ((), (), s32[]{:S(2)}) async-start(), calls=%async_computation.2 | async-start | bytes 8912896 | tf_op jit(solution)/shard_map/all_gather | solution.py:271
  10.1 12.7 %all-to-all-start = ((s32[16,1,72]{2,1,0:T(1,128)}), s32[16,1,72]{2,1,0:T(1,128)S(1)}, u32[]{:S(2)}, u32[]{:S(2)}) async-start(s32[16,1,72]{2,1,0:T(1,128)} %broadcast_in_dim.24), calls=%async_computation | async-start | bytes 16384 | tf_op jit(solution)/shard_map/all_to_all | solution.py:277
  22.8 0.6 copy-start.3
  27.2 76.0 %copy-start.4 = (s32[16,1,72]{2,1,0:T(1,128)S(1)}, s32[16,1,72]{2,1,0:T(1,128)}, u32[]{:S(2)}) copy-start(s32[16,1,72]{2,1,0:T(1,128)} %copy-done.3) | copy-start | bytes 13828
  27.2 76.4 %copy-start.1 = (bf16[4096,256]{1,0:T(8,128)(2,1)S(1)}, bf16[4096,256]{1,0:T(8,128)(2,1)}, u32[]{:S(2)}) copy-start(bf16[4096,256]{1,0:T(8,128)(2,1)} %weight_ref.2) | copy-start | bytes 6291460
  27.2 84.1 %all-to-all-start.1 = ((bf16[16,2,128,512]{3,2,1,0:T(8,128)(2,1)}), bf16[16,2,128,512]{3,2,1,0:T(8,128)(2,1)}, u32[]{:S(2)}, u32[]{:S(2)}) async-start(bf16[16,2,128,512]{3,2,1,0:T(8,128)(2,1)} %select_blocks.1), calls=%async_computation.1 | async-start | bytes 8388608 | tf_op jit(solution)/shard_map/all_to_all | solution.py:280
  102.8 19.1 %collective-permute-start.1 = (bf16[8,256,256]{2,1,0:T(8,128)(2,1)}, bf16[8,256,256]{2,1,0:T(8,128)(2,1)}, u32[]{:S(2)}, u32[]{:S(2)}) collective-permute-start(bf16[8,256,256]{2,1,0:T(8,128)(2,1)} %get-tuple-element.8), channel_id=1, source_target_pairs={{0,1},{1,0},{2,3},{3,2},{4,5},{5,4},{6,7},{7,6},{8,9},{9,8},{10,11... | collective-permute-start | bytes 3145736 | tf_op jit(solution)/shard_map/ppermute | solution.py:297
  103.6 3.4 %copy-start = (bf16[1024,4096]{1,0:T(8,128)(2,1)S(1)}, bf16[1024,4096]{1,0:T(8,128)(2,1)}, u32[]{:S(2)}) copy-start(bf16[1024,4096]{1,0:T(8,128)(2,1)} %all-gather.2.cloned.1.call-done.tokens_ref) | copy-start | bytes 25165828
  111.3 3.5 %copy-start.2 = (bf16[8,256,256]{2,1,0:T(8,128)(2,1)S(1)}, bf16[8,256,256]{2,1,0:T(8,128)(2,1)}, u32[]{:S(2)}) copy-start(bf16[8,256,256]{2,1,0:T(8,128)(2,1)} %get-tuple-element.7) | copy-start | bytes 3145732
  114.4 7.4 %collective-permute-start.9 = (bf16[512,256]{1,0:T(8,128)(2,1)S(1)}, bf16[512,256]{1,0:T(8,128)(2,1)S(1)}, u32[]{:S(2)}, u32[]{:S(2)}) collective-permute-start(bf16[512,256]{1,0:T(8,128)(2,1)S(1)} %attend.3), channel_id=1, source_target_pairs={{0,1},{1,0},{2,3},{3,2},{4,5},{5,4},{6,7},{7,6},{8,9},{9,8},{10,11... | collective-permute-start | bytes 786440 | tf_op jit(solution)/shard_map/ppermute | solution.py:301
  120.0 7.6 %collective-permute-start = (bf16[512,256]{1,0:T(8,128)(2,1)S(1)}, bf16[512,256]{1,0:T(8,128)(2,1)S(1)}, u32[]{:S(2)}, u32[]{:S(2)}) collective-permute-start(bf16[512,256]{1,0:T(8,128)(2,1)S(1)} %attend.2), channel_id=1, source_target_pairs={{0,1},{1,0},{2,3},{3,2},{4,5},{5,4},{6,7},{7,6},{8,9},{9,8},{10,11... | collective-permute-start | bytes 786440 | tf_op jit(solution)/shard_map/ppermute | solution.py:301
  123.0 10.3 %collective-permute-start.13 = (bf16[512,256]{1,0:T(8,128)(2,1)S(1)}, bf16[512,256]{1,0:T(8,128)(2,1)S(1)}, u32[]{:S(2)}, u32[]{:S(2)}) collective-permute-start(bf16[512,256]{1,0:T(8,128)(2,1)S(1)} %fusion.29), channel_id=1, source_target_pairs={{0,14},{2,0},{4,2},{6,4},{8,6},{10,8},{12,10},{14,12},{1,15},{3,1}... | collective-permute-start | bytes 786440 | tf_op jit(solution)/shard_map/ppermute | solution.py:244
  127.5 10.5 %collective-permute-start.10 = (bf16[512,256]{1,0:T(8,128)(2,1)S(1)}, bf16[512,256]{1,0:T(8,128)(2,1)S(1)}, u32[]{:S(2)}, u32[]{:S(2)}) collective-permute-start(bf16[512,256]{1,0:T(8,128)(2,1)S(1)} %fusion.28), channel_id=1, source_target_pairs={{0,2},{2,4},{4,6},{6,8},{8,10},{10,12},{12,14},{14,0},{1,3},{3,5},... | collective-permute-start | bytes 786440 | tf_op jit(solution)/shard_map/ppermute | solution.py:244
  128.7 10.5 %collective-permute-start.6 = (bf16[512,256]{1,0:T(8,128)(2,1)S(1)}, bf16[512,256]{1,0:T(8,128)(2,1)S(1)}, u32[]{:S(2)}, u32[]{:S(2)}) collective-permute-start(bf16[512,256]{1,0:T(8,128)(2,1)S(1)} %fusion.27), channel_id=1, source_target_pairs={{0,14},{2,0},{4,2},{6,4},{8,6},{10,8},{12,10},{14,12},{1,15},{3,1}... | collective-permute-start | bytes 786440 | tf_op jit(solution)/shard_map/ppermute | solution.py:244
  133.1 10.5 %collective-permute-start.2 = (bf16[512,256]{1,0:T(8,128)(2,1)S(1)}, bf16[512,256]{1,0:T(8,128)(2,1)S(1)}, u32[]{:S(2)}, u32[]{:S(2)}) collective-permute-start(bf16[512,256]{1,0:T(8,128)(2,1)S(1)} %fusion.26), channel_id=1, source_target_pairs={{0,2},{2,4},{4,6},{6,8},{8,10},{10,12},{12,14},{14,0},{1,3},{3,5},... | collective-permute-start | bytes 786440 | tf_op jit(solution)/shard_map/ppermute | solution.py:244
  134.4 10.5 %collective-permute-start.14 = (bf16[512,256]{1,0:T(8,128)(2,1)S(1)}, bf16[512,256]{1,0:T(8,128)(2,1)S(1)}, u32[]{:S(2)}, u32[]{:S(2)}) collective-permute-start(bf16[512,256]{1,0:T(8,128)(2,1)S(1)} %fusion.25), channel_id=1, source_target_pairs={{0,14},{2,0},{4,2},{6,4},{8,6},{10,8},{12,10},{14,12},{1,15},{3,1}... | collective-permute-start | bytes 786440 | tf_op jit(solution)/shard_map/ppermute | solution.py:244
  139.1 10.5 %collective-permute-start.11 = (bf16[512,256]{1,0:T(8,128)(2,1)S(1)}, bf16[512,256]{1,0:T(8,128)(2,1)S(1)}, u32[]{:S(2)}, u32[]{:S(2)}) collective-permute-start(bf16[512,256]{1,0:T(8,128)(2,1)S(1)} %fusion.22), channel_id=1, source_target_pairs={{0,2},{2,4},{4,6},{6,8},{8,10},{10,12},{12,14},{14,0},{1,3},{3,5},... | collective-permute-start | bytes 786440 | tf_op jit(solution)/shard_map/ppermute | solution.py:244
  140.3 20.6 %collective-permute-start.7 = (bf16[512,256]{1,0:T(8,128)(2,1)S(1)}, bf16[512,256]{1,0:T(8,128)(2,1)S(1)}, u32[]{:S(2)}, u32[]{:S(2)}) collective-permute-start(bf16[512,256]{1,0:T(8,128)(2,1)S(1)} %fusion.20), channel_id=1, source_target_pairs={{0,14},{2,0},{4,2},{6,4},{8,6},{10,8},{12,10},{14,12},{1,15},{3,1}... | collective-permute-start | bytes 786440 | tf_op jit(solution)/shard_map/ppermute | solution.py:244
  144.8 10.5 %collective-permute-start.3 = (bf16[512,256]{1,0:T(8,128)(2,1)S(1)}, bf16[512,256]{1,0:T(8,128)(2,1)S(1)}, u32[]{:S(2)}, u32[]{:S(2)}) collective-permute-start(bf16[512,256]{1,0:T(8,128)(2,1)S(1)} %fusion.18), channel_id=1, source_target_pairs={{0,2},{2,4},{4,6},{6,8},{8,10},{10,12},{12,14},{14,0},{1,3},{3,5},... | collective-permute-start | bytes 786440 | tf_op jit(solution)/shard_map/ppermute | solution.py:244
  146.0 10.5 %collective-permute-start.15 = (bf16[512,256]{1,0:T(8,128)(2,1)S(1)}, bf16[512,256]{1,0:T(8,128)(2,1)S(1)}, u32[]{:S(2)}, u32[]{:S(2)}) collective-permute-start(bf16[512,256]{1,0:T(8,128)(2,1)S(1)} %fusion.24), channel_id=1, source_target_pairs={{0,14},{2,0},{4,2},{6,4},{8,6},{10,8},{12,10},{14,12},{1,15},{3,1}... | collective-permute-start | bytes 786440 | tf_op jit(solution)/shard_map/ppermute | solution.py:244
  150.8 15.6 %collective-permute-start.12 = (bf16[512,256]{1,0:T(8,128)(2,1)S(1)}, bf16[512,256]{1,0:T(8,128)(2,1)S(1)}, u32[]{:S(2)}, u32[]{:S(2)}) collective-permute-start(bf16[512,256]{1,0:T(8,128)(2,1)S(1)} %fusion.21), channel_id=1, source_target_pairs={{0,2},{2,4},{4,6},{6,8},{8,10},{10,12},{12,14},{14,0},{1,3},{3,5},... | collective-permute-start | bytes 786440 | tf_op jit(solution)/shard_map/ppermute | solution.py:244
  156.4 8.7 %collective-permute-start.4 = (bf16[512,256]{1,0:T(8,128)(2,1)S(1)}, bf16[512,256]{1,0:T(8,128)(2,1)S(1)}, u32[]{:S(2)}, u32[]{:S(2)}) collective-permute-start(bf16[512,256]{1,0:T(8,128)(2,1)S(1)} %fusion.17), channel_id=1, source_target_pairs={{0,2},{2,4},{4,6},{6,8},{8,10},{10,12},{12,14},{14,0},{1,3},{3,5},... | collective-permute-start | bytes 786440 | tf_op jit(solution)/shard_map/ppermute | solution.py:244
  157.7 9.3 %collective-permute-start.16 = (bf16[512,256]{1,0:T(8,128)(2,1)S(1)}, bf16[512,256]{1,0:T(8,128)(2,1)S(1)}, u32[]{:S(2)}, u32[]{:S(2)}) collective-permute-start(bf16[512,256]{1,0:T(8,128)(2,1)S(1)} %fusion.23), channel_id=1, source_target_pairs={{0,14},{2,0},{4,2},{6,4},{8,6},{10,8},{12,10},{14,12},{1,15},{3,1}... | collective-permute-start | bytes 786440 | tf_op jit(solution)/shard_map/ppermute | solution.py:244
  162.1 7.7 %collective-permute-start.8 = (bf16[512,256]{1,0:T(8,128)(2,1)S(1)}, bf16[512,256]{1,0:T(8,128)(2,1)S(1)}, u32[]{:S(2)}, u32[]{:S(2)}) collective-permute-start(bf16[512,256]{1,0:T(8,128)(2,1)S(1)} %fusion.19), channel_id=1, source_target_pairs={{0,14},{2,0},{4,2},{6,4},{8,6},{10,8},{12,10},{14,12},{1,15},{3,1}... | collective-permute-start | bytes 786440 | tf_op jit(solution)/shard_map/ppermute | solution.py:244
  166.3 7.8 %collective-permute-start.5 = (bf16[512,256]{1,0:T(8,128)(2,1)S(1)}, bf16[512,256]{1,0:T(8,128)(2,1)S(1)}, u32[]{:S(2)}, u32[]{:S(2)}) collective-permute-start(bf16[512,256]{1,0:T(8,128)(2,1)S(1)} %fusion.16), channel_id=1, source_target_pairs={{0,2},{2,4},{4,6},{6,8},{8,10},{10,12},{12,14},{14,0},{1,3},{3,5},... | collective-permute-start | bytes 786440 | tf_op jit(solution)/shard_map/ppermute | solution.py:244
Sparse Core Ops, SparseCore 0:
  9.1 67.0 all-gather.1

commit v3 on v2

--- a/solution.py
+++ b/solution.py
@@ -193,19 +193,14 @@
     )(slot_index, lengths, queries, rows)
 
 
-def relay_kernel(place_ref, weight_ref, own_ref, lent_ref, sems):
+def relay_kernel(place_ref, weight_ref, own_ref, lent_ref):
     here, core = place_ref[0], place_ref[1]
     ring, _, width = own_ref.shape
-    copies = []
     for k in range(ring):
         chip = lax.rem(here + k, ring)
-        for i, (ref, which) in enumerate(((own_ref, core), (lent_ref, 1 - core))):
+        for ref, which in ((own_ref, core), (lent_ref, 1 - core)):
             cols = pl.ds(pl.multiple_of((chip * 2 + which) * width, width), width)
-            copy = pltpu.make_async_copy(weight_ref.at[:, cols], ref.at[k], sems.at[i, k])
-            copy.start()
-            copies.append(copy)
-    for copy in copies:
-        copy.wait()
+            ref[k] = weight_ref[:, cols]
 
 
 def relay(place, weight, ring):
@@ -214,36 +209,68 @@
     return pl.pallas_call(
         relay_kernel,
         out_shape=(shape, shape),
-        in_specs=[SMEM, ANY],
-        out_specs=(ANY, ANY),
-        scratch_shapes=[pltpu.SemaphoreType.DMA((2, ring))],
+        in_specs=[SMEM, VMEM],
+        out_specs=(VMEM, VMEM),
+        compiler_params=pltpu.CompilerParams(vmem_limit_bytes=16 << 20),
         cost_estimate=pl.CostEstimate(flops=0, bytes_accessed=4 << 20, transcendentals=0),
         name="relay",
     )(place, weight)
 
 
+def share_kernel(steps, own_ref, partner_ref, own_w_ref, partner_w_ref, *out_refs):
+    for step, ref in zip(steps, out_refs):
+        ref[...] = (
+            jnp.dot(own_ref[...], own_w_ref[step], preferred_element_type=F32)
+            + jnp.dot(partner_ref[...], partner_w_ref[step], preferred_element_type=F32)
+        ).astype(ref.dtype)
+
+
+def shares(starts, rest, own, partner, own_weight, partner_weight):
+    rows, width = own.shape
+    steps = starts + rest
+    outs = [
+        jax.ShapeDtypeStruct((rows, width), BF16 if i < len(starts) else F32)
+        for i in range(len(steps))
+    ]
+    return pl.pallas_call(
+        functools.partial(share_kernel, steps),
+        out_shape=outs,
+        in_specs=[VMEM] * 4,
+        out_specs=[VMEM] * len(outs),
+        compiler_params=pltpu.CompilerParams(vmem_limit_bytes=24 << 20),
+        cost_estimate=pl.CostEstimate(
+            flops=4 * rows * width * width * len(steps), bytes_accessed=6 << 20, transcendentals=0
+        ),
+        name="shares",
+    )(own, partner, own_weight, partner_weight)
+
+
 def reduce_ring(attended, partner_attended, own_weight, partner_weight, ring):
     up = [(i, (i + 1) % ring) for i in range(ring)]
     down = [(i, (i - 1) % ring) for i in range(ring)]
-
-    def share(half, step):
-        return jnp.dot(
-            attended[half], own_weight[step % ring], preferred_element_type=F32
-        ) + jnp.dot(partner_attended[half], partner_weight[step % ring], preferred_element_type=F32)
-
     far = ring // 2
     chains = [(0, 1, far), (1, -1, far), (0, -1, far - 1), (1, 1, far - 1)]
-    held = {}
+    held, part = {}, {}
+    for half in range(2):
+        mine = [(way, first) for rows, way, first in chains if rows == half]
+        starts = [way * first % ring for way, first in mine]
+        rest = [k for k in range(ring) if k not in starts]
+        made = shares(
+            starts, rest, attended[half], partner_attended[half], own_weight, partner_weight
+        )
+        for i, (way, _) in enumerate(mine):
+            held[half, way] = made[i]
+        part.update({(half, k): made[len(starts) + i] for i, k in enumerate(rest)})
     for distance in range(far, 0, -1):
         for half, way, first in chains:
             if distance > first:
                 continue
-            part = share(half, way * distance)
             if distance < first:
-                part = part + held[half, way].astype(F32)
-            held[half, way] = lax.ppermute(part.astype(BF16), "z", up if way == 1 else down)
+                total = held[half, way].astype(F32) + part[half, way * distance % ring]
+                held[half, way] = total.astype(BF16)
+            held[half, way] = lax.ppermute(held[half, way], "z", up if way == 1 else down)
     out = [
-        (share(half, 0) + held[half, 1].astype(F32) + held[half, -1].astype(F32)).astype(BF16)
+        (part[half, 0] + held[half, 1].astype(F32) + held[half, -1].astype(F32)).astype(BF16)
         for half in range(2)
     ]
     return jnp.concatenate(out, axis=0)

time: 184 us -> 162 us (0.88)
  Pallas kernels: 87.3 us -> 23.4 us
  waiting for transfers between devices: 15.3 us -> 74.7 us
  matrix products: 21.7 us -> 0 us
  starting transfers between devices: 36 us -> 39.6 us
    pallas_call x1 -> x3, Pallas kernels: 68.2 us -> 4.34 us  [the longest x2 2.51 us: shares(): pl.pallas_call(functools.partial(share_kernel, steps), out_shape=outs, in...]
    all_gather x1, waiting for transfers between devices: 0.02 us -> 39.9 us  [local(): gathered = lax.all_gather(tokens, ('z', 'c'), axis=1, tiled=True)]
    dot_general x32 -> x0, matrix products: 21.7 us -> none  [the longest x16 18.1 us: share(): jnp.dot(partner_attended[half], partner_weight[step % ring], preferred_el...]
    ppermute x14, waiting for transfers between devices: 14 us -> 24.6 us  [reduce_ring(): lax.ppermute(held[half, way], 'z', up if way == 1 else down)]
    all_to_all x1, waiting for transfers between devices: 0.01 us -> 8.79 us  [local(): rows = lax.all_to_all(sent, DB, split_axis=0, concat_axis=0, tiled=True)]
    ppermute x14, starting transfers between devices: 21.1 us -> 25 us  [reduce_ring(): lax.ppermute(held[half, way], 'z', up if way == 1 else down)]
  transfers between devices with their start and end apart: 20 -> 20, of which waited for: 6 -> 12; matrix products, arithmetic and copies ran while one was open for 13% -> 3% of each run, Pallas kernels for 48% -> 14%
where the time goes in v3:
time: 162 us
  waiting for transfers between devices  74.7 us (46%)
  starting transfers between devices  39.6 us (24%)
  Pallas kernels  23.4 us (14%)
  between operations  13.6 us (8%)
  local copies, waits for them, and re-layouts  7.87 us (5%)
  other arithmetic  2.71 us (2%)
    all_gather x1, waiting for transfers between devices, local(): gathered = lax.all_gather(tokens, ('z', 'c'), axis=1, tiled=True)  39.9 us
    ppermute x14, starting transfers between devices, reduce_ring(): lax.ppermute(held[half, way], 'z', up if way == 1 else down)  25 us
    ppermute x14, waiting for transfers between devices, reduce_ring(): lax.ppermute(held[half, way], 'z', up if way == 1 else down)  24.6 us
    all_to_all x1, waiting for transfers between devices, local(): rows = lax.all_to_all(sent, DB, split_axis=0, concat_axis=0, tiled=True)  8.79 us
    all_to_all x1, starting transfers between devices, local(): heard = lax.all_to_all(notes, DB, split_axis=0, concat_axis=0, tiled=True)  7.17 us
    all_to_all x1, starting transfers between devices, local(): rows = lax.all_to_all(sent, DB, split_axis=0, concat_axis=0, tiled=True)  6.73 us
    pallas_call x2, Pallas kernels, attend(): pl.pallas_call(functools.partial(attend_kernel, part * count), grid=(1,),...  6.13 us
    unnamed x10, local copies, waits for them, and re-layouts  5.58 us
  transfers between devices with their start and end apart: 20, of which 12 were waited for; matrix products, arithmetic and copies ran while one was open for 3% of the time, Pallas kernels for 14%

profile of v3, /device:TPU:24, one launch (start us, length us, event | category | flops | bytes accessed | tf_op | source)
XLA Modules:
  0.0 161.9 jit_solution(17020975987391690461)
XLA Ops:
  6.5 0.7 all-gather.2.cloned.1.call-update
  7.3 0.8 reshape.32
  8.0 0.8 reshape.31
  8.8 0.7 pad_add_fusion
  9.5 0.6 broadcast_in_dim.24
  10.1 7.2 %all-to-all-start = ((s32[16,1,72]{2,1,0:T(1,128)}), s32[16,1,72]{2,1,0:T(1,128)S(1)}, u32[]{:S(2)}, u32[]{:S(2)}) async-start(s32[16,1,72]{2,1,0:T(1,128)} %broadcast_in_dim.24), calls=%async_computation | async-start | bytes 16384 | tf_op jit(solution)/shard_map/all_to_all | solution.py:304
  17.3 4.9 %project_blocks.1.rows_ref = bf16[8,128,512]{2,1,0:T(8,128)(2,1)} custom-call(f32[8,7]{1,0:T(8,128)} %scales_ref.1, bf16[8,128,896]{2,1,0:T(8,128)(2,1)} %codes_ref.1, bf16[896,256]{1,0:T(8,128)(2,1)} %key_ref.1, bf16[896,256]{1,0:T(8,128)(2,1)} %value_ref.1), custom_call_target="tpu_custom_call" | custom-call | flops 939524096 | bytes 5242880 | tf_op jit(solution)/shard_map/project_blocks/pallas_call | solution.py:52
  22.1 0.6 all-to-all-done
  22.8 0.6 copy-done.3
  23.4 3.8 %select_blocks.1 = bf16[16,2,128,512]{3,2,1,0:T(8,128)(2,1)} custom-call(s32[1]{0:T(128)} %bitcast.3.place_ref, s32[16,72]{1,0:T(8,128)} %bitcast.7, bf16[8,128,512]{2,1,0:T(8,128)(2,1)} %project_blocks.1.rows_ref), custom_call_target="tpu_custom_call" | custom-call | bytes 9437184 | tf_op jit(solution)/shard_map/select_blocks/pallas_call | solution.py:92
  27.2 6.7 %all-to-all-start.1 = ((bf16[16,2,128,512]{3,2,1,0:T(8,128)(2,1)}), bf16[16,2,128,512]{3,2,1,0:T(8,128)(2,1)}, u32[]{:S(2)}, u32[]{:S(2)}) async-start(bf16[16,2,128,512]{3,2,1,0:T(8,128)(2,1)} %select_blocks.1), calls=%async_computation.1 | async-start | bytes 8388608 | tf_op jit(solution)/shard_map/all_to_all | solution.py:307
  34.0 1.8 %relay.1 = (bf16[8,256,256]{2,1,0:T(8,128)(2,1)S(1)}, bf16[8,256,256]{2,1,0:T(8,128)(2,1)}) custom-call(s32[2]{0:T(128)S(1)} %pad_add_fusion.1.place_ref, bf16[256,4096]{1,0:T(8,128)(2,1)S(1)} %copy-done.1), custom_call_target="tpu_custom_call" | custom-call | bytes 4194304 | tf_op jit(solution)/shard_map/relay/pallas_call | solution.py:209
  35.9 0.2 convert_reduce_fusion
  36.1 0.1 broadcast_in_dim.25
  36.2 0.2 select_reduce_fusion.length_ref
  36.4 39.9 %all-gather.2.cloned.1.call-done.tokens_ref = bf16[1024,4096]{1,0:T(8,128)(2,1)} async-done(((bf16[1024,256]{1,0:T(8,128)(2,1)}), bf16[1024,4096]{1,0:T(8,128)(2,1)}) %all-gather.2.cloned.1.call-update) | async-done | bytes 8388624 | tf_op jit(solution)/shard_map/all_gather | solution.py:298
  76.3 3.4 %copy-done = bf16[1024,4096]{1,0:T(8,128)(2,1)S(1)} copy-done((bf16[1024,4096]{1,0:T(8,128)(2,1)S(1)}, bf16[1024,4096]{1,0:T(8,128)(2,1)}, u32[]{:S(2)}) %copy-start) | copy-done | bytes 8388632
  79.7 1.6 copy-done.2
  81.3 4.3 %project_queries.1.query_ref = bf16[1024,256]{1,0:T(8,128)(2,1)S(1)} custom-call(bf16[1024,4096]{1,0:T(8,128)(2,1)S(1)} %copy-done, bf16[4096,256]{1,0:T(8,128)(2,1)S(1)} %copy-done.2), custom_call_target="tpu_custom_call" | custom-call | flops 2147483648 | bytes 11534336 | tf_op jit(solution)/shard_map/project_queries/pallas_call | solution.py:113
  85.6 8.8 %all-to-all-done.1 = bf16[16,2,128,512]{3,2,1,0:T(8,128)(2,1)} async-done(((bf16[16,2,128,512]{3,2,1,0:T(8,128)(2,1)}), bf16[16,2,128,512]{3,2,1,0:T(8,128)(2,1)}, u32[]{:S(2)}, u32[]{:S(2)}) %all-to-all-start.1) | async-done | bytes 4194336 | tf_op jit(solution)/shard_map/all_to_all | solution.py:307
  94.4 3.1 %attend.3.own_ref = bf16[512,256]{1,0:T(8,128)(2,1)S(1)} custom-call(s32[32]{0:T(128)S(1)} %get-tuple-element.42.slot_ref, s32[32]{0:T(128)S(1)} %select_reduce_fusion.length_ref, bf16[1024,256]{1,0:T(8,128)(2,1)S(1)} %project_queries.1.query_ref, bf16[32,128,512]{2,1,0:T(8,128)(2,1)} %bitcast.4.rows_ref), custom_call_target="tpu_custom_call" | custom-call | flops 134217728 | bytes 3145728 | tf_op jit(solution)/shard_map/attend/pallas_call | solution.py:178
  97.5 0.1 collective-permute-start.9
  97.6 3.1 %attend.2.own_ref = bf16[512,256]{1,0:T(8,128)(2,1)S(1)} custom-call(s32[32]{0:T(128)S(1)} %get-tuple-element.42.slot_ref, s32[32]{0:T(128)S(1)} %select_reduce_fusion.length_ref, bf16[1024,256]{1,0:T(8,128)(2,1)S(1)} %project_queries.1.query_ref, bf16[32,128,512]{2,1,0:T(8,128)(2,1)} %bitcast.4.rows_ref), custom_call_target="tpu_custom_call" | custom-call | flops 134217728 | bytes 3145728 | tf_op jit(solution)/shard_map/attend/pallas_call | solution.py:178
  100.6 0.6 collective-permute-start
  101.2 1.3 shares.3
  102.5 5.9 %collective-permute-start.13 = (bf16[512,256]{1,0:T(8,128)(2,1)S(1)}, bf16[512,256]{1,0:T(8,128)(2,1)S(1)}, u32[]{:S(2)}, u32[]{:S(2)}) collective-permute-start(bf16[512,256]{1,0:T(8,128)(2,1)S(1)} %get-tuple-element.37), channel_id=1, source_target_pairs={{0,14},{2,0},{4,2},{6,4},{8,6},{10,8},{12,10},{14,12},{1,15},{3,1}... | collective-permute-start | bytes 786440 | tf_op jit(solution)/shard_map/ppermute | solution.py:271
  108.5 1.3 shares.2
  109.7 3.3 %collective-permute-start.6 = (bf16[512,256]{1,0:T(8,128)(2,1)S(1)}, bf16[512,256]{1,0:T(8,128)(2,1)S(1)}, u32[]{:S(2)}, u32[]{:S(2)}) collective-permute-start(bf16[512,256]{1,0:T(8,128)(2,1)S(1)} %get-tuple-element.30), channel_id=1, source_target_pairs={{0,14},{2,0},{4,2},{6,4},{8,6},{10,8},{12,10},{14,12},{1,15},{3,1}... | collective-permute-start | bytes 786440 | tf_op jit(solution)/shard_map/ppermute | solution.py:271
  113.0 2.1 %collective-permute-done.13 = bf16[512,256]{1,0:T(8,128)(2,1)S(1)} collective-permute-done((bf16[512,256]{1,0:T(8,128)(2,1)S(1)}, bf16[512,256]{1,0:T(8,128)(2,1)S(1)}, u32[]{:S(2)}, u32[]{:S(2)}) %collective-permute-start.13) | collective-permute-done | bytes 262176 | tf_op jit(solution)/shard_map/ppermute | solution.py:271
  115.2 3.9 %collective-permute-start.14 = (bf16[512,256]{1,0:T(8,128)(2,1)S(1)}, bf16[512,256]{1,0:T(8,128)(2,1)S(1)}, u32[]{:S(2)}, u32[]{:S(2)}) collective-permute-start(bf16[512,256]{1,0:T(8,128)(2,1)S(1)} %add_convert_fusion.3), channel_id=1, source_target_pairs={{0,14},{2,0},{4,2},{6,4},{8,6},{10,8},{12,10},{14,12},{1,15},{3,1}... | collective-permute-start | bytes 786440 | tf_op jit(solution)/shard_map/ppermute | solution.py:271
  119.2 0.1 collective-permute-start.11
  119.3 1.5 collective-permute-done.6
  120.8 3.8 %collective-permute-start.7 = (bf16[512,256]{1,0:T(8,128)(2,1)S(1)}, bf16[512,256]{1,0:T(8,128)(2,1)S(1)}, u32[]{:S(2)}, u32[]{:S(2)}) collective-permute-start(bf16[512,256]{1,0:T(8,128)(2,1)S(1)} %add_convert_fusion.8), channel_id=1, source_target_pairs={{0,14},{2,0},{4,2},{6,4},{8,6},{10,8},{12,10},{14,12},{1,15},{3,1}... | collective-permute-start | bytes 786440 | tf_op jit(solution)/shard_map/ppermute | solution.py:271
  124.6 0.1 collective-permute-start.3
  124.7 1.6 %collective-permute-done.14 = bf16[512,256]{1,0:T(8,128)(2,1)S(1)} collective-permute-done((bf16[512,256]{1,0:T(8,128)(2,1)S(1)}, bf16[512,256]{1,0:T(8,128)(2,1)S(1)}, u32[]{:S(2)}, u32[]{:S(2)}) %collective-permute-start.14) | collective-permute-done | bytes 262176 | tf_op jit(solution)/shard_map/ppermute | solution.py:271
  126.4 3.8 %collective-permute-start.15 = (bf16[512,256]{1,0:T(8,128)(2,1)S(1)}, bf16[512,256]{1,0:T(8,128)(2,1)S(1)}, u32[]{:S(2)}, u32[]{:S(2)}) collective-permute-start(bf16[512,256]{1,0:T(8,128)(2,1)S(1)} %add_convert_fusion.2), channel_id=1, source_target_pairs={{0,14},{2,0},{4,2},{6,4},{8,6},{10,8},{12,10},{14,12},{1,15},{3,1}... | collective-permute-start | bytes 786440 | tf_op jit(solution)/shard_map/ppermute | solution.py:271
  130.3 0.1 collective-permute-start.12
  130.4 5.4 %collective-permute-done.3 = bf16[512,256]{1,0:T(8,128)(2,1)S(1)} collective-permute-done((bf16[512,256]{1,0:T(8,128)(2,1)S(1)}, bf16[512,256]{1,0:T(8,128)(2,1)S(1)}, u32[]{:S(2)}, u32[]{:S(2)}) %collective-permute-start.3) | collective-permute-done | bytes 262176 | tf_op jit(solution)/shard_map/ppermute | solution.py:271
  135.8 0.1 collective-permute-start.4
  135.9 0.8 collective-permute-done.15
  136.7 3.8 %collective-permute-start.16 = (bf16[512,256]{1,0:T(8,128)(2,1)S(1)}, bf16[512,256]{1,0:T(8,128)(2,1)S(1)}, u32[]{:S(2)}, u32[]{:S(2)}) collective-permute-start(bf16[512,256]{1,0:T(8,128)(2,1)S(1)} %add_convert_fusion.1), channel_id=1, source_target_pairs={{0,14},{2,0},{4,2},{6,4},{8,6},{10,8},{12,10},{14,12},{1,15},{3,1}... | collective-permute-start | bytes 786440 | tf_op jit(solution)/shard_map/ppermute | solution.py:271
  140.6 0.1 collective-permute-start.8
  140.7 5.0 %collective-permute-done.4 = bf16[512,256]{1,0:T(8,128)(2,1)S(1)} collective-permute-done((bf16[512,256]{1,0:T(8,128)(2,1)S(1)}, bf16[512,256]{1,0:T(8,128)(2,1)S(1)}, u32[]{:S(2)}, u32[]{:S(2)}) %collective-permute-start.4) | collective-permute-done | bytes 262176 | tf_op jit(solution)/shard_map/ppermute | solution.py:271
  145.8 0.1 collective-permute-start.5
  145.9 1.4 collective-permute-done.16
  147.4 3.7 %collective-permute-done.8 = bf16[512,256]{1,0:T(8,128)(2,1)S(1)} collective-permute-done((bf16[512,256]{1,0:T(8,128)(2,1)S(1)}, bf16[512,256]{1,0:T(8,128)(2,1)S(1)}, u32[]{:S(2)}, u32[]{:S(2)}) %collective-permute-start.8) | collective-permute-done | bytes 262176 | tf_op jit(solution)/shard_map/ppermute | solution.py:271
  151.0 3.1 %collective-permute-done.5 = bf16[512,256]{1,0:T(8,128)(2,1)S(1)} collective-permute-done((bf16[512,256]{1,0:T(8,128)(2,1)S(1)}, bf16[512,256]{1,0:T(8,128)(2,1)S(1)}, u32[]{:S(2)}, u32[]{:S(2)}) %collective-permute-start.5) | collective-permute-done | bytes 262176 | tf_op jit(solution)/shard_map/ppermute | solution.py:271
  154.2 0.8 pad_maximum_fusion
  (34 shorter events, 0.9 us)
Async XLA Ops:
  6.5 69.8 %all-gather.2.cloned.1.call-start = ((), (), s32[]{:S(2)}) async-start(), calls=%async_computation.2 | async-start | bytes 8912896 | tf_op jit(solution)/shard_map/all_gather | solution.py:298
  10.1 12.7 %all-to-all-start = ((s32[16,1,72]{2,1,0:T(1,128)}), s32[16,1,72]{2,1,0:T(1,128)S(1)}, u32[]{:S(2)}, u32[]{:S(2)}) async-start(s32[16,1,72]{2,1,0:T(1,128)} %broadcast_in_dim.24), calls=%async_computation | async-start | bytes 16384 | tf_op jit(solution)/shard_map/all_to_all | solution.py:304
  22.8 0.6 copy-start.3
  27.2 6.8 %copy-start.1 = (bf16[256,4096]{1,0:T(8,128)(2,1)S(1)}, bf16[256,4096]{1,0:T(8,128)(2,1)}, u32[]{:S(2)}) copy-start(bf16[256,4096]{1,0:T(8,128)(2,1)} %weight_ref.3) | copy-start | bytes 6291460
  27.2 8.8 %copy-start.4 = (s32[16,1,72]{2,1,0:T(1,128)S(1)}, s32[16,1,72]{2,1,0:T(1,128)}, u32[]{:S(2)}) copy-start(s32[16,1,72]{2,1,0:T(1,128)} %copy-done.3) | copy-start | bytes 13828
  27.2 67.2 %all-to-all-start.1 = ((bf16[16,2,128,512]{3,2,1,0:T(8,128)(2,1)}), bf16[16,2,128,512]{3,2,1,0:T(8,128)(2,1)}, u32[]{:S(2)}, u32[]{:S(2)}) async-start(bf16[16,2,128,512]{3,2,1,0:T(8,128)(2,1)} %select_blocks.1), calls=%async_computation.1 | async-start | bytes 8388608 | tf_op jit(solution)/shard_map/all_to_all | solution.py:307
  35.9 65.4 %collective-permute-start.1 = (bf16[8,256,256]{2,1,0:T(8,128)(2,1)}, bf16[8,256,256]{2,1,0:T(8,128)(2,1)S(1)}, u32[]{:S(2)}, u32[]{:S(2)}) collective-permute-start(bf16[8,256,256]{2,1,0:T(8,128)(2,1)} %get-tuple-element.24), channel_id=1, source_target_pairs={{0,1},{1,0},{2,3},{3,2},{4,5},{5,4},{6,7},{7,6},{8,9},{9,8},{10,11... | collective-permute-start | bytes 3145736 | tf_op jit(solution)/shard_map/ppermute | solution.py:324
  76.3 3.4 %copy-start = (bf16[1024,4096]{1,0:T(8,128)(2,1)S(1)}, bf16[1024,4096]{1,0:T(8,128)(2,1)}, u32[]{:S(2)}) copy-start(bf16[1024,4096]{1,0:T(8,128)(2,1)} %all-gather.2.cloned.1.call-done.tokens_ref) | copy-start | bytes 25165828
  79.7 1.6 copy-start.2
  97.5 3.8 %collective-permute-start.9 = (bf16[512,256]{1,0:T(8,128)(2,1)S(1)}, bf16[512,256]{1,0:T(8,128)(2,1)S(1)}, u32[]{:S(2)}, u32[]{:S(2)}) collective-permute-start(bf16[512,256]{1,0:T(8,128)(2,1)S(1)} %attend.3.own_ref), channel_id=1, source_target_pairs={{0,1},{1,0},{2,3},{3,2},{4,5},{5,4},{6,7},{7,6},{8,9},{9,8},{10,11... | collective-permute-start | bytes 786440 | tf_op jit(solution)/shard_map/ppermute | solution.py:328
  100.6 7.8 %collective-permute-start = (bf16[512,256]{1,0:T(8,128)(2,1)S(1)}, bf16[512,256]{1,0:T(8,128)(2,1)S(1)}, u32[]{:S(2)}, u32[]{:S(2)}) collective-permute-start(bf16[512,256]{1,0:T(8,128)(2,1)S(1)} %attend.2.own_ref), channel_id=1, source_target_pairs={{0,1},{1,0},{2,3},{3,2},{4,5},{5,4},{6,7},{7,6},{8,9},{9,8},{10,11... | collective-permute-start | bytes 786440 | tf_op jit(solution)/shard_map/ppermute | solution.py:328
  102.5 12.6 %collective-permute-start.13 = (bf16[512,256]{1,0:T(8,128)(2,1)S(1)}, bf16[512,256]{1,0:T(8,128)(2,1)S(1)}, u32[]{:S(2)}, u32[]{:S(2)}) collective-permute-start(bf16[512,256]{1,0:T(8,128)(2,1)S(1)} %get-tuple-element.37), channel_id=1, source_target_pairs={{0,14},{2,0},{4,2},{6,4},{8,6},{10,8},{12,10},{14,12},{1,15},{3,1}... | collective-permute-start | bytes 786440 | tf_op jit(solution)/shard_map/ppermute | solution.py:271
  108.4 10.7 %collective-permute-start.10 = (bf16[512,256]{1,0:T(8,128)(2,1)S(1)}, bf16[512,256]{1,0:T(8,128)(2,1)S(1)}, u32[]{:S(2)}, u32[]{:S(2)}) collective-permute-start(bf16[512,256]{1,0:T(8,128)(2,1)S(1)} %get-tuple-element.34), channel_id=1, source_target_pairs={{0,2},{2,4},{4,6},{6,8},{8,10},{10,12},{12,14},{14,0},{1,3},{3,5},... | collective-permute-start | bytes 786440 | tf_op jit(solution)/shard_map/ppermute | solution.py:271
  109.7 11.0 %collective-permute-start.6 = (bf16[512,256]{1,0:T(8,128)(2,1)S(1)}, bf16[512,256]{1,0:T(8,128)(2,1)S(1)}, u32[]{:S(2)}, u32[]{:S(2)}) collective-permute-start(bf16[512,256]{1,0:T(8,128)(2,1)S(1)} %get-tuple-element.30), channel_id=1, source_target_pairs={{0,14},{2,0},{4,2},{6,4},{8,6},{10,8},{12,10},{14,12},{1,15},{3,1}... | collective-permute-start | bytes 786440 | tf_op jit(solution)/shard_map/ppermute | solution.py:271
  113.0 11.6 %collective-permute-start.2 = (bf16[512,256]{1,0:T(8,128)(2,1)S(1)}, bf16[512,256]{1,0:T(8,128)(2,1)S(1)}, u32[]{:S(2)}, u32[]{:S(2)}) collective-permute-start(bf16[512,256]{1,0:T(8,128)(2,1)S(1)} %get-tuple-element.26), channel_id=1, source_target_pairs={{0,2},{2,4},{4,6},{6,8},{8,10},{10,12},{12,14},{14,0},{1,3},{3,5},... | collective-permute-start | bytes 786440 | tf_op jit(solution)/shard_map/ppermute | solution.py:271
  115.2 11.2 %collective-permute-start.14 = (bf16[512,256]{1,0:T(8,128)(2,1)S(1)}, bf16[512,256]{1,0:T(8,128)(2,1)S(1)}, u32[]{:S(2)}, u32[]{:S(2)}) collective-permute-start(bf16[512,256]{1,0:T(8,128)(2,1)S(1)} %add_convert_fusion.3), channel_id=1, source_target_pairs={{0,14},{2,0},{4,2},{6,4},{8,6},{10,8},{12,10},{14,12},{1,15},{3,1}... | collective-permute-start | bytes 786440 | tf_op jit(solution)/shard_map/ppermute | solution.py:271
  119.2 11.0 %collective-permute-start.11 = (bf16[512,256]{1,0:T(8,128)(2,1)S(1)}, bf16[512,256]{1,0:T(8,128)(2,1)S(1)}, u32[]{:S(2)}, u32[]{:S(2)}) collective-permute-start(bf16[512,256]{1,0:T(8,128)(2,1)S(1)} %add_convert_fusion.5), channel_id=1, source_target_pairs={{0,2},{2,4},{4,6},{6,8},{8,10},{10,12},{12,14},{14,0},{1,3},{3,5},... | collective-permute-start | bytes 786440 | tf_op jit(solution)/shard_map/ppermute | solution.py:271
  120.8 19.7 %collective-permute-start.7 = (bf16[512,256]{1,0:T(8,128)(2,1)S(1)}, bf16[512,256]{1,0:T(8,128)(2,1)S(1)}, u32[]{:S(2)}, u32[]{:S(2)}) collective-permute-start(bf16[512,256]{1,0:T(8,128)(2,1)S(1)} %add_convert_fusion.8), channel_id=1, source_target_pairs={{0,14},{2,0},{4,2},{6,4},{8,6},{10,8},{12,10},{14,12},{1,15},{3,1}... | collective-permute-start | bytes 786440 | tf_op jit(solution)/shard_map/ppermute | solution.py:271
  124.6 11.1 %collective-permute-start.3 = (bf16[512,256]{1,0:T(8,128)(2,1)S(1)}, bf16[512,256]{1,0:T(8,128)(2,1)S(1)}, u32[]{:S(2)}, u32[]{:S(2)}) collective-permute-start(bf16[512,256]{1,0:T(8,128)(2,1)S(1)} %add_convert_fusion.11), channel_id=1, source_target_pairs={{0,2},{2,4},{4,6},{6,8},{8,10},{10,12},{12,14},{14,0},{1,3},{3,5},... | collective-permute-start | bytes 786440 | tf_op jit(solution)/shard_map/ppermute | solution.py:271
  126.4 10.2 %collective-permute-start.15 = (bf16[512,256]{1,0:T(8,128)(2,1)S(1)}, bf16[512,256]{1,0:T(8,128)(2,1)S(1)}, u32[]{:S(2)}, u32[]{:S(2)}) collective-permute-start(bf16[512,256]{1,0:T(8,128)(2,1)S(1)} %add_convert_fusion.2), channel_id=1, source_target_pairs={{0,14},{2,0},{4,2},{6,4},{8,6},{10,8},{12,10},{14,12},{1,15},{3,1}... | collective-permute-start | bytes 786440 | tf_op jit(solution)/shard_map/ppermute | solution.py:271
  130.3 15.6 %collective-permute-start.12 = (bf16[512,256]{1,0:T(8,128)(2,1)S(1)}, bf16[512,256]{1,0:T(8,128)(2,1)S(1)}, u32[]{:S(2)}, u32[]{:S(2)}) collective-permute-start(bf16[512,256]{1,0:T(8,128)(2,1)S(1)} %add_convert_fusion.4), channel_id=1, source_target_pairs={{0,2},{2,4},{4,6},{6,8},{8,10},{10,12},{12,14},{14,0},{1,3},{3,5},... | collective-permute-start | bytes 786440 | tf_op jit(solution)/shard_map/ppermute | solution.py:271
  135.8 9.9 %collective-permute-start.4 = (bf16[512,256]{1,0:T(8,128)(2,1)S(1)}, bf16[512,256]{1,0:T(8,128)(2,1)S(1)}, u32[]{:S(2)}, u32[]{:S(2)}) collective-permute-start(bf16[512,256]{1,0:T(8,128)(2,1)S(1)} %add_convert_fusion.10), channel_id=1, source_target_pairs={{0,2},{2,4},{4,6},{6,8},{8,10},{10,12},{12,14},{14,0},{1,3},{3,5},... | collective-permute-start | bytes 786440 | tf_op jit(solution)/shard_map/ppermute | solution.py:271
  136.7 10.5 %collective-permute-start.16 = (bf16[512,256]{1,0:T(8,128)(2,1)S(1)}, bf16[512,256]{1,0:T(8,128)(2,1)S(1)}, u32[]{:S(2)}, u32[]{:S(2)}) collective-permute-start(bf16[512,256]{1,0:T(8,128)(2,1)S(1)} %add_convert_fusion.1), channel_id=1, source_target_pairs={{0,14},{2,0},{4,2},{6,4},{8,6},{10,8},{12,10},{14,12},{1,15},{3,1}... | collective-permute-start | bytes 786440 | tf_op jit(solution)/shard_map/ppermute | solution.py:271
  140.6 10.5 %collective-permute-start.8 = (bf16[512,256]{1,0:T(8,128)(2,1)S(1)}, bf16[512,256]{1,0:T(8,128)(2,1)S(1)}, u32[]{:S(2)}, u32[]{:S(2)}) collective-permute-start(bf16[512,256]{1,0:T(8,128)(2,1)S(1)} %add_convert_fusion.7), channel_id=1, source_target_pairs={{0,14},{2,0},{4,2},{6,4},{8,6},{10,8},{12,10},{14,12},{1,15},{3,1}... | collective-permute-start | bytes 786440 | tf_op jit(solution)/shard_map/ppermute | solution.py:271
  145.8 8.4 %collective-permute-start.5 = (bf16[512,256]{1,0:T(8,128)(2,1)S(1)}, bf16[512,256]{1,0:T(8,128)(2,1)S(1)}, u32[]{:S(2)}, u32[]{:S(2)}) collective-permute-start(bf16[512,256]{1,0:T(8,128)(2,1)S(1)} %add_convert_fusion.9), channel_id=1, source_target_pairs={{0,2},{2,4},{4,6},{6,8},{8,10},{10,12},{12,14},{14,0},{1,3},{3,5},... | collective-permute-start | bytes 786440 | tf_op jit(solution)/shard_map/ppermute | solution.py:271
Sparse Core Ops, SparseCore 0:
  9.1 67.1 all-gather.1

commit v4 on v3

--- a/solution.py
+++ b/solution.py
@@ -100,37 +100,50 @@
     )(place, heard, rows)
 
 
-def query_kernel(tokens_ref, weight_ref, out_ref):
-    projected = jnp.dot(tokens_ref[...], weight_ref[...], preferred_element_type=F32)
-    for h in range(weight_ref.shape[1] // HD):
-        cols = slice(h * HD, (h + 1) * HD)
-        out_ref[:, cols] = unit(projected[:, cols]).astype(BF16)
-
-
-def project_queries(tokens, weight):
-    rows, depth = tokens.shape
-    width, tile = weight.shape[1], 128
+def query_kernel(place_ref, *refs):
+    ring = len(refs) - 4
+    weight_ref, partner_ref, own_ref, lent_ref = refs[ring:]
+    here, core = place_ref[0], place_ref[1]
+    own, lent = None, None
+    for k in range(ring):
+        chip = lax.rem(here + ring - k, ring)
+        part = jnp.dot(refs[k][...], weight_ref[chip, core], preferred_element_type=F32)
+        own = part if own is None else own + part
+        part = jnp.dot(refs[k][...], partner_ref[chip], preferred_element_type=F32)
+        lent = part if lent is None else lent + part
+    own_ref[...] = own
+    lent_ref[...] = lent
+
+
+def project_queries(place, pieces, weight, partner_weight):
+    rows, depth = pieces[0].shape
+    width, tile = weight.shape[-1], 256
+    out = jax.ShapeDtypeStruct((rows, width), F32)
     return pl.pallas_call(
         query_kernel,
         grid=(rows // tile,),
-        out_shape=jax.ShapeDtypeStruct((rows, width), BF16),
-        in_specs=[
-            pl.BlockSpec((tile, depth), lambda i: (i, 0)),
-            pl.BlockSpec((depth, width), lambda i: (0, 0)),
+        out_shape=(out, out),
+        in_specs=[SMEM]
+        + [pl.BlockSpec((tile, depth), lambda i: (i, 0)) for _ in pieces]
+        + [
+            pl.BlockSpec(weight.shape, lambda i: (0, 0, 0, 0)),
+            pl.BlockSpec(partner_weight.shape, lambda i: (0, 0, 0)),
         ],
-        out_specs=pl.BlockSpec((tile, width), lambda i: (i, 0)),
+        out_specs=[pl.BlockSpec((tile, width), lambda i: (i, 0))] * 2,
         compiler_params=pltpu.CompilerParams(vmem_limit_bytes=24 << 20),
         cost_estimate=pl.CostEstimate(
-            flops=2 * rows * depth * width, bytes_accessed=11 << 20, transcendentals=0
+            flops=4 * rows * depth * width * len(pieces), bytes_accessed=9 << 20, transcendentals=0
         ),
         name="project_queries",
-    )(tokens, weight)
-
-
-def attend_kernel(first, slot_ref, length_ref, query_ref, rows_ref, out_ref, held_ref, sems):
+    )(place, *pieces, weight, partner_weight)
+
+
+def attend_kernel(
+    first, slot_ref, length_ref, own_ref, lent_ref, rows_ref, out_ref, query_ref, held_ref, sems
+):
     spans = slot_ref.shape[0] // NBRS
     count = sems.shape[0] // NBRS
-    width = query_ref.shape[1]
+    width = out_ref.shape[1]
     keys = NBRS * NBR_LEN
     factor = 2.0 / math.sqrt(HD)
     copies = []
@@ -143,6 +156,9 @@
             )
             copy.start()
             copies.append(copy)
+    for h in range(width // HD):
+        cols = slice(h * HD, (h + 1) * HD)
+        query_ref[:, cols] = unit(own_ref[:, cols] + lent_ref[:, cols]).astype(BF16)
     places = lax.broadcasted_iota(jnp.int32, (SPAN, keys), 1)
     group = 4
     for start in range(0, count, group):
@@ -171,17 +187,18 @@
             out_ref[c * SPAN : (c + 1) * SPAN, h * HD : (h + 1) * HD] = result.astype(BF16)
 
 
-def attend(part, parts, slot_index, lengths, queries, rows):
-    tokens, width = queries.shape[0] // parts, queries.shape[1]
+def attend(part, parts, slot_index, lengths, own, lent, rows):
+    tokens, width = own.shape[0] // parts, own.shape[1]
     count = tokens // SPAN
     requests = count * NBRS
     return pl.pallas_call(
         functools.partial(attend_kernel, part * count),
         grid=(1,),
         out_shape=jax.ShapeDtypeStruct((tokens, width), BF16),
-        in_specs=[SMEM, SMEM, pl.BlockSpec((tokens, width), lambda i: (part, 0)), ANY],
+        in_specs=[SMEM, SMEM] + [pl.BlockSpec((tokens, width), lambda i: (part, 0))] * 2 + [ANY],
         out_specs=pl.BlockSpec((tokens, width), lambda i: (0, 0)),
         scratch_shapes=[
+            pltpu.VMEM((tokens, width), BF16),
             pltpu.VMEM((requests * NBR_LEN, rows.shape[2]), BF16),
             pltpu.SemaphoreType.DMA((requests,)),
         ],
@@ -190,7 +207,7 @@
             flops=4 * tokens * NBRS * NBR_LEN * width, bytes_accessed=3 << 20, transcendentals=0
         ),
         name="attend",
-    )(slot_index, lengths, queries, rows)
+    )(slot_index, lengths, own, lent, rows)
 
 
 def relay_kernel(place_ref, weight_ref, own_ref, lent_ref):
@@ -295,8 +312,7 @@
     here, core = lax.axis_index("z"), lax.axis_index("c")
     swap = [(i, (i + 1) % cores) for i in range(cores)]
 
-    gathered = lax.all_gather(tokens, ("z", "c"), axis=1, tiled=True)
-
+    place = jnp.stack([here, core]).astype(jnp.int32)
     owners = nbr_owner.T.reshape(-1)
     wanted_blocks = nbr_block.T.reshape(-1)
     notes = jnp.concatenate([owners, wanted_blocks, block_len])
@@ -304,6 +320,13 @@
     heard = lax.all_to_all(notes, DB, split_axis=0, concat_axis=0, tiled=True)
     projected = project_blocks(codes, scales, key_weight, value_weight)
     sent = select_blocks(lax.axis_index(DB).astype(jnp.int32).reshape(1), heard, projected)
+    up = [(i, (i + 1) % ring) for i in range(ring)]
+    down = [(i, (i - 1) % ring) for i in range(ring)]
+    pieces = {0: tokens, 1: lax.ppermute(tokens, "z", up)}
+    pieces[ring - 1] = lax.ppermute(tokens, "z", down)
+    sent, pieces[1], pieces[ring - 1] = lax.optimization_barrier(
+        (sent, pieces[1], pieces[ring - 1])
+    )
     rows = lax.all_to_all(sent, DB, split_axis=0, concat_axis=0, tiled=True)
     rows = rows.reshape(shards * NBRS, NBR_LEN, 2 * width)
 
@@ -320,11 +343,20 @@
         jnp.where(block_ids[:, None] == ids[None, :], all_lengths[None, :], 0), axis=1
     )
 
-    own_weight, lent_weight = relay(jnp.stack([here, core]).astype(jnp.int32), out_weight, ring)
+    for k in range(2, ring // 2 + 1):
+        pieces[k] = lax.ppermute(pieces[k - 1], "z", up)
+        if k < ring // 2:
+            pieces[ring - k] = lax.ppermute(pieces[ring - k + 1], "z", down)
+    by_core = query_weight.reshape(ring, cores, width, width)
+    lent_rows = lax.dynamic_index_in_dim(by_core, 1 - core, 1, keepdims=False)
+    partner_rows = lax.ppermute(lent_rows, "c", swap)
+
+    own_weight, lent_weight = relay(place, out_weight, ring)
     partner_weight = lax.ppermute(lent_weight, "c", swap)
 
-    queries = project_queries(gathered, query_weight)
-    attended = [attend(part, 2, slot_index, lengths, queries, rows) for part in range(2)]
+    own, lent = project_queries(place, [pieces[k] for k in range(ring)], by_core, partner_rows)
+    lent = lax.ppermute(lent, "c", swap)
+    attended = [attend(part, 2, slot_index, lengths, own, lent, rows) for part in range(2)]
     partner_attended = [lax.ppermute(part, "c", swap) for part in attended]
     return reduce_ring(attended, partner_attended, own_weight, partner_weight, ring)
 

time: 162 us -> 151 us (0.932)
  waiting for transfers between devices: 74.7 us -> 58 us
  between operations: 13.6 us -> 0.32 us
  starting transfers between devices: 39.6 us -> 52.7 us
  Pallas kernels: 23.4 us -> 27.3 us
    all_gather x1 -> x0, waiting for transfers between devices: 39.9 us -> none  [local(): gathered = lax.all_gather(tokens, ('z', 'c'), axis=1, tiled=True)]
    ppermute x0 -> x9, waiting for transfers between devices: none -> 29.3 us  [the longest x3 23.4 us: local(): pieces[k] = lax.ppermute(pieces[k - 1], 'z', up)]
    ppermute x0 -> x9, starting transfers between devices: none -> 13 us  [the longest x2 7.08 us: local(): pieces[ring - k] = lax.ppermute(pieces[ring - k + 1], 'z', down)]
    ppermute x14, waiting for transfers between devices: 24.6 us -> 18.2 us  [reduce_ring(): lax.ppermute(held[half, way], 'z', up if way == 1 else down)]
    pallas_call x2, Pallas kernels: 2.51 us -> 4.96 us  [shares(): pl.pallas_call(functools.partial(share_kernel, steps), out_shape=outs, in...]
    unnamed x10 -> x20, local copies, waits for them, and re-layouts: 5.58 us -> 5.76 us
  transfers between devices with their start and end apart: 20 -> 28, of which waited for: 12 -> 15; matrix products, arithmetic and copies ran while one was open for 3% -> 3% of each run, Pallas kernels for 14% -> 18%
where the time goes in v4:
time: 151 us; the launch traced here: 150 us
  waiting for transfers between devices  58 us (38%)
  starting transfers between devices  52.7 us (35%)
  Pallas kernels  27.3 us (18%)
  local copies, waits for them, and re-layouts  9.12 us (6%)
  other arithmetic  2.71 us (2%)
    ppermute x14, starting transfers between devices, reduce_ring(): lax.ppermute(held[half, way], 'z', up if way == 1 else down)  24.6 us
    ppermute x3, waiting for transfers between devices, local(): pieces[k] = lax.ppermute(pieces[k - 1], 'z', up)  23.4 us
    ppermute x14, waiting for transfers between devices, reduce_ring(): lax.ppermute(held[half, way], 'z', up if way == 1 else down)  18.2 us
    all_to_all x1, waiting for transfers between devices, local(): rows = lax.all_to_all(sent, DB, split_axis=0, concat_axis=0, tiled=True)  9.88 us
    all_to_all x1, starting transfers between devices, local(): heard = lax.all_to_all(notes, DB, split_axis=0, concat_axis=0, tiled=True)  7.17 us
    ppermute x2, starting transfers between devices, local(): pieces[ring - k] = lax.ppermute(pieces[ring - k + 1], 'z', down)  7.08 us
    all_to_all x1, starting transfers between devices, local(): rows = lax.all_to_all(sent, DB, split_axis=0, concat_axis=0, tiled=True)  6.6 us
    pallas_call x2, Pallas kernels, attend(): pl.pallas_call(functools.partial(attend_kernel, part * count), grid=(1,),...  6.4 us
  transfers between devices with their start and end apart: 28, of which 15 were waited for; matrix products, arithmetic and copies ran while one was open for 3% of the time, Pallas kernels for 18%

profile of v4, /device:TPU:24, one launch (start us, length us, event | category | flops | bytes accessed | tf_op | source)
XLA Modules:
  0.0 150.2 jit_solution(9300815604914645047)
XLA Ops:
  0.0 1.9 %collective-permute-start = (bf16[1024,256]{1,0:T(8,128)(2,1)}, bf16[1024,256]{1,0:T(8,128)(2,1)}, u32[]{:S(2)}, u32[]{:S(2)}) collective-permute-start(bf16[1024,256]{1,0:T(8,128)(2,1)} %refs_0_.1), channel_id=1, source_target_pairs={{0,2},{2,4},{4,6},{6,8},{8,10},{10,12},{12,14},{14,0},{1,3},{3,5},... | collective-permute-start | bytes 1572872 | tf_op jit(solution)/shard_map/ppermute | solution.py:325
  1.9 3.9 %collective-permute-start.1 = (bf16[1024,256]{1,0:T(8,128)(2,1)}, bf16[1024,256]{1,0:T(8,128)(2,1)S(1)}, u32[]{:S(2)}, u32[]{:S(2)}) collective-permute-start(bf16[1024,256]{1,0:T(8,128)(2,1)} %refs_0_.1), channel_id=1, source_target_pairs={{0,14},{2,0},{4,2},{6,4},{8,6},{10,8},{12,10},{14,12},{1,15},{3,1}... | collective-permute-start | bytes 1572872 | tf_op jit(solution)/shard_map/ppermute | solution.py:326
  5.9 0.8 reshape.34
  6.6 0.8 reshape.35
  7.4 0.7 pad_add_fusion
  8.1 0.6 broadcast_in_dim.24
  8.7 7.2 %all-to-all-start = ((s32[16,1,72]{2,1,0:T(1,128)}), s32[16,1,72]{2,1,0:T(1,128)S(1)}, u32[]{:S(2)}, u32[]{:S(2)}) async-start(s32[16,1,72]{2,1,0:T(1,128)} %broadcast_in_dim.24), calls=%async_computation | async-start | bytes 16384 | tf_op jit(solution)/shard_map/all_to_all | solution.py:320
  15.9 4.9 %project_blocks.1.rows_ref = bf16[8,128,512]{2,1,0:T(8,128)(2,1)} custom-call(f32[8,7]{1,0:T(8,128)} %scales_ref.1, bf16[8,128,896]{2,1,0:T(8,128)(2,1)} %codes_ref.1, bf16[896,256]{1,0:T(8,128)(2,1)} %key_ref.1, bf16[896,256]{1,0:T(8,128)(2,1)} %value_ref.1), custom_call_target="tpu_custom_call" | custom-call | flops 939524096 | bytes 5242880 | tf_op jit(solution)/shard_map/project_blocks/pallas_call | solution.py:52
  20.8 0.6 all-to-all-done
  21.4 0.6 copy-done.8
  22.0 3.8 %select_blocks.1 = bf16[16,2,128,512]{3,2,1,0:T(8,128)(2,1)} custom-call(s32[1]{0:T(128)} %bitcast.5.place_ref, s32[16,72]{1,0:T(8,128)} %bitcast.12, bf16[8,128,512]{2,1,0:T(8,128)(2,1)} %project_blocks.1.rows_ref), custom_call_target="tpu_custom_call" | custom-call | bytes 9437184 | tf_op jit(solution)/shard_map/select_blocks/pallas_call | solution.py:92
  25.8 0.8 copy-done.5
  26.6 6.6 %all-to-all-start.1 = ((bf16[16,2,128,512]{3,2,1,0:T(8,128)(2,1)}), bf16[16,2,128,512]{3,2,1,0:T(8,128)(2,1)}, u32[]{:S(2)}, u32[]{:S(2)}) async-start(bf16[16,2,128,512]{3,2,1,0:T(8,128)(2,1)} %select_blocks.1), calls=%async_computation.1 | async-start | bytes 8388608 | tf_op jit(solution)/shard_map/all_to_all | solution.py:330
  33.2 1.1 dynamic-slice_bitcast_fusion
  34.4 3.3 %collective-permute-start.5 = (bf16[1024,256]{1,0:T(8,128)(2,1)S(1)}, bf16[1024,256]{1,0:T(8,128)(2,1)}, u32[]{:S(2)}, u32[]{:S(2)}) collective-permute-start(bf16[1024,256]{1,0:T(8,128)(2,1)S(1)} %copy-done.6), channel_id=1, source_target_pairs={{0,14},{2,0},{4,2},{6,4},{8,6},{10,8},{12,10},{14,12},{1,15},{3,1}... | collective-permute-start | bytes 1572872 | tf_op jit(solution)/shard_map/ppermute | solution.py:349
  37.7 9.3 %collective-permute-done.2.refs_2_ = bf16[1024,256]{1,0:T(8,128)(2,1)} collective-permute-done((bf16[1024,256]{1,0:T(8,128)(2,1)}, bf16[1024,256]{1,0:T(8,128)(2,1)}, u32[]{:S(2)}, u32[]{:S(2)}) %collective-permute-start.2) | collective-permute-done | bytes 524320 | tf_op jit(solution)/shard_map/ppermute | solution.py:347
  47.0 2.4 %collective-permute-done.5.refs_6_ = bf16[1024,256]{1,0:T(8,128)(2,1)} collective-permute-done((bf16[1024,256]{1,0:T(8,128)(2,1)S(1)}, bf16[1024,256]{1,0:T(8,128)(2,1)}, u32[]{:S(2)}, u32[]{:S(2)}) %collective-permute-start.5) | collective-permute-done | bytes 524320 | tf_op jit(solution)/shard_map/ppermute | solution.py:349
  49.4 3.8 %collective-permute-start.6 = (bf16[1024,256]{1,0:T(8,128)(2,1)}, bf16[1024,256]{1,0:T(8,128)(2,1)}, u32[]{:S(2)}, u32[]{:S(2)}) collective-permute-start(bf16[1024,256]{1,0:T(8,128)(2,1)} %collective-permute-done.5.refs_6_), channel_id=1, source_target_pairs={{0,14},{2,0},{4,2},{6,4},{8,6},{10,8},{12,10},{14,12},{1,15},{3,1}... | collective-permute-start | bytes 1572872 | tf_op jit(solution)/shard_map/ppermute | solution.py:349
  53.2 6.7 %collective-permute-done.3.refs_3_ = bf16[1024,256]{1,0:T(8,128)(2,1)} collective-permute-done((bf16[1024,256]{1,0:T(8,128)(2,1)}, bf16[1024,256]{1,0:T(8,128)(2,1)}, u32[]{:S(2)}, u32[]{:S(2)}) %collective-permute-start.3) | collective-permute-done | bytes 524320 | tf_op jit(solution)/shard_map/ppermute | solution.py:347
  59.9 1.0 copy-done.2
  60.9 3.5 %collective-permute-done.6.refs_5_ = bf16[1024,256]{1,0:T(8,128)(2,1)} collective-permute-done((bf16[1024,256]{1,0:T(8,128)(2,1)}, bf16[1024,256]{1,0:T(8,128)(2,1)}, u32[]{:S(2)}, u32[]{:S(2)}) %collective-permute-start.6) | collective-permute-done | bytes 524320 | tf_op jit(solution)/shard_map/ppermute | solution.py:349
  64.4 7.4 %collective-permute-done.4.refs_4_ = bf16[1024,256]{1,0:T(8,128)(2,1)} collective-permute-done((bf16[1024,256]{1,0:T(8,128)(2,1)}, bf16[1024,256]{1,0:T(8,128)(2,1)}, u32[]{:S(2)}, u32[]{:S(2)}) %collective-permute-start.4) | collective-permute-done | bytes 524320 | tf_op jit(solution)/shard_map/ppermute | solution.py:347
  71.8 1.2 copy-done.3
  73.0 1.0 copy-done.4
  74.1 1.0 copy-done.7
  75.1 5.5 %project_queries.1 = (f32[1024,256]{1,0:T(8,128)S(1)}, f32[1024,256]{1,0:T(8,128)}) custom-call(s32[2]{0:T(128)S(1)} %pad_add_fusion.1.place_ref, bf16[1024,256]{1,0:T(8,128)(2,1)S(1)} %copy-done.4, bf16[1024,256]{1,0:T(8,128)(2,1)} %collective-permute-done.refs_1_, bf16[1024,256]{1,0:T(8,128)(2,1)} %collective-permute-done.2.refs_2_, ...), custom_call_target="tpu_custom_call" | custom-call | flops 2147483648 | bytes 9437184 | tf_op jit(solution)/shard_map/project_queries/pallas_call | solution.py:122
  80.6 1.8 %relay.1 = (bf16[8,256,256]{2,1,0:T(8,128)(2,1)S(1)}, bf16[8,256,256]{2,1,0:T(8,128)(2,1)}) custom-call(s32[2]{0:T(128)S(1)} %pad_add_fusion.1.place_ref, bf16[256,4096]{1,0:T(8,128)(2,1)S(1)} %copy-done), custom_call_target="tpu_custom_call" | custom-call | bytes 4194304 | tf_op jit(solution)/shard_map/relay/pallas_call | solution.py:226
  83.5 9.9 %all-to-all-done.1 = bf16[16,2,128,512]{3,2,1,0:T(8,128)(2,1)} async-done(((bf16[16,2,128,512]{3,2,1,0:T(8,128)(2,1)}), bf16[16,2,128,512]{3,2,1,0:T(8,128)(2,1)}, u32[]{:S(2)}, u32[]{:S(2)}) %all-to-all-start.1) | async-done | bytes 4194336 | tf_op jit(solution)/shard_map/all_to_all | solution.py:330
  93.4 3.2 %attend.2.own_ref = bf16[512,256]{1,0:T(8,128)(2,1)S(1)} custom-call(s32[32]{0:T(128)S(1)} %get-tuple-element.52.slot_ref, s32[32]{0:T(128)S(1)} %select_reduce_fusion.length_ref, f32[1024,256]{1,0:T(8,128)S(1)} %get-tuple-element.30.own_ref, f32[1024,256]{1,0:T(8,128)S(1)} %collective-permute-done.8.lent_ref, bf16[32,128,512]{2,1,0:T(8,128)(2,1)} %bitcast.8.rows_ref), custom_call_target="tpu_custom_call" | custom-call | flops 134217728 | bytes 3145728 | tf_op jit(solution)/shard_map/attend/pallas_call | solution.py:194
  96.9 3.2 %attend.3.own_ref = bf16[512,256]{1,0:T(8,128)(2,1)S(1)} custom-call(s32[32]{0:T(128)S(1)} %get-tuple-element.52.slot_ref, s32[32]{0:T(128)S(1)} %select_reduce_fusion.length_ref, f32[1024,256]{1,0:T(8,128)S(1)} %get-tuple-element.30.own_ref, f32[1024,256]{1,0:T(8,128)S(1)} %collective-permute-done.8.lent_ref, bf16[32,128,512]{2,1,0:T(8,128)(2,1)} %bitcast.8.rows_ref), custom_call_target="tpu_custom_call" | custom-call | flops 134217728 | bytes 3145728 | tf_op jit(solution)/shard_map/attend/pallas_call | solution.py:194
  100.7 2.5 %shares.2 = (bf16[512,256]{1,0:T(8,128)(2,1)S(1)}, bf16[512,256]{1,0:T(8,128)(2,1)S(1)}, f32[512,256]{1,0:T(8,128)S(1)}, f32[512,256]{1,0:T(8,128)S(1)}, f32[512...) custom-call(bf16[512,256]{1,0:T(8,128)(2,1)S(1)} %attend.2.own_ref, ...), custom_call_target="tpu_custom_call" | custom-call | flops 1073741824 | bytes 6291456 | tf_op jit(solution)/shard_map/shares/pallas_call | solution.py:252
  103.2 3.2 %collective-permute-start.15 = (bf16[512,256]{1,0:T(8,128)(2,1)S(1)}, bf16[512,256]{1,0:T(8,128)(2,1)S(1)}, u32[]{:S(2)}, u32[]{:S(2)}) collective-permute-start(bf16[512,256]{1,0:T(8,128)(2,1)S(1)} %get-tuple-element.40), channel_id=1, source_target_pairs={{0,14},{2,0},{4,2},{6,4},{8,6},{10,8},{12,10},{14,12},{1,15},{3,1}... | collective-permute-start | bytes 786440 | tf_op jit(solution)/shard_map/ppermute | solution.py:288
  106.5 2.5 %shares.3 = (bf16[512,256]{1,0:T(8,128)(2,1)S(1)}, bf16[512,256]{1,0:T(8,128)(2,1)S(1)}, f32[512,256]{1,0:T(8,128)S(1)}, f32[512,256]{1,0:T(8,128)S(1)}, f32[512...) custom-call(bf16[512,256]{1,0:T(8,128)(2,1)S(1)} %attend.3.own_ref, ...), custom_call_target="tpu_custom_call" | custom-call | flops 1073741824 | bytes 6291456 | tf_op jit(solution)/shard_map/shares/pallas_call | solution.py:252
  109.0 3.2 %collective-permute-start.22 = (bf16[512,256]{1,0:T(8,128)(2,1)S(1)}, bf16[512,256]{1,0:T(8,128)(2,1)S(1)}, u32[]{:S(2)}, u32[]{:S(2)}) collective-permute-start(bf16[512,256]{1,0:T(8,128)(2,1)S(1)} %get-tuple-element.47), channel_id=1, source_target_pairs={{0,14},{2,0},{4,2},{6,4},{8,6},{10,8},{12,10},{14,12},{1,15},{3,1}... | collective-permute-start | bytes 786440 | tf_op jit(solution)/shard_map/ppermute | solution.py:288
  112.3 0.7 collective-permute-done.11
  113.2 3.3 %collective-permute-start.16 = (bf16[512,256]{1,0:T(8,128)(2,1)S(1)}, bf16[512,256]{1,0:T(8,128)(2,1)S(1)}, u32[]{:S(2)}, u32[]{:S(2)}) collective-permute-start(bf16[512,256]{1,0:T(8,128)(2,1)S(1)} %add_convert_fusion.8), channel_id=1, source_target_pairs={{0,14},{2,0},{4,2},{6,4},{8,6},{10,8},{12,10},{14,12},{1,15},{3,1}... | collective-permute-start | bytes 786440 | tf_op jit(solution)/shard_map/ppermute | solution.py:288
  116.5 3.0 %collective-permute-done.19 = bf16[512,256]{1,0:T(8,128)(2,1)S(1)} collective-permute-done((bf16[512,256]{1,0:T(8,128)(2,1)S(1)}, bf16[512,256]{1,0:T(8,128)(2,1)S(1)}, u32[]{:S(2)}, u32[]{:S(2)}) %collective-permute-start.19) | collective-permute-done | bytes 262176 | tf_op jit(solution)/shard_map/ppermute | solution.py:288
  119.7 3.3 %collective-permute-start.23 = (bf16[512,256]{1,0:T(8,128)(2,1)S(1)}, bf16[512,256]{1,0:T(8,128)(2,1)S(1)}, u32[]{:S(2)}, u32[]{:S(2)}) collective-permute-start(bf16[512,256]{1,0:T(8,128)(2,1)S(1)} %add_convert_fusion.3), channel_id=1, source_target_pairs={{0,14},{2,0},{4,2},{6,4},{8,6},{10,8},{12,10},{14,12},{1,15},{3,1}... | collective-permute-start | bytes 786440 | tf_op jit(solution)/shard_map/ppermute | solution.py:288
  123.0 2.1 %collective-permute-done.12 = bf16[512,256]{1,0:T(8,128)(2,1)S(1)} collective-permute-done((bf16[512,256]{1,0:T(8,128)(2,1)S(1)}, bf16[512,256]{1,0:T(8,128)(2,1)S(1)}, u32[]{:S(2)}, u32[]{:S(2)}) %collective-permute-start.12) | collective-permute-done | bytes 262176 | tf_op jit(solution)/shard_map/ppermute | solution.py:288
  125.3 3.3 %collective-permute-start.17 = (bf16[512,256]{1,0:T(8,128)(2,1)S(1)}, bf16[512,256]{1,0:T(8,128)(2,1)S(1)}, u32[]{:S(2)}, u32[]{:S(2)}) collective-permute-start(bf16[512,256]{1,0:T(8,128)(2,1)S(1)} %add_convert_fusion.7), channel_id=1, source_target_pairs={{0,14},{2,0},{4,2},{6,4},{8,6},{10,8},{12,10},{14,12},{1,15},{3,1}... | collective-permute-start | bytes 786440 | tf_op jit(solution)/shard_map/ppermute | solution.py:288
  128.6 1.6 %collective-permute-done.23 = bf16[512,256]{1,0:T(8,128)(2,1)S(1)} collective-permute-done((bf16[512,256]{1,0:T(8,128)(2,1)S(1)}, bf16[512,256]{1,0:T(8,128)(2,1)S(1)}, u32[]{:S(2)}, u32[]{:S(2)}) %collective-permute-start.23) | collective-permute-done | bytes 262176 | tf_op jit(solution)/shard_map/ppermute | solution.py:288
  130.3 4.0 %collective-permute-start.24 = (bf16[512,256]{1,0:T(8,128)(2,1)S(1)}, bf16[512,256]{1,0:T(8,128)(2,1)S(1)}, u32[]{:S(2)}, u32[]{:S(2)}) collective-permute-start(bf16[512,256]{1,0:T(8,128)(2,1)S(1)} %add_convert_fusion.2), channel_id=1, source_target_pairs={{0,14},{2,0},{4,2},{6,4},{8,6},{10,8},{12,10},{14,12},{1,15},{3,1}... | collective-permute-start | bytes 786440 | tf_op jit(solution)/shard_map/ppermute | solution.py:288
  134.3 0.8 collective-permute-done.13
  135.5 4.6 %collective-permute-done.24 = bf16[512,256]{1,0:T(8,128)(2,1)S(1)} collective-permute-done((bf16[512,256]{1,0:T(8,128)(2,1)S(1)}, bf16[512,256]{1,0:T(8,128)(2,1)S(1)}, u32[]{:S(2)}, u32[]{:S(2)}) %collective-permute-start.24) | collective-permute-done | bytes 262176 | tf_op jit(solution)/shard_map/ppermute | solution.py:288
  140.1 3.8 %collective-permute-start.25 = (bf16[512,256]{1,0:T(8,128)(2,1)S(1)}, bf16[512,256]{1,0:T(8,128)(2,1)S(1)}, u32[]{:S(2)}, u32[]{:S(2)}) collective-permute-start(bf16[512,256]{1,0:T(8,128)(2,1)S(1)} %add_convert_fusion.1), channel_id=1, source_target_pairs={{0,14},{2,0},{4,2},{6,4},{8,6},{10,8},{12,10},{14,12},{1,15},{3,1}... | collective-permute-start | bytes 786440 | tf_op jit(solution)/shard_map/ppermute | solution.py:288
  143.9 1.9 %collective-permute-done.14 = bf16[512,256]{1,0:T(8,128)(2,1)S(1)} collective-permute-done((bf16[512,256]{1,0:T(8,128)(2,1)S(1)}, bf16[512,256]{1,0:T(8,128)(2,1)S(1)}, u32[]{:S(2)}, u32[]{:S(2)}) %collective-permute-start.14) | collective-permute-done | bytes 262176 | tf_op jit(solution)/shard_map/ppermute | solution.py:288
  145.8 3.4 %collective-permute-done.21 = bf16[512,256]{1,0:T(8,128)(2,1)S(1)} collective-permute-done((bf16[512,256]{1,0:T(8,128)(2,1)S(1)}, bf16[512,256]{1,0:T(8,128)(2,1)S(1)}, u32[]{:S(2)}, u32[]{:S(2)}) %collective-permute-start.21) | collective-permute-done | bytes 262176 | tf_op jit(solution)/shard_map/ppermute | solution.py:288
  149.3 0.8 pad_maximum_fusion
  (60 shorter events, 3.4 us)
Async XLA Ops:
  0.0 25.8 %collective-permute-start = (bf16[1024,256]{1,0:T(8,128)(2,1)}, bf16[1024,256]{1,0:T(8,128)(2,1)}, u32[]{:S(2)}, u32[]{:S(2)}) collective-permute-start(bf16[1024,256]{1,0:T(8,128)(2,1)} %refs_0_.1), channel_id=1, source_target_pairs={{0,2},{2,4},{4,6},{6,8},{8,10},{10,12},{12,14},{14,0},{1,3},{3,5},... | collective-permute-start | bytes 1572872 | tf_op jit(solution)/shard_map/ppermute | solution.py:325
  1.9 23.9 %collective-permute-start.1 = (bf16[1024,256]{1,0:T(8,128)(2,1)}, bf16[1024,256]{1,0:T(8,128)(2,1)S(1)}, u32[]{:S(2)}, u32[]{:S(2)}) collective-permute-start(bf16[1024,256]{1,0:T(8,128)(2,1)} %refs_0_.1), channel_id=1, source_target_pairs={{0,14},{2,0},{4,2},{6,4},{8,6},{10,8},{12,10},{14,12},{1,15},{3,1}... | collective-permute-start | bytes 1572872 | tf_op jit(solution)/shard_map/ppermute | solution.py:326
  8.7 12.7 %all-to-all-start = ((s32[16,1,72]{2,1,0:T(1,128)}), s32[16,1,72]{2,1,0:T(1,128)S(1)}, u32[]{:S(2)}, u32[]{:S(2)}) async-start(s32[16,1,72]{2,1,0:T(1,128)} %broadcast_in_dim.24), calls=%async_computation | async-start | bytes 16384 | tf_op jit(solution)/shard_map/all_to_all | solution.py:320
  21.4 0.6 copy-start.8
  25.8 7.5 %copy-start.1 = (bf16[4096,256]{1,0:T(8,128)(2,1)S(1)}, bf16[4096,256]{1,0:T(8,128)(2,1)}, u32[]{:S(2)}) copy-start(bf16[4096,256]{1,0:T(8,128)(2,1)} %param.11) | copy-start | bytes 6291460
  25.8 0.8 copy-start.5
  26.6 66.8 %all-to-all-start.1 = ((bf16[16,2,128,512]{3,2,1,0:T(8,128)(2,1)}), bf16[16,2,128,512]{3,2,1,0:T(8,128)(2,1)}, u32[]{:S(2)}, u32[]{:S(2)}) async-start(bf16[16,2,128,512]{3,2,1,0:T(8,128)(2,1)} %select_blocks.1), calls=%async_computation.1 | async-start | bytes 8388608 | tf_op jit(solution)/shard_map/all_to_all | solution.py:330
  33.2 13.8 %collective-permute-start.2 = (bf16[1024,256]{1,0:T(8,128)(2,1)}, bf16[1024,256]{1,0:T(8,128)(2,1)}, u32[]{:S(2)}, u32[]{:S(2)}) collective-permute-start(bf16[1024,256]{1,0:T(8,128)(2,1)} %collective-permute-done.refs_1_), channel_id=1, source_target_pairs={{0,2},{2,4},{4,6},{6,8},{8,10},{10,12},{12,14},{14,0},{1,3},{3,5},... | collective-permute-start | bytes 1572872 | tf_op jit(solution)/shard_map/ppermute | solution.py:347
  33.2 1.2 copy-start.6
  34.3 25.6 %collective-permute-start.7 = (bf16[8,256,256]{2,1,0:T(8,128)(2,1)}, bf16[8,256,256]{2,1,0:T(8,128)(2,1)S(1)}, u32[]{:S(2)}, u32[]{:S(2)}) collective-permute-start(bf16[8,256,256]{2,1,0:T(8,128)(2,1)} %dynamic-slice_bitcast_fusion), channel_id=1, source_target_pairs={{0,1},{1,0},{2,3},{3,2},{4,5},{5,4},{6,7},{7,6},{8,9},{9,8},{10,11... | collective-permute-start | bytes 3145736 | tf_op jit(solution)/shard_map/ppermute | solution.py:352
  34.4 15.0 %collective-permute-start.5 = (bf16[1024,256]{1,0:T(8,128)(2,1)S(1)}, bf16[1024,256]{1,0:T(8,128)(2,1)}, u32[]{:S(2)}, u32[]{:S(2)}) collective-permute-start(bf16[1024,256]{1,0:T(8,128)(2,1)S(1)} %copy-done.6), channel_id=1, source_target_pairs={{0,14},{2,0},{4,2},{6,4},{8,6},{10,8},{12,10},{14,12},{1,15},{3,1}... | collective-permute-start | bytes 1572872 | tf_op jit(solution)/shard_map/ppermute | solution.py:349
  47.0 12.9 %collective-permute-start.3 = (bf16[1024,256]{1,0:T(8,128)(2,1)}, bf16[1024,256]{1,0:T(8,128)(2,1)}, u32[]{:S(2)}, u32[]{:S(2)}) collective-permute-start(bf16[1024,256]{1,0:T(8,128)(2,1)} %collective-permute-done.2.refs_2_), channel_id=1, source_target_pairs={{0,2},{2,4},{4,6},{6,8},{8,10},{10,12},{12,14},{14,0},{1,3},{3,5},... | collective-permute-start | bytes 1572872 | tf_op jit(solution)/shard_map/ppermute | solution.py:347
  49.4 15.0 %collective-permute-start.6 = (bf16[1024,256]{1,0:T(8,128)(2,1)}, bf16[1024,256]{1,0:T(8,128)(2,1)}, u32[]{:S(2)}, u32[]{:S(2)}) collective-permute-start(bf16[1024,256]{1,0:T(8,128)(2,1)} %collective-permute-done.5.refs_6_), channel_id=1, source_target_pairs={{0,14},{2,0},{4,2},{6,4},{8,6},{10,8},{12,10},{14,12},{1,15},{3,1}... | collective-permute-start | bytes 1572872 | tf_op jit(solution)/shard_map/ppermute | solution.py:349
  59.9 11.9 %collective-permute-start.4 = (bf16[1024,256]{1,0:T(8,128)(2,1)}, bf16[1024,256]{1,0:T(8,128)(2,1)}, u32[]{:S(2)}, u32[]{:S(2)}) collective-permute-start(bf16[1024,256]{1,0:T(8,128)(2,1)} %collective-permute-done.3.refs_3_), channel_id=1, source_target_pairs={{0,2},{2,4},{4,6},{6,8},{8,10},{10,12},{12,14},{14,0},{1,3},{3,5},... | collective-permute-start | bytes 1572872 | tf_op jit(solution)/shard_map/ppermute | solution.py:347
  59.9 20.7 %copy-start = (bf16[256,4096]{1,0:T(8,128)(2,1)S(1)}, bf16[256,4096]{1,0:T(8,128)(2,1)}, u32[]{:S(2)}) copy-start(bf16[256,4096]{1,0:T(8,128)(2,1)} %weight_ref.1) | copy-start | bytes 6291460
  59.9 1.0 copy-start.2
  71.8 1.2 copy-start.3
  73.0 1.0 copy-start.4
  74.1 1.0 copy-start.7
  80.6 2.5 %copy-start.9 = (s32[16,1,72]{2,1,0:T(1,128)S(1)}, s32[16,1,72]{2,1,0:T(1,128)}, u32[]{:S(2)}) copy-start(s32[16,1,72]{2,1,0:T(1,128)} %copy-done.8) | copy-start | bytes 13828
  80.6 2.9 %collective-permute-start.8 = (f32[1024,256]{1,0:T(8,128)}, f32[1024,256]{1,0:T(8,128)S(1)}, u32[]{:S(2)}, u32[]{:S(2)}) collective-permute-start(f32[1024,256]{1,0:T(8,128)} %get-tuple-element.31), channel_id=1, source_target_pairs={{0,1},{1,0},{2,3},{3,2},{4,5},{5,4},{6,7},{7,6},{8,9},{9,8},{10,11... | collective-permute-start | bytes 3145736 | tf_op jit(solution)/shard_map/ppermute | solution.py:358
  82.5 18.2 %collective-permute-start.10 = (bf16[8,256,256]{2,1,0:T(8,128)(2,1)}, bf16[8,256,256]{2,1,0:T(8,128)(2,1)}, u32[]{:S(2)}, u32[]{:S(2)}) collective-permute-start(bf16[8,256,256]{2,1,0:T(8,128)(2,1)} %get-tuple-element.34), channel_id=1, source_target_pairs={{0,1},{1,0},{2,3},{3,2},{4,5},{5,4},{6,7},{7,6},{8,9},{9,8},{10,11... | collective-permute-start | bytes 3145736 | tf_op jit(solution)/shard_map/ppermute | solution.py:355
  96.6 4.1 %collective-permute-start.9 = (bf16[512,256]{1,0:T(8,128)(2,1)S(1)}, bf16[512,256]{1,0:T(8,128)(2,1)S(1)}, u32[]{:S(2)}, u32[]{:S(2)}) collective-permute-start(bf16[512,256]{1,0:T(8,128)(2,1)S(1)} %attend.2.own_ref), channel_id=1, source_target_pairs={{0,1},{1,0},{2,3},{3,2},{4,5},{5,4},{6,7},{7,6},{8,9},{9,8},{10,11... | collective-permute-start | bytes 786440 | tf_op jit(solution)/shard_map/ppermute | solution.py:360
  100.1 6.4 %collective-permute-start.18 = (bf16[512,256]{1,0:T(8,128)(2,1)S(1)}, bf16[512,256]{1,0:T(8,128)(2,1)S(1)}, u32[]{:S(2)}, u32[]{:S(2)}) collective-permute-start(bf16[512,256]{1,0:T(8,128)(2,1)S(1)} %attend.3.own_ref), channel_id=1, source_target_pairs={{0,1},{1,0},{2,3},{3,2},{4,5},{5,4},{6,7},{7,6},{8,9},{9,8},{10,11... | collective-permute-start | bytes 786440 | tf_op jit(solution)/shard_map/ppermute | solution.py:360
  103.1 9.8 %collective-permute-start.11 = (bf16[512,256]{1,0:T(8,128)(2,1)S(1)}, bf16[512,256]{1,0:T(8,128)(2,1)S(1)}, u32[]{:S(2)}, u32[]{:S(2)}) collective-permute-start(bf16[512,256]{1,0:T(8,128)(2,1)S(1)} %get-tuple-element.36), channel_id=1, source_target_pairs={{0,2},{2,4},{4,6},{6,8},{8,10},{10,12},{12,14},{14,0},{1,3},{3,5},... | collective-permute-start | bytes 786440 | tf_op jit(solution)/shard_map/ppermute | solution.py:288
  103.2 9.9 %collective-permute-start.15 = (bf16[512,256]{1,0:T(8,128)(2,1)S(1)}, bf16[512,256]{1,0:T(8,128)(2,1)S(1)}, u32[]{:S(2)}, u32[]{:S(2)}) collective-permute-start(bf16[512,256]{1,0:T(8,128)(2,1)S(1)} %get-tuple-element.40), channel_id=1, source_target_pairs={{0,14},{2,0},{4,2},{6,4},{8,6},{10,8},{12,10},{14,12},{1,15},{3,1}... | collective-permute-start | bytes 786440 | tf_op jit(solution)/shard_map/ppermute | solution.py:288
  108.9 10.5 %collective-permute-start.19 = (bf16[512,256]{1,0:T(8,128)(2,1)S(1)}, bf16[512,256]{1,0:T(8,128)(2,1)S(1)}, u32[]{:S(2)}, u32[]{:S(2)}) collective-permute-start(bf16[512,256]{1,0:T(8,128)(2,1)S(1)} %get-tuple-element.44), channel_id=1, source_target_pairs={{0,2},{2,4},{4,6},{6,8},{8,10},{10,12},{12,14},{14,0},{1,3},{3,5},... | collective-permute-start | bytes 786440 | tf_op jit(solution)/shard_map/ppermute | solution.py:288
  109.0 10.6 %collective-permute-start.22 = (bf16[512,256]{1,0:T(8,128)(2,1)S(1)}, bf16[512,256]{1,0:T(8,128)(2,1)S(1)}, u32[]{:S(2)}, u32[]{:S(2)}) collective-permute-start(bf16[512,256]{1,0:T(8,128)(2,1)S(1)} %get-tuple-element.47), channel_id=1, source_target_pairs={{0,14},{2,0},{4,2},{6,4},{8,6},{10,8},{12,10},{14,12},{1,15},{3,1}... | collective-permute-start | bytes 786440 | tf_op jit(solution)/shard_map/ppermute | solution.py:288
  113.0 12.1 %collective-permute-start.12 = (bf16[512,256]{1,0:T(8,128)(2,1)S(1)}, bf16[512,256]{1,0:T(8,128)(2,1)S(1)}, u32[]{:S(2)}, u32[]{:S(2)}) collective-permute-start(bf16[512,256]{1,0:T(8,128)(2,1)S(1)} %add_convert_fusion.11), channel_id=1, source_target_pairs={{0,2},{2,4},{4,6},{6,8},{8,10},{10,12},{12,14},{14,0},{1,3},{3,5},... | collective-permute-start | bytes 786440 | tf_op jit(solution)/shard_map/ppermute | solution.py:288
  113.2 12.0 %collective-permute-start.16 = (bf16[512,256]{1,0:T(8,128)(2,1)S(1)}, bf16[512,256]{1,0:T(8,128)(2,1)S(1)}, u32[]{:S(2)}, u32[]{:S(2)}) collective-permute-start(bf16[512,256]{1,0:T(8,128)(2,1)S(1)} %add_convert_fusion.8), channel_id=1, source_target_pairs={{0,14},{2,0},{4,2},{6,4},{8,6},{10,8},{12,10},{14,12},{1,15},{3,1}... | collective-permute-start | bytes 786440 | tf_op jit(solution)/shard_map/ppermute | solution.py:288
  119.5 15.8 %collective-permute-start.20 = (bf16[512,256]{1,0:T(8,128)(2,1)S(1)}, bf16[512,256]{1,0:T(8,128)(2,1)S(1)}, u32[]{:S(2)}, u32[]{:S(2)}) collective-permute-start(bf16[512,256]{1,0:T(8,128)(2,1)S(1)} %add_convert_fusion.5), channel_id=1, source_target_pairs={{0,2},{2,4},{4,6},{6,8},{8,10},{10,12},{12,14},{14,0},{1,3},{3,5},... | collective-permute-start | bytes 786440 | tf_op jit(solution)/shard_map/ppermute | solution.py:288
  119.7 10.6 %collective-permute-start.23 = (bf16[512,256]{1,0:T(8,128)(2,1)S(1)}, bf16[512,256]{1,0:T(8,128)(2,1)S(1)}, u32[]{:S(2)}, u32[]{:S(2)}) collective-permute-start(bf16[512,256]{1,0:T(8,128)(2,1)S(1)} %add_convert_fusion.3), channel_id=1, source_target_pairs={{0,14},{2,0},{4,2},{6,4},{8,6},{10,8},{12,10},{14,12},{1,15},{3,1}... | collective-permute-start | bytes 786440 | tf_op jit(solution)/shard_map/ppermute | solution.py:288
  125.1 10.0 %collective-permute-start.13 = (bf16[512,256]{1,0:T(8,128)(2,1)S(1)}, bf16[512,256]{1,0:T(8,128)(2,1)S(1)}, u32[]{:S(2)}, u32[]{:S(2)}) collective-permute-start(bf16[512,256]{1,0:T(8,128)(2,1)S(1)} %add_convert_fusion.10), channel_id=1, source_target_pairs={{0,2},{2,4},{4,6},{6,8},{8,10},{10,12},{12,14},{14,0},{1,3},{3,5},... | collective-permute-start | bytes 786440 | tf_op jit(solution)/shard_map/ppermute | solution.py:288
  125.3 18.5 %collective-permute-start.17 = (bf16[512,256]{1,0:T(8,128)(2,1)S(1)}, bf16[512,256]{1,0:T(8,128)(2,1)S(1)}, u32[]{:S(2)}, u32[]{:S(2)}) collective-permute-start(bf16[512,256]{1,0:T(8,128)(2,1)S(1)} %add_convert_fusion.7), channel_id=1, source_target_pairs={{0,14},{2,0},{4,2},{6,4},{8,6},{10,8},{12,10},{14,12},{1,15},{3,1}... | collective-permute-start | bytes 786440 | tf_op jit(solution)/shard_map/ppermute | solution.py:288
  130.3 9.7 %collective-permute-start.24 = (bf16[512,256]{1,0:T(8,128)(2,1)S(1)}, bf16[512,256]{1,0:T(8,128)(2,1)S(1)}, u32[]{:S(2)}, u32[]{:S(2)}) collective-permute-start(bf16[512,256]{1,0:T(8,128)(2,1)S(1)} %add_convert_fusion.2), channel_id=1, source_target_pairs={{0,14},{2,0},{4,2},{6,4},{8,6},{10,8},{12,10},{14,12},{1,15},{3,1}... | collective-permute-start | bytes 786440 | tf_op jit(solution)/shard_map/ppermute | solution.py:288
  135.2 10.5 %collective-permute-start.14 = (bf16[512,256]{1,0:T(8,128)(2,1)S(1)}, bf16[512,256]{1,0:T(8,128)(2,1)S(1)}, u32[]{:S(2)}, u32[]{:S(2)}) collective-permute-start(bf16[512,256]{1,0:T(8,128)(2,1)S(1)} %add_convert_fusion.9), channel_id=1, source_target_pairs={{0,2},{2,4},{4,6},{6,8},{8,10},{10,12},{12,14},{14,0},{1,3},{3,5},... | collective-permute-start | bytes 786440 | tf_op jit(solution)/shard_map/ppermute | solution.py:288
  135.4 13.9 %collective-permute-start.21 = (bf16[512,256]{1,0:T(8,128)(2,1)S(1)}, bf16[512,256]{1,0:T(8,128)(2,1)S(1)}, u32[]{:S(2)}, u32[]{:S(2)}) collective-permute-start(bf16[512,256]{1,0:T(8,128)(2,1)S(1)} %add_convert_fusion.4), channel_id=1, source_target_pairs={{0,2},{2,4},{4,6},{6,8},{8,10},{10,12},{12,14},{14,0},{1,3},{3,5},... | collective-permute-start | bytes 786440 | tf_op jit(solution)/shard_map/ppermute | solution.py:288
  140.1 9.2 %collective-permute-start.25 = (bf16[512,256]{1,0:T(8,128)(2,1)S(1)}, bf16[512,256]{1,0:T(8,128)(2,1)S(1)}, u32[]{:S(2)}, u32[]{:S(2)}) collective-permute-start(bf16[512,256]{1,0:T(8,128)(2,1)S(1)} %add_convert_fusion.1), channel_id=1, source_target_pairs={{0,14},{2,0},{4,2},{6,4},{8,6},{10,8},{12,10},{14,12},{1,15},{3,1}... | collective-permute-start | bytes 786440 | tf_op jit(solution)/shard_map/ppermute | solution.py:288

commit v5 on v3

--- a/solution.py
+++ b/solution.py
@@ -69,16 +69,17 @@
 
 
 def select_kernel(place_ref, heard_ref, rows_ref, out_ref, sems):
-    shards, requests = out_ref.shape[0], out_ref.shape[0] * NBRS
-    here = place_ref[0]
+    shards, spans, blocks = out_ref.shape[0], heard_ref.shape[2], rows_ref.shape[0]
+    lowest = place_ref[0] * blocks
     copies = []
     for e in range(shards):
         first, last = jnp.int32(-1), jnp.int32(0)
-        for r in range(requests):
-            mine = heard_ref[e, r] == here
-            block = heard_ref[e, requests + r]
-            first = jnp.where(mine & (first < 0), block, first)
-            last = jnp.where(mine, block, last)
+        for n in range(NBRS):
+            for c in range(spans):
+                block = heard_ref[e, n, c] - lowest
+                mine = (block >= 0) & (block < blocks)
+                first = jnp.where(mine & (first < 0), block, first)
+                last = jnp.where(mine, block, last)
         for s, block in enumerate((jnp.maximum(first, 0), last)):
             copy = pltpu.make_async_copy(rows_ref.at[block], out_ref.at[e, s], sems.at[e, s])
             copy.start()
@@ -100,37 +101,43 @@
     )(place, heard, rows)
 
 
-def query_kernel(tokens_ref, weight_ref, out_ref):
-    projected = jnp.dot(tokens_ref[...], weight_ref[...], preferred_element_type=F32)
-    for h in range(weight_ref.shape[1] // HD):
-        cols = slice(h * HD, (h + 1) * HD)
-        out_ref[:, cols] = unit(projected[:, cols]).astype(BF16)
-
-
-def project_queries(tokens, weight):
-    rows, depth = tokens.shape
-    width, tile = weight.shape[1], 128
-    return pl.pallas_call(
-        query_kernel,
-        grid=(rows // tile,),
-        out_shape=jax.ShapeDtypeStruct((rows, width), BF16),
-        in_specs=[
-            pl.BlockSpec((tile, depth), lambda i: (i, 0)),
-            pl.BlockSpec((depth, width), lambda i: (0, 0)),
-        ],
-        out_specs=pl.BlockSpec((tile, width), lambda i: (i, 0)),
-        compiler_params=pltpu.CompilerParams(vmem_limit_bytes=24 << 20),
+def query_kernel(steps, place_ref, *refs):
+    pieces, (weight_ref, partner_ref), sums = refs[: len(steps)], refs[len(steps) :][:2], refs[len(steps) + 2 :]
+    ring = weight_ref.shape[0]
+    for matrix_ref, old_ref, new_ref in zip((weight_ref, partner_ref), sums[:2], sums[-2:]):
+        total = old_ref[...] if len(sums) > 2 else None
+        for step, piece in zip(steps, pieces):
+            chip = lax.rem(place_ref[0] + ring - step, ring)
+            part = jnp.dot(piece[...], matrix_ref[chip], preferred_element_type=F32)
+            total = part if total is None else total + part
+        new_ref[...] = total
+
+
+def add_queries(place, steps, pieces, weight, partner_weight, sums):
+    rows, depth = pieces[0].shape
+    width = weight.shape[-1]
+    out = jax.ShapeDtypeStruct((rows, width), F32)
+    held = 3 + len(steps)
+    return pl.pallas_call(
+        functools.partial(query_kernel, steps),
+        out_shape=(out, out),
+        in_specs=[SMEM] + [VMEM] * (len(steps) + 2 + len(sums)),
+        out_specs=(VMEM, VMEM),
+        input_output_aliases={held + i: i for i in range(len(sums))},
+        compiler_params=pltpu.CompilerParams(vmem_limit_bytes=12 << 20),
         cost_estimate=pl.CostEstimate(
-            flops=2 * rows * depth * width, bytes_accessed=11 << 20, transcendentals=0
+            flops=4 * rows * depth * width * len(steps), bytes_accessed=4 << 20, transcendentals=0
         ),
-        name="project_queries",
-    )(tokens, weight)
-
-
-def attend_kernel(first, slot_ref, length_ref, query_ref, rows_ref, out_ref, held_ref, sems):
+        name="add_queries",
+    )(place, *pieces, weight, partner_weight, *sums)
+
+
+def attend_kernel(
+    first, slot_ref, length_ref, own_ref, lent_ref, rows_ref, out_ref, query_ref, held_ref, sems
+):
     spans = slot_ref.shape[0] // NBRS
     count = sems.shape[0] // NBRS
-    width = query_ref.shape[1]
+    width = out_ref.shape[1]
     keys = NBRS * NBR_LEN
     factor = 2.0 / math.sqrt(HD)
     copies = []
@@ -143,6 +150,9 @@
             )
             copy.start()
             copies.append(copy)
+    for h in range(width // HD):
+        cols = slice(h * HD, (h + 1) * HD)
+        query_ref[:, cols] = unit(own_ref[:, cols] + lent_ref[:, cols]).astype(BF16)
     places = lax.broadcasted_iota(jnp.int32, (SPAN, keys), 1)
     group = 4
     for start in range(0, count, group):
@@ -171,26 +181,26 @@
             out_ref[c * SPAN : (c + 1) * SPAN, h * HD : (h + 1) * HD] = result.astype(BF16)
 
 
-def attend(part, parts, slot_index, lengths, queries, rows):
-    tokens, width = queries.shape[0] // parts, queries.shape[1]
+def attend(part, slot_index, lengths, own, lent, rows):
+    tokens, width = own.shape
     count = tokens // SPAN
     requests = count * NBRS
     return pl.pallas_call(
         functools.partial(attend_kernel, part * count),
-        grid=(1,),
         out_shape=jax.ShapeDtypeStruct((tokens, width), BF16),
-        in_specs=[SMEM, SMEM, pl.BlockSpec((tokens, width), lambda i: (part, 0)), ANY],
-        out_specs=pl.BlockSpec((tokens, width), lambda i: (0, 0)),
+        in_specs=[SMEM, SMEM, VMEM, VMEM, ANY],
+        out_specs=VMEM,
         scratch_shapes=[
+            pltpu.VMEM((tokens, width), BF16),
             pltpu.VMEM((requests * NBR_LEN, rows.shape[2]), BF16),
             pltpu.SemaphoreType.DMA((requests,)),
         ],
-        compiler_params=pltpu.CompilerParams(vmem_limit_bytes=24 << 20),
+        compiler_params=pltpu.CompilerParams(vmem_limit_bytes=12 << 20),
         cost_estimate=pl.CostEstimate(
             flops=4 * tokens * NBRS * NBR_LEN * width, bytes_accessed=3 << 20, transcendentals=0
         ),
         name="attend",
-    )(slot_index, lengths, queries, rows)
+    )(slot_index, lengths, own, lent, rows)
 
 
 def relay_kernel(place_ref, weight_ref, own_ref, lent_ref):
@@ -237,7 +247,7 @@
         out_shape=outs,
         in_specs=[VMEM] * 4,
         out_specs=[VMEM] * len(outs),
-        compiler_params=pltpu.CompilerParams(vmem_limit_bytes=24 << 20),
+        compiler_params=pltpu.CompilerParams(vmem_limit_bytes=12 << 20),
         cost_estimate=pl.CostEstimate(
             flops=4 * rows * width * width * len(steps), bytes_accessed=6 << 20, transcendentals=0
         ),
@@ -295,36 +305,76 @@
     here, core = lax.axis_index("z"), lax.axis_index("c")
     swap = [(i, (i + 1) % cores) for i in range(cores)]
 
-    gathered = lax.all_gather(tokens, ("z", "c"), axis=1, tiled=True)
-
-    owners = nbr_owner.T.reshape(-1)
-    wanted_blocks = nbr_block.T.reshape(-1)
-    notes = jnp.concatenate([owners, wanted_blocks, block_len])
-    notes = jnp.broadcast_to(notes[None, :], (shards, notes.shape[0]))
+    place = jnp.stack([here, core]).astype(jnp.int32)
+    spans, blocks = nbr_owner.shape[0], block_len.shape[0]
+
+    block_ids = nbr_owner.T * blocks + nbr_block.T
+    notes = jnp.concatenate([block_ids, jnp.pad(block_len, (0, spans - blocks))[None, :]], axis=0)
+    notes = jnp.broadcast_to(notes[None], (shards,) + notes.shape)
     heard = lax.all_to_all(notes, DB, split_axis=0, concat_axis=0, tiled=True)
     projected = project_blocks(codes, scales, key_weight, value_weight)
+
+    own_weight, lent_weight = relay(place, out_weight, ring)
+    by_core = query_weight.reshape(ring, cores, width, width)
+    own_rows = lax.dynamic_index_in_dim(by_core, core, 1, keepdims=False)
+    lent_rows = lax.dynamic_index_in_dim(by_core, 1 - core, 1, keepdims=False)
+    projected, own_weight, lent_weight, own_rows, lent_rows = lax.optimization_barrier(
+        (projected, own_weight, lent_weight, own_rows, lent_rows)
+    )
     sent = select_blocks(lax.axis_index(DB).astype(jnp.int32).reshape(1), heard, projected)
+    _, tokens, lent_weight, lent_rows = lax.optimization_barrier(
+        (sent, tokens, lent_weight, lent_rows)
+    )
     rows = lax.all_to_all(sent, DB, split_axis=0, concat_axis=0, tiled=True)
     rows = rows.reshape(shards * NBRS, NBR_LEN, 2 * width)
 
+    owners = nbr_owner.T.reshape(-1)
+    block_ids = block_ids.reshape(-1)
     order = jnp.arange(owners.shape[0], dtype=jnp.int32)
     earlier = jnp.sum(
         ((owners[:, None] == owners[None, :]) & (order[:, None] > order[None, :])).astype(jnp.int32),
         axis=1,
     )
     slot_index = owners * NBRS + earlier
-    all_lengths = heard[:, 2 * owners.shape[0] :].reshape(-1)
-    block_ids = owners * block_len.shape[0] + wanted_blocks
+    all_lengths = heard[:, NBRS, :blocks].reshape(-1)
     ids = jnp.arange(all_lengths.shape[0], dtype=jnp.int32)
     lengths = jnp.sum(
         jnp.where(block_ids[:, None] == ids[None, :], all_lengths[None, :], 0), axis=1
     )
 
-    own_weight, lent_weight = relay(jnp.stack([here, core]).astype(jnp.int32), out_weight, ring)
+    up = [(i, (i + 1) % ring) for i in range(ring)]
+    down = [(i, (i - 1) % ring) for i in range(ring)]
+    far = ring // 2
+    partner_rows = lax.ppermute(lent_rows, "c", swap)
     partner_weight = lax.ppermute(lent_weight, "c", swap)
-
-    queries = project_queries(gathered, query_weight)
-    attended = [attend(part, 2, slot_index, lengths, queries, rows) for part in range(2)]
+    pieces = [{0: half} for half in jnp.split(tokens, 2)]
+    sums = [(), ()]
+
+    def add(half, steps):
+        parts = [pieces[half][i] for i in steps]
+        sums[half] = add_queries(place, steps, parts, own_rows, partner_rows, sums[half])
+
+    for k in range(1, far + 1):
+        for half in range(2):
+            part = pieces[half]
+            if k > 1:
+                before, after = k - 1, ring - k + 1
+                part[before], part[after], sums[half] = lax.optimization_barrier(
+                    (part[before], part[after], sums[half])
+                )
+            if k < far or half == 0:
+                part[k] = lax.ppermute(part[k - 1], "z", up)
+            if k < far or half == 1:
+                part[ring - k] = lax.ppermute(part[(ring - k + 1) % ring], "z", down)
+            if k > 1:
+                add(half, ([0] if k == 2 else []) + [before, after])
+    for half in range(2):
+        add(half, [far])
+    attended = []
+    for half in range(2):
+        own, lent = sums[half]
+        lent = lax.ppermute(lent, "c", swap)
+        attended.append(attend(half, slot_index, lengths, own, lent, rows))
     partner_attended = [lax.ppermute(part, "c", swap) for part in attended]
     return reduce_ring(attended, partner_attended, own_weight, partner_weight, ring)
 

time: 162 us -> 154 us (0.951)
  waiting for transfers between devices: 74.7 us -> 37.1 us
  starting transfers between devices: 39.6 us -> 62.1 us
  Pallas kernels: 23.4 us -> 41 us
  between operations: 13.6 us -> 0.27 us
    all_gather x1 -> x0, waiting for transfers between devices: 39.9 us -> none  [local(): gathered = lax.all_gather(tokens, ('z', 'c'), axis=1, tiled=True)]
    ppermute x0 -> x17, starting transfers between devices: none -> 22.3 us  [the longest x7 22.1 us: local(): part[ring - k] = lax.ppermute(part[(ring - k + 1) % ring], 'z', down)]
    pallas_call x3 -> x10, Pallas kernels: 10.4 us -> 24.7 us  [the longest x8 17.8 us: add_queries(): pl.pallas_call(functools.partial(query_kernel, steps), out_shape=(out, ou...]
    ppermute x0 -> x17, waiting for transfers between devices: none -> 13.7 us  [the longest x7 10.3 us: local(): part[k] = lax.ppermute(part[k - 1], 'z', up)]
    all_to_all x1, waiting for transfers between devices: 8.79 us -> 2.47 us  [local(): rows = lax.all_to_all(sent, DB, split_axis=0, concat_axis=0, tiled=True)]
    ppermute x14, waiting for transfers between devices: 24.6 us -> 20.9 us  [reduce_ring(): lax.ppermute(held[half, way], 'z', up if way == 1 else down)]
    squeeze x0 -> x1, local copies, waits for them, and re-layouts: none -> 2.66 us  [local(): lent_rows = lax.dynamic_index_in_dim(by_core, 1 - core, 1, keepdims=False)]
    pallas_call x2, Pallas kernels: 2.51 us -> 4.96 us  [shares(): pl.pallas_call(functools.partial(share_kernel, steps), out_shape=outs, in...]
  transfers between devices with their start and end apart: 20 -> 36, of which waited for: 12 -> 18; matrix products, arithmetic and copies ran while one was open for 3% -> 4% of each run, Pallas kernels for 14% -> 24%
where the time goes in v5:
time: 154 us; the launch traced here: 153 us
  starting transfers between devices  62.1 us (40%)
  Pallas kernels  41 us (27%)
  waiting for transfers between devices  37.1 us (24%)
  local copies, waits for them, and re-layouts  9.3 us (6%)
  other arithmetic  2.72 us (2%)
    ppermute x14, starting transfers between devices, reduce_ring(): lax.ppermute(held[half, way], 'z', up if way == 1 else down)  24.6 us
    ppermute x7, starting transfers between devices, local(): part[ring - k] = lax.ppermute(part[(ring - k + 1) % ring], 'z', down)  22.1 us
    ppermute x14, waiting for transfers between devices, reduce_ring(): lax.ppermute(held[half, way], 'z', up if way == 1 else down)  20.9 us
    pallas_call x8, Pallas kernels, add_queries(): pl.pallas_call(functools.partial(query_kernel, steps), out_shape=(out, ou...  17.8 us
    ppermute x7, waiting for transfers between devices, local(): part[k] = lax.ppermute(part[k - 1], 'z', up)  10.3 us
    all_to_all x1, starting transfers between devices, local(): rows = lax.all_to_all(sent, DB, split_axis=0, concat_axis=0, tiled=True)  7.37 us
    all_to_all x1, starting transfers between devices, local(): heard = lax.all_to_all(notes, DB, split_axis=0, concat_axis=0, tiled=True)  7.17 us
    pallas_call x2, Pallas kernels, attend(): pl.pallas_call(functools.partial(attend_kernel, part * count), out_shape=...  6.9 us
  transfers between devices with their start and end apart: 36, of which 18 were waited for; matrix products, arithmetic and copies ran while one was open for 4% of the time, Pallas kernels for 24%

profile of v5, /device:TPU:24, one launch (start us, length us, event | category | flops | bytes accessed | tf_op | source)
XLA Modules:
  0.0 152.5 jit_solution(4290805126163236162)
XLA Ops:
  2.0 7.2 %all-to-all-start = ((s32[16,3,16]{2,1,0:T(4,128)}), s32[16,3,16]{2,1,0:T(4,128)S(1)}, u32[]{:S(2)}, u32[]{:S(2)}) async-start(s32[16,3,16]{2,1,0:T(4,128)} %broadcast_in_dim.27), calls=%async_computation | async-start | bytes 65536 | tf_op jit(solution)/shard_map/all_to_all | solution.py:314
  9.2 2.7 %dynamic-slice_bitcast_fusion = (bf16[8,256,256]{2,1,0:T(8,128)(2,1)}, bf16[8,256,256]{2,1,0:T(8,128)(2,1)S(1)}) fusion(bf16[8,2,256,256]{3,2,1,0:T(8,128)(2,1)} %bitcast.19, s32[]{:T(128)S(6)} %select_n.13, s32[]{:T(128)S(6)} %select_n.12), kind=kLoop, calls=%fused_computation | loop fusion | bytes 4194312 | tf_op jit(solution)/shard_map/jit(dynamic_index_in_dim)/squeeze | solution.py:320
  11.9 5.0 %project_blocks.1.rows_ref = bf16[8,128,512]{2,1,0:T(8,128)(2,1)} custom-call(f32[8,7]{1,0:T(8,128)} %scales_ref.1, bf16[8,128,896]{2,1,0:T(8,128)(2,1)} %codes_ref.1, bf16[896,256]{1,0:T(8,128)(2,1)} %key_ref.1, bf16[896,256]{1,0:T(8,128)(2,1)} %value_ref.1), custom_call_target="tpu_custom_call" | custom-call | flops 939524096 | bytes 5242880 | tf_op jit(solution)/shard_map/project_blocks/pallas_call | solution.py:52
  16.9 1.8 %relay.1 = (bf16[8,256,256]{2,1,0:T(8,128)(2,1)S(1)}, bf16[8,256,256]{2,1,0:T(8,128)(2,1)}) custom-call(s32[2]{0:T(128)S(1)} %pad_add_fusion.1.place_ref, bf16[256,4096]{1,0:T(8,128)(2,1)S(1)} %copy-done), custom_call_target="tpu_custom_call" | custom-call | bytes 4194304 | tf_op jit(solution)/shard_map/relay/pallas_call | solution.py:219
  18.7 1.0 copy-done.5
  20.3 4.6 %select_blocks.1 = bf16[16,2,128,512]{3,2,1,0:T(8,128)(2,1)} custom-call(s32[1]{0:T(128)} %bitcast.5.place_ref, s32[16,3,16]{2,1,0:T(4,128)} %copy-done.8, bf16[8,128,512]{2,1,0:T(8,128)(2,1)} %project_blocks.1.rows_ref), custom_call_target="tpu_custom_call" | custom-call | bytes 9437184 | tf_op jit(solution)/shard_map/select_blocks/pallas_call | solution.py:93
  24.9 7.4 %all-to-all-start.1 = ((bf16[16,2,128,512]{3,2,1,0:T(8,128)(2,1)}), bf16[16,2,128,512]{3,2,1,0:T(8,128)(2,1)}, u32[]{:S(2)}, u32[]{:S(2)}) async-start(bf16[16,2,128,512]{3,2,1,0:T(8,128)(2,1)} %select_blocks.1), calls=%async_computation.1 | async-start | bytes 8388608 | tf_op jit(solution)/shard_map/all_to_all | solution.py:328
  32.3 1.1 fusion.1
  33.4 5.9 %collective-permute-start.19 = (bf16[512,256]{1,0:T(8,128)(2,1)S(1)}, bf16[512,256]{1,0:T(8,128)(2,1)S(1)}, u32[]{:S(2)}, u32[]{:S(2)}) collective-permute-start(bf16[512,256]{1,0:T(8,128)(2,1)S(1)} %get-tuple-element.132.refs_0_), channel_id=1, source_target_pairs={{0,14},{2,0},{4,2},{6,4},{8,6},{10,8},{12,10},{14,12},{1,15},{3,1}... | collective-permute-start | bytes 786440 | tf_op jit(solution)/shard_map/ppermute | solution.py:368
  39.3 3.2 %collective-permute-start.1 = (bf16[512,256]{1,0:T(8,128)(2,1)S(1)}, bf16[512,256]{1,0:T(8,128)(2,1)S(1)}, u32[]{:S(2)}, u32[]{:S(2)}) collective-permute-start(bf16[512,256]{1,0:T(8,128)(2,1)S(1)} %get-tuple-element.131.refs_0_), channel_id=1, source_target_pairs={{0,14},{2,0},{4,2},{6,4},{8,6},{10,8},{12,10},{14,12},{1,15},{3,1}... | collective-permute-start | bytes 786440 | tf_op jit(solution)/shard_map/ppermute | solution.py:368
  42.6 3.4 %collective-permute-done.19.refs_2_ = bf16[512,256]{1,0:T(8,128)(2,1)S(1)} collective-permute-done((bf16[512,256]{1,0:T(8,128)(2,1)S(1)}, bf16[512,256]{1,0:T(8,128)(2,1)S(1)}, u32[]{:S(2)}, u32[]{:S(2)}) %collective-permute-start.19) | collective-permute-done | bytes 262176 | tf_op jit(solution)/shard_map/ppermute | solution.py:368
  46.0 3.7 %collective-permute-done.18.refs_1_ = bf16[512,256]{1,0:T(8,128)(2,1)S(1)} collective-permute-done((bf16[512,256]{1,0:T(8,128)(2,1)S(1)}, bf16[512,256]{1,0:T(8,128)(2,1)S(1)}, u32[]{:S(2)}, u32[]{:S(2)}) %collective-permute-start.18) | collective-permute-done | bytes 262176 | tf_op jit(solution)/shard_map/ppermute | solution.py:366
  49.7 3.2 %collective-permute-start.21 = (bf16[512,256]{1,0:T(8,128)(2,1)S(1)}, bf16[512,256]{1,0:T(8,128)(2,1)S(1)}, u32[]{:S(2)}, u32[]{:S(2)}) collective-permute-start(bf16[512,256]{1,0:T(8,128)(2,1)S(1)} %collective-permute-done.19.refs_2_), channel_id=1, source_target_pairs={{0,14},{2,0},{4,2},{6,4},{8,6},{10,8},{12,10},{14,12},{1,15},{3,1}... | collective-permute-start | bytes 786440 | tf_op jit(solution)/shard_map/ppermute | solution.py:368
  52.9 2.4 %collective-permute-done.refs_1_ = bf16[512,256]{1,0:T(8,128)(2,1)S(1)} collective-permute-done((bf16[512,256]{1,0:T(8,128)(2,1)S(1)}, bf16[512,256]{1,0:T(8,128)(2,1)S(1)}, u32[]{:S(2)}, u32[]{:S(2)}) %collective-permute-start) | collective-permute-done | bytes 262176 | tf_op jit(solution)/shard_map/ppermute | solution.py:366
  55.3 3.2 %collective-permute-start.3 = (bf16[512,256]{1,0:T(8,128)(2,1)S(1)}, bf16[512,256]{1,0:T(8,128)(2,1)S(1)}, u32[]{:S(2)}, u32[]{:S(2)}) collective-permute-start(bf16[512,256]{1,0:T(8,128)(2,1)S(1)} %collective-permute-done.1.refs_2_), channel_id=1, source_target_pairs={{0,14},{2,0},{4,2},{6,4},{8,6},{10,8},{12,10},{14,12},{1,15},{3,1}... | collective-permute-start | bytes 786440 | tf_op jit(solution)/shard_map/ppermute | solution.py:368
  58.5 1.9 %add_queries.12 = (f32[512,256]{1,0:T(8,128)S(1)}, f32[512,256]{1,0:T(8,128)}) custom-call(s32[2]{0:T(128)S(1)} %pad_add_fusion.1.place_ref, bf16[512,256]{1,0:T(8,128)(2,1)S(1)} %get-tuple-element.132.refs_0_, bf16[512,256]{1,0:T(8,128)(2,1)S(1)} %collective-permute-done.18.refs_1_, bf16[512,256]{1,0:T(8,128)(2,1)S(1)} %collective-permute-done.19.refs_2_, ...), custom_call_target="tpu_custom_call" | custom-call | flops 402653184 | bytes 4194304 | tf_op jit(solution)/shard_map/add_queries/pallas_call | solution.py:121
  60.9 3.2 %collective-permute-start.23 = (bf16[512,256]{1,0:T(8,128)(2,1)S(1)}, bf16[512,256]{1,0:T(8,128)(2,1)}, u32[]{:S(2)}, u32[]{:S(2)}) collective-permute-start(bf16[512,256]{1,0:T(8,128)(2,1)S(1)} %collective-permute-done.21.refs_1_), channel_id=1, source_target_pairs={{0,14},{2,0},{4,2},{6,4},{8,6},{10,8},{12,10},{14,12},{1,15},{3,1}... | collective-permute-start | bytes 786440 | tf_op jit(solution)/shard_map/ppermute | solution.py:368
  64.2 2.0 %add_queries.8 = (f32[512,256]{1,0:T(8,128)S(1)}, f32[512,256]{1,0:T(8,128)}) custom-call(s32[2]{0:T(128)S(1)} %pad_add_fusion.1.place_ref, bf16[512,256]{1,0:T(8,128)(2,1)S(1)} %get-tuple-element.131.refs_0_, bf16[512,256]{1,0:T(8,128)(2,1)S(1)} %collective-permute-done.refs_1_, bf16[512,256]{1,0:T(8,128)(2,1)S(1)} %collective-permute-done.1.refs_2_, ...), custom_call_target="tpu_custom_call" | custom-call | flops 402653184 | bytes 4194304 | tf_op jit(solution)/shard_map/add_queries/pallas_call | solution.py:121
  66.5 3.2 %collective-permute-start.6 = (bf16[512,256]{1,0:T(8,128)(2,1)S(1)}, bf16[512,256]{1,0:T(8,128)(2,1)S(1)}, u32[]{:S(2)}, u32[]{:S(2)}) collective-permute-start(bf16[512,256]{1,0:T(8,128)(2,1)S(1)} %collective-permute-done.3.refs_1_), channel_id=1, source_target_pairs={{0,14},{2,0},{4,2},{6,4},{8,6},{10,8},{12,10},{14,12},{1,15},{3,1}... | collective-permute-start | bytes 786440 | tf_op jit(solution)/shard_map/ppermute | solution.py:368
  69.8 2.3 %add_queries.13 = (f32[512,256]{1,0:T(8,128)S(1)}, f32[512,256]{1,0:T(8,128)}) custom-call(s32[2]{0:T(128)S(1)} %pad_add_fusion.1.place_ref, bf16[512,256]{1,0:T(8,128)(2,1)S(1)} %collective-permute-done.20.refs_0_, bf16[512,256]{1,0:T(8,128)(2,1)S(1)} %collective-permute-done.21.refs_1_, ...), custom_call_target="tpu_custom_call", output_to_operand_aliasing={{0}: (5, {}), {1}: (6, {})} | custom-call | flops 268435456 | bytes 4194304 | tf_op jit(solution)/shard_map/add_queries/pallas_call | solution.py:121
  72.3 2.3 %add_queries.9 = (f32[512,256]{1,0:T(8,128)S(1)}, f32[512,256]{1,0:T(8,128)}) custom-call(s32[2]{0:T(128)S(1)} %pad_add_fusion.1.place_ref, bf16[512,256]{1,0:T(8,128)(2,1)S(1)} %collective-permute-done.2.refs_0_, bf16[512,256]{1,0:T(8,128)(2,1)S(1)} %collective-permute-done.3.refs_1_, ...), custom_call_target="tpu_custom_call", output_to_operand_aliasing={{0}: (5, {}), {1}: (6, {})} | custom-call | flops 268435456 | bytes 4194304 | tf_op jit(solution)/shard_map/add_queries/pallas_call | solution.py:121
  74.6 2.5 %collective-permute-done.5.refs_0_ = bf16[512,256]{1,0:T(8,128)(2,1)} collective-permute-done((bf16[512,256]{1,0:T(8,128)(2,1)S(1)}, bf16[512,256]{1,0:T(8,128)(2,1)}, u32[]{:S(2)}, u32[]{:S(2)}) %collective-permute-start.5) | collective-permute-done | bytes 262176 | tf_op jit(solution)/shard_map/ppermute | solution.py:366
  78.0 0.9 copy-done.2
  78.9 2.4 %add_queries.14 = (f32[512,256]{1,0:T(8,128)S(1)}, f32[512,256]{1,0:T(8,128)}) custom-call(s32[2]{0:T(128)S(1)} %pad_add_fusion.1.place_ref, bf16[512,256]{1,0:T(8,128)(2,1)S(1)} %copy-done.2, bf16[512,256]{1,0:T(8,128)(2,1)} %collective-permute-done.23.refs_1_, ...), custom_call_target="tpu_custom_call", output_to_operand_aliasing={{0}: (5, {}), {1}: (6, {})} | custom-call | flops 268435456 | bytes 4194304 | tf_op jit(solution)/shard_map/add_queries/pallas_call | solution.py:121
  81.3 2.3 %add_queries.15 = (f32[512,256]{1,0:T(8,128)S(1)}, f32[512,256]{1,0:T(8,128)}) custom-call(s32[2]{0:T(128)S(1)} %pad_add_fusion.1.place_ref, bf16[512,256]{1,0:T(8,128)(2,1)} %collective-permute-done.24.refs_0_, bf16[8,256,256]{2,1,0:T(8,128)(2,1)S(1)} %get-tuple-element.75.refs_3_.refs_2_.refs_1_, ...), custom_call_target="tpu_custom_call", output_to_operand_aliasing={{0}: (4, {}), {1}: (5, {})} | custom-call | flops 134217728 | bytes 4194304 | tf_op jit(solution)/shard_map/add_queries/pallas_call | solution.py:121
  83.8 2.4 %add_queries.10 = (f32[512,256]{1,0:T(8,128)S(1)}, f32[512,256]{1,0:T(8,128)}) custom-call(s32[2]{0:T(128)S(1)} %pad_add_fusion.1.place_ref, bf16[512,256]{1,0:T(8,128)(2,1)} %collective-permute-done.5.refs_0_, bf16[512,256]{1,0:T(8,128)(2,1)S(1)} %copy-done.4, ...), custom_call_target="tpu_custom_call", output_to_operand_aliasing={{0}: (5, {}), {1}: (6, {})} | custom-call | flops 268435456 | bytes 4194304 | tf_op jit(solution)/shard_map/add_queries/pallas_call | solution.py:121
  86.9 2.2 %add_queries.11 = (f32[512,256]{1,0:T(8,128)S(1)}, f32[512,256]{1,0:T(8,128)}) custom-call(s32[2]{0:T(128)S(1)} %pad_add_fusion.1.place_ref, bf16[512,256]{1,0:T(8,128)(2,1)S(1)} %collective-permute-done.7.refs_0_, bf16[8,256,256]{2,1,0:T(8,128)(2,1)S(1)} %get-tuple-element.75.refs_3_.refs_2_.refs_1_, ...), custom_call_target="tpu_custom_call", output_to_operand_aliasing={{0}: (4, {}), {1}: (5, {})} | custom-call | flops 134217728 | bytes 4194304 | tf_op jit(solution)/shard_map/add_queries/pallas_call | solution.py:121
  90.2 2.5 %all-to-all-done.1 = bf16[16,2,128,512]{3,2,1,0:T(8,128)(2,1)} async-done(((bf16[16,2,128,512]{3,2,1,0:T(8,128)(2,1)}), bf16[16,2,128,512]{3,2,1,0:T(8,128)(2,1)}, u32[]{:S(2)}, u32[]{:S(2)}) %all-to-all-start.1) | async-done | bytes 4194336 | tf_op jit(solution)/shard_map/all_to_all | solution.py:328
  92.7 3.7 %attend.3.own_ref = bf16[512,256]{1,0:T(8,128)(2,1)S(1)} custom-call(s32[32]{0:T(128)S(1)} %multiply_add_fusion.slot_ref, s32[32]{0:T(128)S(1)} %select_reduce_fusion.length_ref, f32[512,256]{1,0:T(8,128)S(1)} %get-tuple-element.119.own_ref, f32[512,256]{1,0:T(8,128)} %collective-permute-done.25.lent_ref, bf16[32,128,512]{2,1,0:T(8,128)(2,1)} %bitcast.9.rows_ref), custom_call_target="tpu_custom_call" | custom-call | flops 134217728 | bytes 3145728 | tf_op jit(solution)/shard_map/attend/pallas_call | solution.py:188
  96.6 3.2 %attend.2.own_ref = bf16[512,256]{1,0:T(8,128)(2,1)S(1)} custom-call(s32[32]{0:T(128)S(1)} %multiply_add_fusion.slot_ref, s32[32]{0:T(128)S(1)} %select_reduce_fusion.length_ref, f32[512,256]{1,0:T(8,128)S(1)} %get-tuple-element.91.own_ref, f32[512,256]{1,0:T(8,128)S(1)} %collective-permute-done.8.lent_ref, bf16[32,128,512]{2,1,0:T(8,128)(2,1)} %bitcast.9.rows_ref), custom_call_target="tpu_custom_call" | custom-call | flops 134217728 | bytes 3145728 | tf_op jit(solution)/shard_map/attend/pallas_call | solution.py:188
  100.3 2.5 %shares.3 = (bf16[512,256]{1,0:T(8,128)(2,1)S(1)}, bf16[512,256]{1,0:T(8,128)(2,1)S(1)}, f32[512,256]{1,0:T(8,128)S(1)}, f32[512,256]{1,0:T(8,128)S(1)}, f32[512...) custom-call(bf16[512,256]{1,0:T(8,128)(2,1)S(1)} %attend.3.own_ref, ...), custom_call_target="tpu_custom_call" | custom-call | flops 1073741824 | bytes 6291456 | tf_op jit(solution)/shard_map/shares/pallas_call | solution.py:245
  102.8 2.2 %collective-permute-start.27 = (bf16[512,256]{1,0:T(8,128)(2,1)S(1)}, bf16[512,256]{1,0:T(8,128)(2,1)S(1)}, u32[]{:S(2)}, u32[]{:S(2)}) collective-permute-start(bf16[512,256]{1,0:T(8,128)(2,1)S(1)} %get-tuple-element.122), channel_id=1, source_target_pairs={{0,2},{2,4},{4,6},{6,8},{8,10},{10,12},{12,14},{14,0},{1,3},{3,5},... | collective-permute-start | bytes 786440 | tf_op jit(solution)/shard_map/ppermute | solution.py:281
  105.1 4.0 %collective-permute-start.30 = (bf16[512,256]{1,0:T(8,128)(2,1)S(1)}, bf16[512,256]{1,0:T(8,128)(2,1)S(1)}, u32[]{:S(2)}, u32[]{:S(2)}) collective-permute-start(bf16[512,256]{1,0:T(8,128)(2,1)S(1)} %get-tuple-element.125), channel_id=1, source_target_pairs={{0,14},{2,0},{4,2},{6,4},{8,6},{10,8},{12,10},{14,12},{1,15},{3,1}... | collective-permute-start | bytes 786440 | tf_op jit(solution)/shard_map/ppermute | solution.py:281
  109.1 2.5 %shares.2 = (bf16[512,256]{1,0:T(8,128)(2,1)S(1)}, bf16[512,256]{1,0:T(8,128)(2,1)S(1)}, f32[512,256]{1,0:T(8,128)S(1)}, f32[512,256]{1,0:T(8,128)S(1)}, f32[512...) custom-call(bf16[512,256]{1,0:T(8,128)(2,1)S(1)} %attend.2.own_ref, ...), custom_call_target="tpu_custom_call" | custom-call | flops 1073741824 | bytes 6291456 | tf_op jit(solution)/shard_map/shares/pallas_call | solution.py:245
  111.7 3.2 %collective-permute-start.15 = (bf16[512,256]{1,0:T(8,128)(2,1)S(1)}, bf16[512,256]{1,0:T(8,128)(2,1)S(1)}, u32[]{:S(2)}, u32[]{:S(2)}) collective-permute-start(bf16[512,256]{1,0:T(8,128)(2,1)S(1)} %get-tuple-element.100), channel_id=1, source_target_pairs={{0,14},{2,0},{4,2},{6,4},{8,6},{10,8},{12,10},{14,12},{1,15},{3,1}... | collective-permute-start | bytes 786440 | tf_op jit(solution)/shard_map/ppermute | solution.py:281
  114.9 0.8 collective-permute-done.27
  115.9 3.3 %collective-permute-start.31 = (bf16[512,256]{1,0:T(8,128)(2,1)S(1)}, bf16[512,256]{1,0:T(8,128)(2,1)S(1)}, u32[]{:S(2)}, u32[]{:S(2)}) collective-permute-start(bf16[512,256]{1,0:T(8,128)(2,1)S(1)} %add_convert_fusion.3), channel_id=1, source_target_pairs={{0,14},{2,0},{4,2},{6,4},{8,6},{10,8},{12,10},{14,12},{1,15},{3,1}... | collective-permute-start | bytes 786440 | tf_op jit(solution)/shard_map/ppermute | solution.py:281
  119.2 2.8 %collective-permute-done.11 = bf16[512,256]{1,0:T(8,128)(2,1)S(1)} collective-permute-done((bf16[512,256]{1,0:T(8,128)(2,1)S(1)}, bf16[512,256]{1,0:T(8,128)(2,1)S(1)}, u32[]{:S(2)}, u32[]{:S(2)}) %collective-permute-start.11) | collective-permute-done | bytes 262176 | tf_op jit(solution)/shard_map/ppermute | solution.py:281
  122.3 3.3 %collective-permute-start.16 = (bf16[512,256]{1,0:T(8,128)(2,1)S(1)}, bf16[512,256]{1,0:T(8,128)(2,1)S(1)}, u32[]{:S(2)}, u32[]{:S(2)}) collective-permute-start(bf16[512,256]{1,0:T(8,128)(2,1)S(1)} %add_convert_fusion.8), channel_id=1, source_target_pairs={{0,14},{2,0},{4,2},{6,4},{8,6},{10,8},{12,10},{14,12},{1,15},{3,1}... | collective-permute-start | bytes 786440 | tf_op jit(solution)/shard_map/ppermute | solution.py:281
  125.6 1.7 %collective-permute-done.31 = bf16[512,256]{1,0:T(8,128)(2,1)S(1)} collective-permute-done((bf16[512,256]{1,0:T(8,128)(2,1)S(1)}, bf16[512,256]{1,0:T(8,128)(2,1)S(1)}, u32[]{:S(2)}, u32[]{:S(2)}) %collective-permute-start.31) | collective-permute-done | bytes 262176 | tf_op jit(solution)/shard_map/ppermute | solution.py:281
  127.3 3.8 %collective-permute-start.32 = (bf16[512,256]{1,0:T(8,128)(2,1)S(1)}, bf16[512,256]{1,0:T(8,128)(2,1)S(1)}, u32[]{:S(2)}, u32[]{:S(2)}) collective-permute-start(bf16[512,256]{1,0:T(8,128)(2,1)S(1)} %add_convert_fusion.2), channel_id=1, source_target_pairs={{0,14},{2,0},{4,2},{6,4},{8,6},{10,8},{12,10},{14,12},{1,15},{3,1}... | collective-permute-start | bytes 786440 | tf_op jit(solution)/shard_map/ppermute | solution.py:281
  131.2 1.1 collective-permute-done.12
  132.5 4.8 %collective-permute-done.32 = bf16[512,256]{1,0:T(8,128)(2,1)S(1)} collective-permute-done((bf16[512,256]{1,0:T(8,128)(2,1)S(1)}, bf16[512,256]{1,0:T(8,128)(2,1)S(1)}, u32[]{:S(2)}, u32[]{:S(2)}) %collective-permute-start.32) | collective-permute-done | bytes 262176 | tf_op jit(solution)/shard_map/ppermute | solution.py:281
  137.4 3.8 %collective-permute-start.33 = (bf16[512,256]{1,0:T(8,128)(2,1)S(1)}, bf16[512,256]{1,0:T(8,128)(2,1)S(1)}, u32[]{:S(2)}, u32[]{:S(2)}) collective-permute-start(bf16[512,256]{1,0:T(8,128)(2,1)S(1)} %add_convert_fusion.1), channel_id=1, source_target_pairs={{0,14},{2,0},{4,2},{6,4},{8,6},{10,8},{12,10},{14,12},{1,15},{3,1}... | collective-permute-start | bytes 786440 | tf_op jit(solution)/shard_map/ppermute | solution.py:281
  141.7 2.2 %collective-permute-done.13 = bf16[512,256]{1,0:T(8,128)(2,1)S(1)} collective-permute-done((bf16[512,256]{1,0:T(8,128)(2,1)S(1)}, bf16[512,256]{1,0:T(8,128)(2,1)S(1)}, u32[]{:S(2)}, u32[]{:S(2)}) %collective-permute-start.13) | collective-permute-done | bytes 262176 | tf_op jit(solution)/shard_map/ppermute | solution.py:281
  144.1 3.9 %collective-permute-done.33 = bf16[512,256]{1,0:T(8,128)(2,1)S(1)} collective-permute-done((bf16[512,256]{1,0:T(8,128)(2,1)S(1)}, bf16[512,256]{1,0:T(8,128)(2,1)S(1)}, u32[]{:S(2)}, u32[]{:S(2)}) %collective-permute-start.33) | collective-permute-done | bytes 262176 | tf_op jit(solution)/shard_map/ppermute | solution.py:281
  148.0 3.4 %collective-permute-done.17 = bf16[512,256]{1,0:T(8,128)(2,1)S(1)} collective-permute-done((bf16[512,256]{1,0:T(8,128)(2,1)S(1)}, bf16[512,256]{1,0:T(8,128)(2,1)S(1)}, u32[]{:S(2)}, u32[]{:S(2)}) %collective-permute-start.17) | collective-permute-done | bytes 262176 | tf_op jit(solution)/shard_map/ppermute | solution.py:281
  151.7 0.8 pad_maximum_fusion
  (86 shorter events, 9.4 us)
Async XLA Ops:
  2.0 17.7 %all-to-all-start = ((s32[16,3,16]{2,1,0:T(4,128)}), s32[16,3,16]{2,1,0:T(4,128)S(1)}, u32[]{:S(2)}, u32[]{:S(2)}) async-start(s32[16,3,16]{2,1,0:T(4,128)} %broadcast_in_dim.27), calls=%async_computation | async-start | bytes 65536 | tf_op jit(solution)/shard_map/all_to_all | solution.py:314
  11.9 5.0 %copy-start = (bf16[256,4096]{1,0:T(8,128)(2,1)S(1)}, bf16[256,4096]{1,0:T(8,128)(2,1)}, u32[]{:S(2)}) copy-start(bf16[256,4096]{1,0:T(8,128)(2,1)} %weight_ref.1) | copy-start | bytes 6291460
  18.7 1.0 copy-start.5
  19.7 0.6 copy-start.8
  24.9 7.4 %copy-start.7 = (bf16[8,256,256]{2,1,0:T(8,128)(2,1)S(1)}, bf16[8,256,256]{2,1,0:T(8,128)(2,1)}, u32[]{:S(2)}) copy-start(bf16[8,256,256]{2,1,0:T(8,128)(2,1)} %get-tuple-element.76) | copy-start | bytes 3145732
  24.9 67.9 %all-to-all-start.1 = ((bf16[16,2,128,512]{3,2,1,0:T(8,128)(2,1)}), bf16[16,2,128,512]{3,2,1,0:T(8,128)(2,1)}, u32[]{:S(2)}, u32[]{:S(2)}) async-start(bf16[16,2,128,512]{3,2,1,0:T(8,128)(2,1)} %select_blocks.1), calls=%async_computation.1 | async-start | bytes 8388608 | tf_op jit(solution)/shard_map/all_to_all | solution.py:328
  32.2 26.3 %collective-permute-start.4 = (bf16[8,256,256]{2,1,0:T(8,128)(2,1)S(1)}, bf16[8,256,256]{2,1,0:T(8,128)(2,1)S(1)}, u32[]{:S(2)}, u32[]{:S(2)}) collective-permute-start(bf16[8,256,256]{2,1,0:T(8,128)(2,1)S(1)} %copy-done.7), channel_id=1, source_target_pairs={{0,1},{1,0},{2,3},{3,2},{4,5},{5,4},{6,7},{7,6},{8,9},{9,8},{10,11... | collective-permute-start | bytes 3145736 | tf_op jit(solution)/shard_map/ppermute | solution.py:348
  33.4 12.5 %collective-permute-start.19 = (bf16[512,256]{1,0:T(8,128)(2,1)S(1)}, bf16[512,256]{1,0:T(8,128)(2,1)S(1)}, u32[]{:S(2)}, u32[]{:S(2)}) collective-permute-start(bf16[512,256]{1,0:T(8,128)(2,1)S(1)} %get-tuple-element.132.refs_0_), channel_id=1, source_target_pairs={{0,14},{2,0},{4,2},{6,4},{8,6},{10,8},{12,10},{14,12},{1,15},{3,1}... | collective-permute-start | bytes 786440 | tf_op jit(solution)/shard_map/ppermute | solution.py:368
  39.3 10.3 %collective-permute-start.18 = (bf16[512,256]{1,0:T(8,128)(2,1)S(1)}, bf16[512,256]{1,0:T(8,128)(2,1)S(1)}, u32[]{:S(2)}, u32[]{:S(2)}) collective-permute-start(bf16[512,256]{1,0:T(8,128)(2,1)S(1)} %get-tuple-element.132.refs_0_), channel_id=1, source_target_pairs={{0,2},{2,4},{4,6},{6,8},{8,10},{10,12},{12,14},{14,0},{1,3},{3,5},... | collective-permute-start | bytes 786440 | tf_op jit(solution)/shard_map/ppermute | solution.py:366
  39.3 13.6 %collective-permute-start.1 = (bf16[512,256]{1,0:T(8,128)(2,1)S(1)}, bf16[512,256]{1,0:T(8,128)(2,1)S(1)}, u32[]{:S(2)}, u32[]{:S(2)}) collective-permute-start(bf16[512,256]{1,0:T(8,128)(2,1)S(1)} %get-tuple-element.131.refs_0_), channel_id=1, source_target_pairs={{0,14},{2,0},{4,2},{6,4},{8,6},{10,8},{12,10},{14,12},{1,15},{3,1}... | collective-permute-start | bytes 786440 | tf_op jit(solution)/shard_map/ppermute | solution.py:368
  42.6 12.7 %collective-permute-start = (bf16[512,256]{1,0:T(8,128)(2,1)S(1)}, bf16[512,256]{1,0:T(8,128)(2,1)S(1)}, u32[]{:S(2)}, u32[]{:S(2)}) collective-permute-start(bf16[512,256]{1,0:T(8,128)(2,1)S(1)} %get-tuple-element.131.refs_0_), channel_id=1, source_target_pairs={{0,2},{2,4},{4,6},{6,8},{8,10},{10,12},{12,14},{14,0},{1,3},{3,5},... | collective-permute-start | bytes 786440 | tf_op jit(solution)/shard_map/ppermute | solution.py:366
  49.7 11.2 %collective-permute-start.20 = (bf16[512,256]{1,0:T(8,128)(2,1)S(1)}, bf16[512,256]{1,0:T(8,128)(2,1)S(1)}, u32[]{:S(2)}, u32[]{:S(2)}) collective-permute-start(bf16[512,256]{1,0:T(8,128)(2,1)S(1)} %collective-permute-done.18.refs_1_), channel_id=1, source_target_pairs={{0,2},{2,4},{4,6},{6,8},{8,10},{10,12},{12,14},{14,0},{1,3},{3,5},... | collective-permute-start | bytes 786440 | tf_op jit(solution)/shard_map/ppermute | solution.py:366
  49.7 11.2 %collective-permute-start.21 = (bf16[512,256]{1,0:T(8,128)(2,1)S(1)}, bf16[512,256]{1,0:T(8,128)(2,1)S(1)}, u32[]{:S(2)}, u32[]{:S(2)}) collective-permute-start(bf16[512,256]{1,0:T(8,128)(2,1)S(1)} %collective-permute-done.19.refs_2_), channel_id=1, source_target_pairs={{0,14},{2,0},{4,2},{6,4},{8,6},{10,8},{12,10},{14,12},{1,15},{3,1}... | collective-permute-start | bytes 786440 | tf_op jit(solution)/shard_map/ppermute | solution.py:368
  55.3 11.2 %collective-permute-start.2 = (bf16[512,256]{1,0:T(8,128)(2,1)S(1)}, bf16[512,256]{1,0:T(8,128)(2,1)S(1)}, u32[]{:S(2)}, u32[]{:S(2)}) collective-permute-start(bf16[512,256]{1,0:T(8,128)(2,1)S(1)} %collective-permute-done.refs_1_), channel_id=1, source_target_pairs={{0,2},{2,4},{4,6},{6,8},{8,10},{10,12},{12,14},{14,0},{1,3},{3,5},... | collective-permute-start | bytes 786440 | tf_op jit(solution)/shard_map/ppermute | solution.py:366
  55.3 11.2 %collective-permute-start.3 = (bf16[512,256]{1,0:T(8,128)(2,1)S(1)}, bf16[512,256]{1,0:T(8,128)(2,1)S(1)}, u32[]{:S(2)}, u32[]{:S(2)}) collective-permute-start(bf16[512,256]{1,0:T(8,128)(2,1)S(1)} %collective-permute-done.1.refs_2_), channel_id=1, source_target_pairs={{0,14},{2,0},{4,2},{6,4},{8,6},{10,8},{12,10},{14,12},{1,15},{3,1}... | collective-permute-start | bytes 786440 | tf_op jit(solution)/shard_map/ppermute | solution.py:368
  60.9 11.2 %collective-permute-start.22 = (bf16[512,256]{1,0:T(8,128)(2,1)S(1)}, bf16[512,256]{1,0:T(8,128)(2,1)S(1)}, u32[]{:S(2)}, u32[]{:S(2)}) collective-permute-start(bf16[512,256]{1,0:T(8,128)(2,1)S(1)} %collective-permute-done.20.refs_0_), channel_id=1, source_target_pairs={{0,2},{2,4},{4,6},{6,8},{8,10},{10,12},{12,14},{14,0},{1,3},{3,5},... | collective-permute-start | bytes 786440 | tf_op jit(solution)/shard_map/ppermute | solution.py:366
  60.9 11.2 %collective-permute-start.23 = (bf16[512,256]{1,0:T(8,128)(2,1)S(1)}, bf16[512,256]{1,0:T(8,128)(2,1)}, u32[]{:S(2)}, u32[]{:S(2)}) collective-permute-start(bf16[512,256]{1,0:T(8,128)(2,1)S(1)} %collective-permute-done.21.refs_1_), channel_id=1, source_target_pairs={{0,14},{2,0},{4,2},{6,4},{8,6},{10,8},{12,10},{14,12},{1,15},{3,1}... | collective-permute-start | bytes 786440 | tf_op jit(solution)/shard_map/ppermute | solution.py:368
  66.5 10.6 %collective-permute-start.5 = (bf16[512,256]{1,0:T(8,128)(2,1)S(1)}, bf16[512,256]{1,0:T(8,128)(2,1)}, u32[]{:S(2)}, u32[]{:S(2)}) collective-permute-start(bf16[512,256]{1,0:T(8,128)(2,1)S(1)} %collective-permute-done.2.refs_0_), channel_id=1, source_target_pairs={{0,2},{2,4},{4,6},{6,8},{8,10},{10,12},{12,14},{14,0},{1,3},{3,5},... | collective-permute-start | bytes 786440 | tf_op jit(solution)/shard_map/ppermute | solution.py:366
  66.5 10.6 %collective-permute-start.6 = (bf16[512,256]{1,0:T(8,128)(2,1)S(1)}, bf16[512,256]{1,0:T(8,128)(2,1)S(1)}, u32[]{:S(2)}, u32[]{:S(2)}) collective-permute-start(bf16[512,256]{1,0:T(8,128)(2,1)S(1)} %collective-permute-done.3.refs_1_), channel_id=1, source_target_pairs={{0,14},{2,0},{4,2},{6,4},{8,6},{10,8},{12,10},{14,12},{1,15},{3,1}... | collective-permute-start | bytes 786440 | tf_op jit(solution)/shard_map/ppermute | solution.py:368
  72.1 5.8 %copy-start.9 = (s32[16,2]{0,1:T(2,128)S(1)}, s32[16,2]{0,1:T(2,128)}, u32[]{:S(2)}) copy-start(s32[16,2]{0,1:T(2,128)} %param.18) | copy-start | bytes 388
  72.2 5.7 %copy-start.1 = (bf16[512,256]{1,0:T(8,128)(2,1)}, bf16[512,256]{1,0:T(8,128)(2,1)S(1)}, u32[]{:S(2)}) copy-start(bf16[512,256]{1,0:T(8,128)(2,1)S(1)} %collective-permute-done.22.refs_0_) | copy-start | bytes 786436
  72.2 9.1 %collective-permute-start.24 = (bf16[512,256]{1,0:T(8,128)(2,1)}, bf16[512,256]{1,0:T(8,128)(2,1)}, u32[]{:S(2)}, u32[]{:S(2)}) collective-permute-start(bf16[512,256]{1,0:T(8,128)(2,1)} %collective-permute-done.23.refs_1_), channel_id=1, source_target_pairs={{0,14},{2,0},{4,2},{6,4},{8,6},{10,8},{12,10},{14,12},{1,15},{3,1}... | collective-permute-start | bytes 786440 | tf_op jit(solution)/shard_map/ppermute | solution.py:368
  72.2 28.1 %collective-permute-start.10 = (bf16[8,256,256]{2,1,0:T(8,128)(2,1)}, bf16[8,256,256]{2,1,0:T(8,128)(2,1)}, u32[]{:S(2)}, u32[]{:S(2)}) collective-permute-start(bf16[8,256,256]{2,1,0:T(8,128)(2,1)} %get-tuple-element.94), channel_id=1, source_target_pairs={{0,1},{1,0},{2,3},{3,2},{4,5},{5,4},{6,7},{7,6},{8,9},{9,8},{10,11... | collective-permute-start | bytes 3145736 | tf_op jit(solution)/shard_map/ppermute | solution.py:349
  77.2 0.7 copy-start.3
  77.9 9.0 %collective-permute-start.7 = (bf16[512,256]{1,0:T(8,128)(2,1)}, bf16[512,256]{1,0:T(8,128)(2,1)S(1)}, u32[]{:S(2)}, u32[]{:S(2)}) collective-permute-start(bf16[512,256]{1,0:T(8,128)(2,1)} %collective-permute-done.5.refs_0_), channel_id=1, source_target_pairs={{0,2},{2,4},{4,6},{6,8},{8,10},{10,12},{12,14},{14,0},{1,3},{3,5},... | collective-permute-start | bytes 786440 | tf_op jit(solution)/shard_map/ppermute | solution.py:366
  78.0 1.0 copy-start.2
  81.3 2.5 %copy-start.4 = (bf16[512,256]{1,0:T(8,128)(2,1)S(1)}, bf16[512,256]{1,0:T(8,128)(2,1)}, u32[]{:S(2)}) copy-start(bf16[512,256]{1,0:T(8,128)(2,1)} %copy-done.3) | copy-start | bytes 786436
  83.6 6.7 %collective-permute-start.25 = (f32[512,256]{1,0:T(8,128)}, f32[512,256]{1,0:T(8,128)}, u32[]{:S(2)}, u32[]{:S(2)}) collective-permute-start(f32[512,256]{1,0:T(8,128)} %get-tuple-element.120), channel_id=1, source_target_pairs={{0,1},{1,0},{2,3},{3,2},{4,5},{5,4},{6,7},{7,6},{8,9},{9,8},{10,11... | collective-permute-start | bytes 1572872 | tf_op jit(solution)/shard_map/ppermute | solution.py:376
  89.1 7.4 %collective-permute-start.8 = (f32[512,256]{1,0:T(8,128)}, f32[512,256]{1,0:T(8,128)S(1)}, u32[]{:S(2)}, u32[]{:S(2)}) collective-permute-start(f32[512,256]{1,0:T(8,128)} %get-tuple-element.92), channel_id=1, source_target_pairs={{0,1},{1,0},{2,3},{3,2},{4,5},{5,4},{6,7},{7,6},{8,9},{9,8},{10,11... | collective-permute-start | bytes 1572872 | tf_op jit(solution)/shard_map/ppermute | solution.py:376
  96.4 3.9 %collective-permute-start.26 = (bf16[512,256]{1,0:T(8,128)(2,1)S(1)}, bf16[512,256]{1,0:T(8,128)(2,1)S(1)}, u32[]{:S(2)}, u32[]{:S(2)}) collective-permute-start(bf16[512,256]{1,0:T(8,128)(2,1)S(1)} %attend.3.own_ref), channel_id=1, source_target_pairs={{0,1},{1,0},{2,3},{3,2},{4,5},{5,4},{6,7},{7,6},{8,9},{9,8},{10,11... | collective-permute-start | bytes 786440 | tf_op jit(solution)/shard_map/ppermute | solution.py:378
  96.5 3.8 %copy-start.6 = (bf16[8,256,256]{2,1,0:T(8,128)(2,1)S(1)}, bf16[8,256,256]{2,1,0:T(8,128)(2,1)}, u32[]{:S(2)}) copy-start(bf16[8,256,256]{2,1,0:T(8,128)(2,1)} %copy-done.5) | copy-start | bytes 3145732
  99.8 9.3 %collective-permute-start.9 = (bf16[512,256]{1,0:T(8,128)(2,1)S(1)}, bf16[512,256]{1,0:T(8,128)(2,1)S(1)}, u32[]{:S(2)}, u32[]{:S(2)}) collective-permute-start(bf16[512,256]{1,0:T(8,128)(2,1)S(1)} %attend.2.own_ref), channel_id=1, source_target_pairs={{0,1},{1,0},{2,3},{3,2},{4,5},{5,4},{6,7},{7,6},{8,9},{9,8},{10,11... | collective-permute-start | bytes 786440 | tf_op jit(solution)/shard_map/ppermute | solution.py:378
  102.8 12.9 %collective-permute-start.27 = (bf16[512,256]{1,0:T(8,128)(2,1)S(1)}, bf16[512,256]{1,0:T(8,128)(2,1)S(1)}, u32[]{:S(2)}, u32[]{:S(2)}) collective-permute-start(bf16[512,256]{1,0:T(8,128)(2,1)S(1)} %get-tuple-element.122), channel_id=1, source_target_pairs={{0,2},{2,4},{4,6},{6,8},{8,10},{10,12},{12,14},{14,0},{1,3},{3,5},... | collective-permute-start | bytes 786440 | tf_op jit(solution)/shard_map/ppermute | solution.py:281
  105.1 10.8 %collective-permute-start.30 = (bf16[512,256]{1,0:T(8,128)(2,1)S(1)}, bf16[512,256]{1,0:T(8,128)(2,1)S(1)}, u32[]{:S(2)}, u32[]{:S(2)}) collective-permute-start(bf16[512,256]{1,0:T(8,128)(2,1)S(1)} %get-tuple-element.125), channel_id=1, source_target_pairs={{0,14},{2,0},{4,2},{6,4},{8,6},{10,8},{12,10},{14,12},{1,15},{3,1}... | collective-permute-start | bytes 786440 | tf_op jit(solution)/shard_map/ppermute | solution.py:281
  111.6 10.5 %collective-permute-start.11 = (bf16[512,256]{1,0:T(8,128)(2,1)S(1)}, bf16[512,256]{1,0:T(8,128)(2,1)S(1)}, u32[]{:S(2)}, u32[]{:S(2)}) collective-permute-start(bf16[512,256]{1,0:T(8,128)(2,1)S(1)} %get-tuple-element.96), channel_id=1, source_target_pairs={{0,2},{2,4},{4,6},{6,8},{8,10},{10,12},{12,14},{14,0},{1,3},{3,5},... | collective-permute-start | bytes 786440 | tf_op jit(solution)/shard_map/ppermute | solution.py:281
  111.7 10.6 %collective-permute-start.15 = (bf16[512,256]{1,0:T(8,128)(2,1)S(1)}, bf16[512,256]{1,0:T(8,128)(2,1)S(1)}, u32[]{:S(2)}, u32[]{:S(2)}) collective-permute-start(bf16[512,256]{1,0:T(8,128)(2,1)S(1)} %get-tuple-element.100), channel_id=1, source_target_pairs={{0,14},{2,0},{4,2},{6,4},{8,6},{10,8},{12,10},{14,12},{1,15},{3,1}... | collective-permute-start | bytes 786440 | tf_op jit(solution)/shard_map/ppermute | solution.py:281
  115.8 15.3 %collective-permute-start.28 = (bf16[512,256]{1,0:T(8,128)(2,1)S(1)}, bf16[512,256]{1,0:T(8,128)(2,1)S(1)}, u32[]{:S(2)}, u32[]{:S(2)}) collective-permute-start(bf16[512,256]{1,0:T(8,128)(2,1)S(1)} %add_convert_fusion.5), channel_id=1, source_target_pairs={{0,2},{2,4},{4,6},{6,8},{8,10},{10,12},{12,14},{14,0},{1,3},{3,5},... | collective-permute-start | bytes 786440 | tf_op jit(solution)/shard_map/ppermute | solution.py:281
  115.9 11.3 %collective-permute-start.31 = (bf16[512,256]{1,0:T(8,128)(2,1)S(1)}, bf16[512,256]{1,0:T(8,128)(2,1)S(1)}, u32[]{:S(2)}, u32[]{:S(2)}) collective-permute-start(bf16[512,256]{1,0:T(8,128)(2,1)S(1)} %add_convert_fusion.3), channel_id=1, source_target_pairs={{0,14},{2,0},{4,2},{6,4},{8,6},{10,8},{12,10},{14,12},{1,15},{3,1}... | collective-permute-start | bytes 786440 | tf_op jit(solution)/shard_map/ppermute | solution.py:281
  122.1 10.2 %collective-permute-start.12 = (bf16[512,256]{1,0:T(8,128)(2,1)S(1)}, bf16[512,256]{1,0:T(8,128)(2,1)S(1)}, u32[]{:S(2)}, u32[]{:S(2)}) collective-permute-start(bf16[512,256]{1,0:T(8,128)(2,1)S(1)} %add_convert_fusion.11), channel_id=1, source_target_pairs={{0,2},{2,4},{4,6},{6,8},{8,10},{10,12},{12,14},{14,0},{1,3},{3,5},... | collective-permute-start | bytes 786440 | tf_op jit(solution)/shard_map/ppermute | solution.py:281
  122.3 18.9 %collective-permute-start.16 = (bf16[512,256]{1,0:T(8,128)(2,1)S(1)}, bf16[512,256]{1,0:T(8,128)(2,1)S(1)}, u32[]{:S(2)}, u32[]{:S(2)}) collective-permute-start(bf16[512,256]{1,0:T(8,128)(2,1)S(1)} %add_convert_fusion.8), channel_id=1, source_target_pairs={{0,14},{2,0},{4,2},{6,4},{8,6},{10,8},{12,10},{14,12},{1,15},{3,1}... | collective-permute-start | bytes 786440 | tf_op jit(solution)/shard_map/ppermute | solution.py:281
  127.3 10.0 %collective-permute-start.32 = (bf16[512,256]{1,0:T(8,128)(2,1)S(1)}, bf16[512,256]{1,0:T(8,128)(2,1)S(1)}, u32[]{:S(2)}, u32[]{:S(2)}) collective-permute-start(bf16[512,256]{1,0:T(8,128)(2,1)S(1)} %add_convert_fusion.2), channel_id=1, source_target_pairs={{0,14},{2,0},{4,2},{6,4},{8,6},{10,8},{12,10},{14,12},{1,15},{3,1}... | collective-permute-start | bytes 786440 | tf_op jit(solution)/shard_map/ppermute | solution.py:281
  131.2 12.9 %collective-permute-start.29 = (bf16[512,256]{1,0:T(8,128)(2,1)S(1)}, bf16[512,256]{1,0:T(8,128)(2,1)S(1)}, u32[]{:S(2)}, u32[]{:S(2)}) collective-permute-start(bf16[512,256]{1,0:T(8,128)(2,1)S(1)} %add_convert_fusion.4), channel_id=1, source_target_pairs={{0,2},{2,4},{4,6},{6,8},{8,10},{10,12},{12,14},{14,0},{1,3},{3,5},... | collective-permute-start | bytes 786440 | tf_op jit(solution)/shard_map/ppermute | solution.py:281
  132.4 11.5 %collective-permute-start.13 = (bf16[512,256]{1,0:T(8,128)(2,1)S(1)}, bf16[512,256]{1,0:T(8,128)(2,1)S(1)}, u32[]{:S(2)}, u32[]{:S(2)}) collective-permute-start(bf16[512,256]{1,0:T(8,128)(2,1)S(1)} %add_convert_fusion.10), channel_id=1, source_target_pairs={{0,2},{2,4},{4,6},{6,8},{8,10},{10,12},{12,14},{14,0},{1,3},{3,5},... | collective-permute-start | bytes 786440 | tf_op jit(solution)/shard_map/ppermute | solution.py:281
  137.4 10.5 %collective-permute-start.33 = (bf16[512,256]{1,0:T(8,128)(2,1)S(1)}, bf16[512,256]{1,0:T(8,128)(2,1)S(1)}, u32[]{:S(2)}, u32[]{:S(2)}) collective-permute-start(bf16[512,256]{1,0:T(8,128)(2,1)S(1)} %add_convert_fusion.1), channel_id=1, source_target_pairs={{0,14},{2,0},{4,2},{6,4},{8,6},{10,8},{12,10},{14,12},{1,15},{3,1}... | collective-permute-start | bytes 786440 | tf_op jit(solution)/shard_map/ppermute | solution.py:281
  141.2 10.2 %collective-permute-start.17 = (bf16[512,256]{1,0:T(8,128)(2,1)S(1)}, bf16[512,256]{1,0:T(8,128)(2,1)S(1)}, u32[]{:S(2)}, u32[]{:S(2)}) collective-permute-start(bf16[512,256]{1,0:T(8,128)(2,1)S(1)} %add_convert_fusion.7), channel_id=1, source_target_pairs={{0,14},{2,0},{4,2},{6,4},{8,6},{10,8},{12,10},{14,12},{1,15},{3,1}... | collective-permute-start | bytes 786440 | tf_op jit(solution)/shard_map/ppermute | solution.py:281
  143.9 7.7 %collective-permute-start.14 = (bf16[512,256]{1,0:T(8,128)(2,1)S(1)}, bf16[512,256]{1,0:T(8,128)(2,1)S(1)}, u32[]{:S(2)}, u32[]{:S(2)}) collective-permute-start(bf16[512,256]{1,0:T(8,128)(2,1)S(1)} %add_convert_fusion.9), channel_id=1, source_target_pairs={{0,2},{2,4},{4,6},{6,8},{8,10},{10,12},{12,14},{14,0},{1,3},{3,5},... | collective-permute-start | bytes 786440 | tf_op jit(solution)/shard_map/ppermute | solution.py:281

commit v6 on v3

--- a/solution.py
+++ b/solution.py
@@ -69,17 +69,16 @@
 
 
 def select_kernel(place_ref, heard_ref, rows_ref, out_ref, sems):
-    shards, requests = out_ref.shape[0], out_ref.shape[0] * NBRS
-    here = place_ref[0]
+    shards, spans, blocks = out_ref.shape[0], heard_ref.shape[2], rows_ref.shape[0]
+    lowest = place_ref[0] * blocks
     copies = []
     for e in range(shards):
-        first, last = jnp.int32(-1), jnp.int32(0)
-        for r in range(requests):
-            mine = heard_ref[e, r] == here
-            block = heard_ref[e, requests + r]
-            first = jnp.where(mine & (first < 0), block, first)
-            last = jnp.where(mine, block, last)
-        for s, block in enumerate((jnp.maximum(first, 0), last)):
+        named = [heard_ref[e, n, c] - lowest for n in range(NBRS) for c in range(spans)]
+        first, last = jnp.int32(0), jnp.int32(0)
+        for up, down in zip(named, reversed(named)):
+            last = jnp.where((up >= 0) & (up < blocks), up, last)
+            first = jnp.where((down >= 0) & (down < blocks), down, first)
+        for s, block in enumerate((first, last)):
             copy = pltpu.make_async_copy(rows_ref.at[block], out_ref.at[e, s], sems.at[e, s])
             copy.start()
             copies.append(copy)
@@ -119,7 +118,7 @@
             pl.BlockSpec((depth, width), lambda i: (0, 0)),
         ],
         out_specs=pl.BlockSpec((tile, width), lambda i: (i, 0)),
-        compiler_params=pltpu.CompilerParams(vmem_limit_bytes=24 << 20),
+        compiler_params=pltpu.CompilerParams(vmem_limit_bytes=48 << 20),
         cost_estimate=pl.CostEstimate(
             flops=2 * rows * depth * width, bytes_accessed=11 << 20, transcendentals=0
         ),
@@ -185,7 +184,7 @@
             pltpu.VMEM((requests * NBR_LEN, rows.shape[2]), BF16),
             pltpu.SemaphoreType.DMA((requests,)),
         ],
-        compiler_params=pltpu.CompilerParams(vmem_limit_bytes=24 << 20),
+        compiler_params=pltpu.CompilerParams(vmem_limit_bytes=12 << 20),
         cost_estimate=pl.CostEstimate(
             flops=4 * tokens * NBRS * NBR_LEN * width, bytes_accessed=3 << 20, transcendentals=0
         ),
@@ -193,59 +192,56 @@
     )(slot_index, lengths, queries, rows)
 
 
-def relay_kernel(place_ref, weight_ref, own_ref, lent_ref):
+def relay_kernel(place_ref, weight_ref, lent_ref):
     here, core = place_ref[0], place_ref[1]
-    ring, _, width = own_ref.shape
+    ring, _, width = lent_ref.shape
     for k in range(ring):
         chip = lax.rem(here + k, ring)
-        for ref, which in ((own_ref, core), (lent_ref, 1 - core)):
-            cols = pl.ds(pl.multiple_of((chip * 2 + which) * width, width), width)
-            ref[k] = weight_ref[:, cols]
+        cols = pl.ds(pl.multiple_of((chip * 2 + 1 - core) * width, width), width)
+        lent_ref[k] = weight_ref[:, cols]
 
 
 def relay(place, weight, ring):
     depth = weight.shape[0]
-    shape = jax.ShapeDtypeStruct((ring, depth, weight.shape[1] // (2 * ring)), BF16)
     return pl.pallas_call(
         relay_kernel,
-        out_shape=(shape, shape),
+        out_shape=jax.ShapeDtypeStruct((ring, depth, weight.shape[1] // (2 * ring)), BF16),
         in_specs=[SMEM, VMEM],
-        out_specs=(VMEM, VMEM),
-        compiler_params=pltpu.CompilerParams(vmem_limit_bytes=16 << 20),
-        cost_estimate=pl.CostEstimate(flops=0, bytes_accessed=4 << 20, transcendentals=0),
+        out_specs=VMEM,
+        compiler_params=pltpu.CompilerParams(vmem_limit_bytes=8 << 20),
+        cost_estimate=pl.CostEstimate(flops=0, bytes_accessed=3 << 20, transcendentals=0),
         name="relay",
     )(place, weight)
 
 
-def share_kernel(steps, own_ref, partner_ref, own_w_ref, partner_w_ref, *out_refs):
+def share_kernel(steps, place_ref, own_ref, partner_ref, weight_ref, partner_w_ref, *out_refs):
+    here, core = place_ref[0], place_ref[1]
+    ring, _, width = partner_w_ref.shape
     for step, ref in zip(steps, out_refs):
+        chip = lax.rem(here + step, ring)
+        cols = pl.ds(pl.multiple_of((chip * 2 + core) * width, width), width)
         ref[...] = (
-            jnp.dot(own_ref[...], own_w_ref[step], preferred_element_type=F32)
+            jnp.dot(own_ref[...], weight_ref[:, cols], preferred_element_type=F32)
             + jnp.dot(partner_ref[...], partner_w_ref[step], preferred_element_type=F32)
         ).astype(ref.dtype)
 
 
-def shares(starts, rest, own, partner, own_weight, partner_weight):
+def shares(place, steps, dtype, own, partner, weight, partner_weight):
     rows, width = own.shape
-    steps = starts + rest
-    outs = [
-        jax.ShapeDtypeStruct((rows, width), BF16 if i < len(starts) else F32)
-        for i in range(len(steps))
-    ]
     return pl.pallas_call(
         functools.partial(share_kernel, steps),
-        out_shape=outs,
-        in_specs=[VMEM] * 4,
-        out_specs=[VMEM] * len(outs),
-        compiler_params=pltpu.CompilerParams(vmem_limit_bytes=24 << 20),
+        out_shape=[jax.ShapeDtypeStruct((rows, width), dtype)] * len(steps),
+        in_specs=[SMEM] + [VMEM] * 4,
+        out_specs=[VMEM] * len(steps),
+        compiler_params=pltpu.CompilerParams(vmem_limit_bytes=12 << 20),
         cost_estimate=pl.CostEstimate(
-            flops=4 * rows * width * width * len(steps), bytes_accessed=6 << 20, transcendentals=0
+            flops=4 * rows * width * width * len(steps), bytes_accessed=4 << 20, transcendentals=0
         ),
         name="shares",
-    )(own, partner, own_weight, partner_weight)
-
-
-def reduce_ring(attended, partner_attended, own_weight, partner_weight, ring):
+    )(place, own, partner, weight, partner_weight)
+
+
+def reduce_ring(place, attended, partner_attended, weight, partner_weight, ring):
     up = [(i, (i + 1) % ring) for i in range(ring)]
     down = [(i, (i - 1) % ring) for i in range(ring)]
     far = ring // 2
@@ -255,12 +251,11 @@
         mine = [(way, first) for rows, way, first in chains if rows == half]
         starts = [way * first % ring for way, first in mine]
         rest = [k for k in range(ring) if k not in starts]
-        made = shares(
-            starts, rest, attended[half], partner_attended[half], own_weight, partner_weight
-        )
-        for i, (way, _) in enumerate(mine):
-            held[half, way] = made[i]
-        part.update({(half, k): made[len(starts) + i] for i, k in enumerate(rest)})
+        operands = (attended[half], partner_attended[half], weight, partner_weight)
+        begun = shares(place, starts, BF16, *operands)
+        held.update({(half, way): begun[i] for i, (way, _) in enumerate(mine)})
+        others = shares(place, rest, F32, *operands)
+        part.update({(half, k): others[i] for i, k in enumerate(rest)})
     for distance in range(far, 0, -1):
         for half, way, first in chains:
             if distance > first:
@@ -295,38 +290,40 @@
     here, core = lax.axis_index("z"), lax.axis_index("c")
     swap = [(i, (i + 1) % cores) for i in range(cores)]
 
-    gathered = lax.all_gather(tokens, ("z", "c"), axis=1, tiled=True)
-
-    owners = nbr_owner.T.reshape(-1)
-    wanted_blocks = nbr_block.T.reshape(-1)
-    notes = jnp.concatenate([owners, wanted_blocks, block_len])
-    notes = jnp.broadcast_to(notes[None, :], (shards, notes.shape[0]))
+    place = jnp.stack([here, core]).astype(jnp.int32)
+    spans, blocks = nbr_owner.shape[0], block_len.shape[0]
+
+    block_ids = nbr_owner.T * blocks + nbr_block.T
+    notes = jnp.concatenate([block_ids, jnp.pad(block_len, (0, spans - blocks))[None, :]], axis=0)
+    notes = jnp.broadcast_to(notes[None], (shards,) + notes.shape)
+    notes, tokens = lax.optimization_barrier((notes, tokens))
     heard = lax.all_to_all(notes, DB, split_axis=0, concat_axis=0, tiled=True)
     projected = project_blocks(codes, scales, key_weight, value_weight)
+
+    gathered = lax.all_gather(tokens, ("z", "c"), axis=1, tiled=True)
     sent = select_blocks(lax.axis_index(DB).astype(jnp.int32).reshape(1), heard, projected)
     rows = lax.all_to_all(sent, DB, split_axis=0, concat_axis=0, tiled=True)
     rows = rows.reshape(shards * NBRS, NBR_LEN, 2 * width)
 
+    owners = nbr_owner.T.reshape(-1)
+    block_ids = block_ids.reshape(-1)
     order = jnp.arange(owners.shape[0], dtype=jnp.int32)
     earlier = jnp.sum(
         ((owners[:, None] == owners[None, :]) & (order[:, None] > order[None, :])).astype(jnp.int32),
         axis=1,
     )
     slot_index = owners * NBRS + earlier
-    all_lengths = heard[:, 2 * owners.shape[0] :].reshape(-1)
-    block_ids = owners * block_len.shape[0] + wanted_blocks
+    all_lengths = heard[:, NBRS, :blocks].reshape(-1)
     ids = jnp.arange(all_lengths.shape[0], dtype=jnp.int32)
     lengths = jnp.sum(
         jnp.where(block_ids[:, None] == ids[None, :], all_lengths[None, :], 0), axis=1
     )
 
-    own_weight, lent_weight = relay(jnp.stack([here, core]).astype(jnp.int32), out_weight, ring)
-    partner_weight = lax.ppermute(lent_weight, "c", swap)
-
+    partner_weight = lax.ppermute(relay(place, out_weight, ring), "c", swap)
     queries = project_queries(gathered, query_weight)
     attended = [attend(part, 2, slot_index, lengths, queries, rows) for part in range(2)]
     partner_attended = [lax.ppermute(part, "c", swap) for part in attended]
-    return reduce_ring(attended, partner_attended, own_weight, partner_weight, ring)
+    return reduce_ring(place, attended, partner_attended, out_weight, partner_weight, ring)
 
 
 def solution(mesh):

time: 162 us -> 162 us (level)
  Pallas kernels: 23.4 us -> 29.5 us
  waiting for transfers between devices: 74.7 us -> 70.2 us
    pallas_call x1, Pallas kernels: 4.3 us -> 7.84 us  [project_queries(): pl.pallas_call(query_kernel, grid=(rows // tile,), out_shape=jax.ShapeDty...]
    pallas_call x3 -> x5, Pallas kernels: 4.34 us -> 6.7 us  [the longest x4 5.02 us: shares(): pl.pallas_call(functools.partial(share_kernel, steps), out_shape=[jax.Sha...]
    ppermute x14, waiting for transfers between devices: 24.6 us -> 22.3 us  [reduce_ring(): lax.ppermute(held[half, way], 'z', up if way == 1 else down)]
    all_to_all x1, waiting for transfers between devices: 8.79 us -> 6.65 us  [local(): rows = lax.all_to_all(sent, DB, split_axis=0, concat_axis=0, tiled=True)]
    unnamed x10 -> x12, local copies, waits for them, and re-layouts: 5.58 us -> 4.05 us
  transfers between devices with their start and end apart: 20 -> 20, of which waited for: 12 -> 11; matrix products, arithmetic and copies ran while one was open for 3% -> 1% of each run, Pallas kernels for 14% -> 18%
where the time goes in v6:
time: 162 us; the launch traced here: 161 us
  waiting for transfers between devices  70.2 us (43%)
  starting transfers between devices  39 us (24%)
  Pallas kernels  29.5 us (18%)
  between operations  13.6 us (8%)
  local copies, waits for them, and re-layouts  6.36 us (4%)
  other arithmetic  2.75 us (2%)
    all_gather x1, waiting for transfers between devices, local(): gathered = lax.all_gather(tokens, ('z', 'c'), axis=1, tiled=True)  40.4 us
    ppermute x14, starting transfers between devices, reduce_ring(): lax.ppermute(held[half, way], 'z', up if way == 1 else down)  24.5 us
    ppermute x14, waiting for transfers between devices, reduce_ring(): lax.ppermute(held[half, way], 'z', up if way == 1 else down)  22.3 us
    pallas_call x1, Pallas kernels, project_queries(): pl.pallas_call(query_kernel, grid=(rows // tile,), out_shape=jax.ShapeDty...  7.84 us
    all_to_all x1, starting transfers between devices, local(): heard = lax.all_to_all(notes, DB, split_axis=0, concat_axis=0, tiled=True)  7.18 us
    all_to_all x1, waiting for transfers between devices, local(): rows = lax.all_to_all(sent, DB, split_axis=0, concat_axis=0, tiled=True)  6.65 us
    all_to_all x1, starting transfers between devices, local(): rows = lax.all_to_all(sent, DB, split_axis=0, concat_axis=0, tiled=True)  6.62 us
    pallas_call x2, Pallas kernels, attend(): pl.pallas_call(functools.partial(attend_kernel, part * count), grid=(1,),...  6.14 us
  transfers between devices with their start and end apart: 20, of which 11 were waited for; matrix products, arithmetic and copies ran while one was open for 1% of the time, Pallas kernels for 18%

profile of v6, /device:TPU:24, one launch (start us, length us, event | category | flops | bytes accessed | tf_op | source)
XLA Modules:
  0.0 161.4 jit_solution(10661407356796263103)
XLA Ops:
  6.5 0.7 pad_bitcast_fusion
  7.2 0.7 bitcast_add_fusion
  7.9 0.6 broadcast_in_dim.27
  8.6 7.2 %all-to-all-start = ((s32[16,3,16]{2,1,0:T(4,128)}), s32[16,3,16]{2,1,0:T(4,128)S(1)}, u32[]{:S(2)}, u32[]{:S(2)}) async-start(s32[16,3,16]{2,1,0:T(4,128)} %broadcast_in_dim.27), calls=%async_computation | async-start | bytes 65536 | tf_op jit(solution)/shard_map/all_to_all | solution.py:300
  15.7 4.9 %project_blocks.1.rows_ref = bf16[8,128,512]{2,1,0:T(8,128)(2,1)} custom-call(f32[8,7]{1,0:T(8,128)} %scales_ref.1, bf16[8,128,896]{2,1,0:T(8,128)(2,1)} %codes_ref.1, bf16[896,256]{1,0:T(8,128)(2,1)} %key_ref.1, bf16[896,256]{1,0:T(8,128)(2,1)} %value_ref.1), custom_call_target="tpu_custom_call" | custom-call | flops 939524096 | bytes 5242880 | tf_op jit(solution)/shard_map/project_blocks/pallas_call | solution.py:52
  20.6 0.7 all-to-all-done.heard_ref
  21.4 0.6 copy-done.4
  22.0 3.9 %select_blocks.1 = bf16[16,2,128,512]{3,2,1,0:T(8,128)(2,1)} custom-call(s32[1]{0:T(128)} %bitcast.5.place_ref, s32[16,3,16]{2,1,0:T(4,128)} %copy-done.4, bf16[8,128,512]{2,1,0:T(8,128)(2,1)} %project_blocks.1.rows_ref), custom_call_target="tpu_custom_call" | custom-call | bytes 9437184 | tf_op jit(solution)/shard_map/select_blocks/pallas_call | solution.py:91
  25.9 6.6 %all-to-all-start.1 = ((bf16[16,2,128,512]{3,2,1,0:T(8,128)(2,1)}), bf16[16,2,128,512]{3,2,1,0:T(8,128)(2,1)}, u32[]{:S(2)}, u32[]{:S(2)}) async-start(bf16[16,2,128,512]{3,2,1,0:T(8,128)(2,1)} %select_blocks.1), calls=%async_computation.1 | async-start | bytes 8388608 | tf_op jit(solution)/shard_map/all_to_all | solution.py:305
  32.6 1.7 %relay.1 = bf16[8,256,256]{2,1,0:T(8,128)(2,1)} custom-call(s32[2]{0:T(128)S(1)} %pad_add_fusion.1.place_ref, bf16[256,4096]{1,0:T(8,128)(2,1)S(1)} %copy-done), custom_call_target="tpu_custom_call" | custom-call | bytes 3145728 | tf_op jit(solution)/shard_map/relay/pallas_call | solution.py:206
  34.5 0.2 convert_reduce_fusion
  34.7 0.8 slice_reduce_fusion
  35.5 0.1 broadcast_in_dim.28
  35.6 0.2 select_reduce_fusion.length_ref
  35.8 40.4 %all-gather.2.cloned.1.call-done.tokens_ref = bf16[1024,4096]{1,0:T(8,128)(2,1)} async-done(((bf16[1024,256]{1,0:T(8,128)(2,1)}), bf16[1024,4096]{1,0:T(8,128)(2,1)}) %all-gather.2.cloned.1.call-update) | async-done | bytes 8388624 | tf_op jit(solution)/shard_map/all_gather | solution.py:303
  76.2 1.6 copy-done.3
  77.8 7.8 %project_queries.1.query_ref = bf16[1024,256]{1,0:T(8,128)(2,1)S(1)} custom-call(bf16[1024,4096]{1,0:T(8,128)(2,1)} %all-gather.2.cloned.1.call-done.tokens_ref, bf16[4096,256]{1,0:T(8,128)(2,1)S(1)} %copy-done.3), custom_call_target="tpu_custom_call" | custom-call | flops 2147483648 | bytes 11534336 | tf_op jit(solution)/shard_map/project_queries/pallas_call | solution.py:112
  85.6 0.8 copy-done.1
  86.4 6.7 %all-to-all-done.1 = bf16[16,2,128,512]{3,2,1,0:T(8,128)(2,1)} async-done(((bf16[16,2,128,512]{3,2,1,0:T(8,128)(2,1)}), bf16[16,2,128,512]{3,2,1,0:T(8,128)(2,1)}, u32[]{:S(2)}, u32[]{:S(2)}) %all-to-all-start.1) | async-done | bytes 4194336 | tf_op jit(solution)/shard_map/all_to_all | solution.py:305
  93.1 1.0 copy-done.2
  94.1 3.1 %attend.3.own_ref = bf16[512,256]{1,0:T(8,128)(2,1)S(1)} custom-call(s32[32]{0:T(128)S(1)} %multiply_add_fusion.slot_ref, s32[32]{0:T(128)S(1)} %select_reduce_fusion.length_ref, bf16[1024,256]{1,0:T(8,128)(2,1)S(1)} %copy-done.2, bf16[32,128,512]{2,1,0:T(8,128)(2,1)} %bitcast.6.rows_ref), custom_call_target="tpu_custom_call" | custom-call | flops 134217728 | bytes 3145728 | tf_op jit(solution)/shard_map/attend/pallas_call | solution.py:177
  97.2 0.1 collective-permute-start.9
  97.3 3.1 %attend.2.own_ref = bf16[512,256]{1,0:T(8,128)(2,1)S(1)} custom-call(s32[32]{0:T(128)S(1)} %multiply_add_fusion.slot_ref, s32[32]{0:T(128)S(1)} %select_reduce_fusion.length_ref, bf16[1024,256]{1,0:T(8,128)(2,1)S(1)} %copy-done.2, bf16[32,128,512]{2,1,0:T(8,128)(2,1)} %bitcast.6.rows_ref), custom_call_target="tpu_custom_call" | custom-call | flops 134217728 | bytes 3145728 | tf_op jit(solution)/shard_map/attend/pallas_call | solution.py:177
  100.4 0.6 collective-permute-start
  100.9 1.0 shares.7
  101.9 6.0 %collective-permute-start.13 = (bf16[512,256]{1,0:T(8,128)(2,1)S(1)}, bf16[512,256]{1,0:T(8,128)(2,1)S(1)}, u32[]{:S(2)}, u32[]{:S(2)}) collective-permute-start(bf16[512,256]{1,0:T(8,128)(2,1)S(1)} %get-tuple-element.37), channel_id=1, source_target_pairs={{0,14},{2,0},{4,2},{6,4},{8,6},{10,8},{12,10},{14,12},{1,15},{3,1}... | collective-permute-start | bytes 786440 | tf_op jit(solution)/shard_map/ppermute | solution.py:266
  107.9 1.0 shares.5
  108.9 3.3 %collective-permute-start.6 = (bf16[512,256]{1,0:T(8,128)(2,1)S(1)}, bf16[512,256]{1,0:T(8,128)(2,1)S(1)}, u32[]{:S(2)}, u32[]{:S(2)}) collective-permute-start(bf16[512,256]{1,0:T(8,128)(2,1)S(1)} %get-tuple-element.30), channel_id=1, source_target_pairs={{0,14},{2,0},{4,2},{6,4},{8,6},{10,8},{12,10},{14,12},{1,15},{3,1}... | collective-permute-start | bytes 786440 | tf_op jit(solution)/shard_map/ppermute | solution.py:266
  112.2 1.5 shares.6
  113.7 1.5 shares.4
  115.3 3.3 %collective-permute-start.14 = (bf16[512,256]{1,0:T(8,128)(2,1)S(1)}, bf16[512,256]{1,0:T(8,128)(2,1)S(1)}, u32[]{:S(2)}, u32[]{:S(2)}) collective-permute-start(bf16[512,256]{1,0:T(8,128)(2,1)S(1)} %add_convert_fusion.3), channel_id=1, source_target_pairs={{0,14},{2,0},{4,2},{6,4},{8,6},{10,8},{12,10},{14,12},{1,15},{3,1}... | collective-permute-start | bytes 786440 | tf_op jit(solution)/shard_map/ppermute | solution.py:266
  118.7 0.1 collective-permute-start.11
  118.8 1.4 collective-permute-done.6
  120.3 3.8 %collective-permute-start.7 = (bf16[512,256]{1,0:T(8,128)(2,1)S(1)}, bf16[512,256]{1,0:T(8,128)(2,1)S(1)}, u32[]{:S(2)}, u32[]{:S(2)}) collective-permute-start(bf16[512,256]{1,0:T(8,128)(2,1)S(1)} %add_convert_fusion.8), channel_id=1, source_target_pairs={{0,14},{2,0},{4,2},{6,4},{8,6},{10,8},{12,10},{14,12},{1,15},{3,1}... | collective-permute-start | bytes 786440 | tf_op jit(solution)/shard_map/ppermute | solution.py:266
  124.1 0.1 collective-permute-start.3
  124.2 1.6 %collective-permute-done.14 = bf16[512,256]{1,0:T(8,128)(2,1)S(1)} collective-permute-done((bf16[512,256]{1,0:T(8,128)(2,1)S(1)}, bf16[512,256]{1,0:T(8,128)(2,1)S(1)}, u32[]{:S(2)}, u32[]{:S(2)}) %collective-permute-start.14) | collective-permute-done | bytes 262176 | tf_op jit(solution)/shard_map/ppermute | solution.py:266
  125.9 3.8 %collective-permute-start.15 = (bf16[512,256]{1,0:T(8,128)(2,1)S(1)}, bf16[512,256]{1,0:T(8,128)(2,1)S(1)}, u32[]{:S(2)}, u32[]{:S(2)}) collective-permute-start(bf16[512,256]{1,0:T(8,128)(2,1)S(1)} %add_convert_fusion.2), channel_id=1, source_target_pairs={{0,14},{2,0},{4,2},{6,4},{8,6},{10,8},{12,10},{14,12},{1,15},{3,1}... | collective-permute-start | bytes 786440 | tf_op jit(solution)/shard_map/ppermute | solution.py:266
  129.8 5.4 %collective-permute-done.3 = bf16[512,256]{1,0:T(8,128)(2,1)S(1)} collective-permute-done((bf16[512,256]{1,0:T(8,128)(2,1)S(1)}, bf16[512,256]{1,0:T(8,128)(2,1)S(1)}, u32[]{:S(2)}, u32[]{:S(2)}) %collective-permute-start.3) | collective-permute-done | bytes 262176 | tf_op jit(solution)/shard_map/ppermute | solution.py:266
  135.3 0.8 collective-permute-done.15
  136.2 3.8 %collective-permute-start.16 = (bf16[512,256]{1,0:T(8,128)(2,1)S(1)}, bf16[512,256]{1,0:T(8,128)(2,1)S(1)}, u32[]{:S(2)}, u32[]{:S(2)}) collective-permute-start(bf16[512,256]{1,0:T(8,128)(2,1)S(1)} %add_convert_fusion.1), channel_id=1, source_target_pairs={{0,14},{2,0},{4,2},{6,4},{8,6},{10,8},{12,10},{14,12},{1,15},{3,1}... | collective-permute-start | bytes 786440 | tf_op jit(solution)/shard_map/ppermute | solution.py:266
  140.0 0.2 collective-permute-start.8
  140.2 5.0 %collective-permute-done.4 = bf16[512,256]{1,0:T(8,128)(2,1)S(1)} collective-permute-done((bf16[512,256]{1,0:T(8,128)(2,1)S(1)}, bf16[512,256]{1,0:T(8,128)(2,1)S(1)}, u32[]{:S(2)}, u32[]{:S(2)}) %collective-permute-start.4) | collective-permute-done | bytes 262176 | tf_op jit(solution)/shard_map/ppermute | solution.py:266
  145.3 1.4 collective-permute-done.16
  146.7 0.1 add_convert_fusion
  146.8 3.7 %collective-permute-done.8 = bf16[512,256]{1,0:T(8,128)(2,1)S(1)} collective-permute-done((bf16[512,256]{1,0:T(8,128)(2,1)S(1)}, bf16[512,256]{1,0:T(8,128)(2,1)S(1)}, u32[]{:S(2)}, u32[]{:S(2)}) %collective-permute-start.8) | collective-permute-done | bytes 262176 | tf_op jit(solution)/shard_map/ppermute | solution.py:266
  150.5 3.1 %collective-permute-done.5 = bf16[512,256]{1,0:T(8,128)(2,1)S(1)} collective-permute-done((bf16[512,256]{1,0:T(8,128)(2,1)S(1)}, bf16[512,256]{1,0:T(8,128)(2,1)S(1)}, u32[]{:S(2)}, u32[]{:S(2)}) %collective-permute-start.5) | collective-permute-done | bytes 262176 | tf_op jit(solution)/shard_map/ppermute | solution.py:266
  153.6 0.1 add_convert_fusion.6
  153.7 0.8 pad_maximum_fusion
  (40 shorter events, 1.2 us)
Async XLA Ops:
  6.5 69.6 %all-gather.2.cloned.1.call-start = ((), (), s32[]{:S(2)}) async-start(), calls=%async_computation.2 | async-start | bytes 8912896 | tf_op jit(solution)/shard_map/all_gather | solution.py:303
  8.6 12.8 %all-to-all-start = ((s32[16,3,16]{2,1,0:T(4,128)}), s32[16,3,16]{2,1,0:T(4,128)S(1)}, u32[]{:S(2)}, u32[]{:S(2)}) async-start(s32[16,3,16]{2,1,0:T(4,128)} %broadcast_in_dim.27), calls=%async_computation | async-start | bytes 65536 | tf_op jit(solution)/shard_map/all_to_all | solution.py:300
  21.4 0.6 copy-start.4
  25.9 6.7 %copy-start = (bf16[256,4096]{1,0:T(8,128)(2,1)S(1)}, bf16[256,4096]{1,0:T(8,128)(2,1)}, u32[]{:S(2)}) copy-start(bf16[256,4096]{1,0:T(8,128)(2,1)} %weight_ref.11) | copy-start | bytes 6291460
  25.9 8.5 %copy-start.5 = (s32[16,2]{0,1:T(2,128)S(1)}, s32[16,2]{0,1:T(2,128)}, u32[]{:S(2)}) copy-start(s32[16,2]{0,1:T(2,128)} %param.18) | copy-start | bytes 388
  25.9 67.1 %all-to-all-start.1 = ((bf16[16,2,128,512]{3,2,1,0:T(8,128)(2,1)}), bf16[16,2,128,512]{3,2,1,0:T(8,128)(2,1)}, u32[]{:S(2)}, u32[]{:S(2)}) async-start(bf16[16,2,128,512]{3,2,1,0:T(8,128)(2,1)} %select_blocks.1), calls=%async_computation.1 | async-start | bytes 8388608 | tf_op jit(solution)/shard_map/all_to_all | solution.py:305
  34.3 66.6 %collective-permute-start.1 = (bf16[8,256,256]{2,1,0:T(8,128)(2,1)}, bf16[8,256,256]{2,1,0:T(8,128)(2,1)S(1)}, u32[]{:S(2)}, u32[]{:S(2)}) collective-permute-start(bf16[8,256,256]{2,1,0:T(8,128)(2,1)} %relay.1), channel_id=1, source_target_pairs={{0,1},{1,0},{2,3},{3,2},{4,5},{5,4},{6,7},{7,6},{8,9},{9,8},{10,11... | collective-permute-start | bytes 3145736 | tf_op jit(solution)/shard_map/ppermute | solution.py:322
  76.2 1.6 copy-start.3
  85.6 0.8 copy-start.1
  93.1 1.0 copy-start.2
  97.2 3.8 %collective-permute-start.9 = (bf16[512,256]{1,0:T(8,128)(2,1)S(1)}, bf16[512,256]{1,0:T(8,128)(2,1)S(1)}, u32[]{:S(2)}, u32[]{:S(2)}) collective-permute-start(bf16[512,256]{1,0:T(8,128)(2,1)S(1)} %attend.3.own_ref), channel_id=1, source_target_pairs={{0,1},{1,0},{2,3},{3,2},{4,5},{5,4},{6,7},{7,6},{8,9},{9,8},{10,11... | collective-permute-start | bytes 786440 | tf_op jit(solution)/shard_map/ppermute | solution.py:325
  100.4 7.5 %collective-permute-start = (bf16[512,256]{1,0:T(8,128)(2,1)S(1)}, bf16[512,256]{1,0:T(8,128)(2,1)S(1)}, u32[]{:S(2)}, u32[]{:S(2)}) collective-permute-start(bf16[512,256]{1,0:T(8,128)(2,1)S(1)} %attend.2.own_ref), channel_id=1, source_target_pairs={{0,1},{1,0},{2,3},{3,2},{4,5},{5,4},{6,7},{7,6},{8,9},{9,8},{10,11... | collective-permute-start | bytes 786440 | tf_op jit(solution)/shard_map/ppermute | solution.py:325
  101.9 13.3 %collective-permute-start.13 = (bf16[512,256]{1,0:T(8,128)(2,1)S(1)}, bf16[512,256]{1,0:T(8,128)(2,1)S(1)}, u32[]{:S(2)}, u32[]{:S(2)}) collective-permute-start(bf16[512,256]{1,0:T(8,128)(2,1)S(1)} %get-tuple-element.37), channel_id=1, source_target_pairs={{0,14},{2,0},{4,2},{6,4},{8,6},{10,8},{12,10},{14,12},{1,15},{3,1}... | collective-permute-start | bytes 786440 | tf_op jit(solution)/shard_map/ppermute | solution.py:266
  107.9 10.8 %collective-permute-start.10 = (bf16[512,256]{1,0:T(8,128)(2,1)S(1)}, bf16[512,256]{1,0:T(8,128)(2,1)S(1)}, u32[]{:S(2)}, u32[]{:S(2)}) collective-permute-start(bf16[512,256]{1,0:T(8,128)(2,1)S(1)} %get-tuple-element.34), channel_id=1, source_target_pairs={{0,2},{2,4},{4,6},{6,8},{8,10},{10,12},{12,14},{14,0},{1,3},{3,5},... | collective-permute-start | bytes 786440 | tf_op jit(solution)/shard_map/ppermute | solution.py:266
  108.9 11.3 %collective-permute-start.6 = (bf16[512,256]{1,0:T(8,128)(2,1)S(1)}, bf16[512,256]{1,0:T(8,128)(2,1)S(1)}, u32[]{:S(2)}, u32[]{:S(2)}) collective-permute-start(bf16[512,256]{1,0:T(8,128)(2,1)S(1)} %get-tuple-element.30), channel_id=1, source_target_pairs={{0,14},{2,0},{4,2},{6,4},{8,6},{10,8},{12,10},{14,12},{1,15},{3,1}... | collective-permute-start | bytes 786440 | tf_op jit(solution)/shard_map/ppermute | solution.py:266
  112.2 11.8 %collective-permute-start.2 = (bf16[512,256]{1,0:T(8,128)(2,1)S(1)}, bf16[512,256]{1,0:T(8,128)(2,1)S(1)}, u32[]{:S(2)}, u32[]{:S(2)}) collective-permute-start(bf16[512,256]{1,0:T(8,128)(2,1)S(1)} %get-tuple-element.26), channel_id=1, source_target_pairs={{0,2},{2,4},{4,6},{6,8},{8,10},{10,12},{12,14},{14,0},{1,3},{3,5},... | collective-permute-start | bytes 786440 | tf_op jit(solution)/shard_map/ppermute | solution.py:266
  115.3 10.5 %collective-permute-start.14 = (bf16[512,256]{1,0:T(8,128)(2,1)S(1)}, bf16[512,256]{1,0:T(8,128)(2,1)S(1)}, u32[]{:S(2)}, u32[]{:S(2)}) collective-permute-start(bf16[512,256]{1,0:T(8,128)(2,1)S(1)} %add_convert_fusion.3), channel_id=1, source_target_pairs={{0,14},{2,0},{4,2},{6,4},{8,6},{10,8},{12,10},{14,12},{1,15},{3,1}... | collective-permute-start | bytes 786440 | tf_op jit(solution)/shard_map/ppermute | solution.py:266
  118.7 10.9 %collective-permute-start.11 = (bf16[512,256]{1,0:T(8,128)(2,1)S(1)}, bf16[512,256]{1,0:T(8,128)(2,1)S(1)}, u32[]{:S(2)}, u32[]{:S(2)}) collective-permute-start(bf16[512,256]{1,0:T(8,128)(2,1)S(1)} %add_convert_fusion.5), channel_id=1, source_target_pairs={{0,2},{2,4},{4,6},{6,8},{8,10},{10,12},{12,14},{14,0},{1,3},{3,5},... | collective-permute-start | bytes 786440 | tf_op jit(solution)/shard_map/ppermute | solution.py:266
  120.3 19.7 %collective-permute-start.7 = (bf16[512,256]{1,0:T(8,128)(2,1)S(1)}, bf16[512,256]{1,0:T(8,128)(2,1)S(1)}, u32[]{:S(2)}, u32[]{:S(2)}) collective-permute-start(bf16[512,256]{1,0:T(8,128)(2,1)S(1)} %add_convert_fusion.8), channel_id=1, source_target_pairs={{0,14},{2,0},{4,2},{6,4},{8,6},{10,8},{12,10},{14,12},{1,15},{3,1}... | collective-permute-start | bytes 786440 | tf_op jit(solution)/shard_map/ppermute | solution.py:266
  124.1 11.1 %collective-permute-start.3 = (bf16[512,256]{1,0:T(8,128)(2,1)S(1)}, bf16[512,256]{1,0:T(8,128)(2,1)S(1)}, u32[]{:S(2)}, u32[]{:S(2)}) collective-permute-start(bf16[512,256]{1,0:T(8,128)(2,1)S(1)} %add_convert_fusion.11), channel_id=1, source_target_pairs={{0,2},{2,4},{4,6},{6,8},{8,10},{10,12},{12,14},{14,0},{1,3},{3,5},... | collective-permute-start | bytes 786440 | tf_op jit(solution)/shard_map/ppermute | solution.py:266
  125.9 10.2 %collective-permute-start.15 = (bf16[512,256]{1,0:T(8,128)(2,1)S(1)}, bf16[512,256]{1,0:T(8,128)(2,1)S(1)}, u32[]{:S(2)}, u32[]{:S(2)}) collective-permute-start(bf16[512,256]{1,0:T(8,128)(2,1)S(1)} %add_convert_fusion.2), channel_id=1, source_target_pairs={{0,14},{2,0},{4,2},{6,4},{8,6},{10,8},{12,10},{14,12},{1,15},{3,1}... | collective-permute-start | bytes 786440 | tf_op jit(solution)/shard_map/ppermute | solution.py:266
  129.7 15.6 %collective-permute-start.12 = (bf16[512,256]{1,0:T(8,128)(2,1)S(1)}, bf16[512,256]{1,0:T(8,128)(2,1)S(1)}, u32[]{:S(2)}, u32[]{:S(2)}) collective-permute-start(bf16[512,256]{1,0:T(8,128)(2,1)S(1)} %add_convert_fusion.4), channel_id=1, source_target_pairs={{0,2},{2,4},{4,6},{6,8},{8,10},{10,12},{12,14},{14,0},{1,3},{3,5},... | collective-permute-start | bytes 786440 | tf_op jit(solution)/shard_map/ppermute | solution.py:266
  135.2 9.9 %collective-permute-start.4 = (bf16[512,256]{1,0:T(8,128)(2,1)S(1)}, bf16[512,256]{1,0:T(8,128)(2,1)S(1)}, u32[]{:S(2)}, u32[]{:S(2)}) collective-permute-start(bf16[512,256]{1,0:T(8,128)(2,1)S(1)} %add_convert_fusion.10), channel_id=1, source_target_pairs={{0,2},{2,4},{4,6},{6,8},{8,10},{10,12},{12,14},{14,0},{1,3},{3,5},... | collective-permute-start | bytes 786440 | tf_op jit(solution)/shard_map/ppermute | solution.py:266
  136.2 10.5 %collective-permute-start.16 = (bf16[512,256]{1,0:T(8,128)(2,1)S(1)}, bf16[512,256]{1,0:T(8,128)(2,1)S(1)}, u32[]{:S(2)}, u32[]{:S(2)}) collective-permute-start(bf16[512,256]{1,0:T(8,128)(2,1)S(1)} %add_convert_fusion.1), channel_id=1, source_target_pairs={{0,14},{2,0},{4,2},{6,4},{8,6},{10,8},{12,10},{14,12},{1,15},{3,1}... | collective-permute-start | bytes 786440 | tf_op jit(solution)/shard_map/ppermute | solution.py:266
  140.0 10.5 %collective-permute-start.8 = (bf16[512,256]{1,0:T(8,128)(2,1)S(1)}, bf16[512,256]{1,0:T(8,128)(2,1)S(1)}, u32[]{:S(2)}, u32[]{:S(2)}) collective-permute-start(bf16[512,256]{1,0:T(8,128)(2,1)S(1)} %add_convert_fusion.7), channel_id=1, source_target_pairs={{0,14},{2,0},{4,2},{6,4},{8,6},{10,8},{12,10},{14,12},{1,15},{3,1}... | collective-permute-start | bytes 786440 | tf_op jit(solution)/shard_map/ppermute | solution.py:266
  145.2 8.4 %collective-permute-start.5 = (bf16[512,256]{1,0:T(8,128)(2,1)S(1)}, bf16[512,256]{1,0:T(8,128)(2,1)S(1)}, u32[]{:S(2)}, u32[]{:S(2)}) collective-permute-start(bf16[512,256]{1,0:T(8,128)(2,1)S(1)} %add_convert_fusion.9), channel_id=1, source_target_pairs={{0,2},{2,4},{4,6},{6,8},{8,10},{10,12},{12,14},{14,0},{1,3},{3,5},... | collective-permute-start | bytes 786440 | tf_op jit(solution)/shard_map/ppermute | solution.py:266
Sparse Core Ops, SparseCore 0:
  9.1 67.0 all-gather.1

commit v7 on v6

--- a/solution.py
+++ b/solution.py
@@ -99,37 +99,50 @@
     )(place, heard, rows)
 
 
-def query_kernel(tokens_ref, weight_ref, out_ref):
-    projected = jnp.dot(tokens_ref[...], weight_ref[...], preferred_element_type=F32)
-    for h in range(weight_ref.shape[1] // HD):
-        cols = slice(h * HD, (h + 1) * HD)
-        out_ref[:, cols] = unit(projected[:, cols]).astype(BF16)
-
-
-def project_queries(tokens, weight):
-    rows, depth = tokens.shape
-    width, tile = weight.shape[1], 128
+def query_kernel(place_ref, *refs):
+    ring = len(refs) - 4
+    weight_ref, partner_ref, own_ref, lent_ref = refs[ring:]
+    here, core = place_ref[0], place_ref[1]
+    own, lent = None, None
+    for k in range(ring):
+        chip = lax.rem(here + ring - k, ring)
+        part = jnp.dot(refs[k][...], weight_ref[chip, core], preferred_element_type=F32)
+        own = part if own is None else own + part
+        part = jnp.dot(refs[k][...], partner_ref[chip], preferred_element_type=F32)
+        lent = part if lent is None else lent + part
+    own_ref[...] = own
+    lent_ref[...] = lent
+
+
+def project_queries(place, pieces, weight, partner_weight):
+    rows, depth = pieces[0].shape
+    width, tile = weight.shape[-1], 256
+    out = jax.ShapeDtypeStruct((rows, width), F32)
     return pl.pallas_call(
         query_kernel,
         grid=(rows // tile,),
-        out_shape=jax.ShapeDtypeStruct((rows, width), BF16),
-        in_specs=[
-            pl.BlockSpec((tile, depth), lambda i: (i, 0)),
-            pl.BlockSpec((depth, width), lambda i: (0, 0)),
+        out_shape=(out, out),
+        in_specs=[SMEM]
+        + [pl.BlockSpec((tile, depth), lambda i: (i, 0)) for _ in pieces]
+        + [
+            pl.BlockSpec(weight.shape, lambda i: (0, 0, 0, 0)),
+            pl.BlockSpec(partner_weight.shape, lambda i: (0, 0, 0)),
         ],
-        out_specs=pl.BlockSpec((tile, width), lambda i: (i, 0)),
-        compiler_params=pltpu.CompilerParams(vmem_limit_bytes=48 << 20),
+        out_specs=[pl.BlockSpec((tile, width), lambda i: (i, 0))] * 2,
+        compiler_params=pltpu.CompilerParams(vmem_limit_bytes=56 << 20),
         cost_estimate=pl.CostEstimate(
-            flops=2 * rows * depth * width, bytes_accessed=11 << 20, transcendentals=0
+            flops=4 * rows * depth * width * len(pieces), bytes_accessed=9 << 20, transcendentals=0
         ),
         name="project_queries",
-    )(tokens, weight)
-
-
-def attend_kernel(first, slot_ref, length_ref, query_ref, rows_ref, out_ref, held_ref, sems):
+    )(place, *pieces, weight, partner_weight)
+
+
+def attend_kernel(
+    first, slot_ref, length_ref, own_ref, lent_ref, rows_ref, out_ref, query_ref, held_ref, sems
+):
     spans = slot_ref.shape[0] // NBRS
     count = sems.shape[0] // NBRS
-    width = query_ref.shape[1]
+    width = out_ref.shape[1]
     keys = NBRS * NBR_LEN
     factor = 2.0 / math.sqrt(HD)
     copies = []
@@ -142,6 +155,9 @@
             )
             copy.start()
             copies.append(copy)
+    for h in range(width // HD):
+        cols = slice(h * HD, (h + 1) * HD)
+        query_ref[:, cols] = unit(own_ref[:, cols] + lent_ref[:, cols]).astype(BF16)
     places = lax.broadcasted_iota(jnp.int32, (SPAN, keys), 1)
     group = 4
     for start in range(0, count, group):
@@ -170,26 +186,27 @@
             out_ref[c * SPAN : (c + 1) * SPAN, h * HD : (h + 1) * HD] = result.astype(BF16)
 
 
-def attend(part, parts, slot_index, lengths, queries, rows):
-    tokens, width = queries.shape[0] // parts, queries.shape[1]
+def attend(part, parts, slot_index, lengths, own, lent, rows):
+    tokens, width = own.shape[0] // parts, own.shape[1]
     count = tokens // SPAN
     requests = count * NBRS
     return pl.pallas_call(
         functools.partial(attend_kernel, part * count),
         grid=(1,),
         out_shape=jax.ShapeDtypeStruct((tokens, width), BF16),
-        in_specs=[SMEM, SMEM, pl.BlockSpec((tokens, width), lambda i: (part, 0)), ANY],
+        in_specs=[SMEM, SMEM] + [pl.BlockSpec((tokens, width), lambda i: (part, 0))] * 2 + [ANY],
         out_specs=pl.BlockSpec((tokens, width), lambda i: (0, 0)),
         scratch_shapes=[
+            pltpu.VMEM((tokens, width), BF16),
             pltpu.VMEM((requests * NBR_LEN, rows.shape[2]), BF16),
             pltpu.SemaphoreType.DMA((requests,)),
         ],
-        compiler_params=pltpu.CompilerParams(vmem_limit_bytes=12 << 20),
+        compiler_params=pltpu.CompilerParams(vmem_limit_bytes=56 << 20),
         cost_estimate=pl.CostEstimate(
             flops=4 * tokens * NBRS * NBR_LEN * width, bytes_accessed=3 << 20, transcendentals=0
         ),
         name="attend",
-    )(slot_index, lengths, queries, rows)
+    )(slot_index, lengths, own, lent, rows)
 
 
 def relay_kernel(place_ref, weight_ref, lent_ref):
@@ -296,12 +313,16 @@
     block_ids = nbr_owner.T * blocks + nbr_block.T
     notes = jnp.concatenate([block_ids, jnp.pad(block_len, (0, spans - blocks))[None, :]], axis=0)
     notes = jnp.broadcast_to(notes[None], (shards,) + notes.shape)
-    notes, tokens = lax.optimization_barrier((notes, tokens))
     heard = lax.all_to_all(notes, DB, split_axis=0, concat_axis=0, tiled=True)
     projected = project_blocks(codes, scales, key_weight, value_weight)
-
-    gathered = lax.all_gather(tokens, ("z", "c"), axis=1, tiled=True)
     sent = select_blocks(lax.axis_index(DB).astype(jnp.int32).reshape(1), heard, projected)
+    up = [(i, (i + 1) % ring) for i in range(ring)]
+    down = [(i, (i - 1) % ring) for i in range(ring)]
+    pieces = {0: tokens, 1: lax.ppermute(tokens, "z", up)}
+    pieces[ring - 1] = lax.ppermute(tokens, "z", down)
+    sent, pieces[1], pieces[ring - 1] = lax.optimization_barrier(
+        (sent, pieces[1], pieces[ring - 1])
+    )
     rows = lax.all_to_all(sent, DB, split_axis=0, concat_axis=0, tiled=True)
     rows = rows.reshape(shards * NBRS, NBR_LEN, 2 * width)
 
@@ -319,9 +340,19 @@
         jnp.where(block_ids[:, None] == ids[None, :], all_lengths[None, :], 0), axis=1
     )
 
+    for k in range(2, ring // 2 + 1):
+        pieces[k] = lax.ppermute(pieces[k - 1], "z", up)
+        if k < ring // 2:
+            pieces[ring - k] = lax.ppermute(pieces[ring - k + 1], "z", down)
+    by_core = query_weight.reshape(ring, cores, width, width)
+    lent_rows = lax.dynamic_index_in_dim(by_core, 1 - core, 1, keepdims=False)
+    partner_rows = lax.ppermute(lent_rows, "c", swap)
+
     partner_weight = lax.ppermute(relay(place, out_weight, ring), "c", swap)
-    queries = project_queries(gathered, query_weight)
-    attended = [attend(part, 2, slot_index, lengths, queries, rows) for part in range(2)]
+
+    own, lent = project_queries(place, [pieces[k] for k in range(ring)], by_core, partner_rows)
+    lent = lax.ppermute(lent, "c", swap)
+    attended = [attend(part, 2, slot_index, lengths, own, lent, rows) for part in range(2)]
     partner_attended = [lax.ppermute(part, "c", swap) for part in attended]
     return reduce_ring(place, attended, partner_attended, out_weight, partner_weight, ring)
 

time: 162 us -> 151 us (0.932)
  starting transfers between devices: 39 us -> 52.7 us
  between operations: 13.6 us -> 0.38 us
  waiting for transfers between devices: 70.2 us -> 57.3 us
  Pallas kernels: 29.5 us -> 31.3 us
  local copies, waits for them, and re-layouts: 6.36 us -> 4.65 us
  other arithmetic: 2.75 us -> 4.38 us
    all_gather x1 -> x0, waiting for transfers between devices: 40.4 us -> none  [local(): gathered = lax.all_gather(tokens, ('z', 'c'), axis=1, tiled=True)]
    ppermute x0 -> x9, waiting for transfers between devices: none -> 29.9 us  [the longest x3 26.3 us: local(): pieces[k] = lax.ppermute(pieces[k - 1], 'z', up)]
    ppermute x0 -> x9, starting transfers between devices: none -> 13.1 us  [the longest x2 7.02 us: local(): pieces[ring - k] = lax.ppermute(pieces[ring - k + 1], 'z', down)]
    ppermute x14, waiting for transfers between devices: 22.3 us -> 16.9 us  [reduce_ring(): lax.ppermute(held[half, way], 'z', up if way == 1 else down)]
    all_to_all x1, waiting for transfers between devices: 6.65 us -> 9.79 us  [local(): rows = lax.all_to_all(sent, DB, split_axis=0, concat_axis=0, tiled=True)]
    pallas_call x2, Pallas kernels: 6.14 us -> 8.88 us  [attend(): pl.pallas_call(functools.partial(attend_kernel, part * count), grid=(1,),...]
    unnamed x12 -> x18, local copies, waits for them, and re-layouts: 4.05 us -> 2.26 us
  transfers between devices with their start and end apart: 20 -> 28, of which waited for: 11 -> 14; matrix products, arithmetic and copies ran while one was open for 1% -> 4% of each run, Pallas kernels for 18% -> 21%
where the time goes in v7:
time: 151 us
  waiting for transfers between devices  57.3 us (38%)
  starting transfers between devices  52.7 us (35%)
  Pallas kernels  31.3 us (21%)
  local copies, waits for them, and re-layouts  4.65 us (3%)
  other arithmetic  4.38 us (3%)
    ppermute x3, waiting for transfers between devices, local(): pieces[k] = lax.ppermute(pieces[k - 1], 'z', up)  26.3 us
    ppermute x14, starting transfers between devices, reduce_ring(): lax.ppermute(held[half, way], 'z', up if way == 1 else down)  24.6 us
    ppermute x14, waiting for transfers between devices, reduce_ring(): lax.ppermute(held[half, way], 'z', up if way == 1 else down)  16.9 us
    all_to_all x1, waiting for transfers between devices, local(): rows = lax.all_to_all(sent, DB, split_axis=0, concat_axis=0, tiled=True)  9.79 us
    pallas_call x2, Pallas kernels, attend(): pl.pallas_call(functools.partial(attend_kernel, part * count), grid=(1,),...  8.88 us
    all_to_all x1, starting transfers between devices, local(): heard = lax.all_to_all(notes, DB, split_axis=0, concat_axis=0, tiled=True)  7.17 us
    ppermute x2, starting transfers between devices, local(): pieces[ring - k] = lax.ppermute(pieces[ring - k + 1], 'z', down)  7.02 us
    pallas_call x1, Pallas kernels, project_queries(): pl.pallas_call(query_kernel, grid=(rows // tile,), out_shape=(out, out),...  6.94 us
  transfers between devices with their start and end apart: 28, of which 14 were waited for; matrix products, arithmetic and copies ran while one was open for 4% of the time, Pallas kernels for 21%

profile of v7, /device:TPU:24, one launch (start us, length us, event | category | flops | bytes accessed | tf_op | source)
XLA Modules:
  0.0 150.8 jit_solution(10131814454895669766)
XLA Ops:
  0.0 1.9 %collective-permute-start = (bf16[1024,256]{1,0:T(8,128)(2,1)}, bf16[1024,256]{1,0:T(8,128)(2,1)}, u32[]{:S(2)}, u32[]{:S(2)}) collective-permute-start(bf16[1024,256]{1,0:T(8,128)(2,1)} %refs_0_.1), channel_id=1, source_target_pairs={{0,2},{2,4},{4,6},{6,8},{8,10},{10,12},{12,14},{14,0},{1,3},{3,5},... | collective-permute-start | bytes 1572872 | tf_op jit(solution)/shard_map/ppermute | solution.py:321
  1.9 3.9 %collective-permute-start.1 = (bf16[1024,256]{1,0:T(8,128)(2,1)}, bf16[1024,256]{1,0:T(8,128)(2,1)S(1)}, u32[]{:S(2)}, u32[]{:S(2)}) collective-permute-start(bf16[1024,256]{1,0:T(8,128)(2,1)} %refs_0_.1), channel_id=1, source_target_pairs={{0,14},{2,0},{4,2},{6,4},{8,6},{10,8},{12,10},{14,12},{1,15},{3,1}... | collective-permute-start | bytes 1572872 | tf_op jit(solution)/shard_map/ppermute | solution.py:322
  5.9 0.7 pad_bitcast_fusion
  6.5 0.7 bitcast_add_fusion
  7.2 0.6 broadcast_in_dim.27
  7.9 7.2 %all-to-all-start = ((s32[16,3,16]{2,1,0:T(4,128)}), s32[16,3,16]{2,1,0:T(4,128)S(1)}, u32[]{:S(2)}, u32[]{:S(2)}) async-start(s32[16,3,16]{2,1,0:T(4,128)} %broadcast_in_dim.27), calls=%async_computation | async-start | bytes 65536 | tf_op jit(solution)/shard_map/all_to_all | solution.py:316
  15.0 4.9 %project_blocks.1.rows_ref = bf16[8,128,512]{2,1,0:T(8,128)(2,1)} custom-call(f32[8,7]{1,0:T(8,128)} %scales_ref.1, bf16[8,128,896]{2,1,0:T(8,128)(2,1)} %codes_ref.1, bf16[896,256]{1,0:T(8,128)(2,1)} %key_ref.1, bf16[896,256]{1,0:T(8,128)(2,1)} %value_ref.1), custom_call_target="tpu_custom_call" | custom-call | flops 939524096 | bytes 5242880 | tf_op jit(solution)/shard_map/project_blocks/pallas_call | solution.py:52
  19.9 0.7 all-to-all-done.heard_ref
  20.6 0.6 copy-done.5
  21.2 3.9 %select_blocks.1 = bf16[16,2,128,512]{3,2,1,0:T(8,128)(2,1)} custom-call(s32[1]{0:T(128)} %bitcast.5.place_ref, s32[16,3,16]{2,1,0:T(4,128)} %copy-done.5, bf16[8,128,512]{2,1,0:T(8,128)(2,1)} %project_blocks.1.rows_ref), custom_call_target="tpu_custom_call" | custom-call | bytes 9437184 | tf_op jit(solution)/shard_map/select_blocks/pallas_call | solution.py:91
  25.2 0.8 copy-done.7
  26.0 6.5 %all-to-all-start.1 = ((bf16[16,2,128,512]{3,2,1,0:T(8,128)(2,1)}), bf16[16,2,128,512]{3,2,1,0:T(8,128)(2,1)}, u32[]{:S(2)}, u32[]{:S(2)}) async-start(bf16[16,2,128,512]{3,2,1,0:T(8,128)(2,1)} %select_blocks.1), calls=%async_computation.1 | async-start | bytes 8388608 | tf_op jit(solution)/shard_map/all_to_all | solution.py:326
  32.7 0.8 copy-done.8
  33.6 3.2 %collective-permute-start.5 = (bf16[1024,256]{1,0:T(8,128)(2,1)S(1)}, bf16[1024,256]{1,0:T(8,128)(2,1)}, u32[]{:S(2)}, u32[]{:S(2)}) collective-permute-start(bf16[1024,256]{1,0:T(8,128)(2,1)S(1)} %copy-done.8), channel_id=1, source_target_pairs={{0,14},{2,0},{4,2},{6,4},{8,6},{10,8},{12,10},{14,12},{1,15},{3,1}... | collective-permute-start | bytes 1572872 | tf_op jit(solution)/shard_map/ppermute | solution.py:346
  36.8 9.5 %collective-permute-done.2.refs_2_ = bf16[1024,256]{1,0:T(8,128)(2,1)} collective-permute-done((bf16[1024,256]{1,0:T(8,128)(2,1)}, bf16[1024,256]{1,0:T(8,128)(2,1)}, u32[]{:S(2)}, u32[]{:S(2)}) %collective-permute-start.2) | collective-permute-done | bytes 524320 | tf_op jit(solution)/shard_map/ppermute | solution.py:344
  46.3 1.5 collective-permute-done.5.refs_6_
  47.8 3.8 %collective-permute-start.6 = (bf16[1024,256]{1,0:T(8,128)(2,1)}, bf16[1024,256]{1,0:T(8,128)(2,1)}, u32[]{:S(2)}, u32[]{:S(2)}) collective-permute-start(bf16[1024,256]{1,0:T(8,128)(2,1)} %collective-permute-done.5.refs_6_), channel_id=1, source_target_pairs={{0,14},{2,0},{4,2},{6,4},{8,6},{10,8},{12,10},{14,12},{1,15},{3,1}... | collective-permute-start | bytes 1572872 | tf_op jit(solution)/shard_map/ppermute | solution.py:346
  51.6 7.6 %collective-permute-done.3.refs_3_ = bf16[1024,256]{1,0:T(8,128)(2,1)} collective-permute-done((bf16[1024,256]{1,0:T(8,128)(2,1)}, bf16[1024,256]{1,0:T(8,128)(2,1)}, u32[]{:S(2)}, u32[]{:S(2)}) %collective-permute-start.3) | collective-permute-done | bytes 524320 | tf_op jit(solution)/shard_map/ppermute | solution.py:344
  59.2 0.6 pad_add_fusion.1.place_ref
  59.8 2.2 %collective-permute-done.6.refs_5_ = bf16[1024,256]{1,0:T(8,128)(2,1)} collective-permute-done((bf16[1024,256]{1,0:T(8,128)(2,1)}, bf16[1024,256]{1,0:T(8,128)(2,1)}, u32[]{:S(2)}, u32[]{:S(2)}) %collective-permute-start.6) | collective-permute-done | bytes 524320 | tf_op jit(solution)/shard_map/ppermute | solution.py:346
  62.0 9.2 %collective-permute-done.4.refs_4_ = bf16[1024,256]{1,0:T(8,128)(2,1)} collective-permute-done((bf16[1024,256]{1,0:T(8,128)(2,1)}, bf16[1024,256]{1,0:T(8,128)(2,1)}, u32[]{:S(2)}, u32[]{:S(2)}) %collective-permute-start.4) | collective-permute-done | bytes 524320 | tf_op jit(solution)/shard_map/ppermute | solution.py:344
  71.1 6.9 %project_queries.1 = (f32[1024,256]{1,0:T(8,128)}, f32[1024,256]{1,0:T(8,128)}) custom-call(s32[2]{0:T(128)} %pad_add_fusion.1.place_ref, bf16[1024,256]{1,0:T(8,128)(2,1)} %refs_0_.1, bf16[1024,256]{1,0:T(8,128)(2,1)} %collective-permute-done.refs_1_, bf16[1024,256]{1,0:T(8,128)(2,1)} %collective-permute-done.2.refs_2_, ...), custom_call_target="tpu_custom_call" | custom-call | flops 2147483648 | bytes 9437184 | tf_op jit(solution)/shard_map/project_queries/pallas_call | solution.py:121
  78.2 1.7 %relay.1 = bf16[8,256,256]{2,1,0:T(8,128)(2,1)} custom-call(s32[2]{0:T(128)S(1)} %copy-done.3, bf16[256,4096]{1,0:T(8,128)(2,1)S(1)} %copy-done), custom_call_target="tpu_custom_call" | custom-call | bytes 3145728 | tf_op jit(solution)/shard_map/relay/pallas_call | solution.py:223
  80.7 0.6 multiply_add_fusion.slot_ref
  81.3 0.8 slice_reduce_fusion
  82.2 0.8 select_reduce_fusion.length_ref
  82.9 9.8 %all-to-all-done.1 = bf16[16,2,128,512]{3,2,1,0:T(8,128)(2,1)} async-done(((bf16[16,2,128,512]{3,2,1,0:T(8,128)(2,1)}), bf16[16,2,128,512]{3,2,1,0:T(8,128)(2,1)}, u32[]{:S(2)}, u32[]{:S(2)}) %all-to-all-start.1) | async-done | bytes 4194336 | tf_op jit(solution)/shard_map/all_to_all | solution.py:326
  92.7 4.4 %attend.2.own_ref = bf16[512,256]{1,0:T(8,128)(2,1)} custom-call(s32[32]{0:T(128)} %multiply_add_fusion.slot_ref, s32[32]{0:T(128)} %select_reduce_fusion.length_ref, f32[1024,256]{1,0:T(8,128)} %get-tuple-element.28.own_ref, f32[1024,256]{1,0:T(8,128)} %collective-permute-done.8.lent_ref, bf16[32,128,512]{2,1,0:T(8,128)(2,1)} %bitcast.8.rows_ref), custom_call_target="tpu_custom_call" | custom-call | flops 134217728 | bytes 3145728 | tf_op jit(solution)/shard_map/attend/pallas_call | solution.py:193
  97.5 4.4 %attend.3.own_ref = bf16[512,256]{1,0:T(8,128)(2,1)} custom-call(s32[32]{0:T(128)} %multiply_add_fusion.slot_ref, s32[32]{0:T(128)} %select_reduce_fusion.length_ref, f32[1024,256]{1,0:T(8,128)} %get-tuple-element.28.own_ref, f32[1024,256]{1,0:T(8,128)} %collective-permute-done.8.lent_ref, bf16[32,128,512]{2,1,0:T(8,128)(2,1)} %bitcast.8.rows_ref), custom_call_target="tpu_custom_call" | custom-call | flops 134217728 | bytes 3145728 | tf_op jit(solution)/shard_map/attend/pallas_call | solution.py:193
  102.5 1.0 shares.5
  103.6 3.2 %collective-permute-start.15 = (bf16[512,256]{1,0:T(8,128)(2,1)S(1)}, bf16[512,256]{1,0:T(8,128)(2,1)S(1)}, u32[]{:S(2)}, u32[]{:S(2)}) collective-permute-start(bf16[512,256]{1,0:T(8,128)(2,1)S(1)} %get-tuple-element.36), channel_id=1, source_target_pairs={{0,14},{2,0},{4,2},{6,4},{8,6},{10,8},{12,10},{14,12},{1,15},{3,1}... | collective-permute-start | bytes 786440 | tf_op jit(solution)/shard_map/ppermute | solution.py:283
  106.8 1.0 shares.7
  107.9 3.2 %collective-permute-start.22 = (bf16[512,256]{1,0:T(8,128)(2,1)S(1)}, bf16[512,256]{1,0:T(8,128)(2,1)S(1)}, u32[]{:S(2)}, u32[]{:S(2)}) collective-permute-start(bf16[512,256]{1,0:T(8,128)(2,1)S(1)} %get-tuple-element.43), channel_id=1, source_target_pairs={{0,14},{2,0},{4,2},{6,4},{8,6},{10,8},{12,10},{14,12},{1,15},{3,1}... | collective-permute-start | bytes 786440 | tf_op jit(solution)/shard_map/ppermute | solution.py:283
  111.1 1.5 %shares.4 = (f32[512,256]{1,0:T(8,128)S(1)}, f32[512,256]{1,0:T(8,128)S(1)}, f32[512,256]{1,0:T(8,128)S(1)}, f32[512,256]{1,0:T(8,128)S(1)}, f32[512,256]{1,0:T(8,128)S(1)}, /*index=5*/f32[512,256]{1,0:T(8,128)S(1)}) custom-call(s32[2]{0:T(128)S(1)} %copy-done.3, bf16[512,256]{1,0:T(8,128)(2,1)S(1)} %copy-done.2, ...), custom_call_target="tpu_custom_call" | custom-call | flops 805306368 | bytes 4194304 | tf_op jit(solution)/shard_map/shares/pallas_call | solution.py:248
  112.6 1.5 %shares.6 = (f32[512,256]{1,0:T(8,128)S(1)}, f32[512,256]{1,0:T(8,128)S(1)}, f32[512,256]{1,0:T(8,128)S(1)}, f32[512,256]{1,0:T(8,128)S(1)}, f32[512,256]{1,0:T(8,128)S(1)}, /*index=5*/f32[512,256]{1,0:T(8,128)S(1)}) custom-call(s32[2]{0:T(128)S(1)} %copy-done.3, bf16[512,256]{1,0:T(8,128)(2,1)S(1)} %copy-done.1, ...), custom_call_target="tpu_custom_call" | custom-call | flops 805306368 | bytes 4194304 | tf_op jit(solution)/shard_map/shares/pallas_call | solution.py:248
  114.4 3.3 %collective-permute-start.16 = (bf16[512,256]{1,0:T(8,128)(2,1)S(1)}, bf16[512,256]{1,0:T(8,128)(2,1)S(1)}, u32[]{:S(2)}, u32[]{:S(2)}) collective-permute-start(bf16[512,256]{1,0:T(8,128)(2,1)S(1)} %add_convert_fusion.8), channel_id=1, source_target_pairs={{0,14},{2,0},{4,2},{6,4},{8,6},{10,8},{12,10},{14,12},{1,15},{3,1}... | collective-permute-start | bytes 786440 | tf_op jit(solution)/shard_map/ppermute | solution.py:283
  117.7 1.9 %collective-permute-done.19 = bf16[512,256]{1,0:T(8,128)(2,1)S(1)} collective-permute-done((bf16[512,256]{1,0:T(8,128)(2,1)S(1)}, bf16[512,256]{1,0:T(8,128)(2,1)S(1)}, u32[]{:S(2)}, u32[]{:S(2)}) %collective-permute-start.19) | collective-permute-done | bytes 262176 | tf_op jit(solution)/shard_map/ppermute | solution.py:283
  119.8 3.3 %collective-permute-start.23 = (bf16[512,256]{1,0:T(8,128)(2,1)S(1)}, bf16[512,256]{1,0:T(8,128)(2,1)S(1)}, u32[]{:S(2)}, u32[]{:S(2)}) collective-permute-start(bf16[512,256]{1,0:T(8,128)(2,1)S(1)} %add_convert_fusion.3), channel_id=1, source_target_pairs={{0,14},{2,0},{4,2},{6,4},{8,6},{10,8},{12,10},{14,12},{1,15},{3,1}... | collective-permute-start | bytes 786440 | tf_op jit(solution)/shard_map/ppermute | solution.py:283
  123.1 2.1 %collective-permute-done.12 = bf16[512,256]{1,0:T(8,128)(2,1)S(1)} collective-permute-done((bf16[512,256]{1,0:T(8,128)(2,1)S(1)}, bf16[512,256]{1,0:T(8,128)(2,1)S(1)}, u32[]{:S(2)}, u32[]{:S(2)}) %collective-permute-start.12) | collective-permute-done | bytes 262176 | tf_op jit(solution)/shard_map/ppermute | solution.py:283
  125.4 3.3 %collective-permute-start.17 = (bf16[512,256]{1,0:T(8,128)(2,1)S(1)}, bf16[512,256]{1,0:T(8,128)(2,1)S(1)}, u32[]{:S(2)}, u32[]{:S(2)}) collective-permute-start(bf16[512,256]{1,0:T(8,128)(2,1)S(1)} %add_convert_fusion.7), channel_id=1, source_target_pairs={{0,14},{2,0},{4,2},{6,4},{8,6},{10,8},{12,10},{14,12},{1,15},{3,1}... | collective-permute-start | bytes 786440 | tf_op jit(solution)/shard_map/ppermute | solution.py:283
  128.7 1.7 %collective-permute-done.23 = bf16[512,256]{1,0:T(8,128)(2,1)S(1)} collective-permute-done((bf16[512,256]{1,0:T(8,128)(2,1)S(1)}, bf16[512,256]{1,0:T(8,128)(2,1)S(1)}, u32[]{:S(2)}, u32[]{:S(2)}) %collective-permute-start.23) | collective-permute-done | bytes 262176 | tf_op jit(solution)/shard_map/ppermute | solution.py:283
  130.4 4.0 %collective-permute-start.24 = (bf16[512,256]{1,0:T(8,128)(2,1)S(1)}, bf16[512,256]{1,0:T(8,128)(2,1)S(1)}, u32[]{:S(2)}, u32[]{:S(2)}) collective-permute-start(bf16[512,256]{1,0:T(8,128)(2,1)S(1)} %add_convert_fusion.2), channel_id=1, source_target_pairs={{0,14},{2,0},{4,2},{6,4},{8,6},{10,8},{12,10},{14,12},{1,15},{3,1}... | collective-permute-start | bytes 786440 | tf_op jit(solution)/shard_map/ppermute | solution.py:283
  134.4 1.1 collective-permute-done.13
  135.8 4.6 %collective-permute-done.24 = bf16[512,256]{1,0:T(8,128)(2,1)S(1)} collective-permute-done((bf16[512,256]{1,0:T(8,128)(2,1)S(1)}, bf16[512,256]{1,0:T(8,128)(2,1)S(1)}, u32[]{:S(2)}, u32[]{:S(2)}) %collective-permute-start.24) | collective-permute-done | bytes 262176 | tf_op jit(solution)/shard_map/ppermute | solution.py:283
  140.4 3.8 %collective-permute-start.25 = (bf16[512,256]{1,0:T(8,128)(2,1)S(1)}, bf16[512,256]{1,0:T(8,128)(2,1)S(1)}, u32[]{:S(2)}, u32[]{:S(2)}) collective-permute-start(bf16[512,256]{1,0:T(8,128)(2,1)S(1)} %add_convert_fusion.1), channel_id=1, source_target_pairs={{0,14},{2,0},{4,2},{6,4},{8,6},{10,8},{12,10},{14,12},{1,15},{3,1}... | collective-permute-start | bytes 786440 | tf_op jit(solution)/shard_map/ppermute | solution.py:283
  144.2 1.9 %collective-permute-done.14 = bf16[512,256]{1,0:T(8,128)(2,1)S(1)} collective-permute-done((bf16[512,256]{1,0:T(8,128)(2,1)S(1)}, bf16[512,256]{1,0:T(8,128)(2,1)S(1)}, u32[]{:S(2)}, u32[]{:S(2)}) %collective-permute-start.14) | collective-permute-done | bytes 262176 | tf_op jit(solution)/shard_map/ppermute | solution.py:283
  146.2 3.7 %collective-permute-done.21 = bf16[512,256]{1,0:T(8,128)(2,1)S(1)} collective-permute-done((bf16[512,256]{1,0:T(8,128)(2,1)S(1)}, bf16[512,256]{1,0:T(8,128)(2,1)S(1)}, u32[]{:S(2)}, u32[]{:S(2)}) %collective-permute-start.21) | collective-permute-done | bytes 262176 | tf_op jit(solution)/shard_map/ppermute | solution.py:283
  149.9 0.8 pad_maximum_fusion
  (62 shorter events, 3.4 us)
Async XLA Ops:
  0.0 25.2 %collective-permute-start = (bf16[1024,256]{1,0:T(8,128)(2,1)}, bf16[1024,256]{1,0:T(8,128)(2,1)}, u32[]{:S(2)}, u32[]{:S(2)}) collective-permute-start(bf16[1024,256]{1,0:T(8,128)(2,1)} %refs_0_.1), channel_id=1, source_target_pairs={{0,2},{2,4},{4,6},{6,8},{8,10},{10,12},{12,14},{14,0},{1,3},{3,5},... | collective-permute-start | bytes 1572872 | tf_op jit(solution)/shard_map/ppermute | solution.py:321
  1.9 23.3 %collective-permute-start.1 = (bf16[1024,256]{1,0:T(8,128)(2,1)}, bf16[1024,256]{1,0:T(8,128)(2,1)S(1)}, u32[]{:S(2)}, u32[]{:S(2)}) collective-permute-start(bf16[1024,256]{1,0:T(8,128)(2,1)} %refs_0_.1), channel_id=1, source_target_pairs={{0,14},{2,0},{4,2},{6,4},{8,6},{10,8},{12,10},{14,12},{1,15},{3,1}... | collective-permute-start | bytes 1572872 | tf_op jit(solution)/shard_map/ppermute | solution.py:322
  7.9 12.8 %all-to-all-start = ((s32[16,3,16]{2,1,0:T(4,128)}), s32[16,3,16]{2,1,0:T(4,128)S(1)}, u32[]{:S(2)}, u32[]{:S(2)}) async-start(s32[16,3,16]{2,1,0:T(4,128)} %broadcast_in_dim.27), calls=%async_computation | async-start | bytes 65536 | tf_op jit(solution)/shard_map/all_to_all | solution.py:316
  20.6 0.6 copy-start.5
  25.2 7.3 %copy-start.4 = (bf16[4096,256]{1,0:T(8,128)(2,1)S(1)}, bf16[4096,256]{1,0:T(8,128)(2,1)}, u32[]{:S(2)}) copy-start(bf16[4096,256]{1,0:T(8,128)(2,1)} %param.11) | copy-start | bytes 6291460
  25.2 0.8 copy-start.7
  26.0 66.7 %all-to-all-start.1 = ((bf16[16,2,128,512]{3,2,1,0:T(8,128)(2,1)}), bf16[16,2,128,512]{3,2,1,0:T(8,128)(2,1)}, u32[]{:S(2)}, u32[]{:S(2)}) async-start(bf16[16,2,128,512]{3,2,1,0:T(8,128)(2,1)} %select_blocks.1), calls=%async_computation.1 | async-start | bytes 8388608 | tf_op jit(solution)/shard_map/all_to_all | solution.py:326
  32.5 13.8 %collective-permute-start.2 = (bf16[1024,256]{1,0:T(8,128)(2,1)}, bf16[1024,256]{1,0:T(8,128)(2,1)}, u32[]{:S(2)}, u32[]{:S(2)}) collective-permute-start(bf16[1024,256]{1,0:T(8,128)(2,1)} %collective-permute-done.refs_1_), channel_id=1, source_target_pairs={{0,2},{2,4},{4,6},{6,8},{8,10},{10,12},{12,14},{14,0},{1,3},{3,5},... | collective-permute-start | bytes 1572872 | tf_op jit(solution)/shard_map/ppermute | solution.py:344
  32.5 1.0 copy-start.8
  32.6 27.1 %collective-permute-start.7 = (bf16[8,256,256]{2,1,0:T(8,128)(2,1)S(1)}, bf16[8,256,256]{2,1,0:T(8,128)(2,1)}, u32[]{:S(2)}, u32[]{:S(2)}) collective-permute-start(bf16[8,256,256]{2,1,0:T(8,128)(2,1)S(1)} %dynamic-slice_bitcast_fusion), channel_id=1, source_target_pairs={{0,1},{1,0},{2,3},{3,2},{4,5},{5,4},{6,7},{7,6},{8,9},{9,8},{10,11... | collective-permute-start | bytes 3145736 | tf_op jit(solution)/shard_map/ppermute | solution.py:349
  33.6 14.2 %collective-permute-start.5 = (bf16[1024,256]{1,0:T(8,128)(2,1)S(1)}, bf16[1024,256]{1,0:T(8,128)(2,1)}, u32[]{:S(2)}, u32[]{:S(2)}) collective-permute-start(bf16[1024,256]{1,0:T(8,128)(2,1)S(1)} %copy-done.8), channel_id=1, source_target_pairs={{0,14},{2,0},{4,2},{6,4},{8,6},{10,8},{12,10},{14,12},{1,15},{3,1}... | collective-permute-start | bytes 1572872 | tf_op jit(solution)/shard_map/ppermute | solution.py:346
  46.3 12.9 %collective-permute-start.3 = (bf16[1024,256]{1,0:T(8,128)(2,1)}, bf16[1024,256]{1,0:T(8,128)(2,1)}, u32[]{:S(2)}, u32[]{:S(2)}) collective-permute-start(bf16[1024,256]{1,0:T(8,128)(2,1)} %collective-permute-done.2.refs_2_), channel_id=1, source_target_pairs={{0,2},{2,4},{4,6},{6,8},{8,10},{10,12},{12,14},{14,0},{1,3},{3,5},... | collective-permute-start | bytes 1572872 | tf_op jit(solution)/shard_map/ppermute | solution.py:344
  47.8 14.2 %collective-permute-start.6 = (bf16[1024,256]{1,0:T(8,128)(2,1)}, bf16[1024,256]{1,0:T(8,128)(2,1)}, u32[]{:S(2)}, u32[]{:S(2)}) collective-permute-start(bf16[1024,256]{1,0:T(8,128)(2,1)} %collective-permute-done.5.refs_6_), channel_id=1, source_target_pairs={{0,14},{2,0},{4,2},{6,4},{8,6},{10,8},{12,10},{14,12},{1,15},{3,1}... | collective-permute-start | bytes 1572872 | tf_op jit(solution)/shard_map/ppermute | solution.py:346
  59.2 11.9 %collective-permute-start.4 = (bf16[1024,256]{1,0:T(8,128)(2,1)}, bf16[1024,256]{1,0:T(8,128)(2,1)}, u32[]{:S(2)}, u32[]{:S(2)}) collective-permute-start(bf16[1024,256]{1,0:T(8,128)(2,1)} %collective-permute-done.3.refs_3_), channel_id=1, source_target_pairs={{0,2},{2,4},{4,6},{6,8},{8,10},{10,12},{12,14},{14,0},{1,3},{3,5},... | collective-permute-start | bytes 1572872 | tf_op jit(solution)/shard_map/ppermute | solution.py:344
  59.8 18.4 %copy-start = (bf16[256,4096]{1,0:T(8,128)(2,1)S(1)}, bf16[256,4096]{1,0:T(8,128)(2,1)}, u32[]{:S(2)}) copy-start(bf16[256,4096]{1,0:T(8,128)(2,1)} %weight_ref.9) | copy-start | bytes 6291460
  59.8 18.4 %copy-start.3 = (s32[2]{0:T(128)S(1)}, s32[2]{0:T(128)}, u32[]{:S(2)}) copy-start(s32[2]{0:T(128)} %pad_add_fusion.1.place_ref) | copy-start | bytes 28
  78.1 2.4 %copy-start.6 = (s32[16,2]{0,1:T(2,128)S(1)}, s32[16,2]{0,1:T(2,128)}, u32[]{:S(2)}) copy-start(s32[16,2]{0,1:T(2,128)} %param.18) | copy-start | bytes 388
  78.1 4.8 %collective-permute-start.8 = (f32[1024,256]{1,0:T(8,128)}, f32[1024,256]{1,0:T(8,128)}, u32[]{:S(2)}, u32[]{:S(2)}) collective-permute-start(f32[1024,256]{1,0:T(8,128)} %get-tuple-element.29), channel_id=1, source_target_pairs={{0,1},{1,0},{2,3},{3,2},{4,5},{5,4},{6,7},{7,6},{8,9},{9,8},{10,11... | collective-permute-start | bytes 3145736 | tf_op jit(solution)/shard_map/ppermute | solution.py:354
  79.9 22.6 %collective-permute-start.10 = (bf16[8,256,256]{2,1,0:T(8,128)(2,1)}, bf16[8,256,256]{2,1,0:T(8,128)(2,1)S(1)}, u32[]{:S(2)}, u32[]{:S(2)}) collective-permute-start(bf16[8,256,256]{2,1,0:T(8,128)(2,1)} %relay.1), channel_id=1, source_target_pairs={{0,1},{1,0},{2,3},{3,2},{4,5},{5,4},{6,7},{7,6},{8,9},{9,8},{10,11... | collective-permute-start | bytes 3145736 | tf_op jit(solution)/shard_map/ppermute | solution.py:351
  97.2 5.3 %copy-start.2 = (bf16[512,256]{1,0:T(8,128)(2,1)S(1)}, bf16[512,256]{1,0:T(8,128)(2,1)}, u32[]{:S(2)}) copy-start(bf16[512,256]{1,0:T(8,128)(2,1)} %attend.2.own_ref) | copy-start | bytes 786436
  97.2 5.3 %collective-permute-start.9 = (bf16[512,256]{1,0:T(8,128)(2,1)}, bf16[512,256]{1,0:T(8,128)(2,1)S(1)}, u32[]{:S(2)}, u32[]{:S(2)}) collective-permute-start(bf16[512,256]{1,0:T(8,128)(2,1)} %attend.2.own_ref), channel_id=1, source_target_pairs={{0,1},{1,0},{2,3},{3,2},{4,5},{5,4},{6,7},{7,6},{8,9},{9,8},{10,11... | collective-permute-start | bytes 786440 | tf_op jit(solution)/shard_map/ppermute | solution.py:356
  101.9 4.9 %copy-start.1 = (bf16[512,256]{1,0:T(8,128)(2,1)S(1)}, bf16[512,256]{1,0:T(8,128)(2,1)}, u32[]{:S(2)}) copy-start(bf16[512,256]{1,0:T(8,128)(2,1)} %attend.3.own_ref) | copy-start | bytes 786436
  101.9 4.9 %collective-permute-start.18 = (bf16[512,256]{1,0:T(8,128)(2,1)}, bf16[512,256]{1,0:T(8,128)(2,1)S(1)}, u32[]{:S(2)}, u32[]{:S(2)}) collective-permute-start(bf16[512,256]{1,0:T(8,128)(2,1)} %attend.3.own_ref), channel_id=1, source_target_pairs={{0,1},{1,0},{2,3},{3,2},{4,5},{5,4},{6,7},{7,6},{8,9},{9,8},{10,11... | collective-permute-start | bytes 786440 | tf_op jit(solution)/shard_map/ppermute | solution.py:356
  103.5 10.7 %collective-permute-start.11 = (bf16[512,256]{1,0:T(8,128)(2,1)S(1)}, bf16[512,256]{1,0:T(8,128)(2,1)S(1)}, u32[]{:S(2)}, u32[]{:S(2)}) collective-permute-start(bf16[512,256]{1,0:T(8,128)(2,1)S(1)} %get-tuple-element.32), channel_id=1, source_target_pairs={{0,2},{2,4},{4,6},{6,8},{8,10},{10,12},{12,14},{14,0},{1,3},{3,5},... | collective-permute-start | bytes 786440 | tf_op jit(solution)/shard_map/ppermute | solution.py:283
  103.6 10.8 %collective-permute-start.15 = (bf16[512,256]{1,0:T(8,128)(2,1)S(1)}, bf16[512,256]{1,0:T(8,128)(2,1)S(1)}, u32[]{:S(2)}, u32[]{:S(2)}) collective-permute-start(bf16[512,256]{1,0:T(8,128)(2,1)S(1)} %get-tuple-element.36), channel_id=1, source_target_pairs={{0,14},{2,0},{4,2},{6,4},{8,6},{10,8},{12,10},{14,12},{1,15},{3,1}... | collective-permute-start | bytes 786440 | tf_op jit(solution)/shard_map/ppermute | solution.py:283
  107.8 11.8 %collective-permute-start.19 = (bf16[512,256]{1,0:T(8,128)(2,1)S(1)}, bf16[512,256]{1,0:T(8,128)(2,1)S(1)}, u32[]{:S(2)}, u32[]{:S(2)}) collective-permute-start(bf16[512,256]{1,0:T(8,128)(2,1)S(1)} %get-tuple-element.40), channel_id=1, source_target_pairs={{0,2},{2,4},{4,6},{6,8},{8,10},{10,12},{12,14},{14,0},{1,3},{3,5},... | collective-permute-start | bytes 786440 | tf_op jit(solution)/shard_map/ppermute | solution.py:283
  107.9 11.8 %collective-permute-start.22 = (bf16[512,256]{1,0:T(8,128)(2,1)S(1)}, bf16[512,256]{1,0:T(8,128)(2,1)S(1)}, u32[]{:S(2)}, u32[]{:S(2)}) collective-permute-start(bf16[512,256]{1,0:T(8,128)(2,1)S(1)} %get-tuple-element.43), channel_id=1, source_target_pairs={{0,14},{2,0},{4,2},{6,4},{8,6},{10,8},{12,10},{14,12},{1,15},{3,1}... | collective-permute-start | bytes 786440 | tf_op jit(solution)/shard_map/ppermute | solution.py:283
  114.2 10.9 %collective-permute-start.12 = (bf16[512,256]{1,0:T(8,128)(2,1)S(1)}, bf16[512,256]{1,0:T(8,128)(2,1)S(1)}, u32[]{:S(2)}, u32[]{:S(2)}) collective-permute-start(bf16[512,256]{1,0:T(8,128)(2,1)S(1)} %add_convert_fusion.11), channel_id=1, source_target_pairs={{0,2},{2,4},{4,6},{6,8},{8,10},{10,12},{12,14},{14,0},{1,3},{3,5},... | collective-permute-start | bytes 786440 | tf_op jit(solution)/shard_map/ppermute | solution.py:283
  114.4 10.9 %collective-permute-start.16 = (bf16[512,256]{1,0:T(8,128)(2,1)S(1)}, bf16[512,256]{1,0:T(8,128)(2,1)S(1)}, u32[]{:S(2)}, u32[]{:S(2)}) collective-permute-start(bf16[512,256]{1,0:T(8,128)(2,1)S(1)} %add_convert_fusion.8), channel_id=1, source_target_pairs={{0,14},{2,0},{4,2},{6,4},{8,6},{10,8},{12,10},{14,12},{1,15},{3,1}... | collective-permute-start | bytes 786440 | tf_op jit(solution)/shard_map/ppermute | solution.py:283
  119.6 16.0 %collective-permute-start.20 = (bf16[512,256]{1,0:T(8,128)(2,1)S(1)}, bf16[512,256]{1,0:T(8,128)(2,1)S(1)}, u32[]{:S(2)}, u32[]{:S(2)}) collective-permute-start(bf16[512,256]{1,0:T(8,128)(2,1)S(1)} %add_convert_fusion.5), channel_id=1, source_target_pairs={{0,2},{2,4},{4,6},{6,8},{8,10},{10,12},{12,14},{14,0},{1,3},{3,5},... | collective-permute-start | bytes 786440 | tf_op jit(solution)/shard_map/ppermute | solution.py:283
  119.8 10.6 %collective-permute-start.23 = (bf16[512,256]{1,0:T(8,128)(2,1)S(1)}, bf16[512,256]{1,0:T(8,128)(2,1)S(1)}, u32[]{:S(2)}, u32[]{:S(2)}) collective-permute-start(bf16[512,256]{1,0:T(8,128)(2,1)S(1)} %add_convert_fusion.3), channel_id=1, source_target_pairs={{0,14},{2,0},{4,2},{6,4},{8,6},{10,8},{12,10},{14,12},{1,15},{3,1}... | collective-permute-start | bytes 786440 | tf_op jit(solution)/shard_map/ppermute | solution.py:283
  125.2 10.3 %collective-permute-start.13 = (bf16[512,256]{1,0:T(8,128)(2,1)S(1)}, bf16[512,256]{1,0:T(8,128)(2,1)S(1)}, u32[]{:S(2)}, u32[]{:S(2)}) collective-permute-start(bf16[512,256]{1,0:T(8,128)(2,1)S(1)} %add_convert_fusion.10), channel_id=1, source_target_pairs={{0,2},{2,4},{4,6},{6,8},{8,10},{10,12},{12,14},{14,0},{1,3},{3,5},... | collective-permute-start | bytes 786440 | tf_op jit(solution)/shard_map/ppermute | solution.py:283
  125.4 18.8 %collective-permute-start.17 = (bf16[512,256]{1,0:T(8,128)(2,1)S(1)}, bf16[512,256]{1,0:T(8,128)(2,1)S(1)}, u32[]{:S(2)}, u32[]{:S(2)}) collective-permute-start(bf16[512,256]{1,0:T(8,128)(2,1)S(1)} %add_convert_fusion.7), channel_id=1, source_target_pairs={{0,14},{2,0},{4,2},{6,4},{8,6},{10,8},{12,10},{14,12},{1,15},{3,1}... | collective-permute-start | bytes 786440 | tf_op jit(solution)/shard_map/ppermute | solution.py:283
  130.4 9.9 %collective-permute-start.24 = (bf16[512,256]{1,0:T(8,128)(2,1)S(1)}, bf16[512,256]{1,0:T(8,128)(2,1)S(1)}, u32[]{:S(2)}, u32[]{:S(2)}) collective-permute-start(bf16[512,256]{1,0:T(8,128)(2,1)S(1)} %add_convert_fusion.2), channel_id=1, source_target_pairs={{0,14},{2,0},{4,2},{6,4},{8,6},{10,8},{12,10},{14,12},{1,15},{3,1}... | collective-permute-start | bytes 786440 | tf_op jit(solution)/shard_map/ppermute | solution.py:283
  135.6 10.5 %collective-permute-start.14 = (bf16[512,256]{1,0:T(8,128)(2,1)S(1)}, bf16[512,256]{1,0:T(8,128)(2,1)S(1)}, u32[]{:S(2)}, u32[]{:S(2)}) collective-permute-start(bf16[512,256]{1,0:T(8,128)(2,1)S(1)} %add_convert_fusion.9), channel_id=1, source_target_pairs={{0,2},{2,4},{4,6},{6,8},{8,10},{10,12},{12,14},{14,0},{1,3},{3,5},... | collective-permute-start | bytes 786440 | tf_op jit(solution)/shard_map/ppermute | solution.py:283
  135.7 14.1 %collective-permute-start.21 = (bf16[512,256]{1,0:T(8,128)(2,1)S(1)}, bf16[512,256]{1,0:T(8,128)(2,1)S(1)}, u32[]{:S(2)}, u32[]{:S(2)}) collective-permute-start(bf16[512,256]{1,0:T(8,128)(2,1)S(1)} %add_convert_fusion.4), channel_id=1, source_target_pairs={{0,2},{2,4},{4,6},{6,8},{8,10},{10,12},{12,14},{14,0},{1,3},{3,5},... | collective-permute-start | bytes 786440 | tf_op jit(solution)/shard_map/ppermute | solution.py:283
  140.4 9.4 %collective-permute-start.25 = (bf16[512,256]{1,0:T(8,128)(2,1)S(1)}, bf16[512,256]{1,0:T(8,128)(2,1)S(1)}, u32[]{:S(2)}, u32[]{:S(2)}) collective-permute-start(bf16[512,256]{1,0:T(8,128)(2,1)S(1)} %add_convert_fusion.1), channel_id=1, source_target_pairs={{0,14},{2,0},{4,2},{6,4},{8,6},{10,8},{12,10},{14,12},{1,15},{3,1}... | collective-permute-start | bytes 786440 | tf_op jit(solution)/shard_map/ppermute | solution.py:283

commit v8 on v7

--- a/solution.py
+++ b/solution.py
@@ -21,6 +21,7 @@
 VMEM = pl.BlockSpec(memory_space=pltpu.VMEM)
 SMEM = pl.BlockSpec(memory_space=pltpu.SMEM)
 ANY = pl.BlockSpec(memory_space=pl.ANY)
+SMALL = pl.CostEstimate(flops=1024, bytes_accessed=1024, transcendentals=0)
 
 
 def unit(values):
@@ -137,11 +138,34 @@
     )(place, *pieces, weight, partner_weight)
 
 
+def finish_kernel(own_ref, lent_ref, out_ref):
+    for h in range(out_ref.shape[1] // HD):
+        cols = slice(h * HD, (h + 1) * HD)
+        out_ref[:, cols] = unit(own_ref[:, cols] + lent_ref[:, cols]).astype(BF16)
+
+
+def finish_queries(own, lent):
+    return pl.pallas_call(
+        finish_kernel,
+        out_shape=jax.ShapeDtypeStruct(own.shape, BF16),
+        in_specs=[VMEM, VMEM],
+        out_specs=VMEM,
+        compiler_params=pltpu.CompilerParams(vmem_limit_bytes=8 << 20),
+        cost_estimate=pl.CostEstimate(flops=1 << 20, bytes_accessed=3 << 20, transcendentals=0),
+        name="finish_queries",
+    )(own, lent)
+
+
 def attend_kernel(
-    first, slot_ref, length_ref, own_ref, lent_ref, rows_ref, out_ref, query_ref, held_ref, sems
+    part, slot_ref, length_ref, queries_ref, rows_ref, out_ref, query_ref, held_ref, sems, query_sem
 ):
     spans = slot_ref.shape[0] // NBRS
     count = sems.shape[0] // NBRS
+    first = part * count
+    query_copy = pltpu.make_async_copy(
+        queries_ref.at[pl.ds(first * SPAN, count * SPAN)], query_ref, query_sem
+    )
+    query_copy.start()
     width = out_ref.shape[1]
     keys = NBRS * NBR_LEN
     factor = 2.0 / math.sqrt(HD)
@@ -155,9 +179,7 @@
             )
             copy.start()
             copies.append(copy)
-    for h in range(width // HD):
-        cols = slice(h * HD, (h + 1) * HD)
-        query_ref[:, cols] = unit(own_ref[:, cols] + lent_ref[:, cols]).astype(BF16)
+    query_copy.wait()
     places = lax.broadcasted_iota(jnp.int32, (SPAN, keys), 1)
     group = 4
     for start in range(0, count, group):
@@ -186,27 +208,24 @@
             out_ref[c * SPAN : (c + 1) * SPAN, h * HD : (h + 1) * HD] = result.astype(BF16)
 
 
-def attend(part, parts, slot_index, lengths, own, lent, rows):
-    tokens, width = own.shape[0] // parts, own.shape[1]
-    count = tokens // SPAN
-    requests = count * NBRS
-    return pl.pallas_call(
-        functools.partial(attend_kernel, part * count),
-        grid=(1,),
+def attend(part, parts, slot_index, lengths, queries, rows):
+    tokens, width = queries.shape[0] // parts, queries.shape[1]
+    requests = tokens // SPAN * NBRS
+    return pl.pallas_call(
+        functools.partial(attend_kernel, part),
         out_shape=jax.ShapeDtypeStruct((tokens, width), BF16),
-        in_specs=[SMEM, SMEM] + [pl.BlockSpec((tokens, width), lambda i: (part, 0))] * 2 + [ANY],
-        out_specs=pl.BlockSpec((tokens, width), lambda i: (0, 0)),
+        in_specs=[SMEM, SMEM, ANY, ANY],
+        out_specs=VMEM,
         scratch_shapes=[
             pltpu.VMEM((tokens, width), BF16),
             pltpu.VMEM((requests * NBR_LEN, rows.shape[2]), BF16),
             pltpu.SemaphoreType.DMA((requests,)),
+            pltpu.SemaphoreType.DMA,
         ],
         compiler_params=pltpu.CompilerParams(vmem_limit_bytes=56 << 20),
-        cost_estimate=pl.CostEstimate(
-            flops=4 * tokens * NBRS * NBR_LEN * width, bytes_accessed=3 << 20, transcendentals=0
-        ),
+        cost_estimate=SMALL,
         name="attend",
-    )(slot_index, lengths, own, lent, rows)
+    )(slot_index, lengths, queries, rows)
 
 
 def relay_kernel(place_ref, weight_ref, lent_ref):
@@ -251,9 +270,7 @@
         in_specs=[SMEM] + [VMEM] * 4,
         out_specs=[VMEM] * len(steps),
         compiler_params=pltpu.CompilerParams(vmem_limit_bytes=12 << 20),
-        cost_estimate=pl.CostEstimate(
-            flops=4 * rows * width * width * len(steps), bytes_accessed=4 << 20, transcendentals=0
-        ),
+        cost_estimate=SMALL,
         name="shares",
     )(place, own, partner, weight, partner_weight)
 
@@ -261,6 +278,10 @@
 def reduce_ring(place, attended, partner_attended, weight, partner_weight, ring):
     up = [(i, (i + 1) % ring) for i in range(ring)]
     down = [(i, (i - 1) % ring) for i in range(ring)]
+
+    def send(sums, way):
+        return lax.ppermute(sums, "z", up if way == 1 else down)
+
     far = ring // 2
     chains = [(0, 1, far), (1, -1, far), (0, -1, far - 1), (1, 1, far - 1)]
     held, part = {}, {}
@@ -270,17 +291,14 @@
         rest = [k for k in range(ring) if k not in starts]
         operands = (attended[half], partner_attended[half], weight, partner_weight)
         begun = shares(place, starts, BF16, *operands)
-        held.update({(half, way): begun[i] for i, (way, _) in enumerate(mine)})
+        held.update({(half, way): send(begun[i], way) for i, (way, _) in enumerate(mine)})
         others = shares(place, rest, F32, *operands)
         part.update({(half, k): others[i] for i, k in enumerate(rest)})
     for distance in range(far, 0, -1):
         for half, way, first in chains:
-            if distance > first:
-                continue
             if distance < first:
                 total = held[half, way].astype(F32) + part[half, way * distance % ring]
-                held[half, way] = total.astype(BF16)
-            held[half, way] = lax.ppermute(held[half, way], "z", up if way == 1 else down)
+                held[half, way] = send(total.astype(BF16), way)
     out = [
         (part[half, 0] + held[half, 1].astype(F32) + held[half, -1].astype(F32)).astype(BF16)
         for half in range(2)
@@ -320,9 +338,8 @@
     down = [(i, (i - 1) % ring) for i in range(ring)]
     pieces = {0: tokens, 1: lax.ppermute(tokens, "z", up)}
     pieces[ring - 1] = lax.ppermute(tokens, "z", down)
-    sent, pieces[1], pieces[ring - 1] = lax.optimization_barrier(
-        (sent, pieces[1], pieces[ring - 1])
-    )
+    sent, pieces[1] = lax.optimization_barrier((sent, pieces[1]))
+    _, pieces[ring - 1] = lax.optimization_barrier((sent, pieces[ring - 1]))
     rows = lax.all_to_all(sent, DB, split_axis=0, concat_axis=0, tiled=True)
     rows = rows.reshape(shards * NBRS, NBR_LEN, 2 * width)
 
@@ -352,7 +369,9 @@
 
     own, lent = project_queries(place, [pieces[k] for k in range(ring)], by_core, partner_rows)
     lent = lax.ppermute(lent, "c", swap)
-    attended = [attend(part, 2, slot_index, lengths, own, lent, rows) for part in range(2)]
+    queries = finish_queries(own, lent)
+
+    attended = [attend(part, 2, slot_index, lengths, queries, rows) for part in range(2)]
     partner_attended = [lax.ppermute(part, "c", swap) for part in attended]
     return reduce_ring(place, attended, partner_attended, out_weight, partner_weight, ring)
 

time: 151 us -> 150 us (level)
  waiting for transfers between devices: 57.3 us -> 55 us
    ppermute x3, waiting for transfers between devices: 26.3 us -> 3.42 us  [local(): pieces[k] = lax.ppermute(pieces[k - 1], 'z', up)]
    ppermute x2, waiting for transfers between devices: 3.65 us -> 17.3 us  [local(): pieces[ring - k] = lax.ppermute(pieces[ring - k + 1], 'z', down)]
    ppermute x1, waiting for transfers between devices: 0.01 us -> 10.2 us  [local(): pieces[ring - 1] = lax.ppermute(tokens, 'z', down)]
    all_to_all x1, waiting for transfers between devices: 9.79 us -> 1.66 us  [local(): rows = lax.all_to_all(sent, DB, split_axis=0, concat_axis=0, tiled=True)]
    ppermute x14, waiting for transfers between devices: 16.9 us -> 21.7 us  [send(): return lax.ppermute(sums, 'z', up if way == 1 else down)]
    pallas_call x2 -> x3, Pallas kernels: 8.88 us -> 10.1 us  [the longest x2 8.51 us: attend(): pl.pallas_call(functools.partial(attend_kernel, part), out_shape=jax.Shap...]
  transfers between devices with their start and end apart: 28 -> 28, of which waited for: 14 -> 14; matrix products, arithmetic and copies ran while one was open for 4% -> 4% of each run, Pallas kernels for 21% -> 22%
where the time goes in v8:
time: 150 us; the launch traced here: 149 us
  waiting for transfers between devices  55 us (37%)
  starting transfers between devices  51.9 us (35%)
  Pallas kernels  32.5 us (22%)
  local copies, waits for them, and re-layouts  5.04 us (3%)
  other arithmetic  4.55 us (3%)
    ppermute x14, starting transfers between devices, send(): return lax.ppermute(sums, 'z', up if way == 1 else down)  23.5 us
    ppermute x14, waiting for transfers between devices, send(): return lax.ppermute(sums, 'z', up if way == 1 else down)  21.7 us
    ppermute x2, waiting for transfers between devices, local(): pieces[ring - k] = lax.ppermute(pieces[ring - k + 1], 'z', down)  17.3 us
    ppermute x1, waiting for transfers between devices, local(): pieces[ring - 1] = lax.ppermute(tokens, 'z', down)  10.2 us
    pallas_call x2, Pallas kernels, attend(): pl.pallas_call(functools.partial(attend_kernel, part), out_shape=jax.Shap...  8.51 us
    ppermute x2, starting transfers between devices, local(): pieces[ring - k] = lax.ppermute(pieces[ring - k + 1], 'z', down)  7.38 us
    all_to_all x1, starting transfers between devices, local(): heard = lax.all_to_all(notes, DB, split_axis=0, concat_axis=0, tiled=True)  7.17 us
    pallas_call x1, Pallas kernels, project_queries(): pl.pallas_call(query_kernel, grid=(rows // tile,), out_shape=(out, out),...  6.94 us
  transfers between devices with their start and end apart: 28, of which 14 were waited for; matrix products, arithmetic and copies ran while one was open for 4% of the time, Pallas kernels for 22%

profile of v8, /device:TPU:24, one launch (start us, length us, event | category | flops | bytes accessed | tf_op | source)
XLA Modules:
  0.0 149.3 jit_solution(17745088309192322753)
XLA Ops:
  0.0 1.9 %collective-permute-start = (bf16[1024,256]{1,0:T(8,128)(2,1)}, bf16[1024,256]{1,0:T(8,128)(2,1)}, u32[]{:S(2)}, u32[]{:S(2)}) collective-permute-start(bf16[1024,256]{1,0:T(8,128)(2,1)} %refs_0_.1), channel_id=1, source_target_pairs={{0,2},{2,4},{4,6},{6,8},{8,10},{10,12},{12,14},{14,0},{1,3},{3,5},... | collective-permute-start | bytes 1572872 | tf_op jit(solution)/shard_map/ppermute | solution.py:339
  1.9 0.7 pad_bitcast_fusion
  2.6 0.7 bitcast_add_fusion
  3.3 0.6 broadcast_in_dim.27
  3.9 7.2 %all-to-all-start = ((s32[16,3,16]{2,1,0:T(4,128)}), s32[16,3,16]{2,1,0:T(4,128)S(1)}, u32[]{:S(2)}, u32[]{:S(2)}) async-start(s32[16,3,16]{2,1,0:T(4,128)} %broadcast_in_dim.27), calls=%async_computation | async-start | bytes 65536 | tf_op jit(solution)/shard_map/all_to_all | solution.py:334
  11.1 4.9 %project_blocks.1.rows_ref = bf16[8,128,512]{2,1,0:T(8,128)(2,1)} custom-call(f32[8,7]{1,0:T(8,128)} %scales_ref.1, bf16[8,128,896]{2,1,0:T(8,128)(2,1)} %codes_ref.1, bf16[896,256]{1,0:T(8,128)(2,1)} %key_ref.1, bf16[896,256]{1,0:T(8,128)(2,1)} %value_ref.1), custom_call_target="tpu_custom_call" | custom-call | flops 939524096 | bytes 5242880 | tf_op jit(solution)/shard_map/project_blocks/pallas_call | solution.py:53
  15.9 0.8 all-to-all-done.heard_ref
  16.7 0.6 copy-done.7
  17.3 4.0 %select_blocks.1 = bf16[16,2,128,512]{3,2,1,0:T(8,128)(2,1)} custom-call(s32[1]{0:T(128)} %bitcast.5.place_ref, s32[16,3,16]{2,1,0:T(4,128)} %copy-done.7, bf16[8,128,512]{2,1,0:T(8,128)(2,1)} %project_blocks.1.rows_ref), custom_call_target="tpu_custom_call" | custom-call | bytes 9437184 | tf_op jit(solution)/shard_map/select_blocks/pallas_call | solution.py:92
  21.3 6.6 %all-to-all-start.1 = ((bf16[16,2,128,512]{3,2,1,0:T(8,128)(2,1)}), bf16[16,2,128,512]{3,2,1,0:T(8,128)(2,1)}, u32[]{:S(2)}, u32[]{:S(2)}) async-start(bf16[16,2,128,512]{3,2,1,0:T(8,128)(2,1)} %select_blocks.1), calls=%async_computation.1 | async-start | bytes 8388608 | tf_op jit(solution)/shard_map/all_to_all | solution.py:343
  27.9 3.9 %collective-permute-start.4 = (bf16[1024,256]{1,0:T(8,128)(2,1)}, bf16[1024,256]{1,0:T(8,128)(2,1)}, u32[]{:S(2)}, u32[]{:S(2)}) collective-permute-start(bf16[1024,256]{1,0:T(8,128)(2,1)} %refs_0_.1), channel_id=1, source_target_pairs={{0,14},{2,0},{4,2},{6,4},{8,6},{10,8},{12,10},{14,12},{1,15},{3,1}... | collective-permute-start | bytes 1572872 | tf_op jit(solution)/shard_map/ppermute | solution.py:340
  32.1 10.2 %collective-permute-done.4.refs_7_ = bf16[1024,256]{1,0:T(8,128)(2,1)} collective-permute-done((bf16[1024,256]{1,0:T(8,128)(2,1)}, bf16[1024,256]{1,0:T(8,128)(2,1)}, u32[]{:S(2)}, u32[]{:S(2)}) %collective-permute-start.4) | collective-permute-done | bytes 524320 | tf_op jit(solution)/shard_map/ppermute | solution.py:340
  42.3 3.7 %collective-permute-start.5 = (bf16[1024,256]{1,0:T(8,128)(2,1)}, bf16[1024,256]{1,0:T(8,128)(2,1)}, u32[]{:S(2)}, u32[]{:S(2)}) collective-permute-start(bf16[1024,256]{1,0:T(8,128)(2,1)} %collective-permute-done.4.refs_7_), channel_id=1, source_target_pairs={{0,14},{2,0},{4,2},{6,4},{8,6},{10,8},{12,10},{14,12},{1,15},{3,1}... | collective-permute-start | bytes 1572872 | tf_op jit(solution)/shard_map/ppermute | solution.py:363
  46.0 9.5 %collective-permute-done.5.refs_6_ = bf16[1024,256]{1,0:T(8,128)(2,1)} collective-permute-done((bf16[1024,256]{1,0:T(8,128)(2,1)}, bf16[1024,256]{1,0:T(8,128)(2,1)}, u32[]{:S(2)}, u32[]{:S(2)}) %collective-permute-start.5) | collective-permute-done | bytes 524320 | tf_op jit(solution)/shard_map/ppermute | solution.py:363
  55.4 3.7 %collective-permute-start.6 = (bf16[1024,256]{1,0:T(8,128)(2,1)}, bf16[1024,256]{1,0:T(8,128)(2,1)}, u32[]{:S(2)}, u32[]{:S(2)}) collective-permute-start(bf16[1024,256]{1,0:T(8,128)(2,1)} %collective-permute-done.5.refs_6_), channel_id=1, source_target_pairs={{0,14},{2,0},{4,2},{6,4},{8,6},{10,8},{12,10},{14,12},{1,15},{3,1}... | collective-permute-start | bytes 1572872 | tf_op jit(solution)/shard_map/ppermute | solution.py:363
  59.1 0.7 pad_add_fusion.1.place_ref
  59.8 7.9 %collective-permute-done.6.refs_5_ = bf16[1024,256]{1,0:T(8,128)(2,1)} collective-permute-done((bf16[1024,256]{1,0:T(8,128)(2,1)}, bf16[1024,256]{1,0:T(8,128)(2,1)}, u32[]{:S(2)}, u32[]{:S(2)}) %collective-permute-start.6) | collective-permute-done | bytes 524320 | tf_op jit(solution)/shard_map/ppermute | solution.py:363
  67.7 3.4 %collective-permute-done.3.refs_4_ = bf16[1024,256]{1,0:T(8,128)(2,1)} collective-permute-done((bf16[1024,256]{1,0:T(8,128)(2,1)}, bf16[1024,256]{1,0:T(8,128)(2,1)}, u32[]{:S(2)}, u32[]{:S(2)}) %collective-permute-start.3) | collective-permute-done | bytes 524320 | tf_op jit(solution)/shard_map/ppermute | solution.py:361
  71.1 6.9 %project_queries.1 = (f32[1024,256]{1,0:T(8,128)}, f32[1024,256]{1,0:T(8,128)}) custom-call(s32[2]{0:T(128)} %pad_add_fusion.1.place_ref, bf16[1024,256]{1,0:T(8,128)(2,1)} %refs_0_.1, bf16[1024,256]{1,0:T(8,128)(2,1)} %collective-permute-done.refs_1_, bf16[1024,256]{1,0:T(8,128)(2,1)} %collective-permute-done.1.refs_2_, ...), custom_call_target="tpu_custom_call" | custom-call | flops 2147483648 | bytes 9437184 | tf_op jit(solution)/shard_map/project_queries/pallas_call | solution.py:122
  78.1 1.7 %relay.1 = bf16[8,256,256]{2,1,0:T(8,128)(2,1)} custom-call(s32[2]{0:T(128)S(1)} %copy-done.5, bf16[256,4096]{1,0:T(8,128)(2,1)S(1)} %copy-done), custom_call_target="tpu_custom_call" | custom-call | bytes 3145728 | tf_op jit(solution)/shard_map/relay/pallas_call | solution.py:242
  80.6 0.6 multiply_add_fusion.slot_ref
  81.2 0.8 slice_reduce_fusion
  82.1 0.8 select_reduce_fusion.length_ref
  82.9 1.2 copy-done.4
  84.1 1.6 %finish_queries.1.queries_ref = bf16[1024,256]{1,0:T(8,128)(2,1)S(1)} custom-call(f32[1024,256]{1,0:T(8,128)S(1)} %copy-done.4, f32[1024,256]{1,0:T(8,128)} %collective-permute-done.8.lent_ref), custom_call_target="tpu_custom_call" | custom-call | flops 1048576 | bytes 3145728 | tf_op jit(solution)/shard_map/finish_queries/pallas_call | solution.py:148
  85.7 0.8 copy-done.1
  86.5 1.7 %all-to-all-done.1 = bf16[16,2,128,512]{3,2,1,0:T(8,128)(2,1)} async-done(((bf16[16,2,128,512]{3,2,1,0:T(8,128)(2,1)}), bf16[16,2,128,512]{3,2,1,0:T(8,128)(2,1)}, u32[]{:S(2)}, u32[]{:S(2)}) %all-to-all-start.1) | async-done | bytes 4194336 | tf_op jit(solution)/shard_map/all_to_all | solution.py:343
  88.1 4.2 %attend.3.own_ref = bf16[512,256]{1,0:T(8,128)(2,1)} custom-call(s32[32]{0:T(128)} %multiply_add_fusion.slot_ref, s32[32]{0:T(128)} %select_reduce_fusion.length_ref, bf16[1024,256]{1,0:T(8,128)(2,1)} %copy-done.1, bf16[32,128,512]{2,1,0:T(8,128)(2,1)} %bitcast.8.rows_ref), custom_call_target="tpu_custom_call" | custom-call | flops 1024 | bytes 1024 | tf_op jit(solution)/shard_map/attend/pallas_call | solution.py:214
  92.5 4.3 %attend.2.own_ref = bf16[512,256]{1,0:T(8,128)(2,1)} custom-call(s32[32]{0:T(128)} %multiply_add_fusion.slot_ref, s32[32]{0:T(128)} %select_reduce_fusion.length_ref, bf16[1024,256]{1,0:T(8,128)(2,1)} %copy-done.1, bf16[32,128,512]{2,1,0:T(8,128)(2,1)} %bitcast.8.rows_ref), custom_call_target="tpu_custom_call" | custom-call | flops 1024 | bytes 1024 | tf_op jit(solution)/shard_map/attend/pallas_call | solution.py:214
  97.4 1.0 shares.7
  98.4 4.3 %collective-permute-start.22 = (bf16[512,256]{1,0:T(8,128)(2,1)S(1)}, bf16[512,256]{1,0:T(8,128)(2,1)S(1)}, u32[]{:S(2)}, u32[]{:S(2)}) collective-permute-start(bf16[512,256]{1,0:T(8,128)(2,1)S(1)} %get-tuple-element.43), channel_id=1, source_target_pairs={{0,14},{2,0},{4,2},{6,4},{8,6},{10,8},{12,10},{14,12},{1,15},{3,1}... | collective-permute-start | bytes 786440 | tf_op jit(solution)/shard_map/ppermute | solution.py:283
  102.7 1.0 shares.5
  103.7 3.3 %collective-permute-start.15 = (bf16[512,256]{1,0:T(8,128)(2,1)S(1)}, bf16[512,256]{1,0:T(8,128)(2,1)S(1)}, u32[]{:S(2)}, u32[]{:S(2)}) collective-permute-start(bf16[512,256]{1,0:T(8,128)(2,1)S(1)} %get-tuple-element.36), channel_id=1, source_target_pairs={{0,14},{2,0},{4,2},{6,4},{8,6},{10,8},{12,10},{14,12},{1,15},{3,1}... | collective-permute-start | bytes 786440 | tf_op jit(solution)/shard_map/ppermute | solution.py:283
  107.0 1.5 %shares.6 = (f32[512,256]{1,0:T(8,128)S(1)}, f32[512,256]{1,0:T(8,128)S(1)}, f32[512,256]{1,0:T(8,128)S(1)}, f32[512,256]{1,0:T(8,128)S(1)}, f32[512,256]{1,0:T(8,128)S(1)}, /*index=5*/f32[512,256]{1,0:T(8,128)S(1)}) custom-call(s32[2]{0:T(128)S(1)} %copy-done.5, bf16[512,256]{1,0:T(8,128)(2,1)S(1)} %copy-done.3, ...), custom_call_target="tpu_custom_call" | custom-call | flops 1024 | bytes 1024 | tf_op jit(solution)/shard_map/shares/pallas_call | solution.py:267
  108.5 1.5 %shares.4 = (f32[512,256]{1,0:T(8,128)S(1)}, f32[512,256]{1,0:T(8,128)S(1)}, f32[512,256]{1,0:T(8,128)S(1)}, f32[512,256]{1,0:T(8,128)S(1)}, f32[512,256]{1,0:T(8,128)S(1)}, /*index=5*/f32[512,256]{1,0:T(8,128)S(1)}) custom-call(s32[2]{0:T(128)S(1)} %copy-done.5, bf16[512,256]{1,0:T(8,128)(2,1)S(1)} %copy-done.2, ...), custom_call_target="tpu_custom_call" | custom-call | flops 1024 | bytes 1024 | tf_op jit(solution)/shard_map/shares/pallas_call | solution.py:267
  110.1 3.3 %collective-permute-start.23 = (bf16[512,256]{1,0:T(8,128)(2,1)S(1)}, bf16[512,256]{1,0:T(8,128)(2,1)S(1)}, u32[]{:S(2)}, u32[]{:S(2)}) collective-permute-start(bf16[512,256]{1,0:T(8,128)(2,1)S(1)} %add_convert_fusion.3), channel_id=1, source_target_pairs={{0,14},{2,0},{4,2},{6,4},{8,6},{10,8},{12,10},{14,12},{1,15},{3,1}... | collective-permute-start | bytes 786440 | tf_op jit(solution)/shard_map/ppermute | solution.py:283
  113.6 1.4 collective-permute-done.15
  115.0 3.8 %collective-permute-start.16 = (bf16[512,256]{1,0:T(8,128)(2,1)S(1)}, bf16[512,256]{1,0:T(8,128)(2,1)S(1)}, u32[]{:S(2)}, u32[]{:S(2)}) collective-permute-start(bf16[512,256]{1,0:T(8,128)(2,1)S(1)} %add_convert_fusion.8), channel_id=1, source_target_pairs={{0,14},{2,0},{4,2},{6,4},{8,6},{10,8},{12,10},{14,12},{1,15},{3,1}... | collective-permute-start | bytes 786440 | tf_op jit(solution)/shard_map/ppermute | solution.py:283
  119.0 1.6 %collective-permute-done.23 = bf16[512,256]{1,0:T(8,128)(2,1)S(1)} collective-permute-done((bf16[512,256]{1,0:T(8,128)(2,1)S(1)}, bf16[512,256]{1,0:T(8,128)(2,1)S(1)}, u32[]{:S(2)}, u32[]{:S(2)}) %collective-permute-start.23) | collective-permute-done | bytes 262176 | tf_op jit(solution)/shard_map/ppermute | solution.py:283
  120.7 4.0 %collective-permute-start.24 = (bf16[512,256]{1,0:T(8,128)(2,1)S(1)}, bf16[512,256]{1,0:T(8,128)(2,1)S(1)}, u32[]{:S(2)}, u32[]{:S(2)}) collective-permute-start(bf16[512,256]{1,0:T(8,128)(2,1)S(1)} %add_convert_fusion.2), channel_id=1, source_target_pairs={{0,14},{2,0},{4,2},{6,4},{8,6},{10,8},{12,10},{14,12},{1,15},{3,1}... | collective-permute-start | bytes 786440 | tf_op jit(solution)/shard_map/ppermute | solution.py:283
  124.8 5.1 %collective-permute-done.12 = bf16[512,256]{1,0:T(8,128)(2,1)S(1)} collective-permute-done((bf16[512,256]{1,0:T(8,128)(2,1)S(1)}, bf16[512,256]{1,0:T(8,128)(2,1)S(1)}, u32[]{:S(2)}, u32[]{:S(2)}) %collective-permute-start.12) | collective-permute-done | bytes 262176 | tf_op jit(solution)/shard_map/ppermute | solution.py:283
  130.1 0.8 collective-permute-done.24
  131.0 3.8 %collective-permute-start.25 = (bf16[512,256]{1,0:T(8,128)(2,1)S(1)}, bf16[512,256]{1,0:T(8,128)(2,1)S(1)}, u32[]{:S(2)}, u32[]{:S(2)}) collective-permute-start(bf16[512,256]{1,0:T(8,128)(2,1)S(1)} %add_convert_fusion.1), channel_id=1, source_target_pairs={{0,14},{2,0},{4,2},{6,4},{8,6},{10,8},{12,10},{14,12},{1,15},{3,1}... | collective-permute-start | bytes 786440 | tf_op jit(solution)/shard_map/ppermute | solution.py:283
  135.4 4.5 %collective-permute-done.13 = bf16[512,256]{1,0:T(8,128)(2,1)S(1)} collective-permute-done((bf16[512,256]{1,0:T(8,128)(2,1)S(1)}, bf16[512,256]{1,0:T(8,128)(2,1)S(1)}, u32[]{:S(2)}, u32[]{:S(2)}) %collective-permute-start.13) | collective-permute-done | bytes 262176 | tf_op jit(solution)/shard_map/ppermute | solution.py:283
  140.1 1.4 collective-permute-done.25
  141.6 3.7 %collective-permute-done.17 = bf16[512,256]{1,0:T(8,128)(2,1)S(1)} collective-permute-done((bf16[512,256]{1,0:T(8,128)(2,1)S(1)}, bf16[512,256]{1,0:T(8,128)(2,1)S(1)}, u32[]{:S(2)}, u32[]{:S(2)}) %collective-permute-start.17) | collective-permute-done | bytes 262176 | tf_op jit(solution)/shard_map/ppermute | solution.py:283
  145.3 3.1 %collective-permute-done.14 = bf16[512,256]{1,0:T(8,128)(2,1)S(1)} collective-permute-done((bf16[512,256]{1,0:T(8,128)(2,1)S(1)}, bf16[512,256]{1,0:T(8,128)(2,1)S(1)}, u32[]{:S(2)}, u32[]{:S(2)}) %collective-permute-start.14) | collective-permute-done | bytes 262176 | tf_op jit(solution)/shard_map/ppermute | solution.py:283
  148.5 0.8 pad_maximum_fusion
  (63 shorter events, 3.7 us)
Async XLA Ops:
  0.0 21.3 %collective-permute-start = (bf16[1024,256]{1,0:T(8,128)(2,1)}, bf16[1024,256]{1,0:T(8,128)(2,1)}, u32[]{:S(2)}, u32[]{:S(2)}) collective-permute-start(bf16[1024,256]{1,0:T(8,128)(2,1)} %refs_0_.1), channel_id=1, source_target_pairs={{0,2},{2,4},{4,6},{6,8},{8,10},{10,12},{12,14},{14,0},{1,3},{3,5},... | collective-permute-start | bytes 1572872 | tf_op jit(solution)/shard_map/ppermute | solution.py:339
  3.9 12.8 %all-to-all-start = ((s32[16,3,16]{2,1,0:T(4,128)}), s32[16,3,16]{2,1,0:T(4,128)S(1)}, u32[]{:S(2)}, u32[]{:S(2)}) async-start(s32[16,3,16]{2,1,0:T(4,128)} %broadcast_in_dim.27), calls=%async_computation | async-start | bytes 65536 | tf_op jit(solution)/shard_map/all_to_all | solution.py:334
  16.7 0.6 copy-start.7
  21.3 10.6 %copy-start.6 = (bf16[4096,256]{1,0:T(8,128)(2,1)S(1)}, bf16[4096,256]{1,0:T(8,128)(2,1)}, u32[]{:S(2)}) copy-start(bf16[4096,256]{1,0:T(8,128)(2,1)} %param.11) | copy-start | bytes 6291460
  21.3 66.8 %all-to-all-start.1 = ((bf16[16,2,128,512]{3,2,1,0:T(8,128)(2,1)}), bf16[16,2,128,512]{3,2,1,0:T(8,128)(2,1)}, u32[]{:S(2)}, u32[]{:S(2)}) async-start(bf16[16,2,128,512]{3,2,1,0:T(8,128)(2,1)} %select_blocks.1), calls=%async_computation.1 | async-start | bytes 8388608 | tf_op jit(solution)/shard_map/all_to_all | solution.py:343
  27.9 14.3 %collective-permute-start.4 = (bf16[1024,256]{1,0:T(8,128)(2,1)}, bf16[1024,256]{1,0:T(8,128)(2,1)}, u32[]{:S(2)}, u32[]{:S(2)}) collective-permute-start(bf16[1024,256]{1,0:T(8,128)(2,1)} %refs_0_.1), channel_id=1, source_target_pairs={{0,14},{2,0},{4,2},{6,4},{8,6},{10,8},{12,10},{14,12},{1,15},{3,1}... | collective-permute-start | bytes 1572872 | tf_op jit(solution)/shard_map/ppermute | solution.py:340
  31.9 14.1 %collective-permute-start.1 = (bf16[1024,256]{1,0:T(8,128)(2,1)}, bf16[1024,256]{1,0:T(8,128)(2,1)}, u32[]{:S(2)}, u32[]{:S(2)}) collective-permute-start(bf16[1024,256]{1,0:T(8,128)(2,1)} %collective-permute-done.refs_1_), channel_id=1, source_target_pairs={{0,2},{2,4},{4,6},{6,8},{8,10},{10,12},{12,14},{14,0},{1,3},{3,5},... | collective-permute-start | bytes 1572872 | tf_op jit(solution)/shard_map/ppermute | solution.py:361
  32.0 27.8 %collective-permute-start.7 = (bf16[8,256,256]{2,1,0:T(8,128)(2,1)S(1)}, bf16[8,256,256]{2,1,0:T(8,128)(2,1)}, u32[]{:S(2)}, u32[]{:S(2)}) collective-permute-start(bf16[8,256,256]{2,1,0:T(8,128)(2,1)S(1)} %dynamic-slice_bitcast_fusion), channel_id=1, source_target_pairs={{0,1},{1,0},{2,3},{3,2},{4,5},{5,4},{6,7},{7,6},{8,9},{9,8},{10,11... | collective-permute-start | bytes 3145736 | tf_op jit(solution)/shard_map/ppermute | solution.py:366
  42.3 13.2 %collective-permute-start.5 = (bf16[1024,256]{1,0:T(8,128)(2,1)}, bf16[1024,256]{1,0:T(8,128)(2,1)}, u32[]{:S(2)}, u32[]{:S(2)}) collective-permute-start(bf16[1024,256]{1,0:T(8,128)(2,1)} %collective-permute-done.4.refs_7_), channel_id=1, source_target_pairs={{0,14},{2,0},{4,2},{6,4},{8,6},{10,8},{12,10},{14,12},{1,15},{3,1}... | collective-permute-start | bytes 1572872 | tf_op jit(solution)/shard_map/ppermute | solution.py:363
  46.0 13.2 %collective-permute-start.2 = (bf16[1024,256]{1,0:T(8,128)(2,1)}, bf16[1024,256]{1,0:T(8,128)(2,1)}, u32[]{:S(2)}, u32[]{:S(2)}) collective-permute-start(bf16[1024,256]{1,0:T(8,128)(2,1)} %collective-permute-done.1.refs_2_), channel_id=1, source_target_pairs={{0,2},{2,4},{4,6},{6,8},{8,10},{10,12},{12,14},{14,0},{1,3},{3,5},... | collective-permute-start | bytes 1572872 | tf_op jit(solution)/shard_map/ppermute | solution.py:361
  55.4 12.2 %collective-permute-start.6 = (bf16[1024,256]{1,0:T(8,128)(2,1)}, bf16[1024,256]{1,0:T(8,128)(2,1)}, u32[]{:S(2)}, u32[]{:S(2)}) collective-permute-start(bf16[1024,256]{1,0:T(8,128)(2,1)} %collective-permute-done.5.refs_6_), channel_id=1, source_target_pairs={{0,14},{2,0},{4,2},{6,4},{8,6},{10,8},{12,10},{14,12},{1,15},{3,1}... | collective-permute-start | bytes 1572872 | tf_op jit(solution)/shard_map/ppermute | solution.py:363
  59.1 11.9 %collective-permute-start.3 = (bf16[1024,256]{1,0:T(8,128)(2,1)}, bf16[1024,256]{1,0:T(8,128)(2,1)}, u32[]{:S(2)}, u32[]{:S(2)}) collective-permute-start(bf16[1024,256]{1,0:T(8,128)(2,1)} %collective-permute-done.2.refs_3_), channel_id=1, source_target_pairs={{0,2},{2,4},{4,6},{6,8},{8,10},{10,12},{12,14},{14,0},{1,3},{3,5},... | collective-permute-start | bytes 1572872 | tf_op jit(solution)/shard_map/ppermute | solution.py:361
  59.8 18.3 %copy-start = (bf16[256,4096]{1,0:T(8,128)(2,1)S(1)}, bf16[256,4096]{1,0:T(8,128)(2,1)}, u32[]{:S(2)}) copy-start(bf16[256,4096]{1,0:T(8,128)(2,1)} %weight_ref.9) | copy-start | bytes 6291460
  59.8 18.3 %copy-start.5 = (s32[2]{0:T(128)S(1)}, s32[2]{0:T(128)}, u32[]{:S(2)}) copy-start(s32[2]{0:T(128)} %pad_add_fusion.1.place_ref) | copy-start | bytes 28
  78.0 2.4 %copy-start.8 = (s32[16,2]{0,1:T(2,128)S(1)}, s32[16,2]{0,1:T(2,128)}, u32[]{:S(2)}) copy-start(s32[16,2]{0,1:T(2,128)} %param.18) | copy-start | bytes 388
  78.0 4.8 %collective-permute-start.8 = (f32[1024,256]{1,0:T(8,128)}, f32[1024,256]{1,0:T(8,128)}, u32[]{:S(2)}, u32[]{:S(2)}) collective-permute-start(f32[1024,256]{1,0:T(8,128)} %get-tuple-element.30), channel_id=1, source_target_pairs={{0,1},{1,0},{2,3},{3,2},{4,5},{5,4},{6,7},{7,6},{8,9},{9,8},{10,11... | collective-permute-start | bytes 3145736 | tf_op jit(solution)/shard_map/ppermute | solution.py:371
  79.8 17.6 %collective-permute-start.10 = (bf16[8,256,256]{2,1,0:T(8,128)(2,1)}, bf16[8,256,256]{2,1,0:T(8,128)(2,1)S(1)}, u32[]{:S(2)}, u32[]{:S(2)}) collective-permute-start(bf16[8,256,256]{2,1,0:T(8,128)(2,1)} %relay.1), channel_id=1, source_target_pairs={{0,1},{1,0},{2,3},{3,2},{4,5},{5,4},{6,7},{7,6},{8,9},{9,8},{10,11... | collective-permute-start | bytes 3145736 | tf_op jit(solution)/shard_map/ppermute | solution.py:368
  82.9 1.2 copy-start.4
  85.7 0.8 copy-start.1
  92.4 5.0 %copy-start.3 = (bf16[512,256]{1,0:T(8,128)(2,1)S(1)}, bf16[512,256]{1,0:T(8,128)(2,1)}, u32[]{:S(2)}) copy-start(bf16[512,256]{1,0:T(8,128)(2,1)} %attend.3.own_ref) | copy-start | bytes 786436
  92.4 5.0 %collective-permute-start.18 = (bf16[512,256]{1,0:T(8,128)(2,1)}, bf16[512,256]{1,0:T(8,128)(2,1)S(1)}, u32[]{:S(2)}, u32[]{:S(2)}) collective-permute-start(bf16[512,256]{1,0:T(8,128)(2,1)} %attend.3.own_ref), channel_id=1, source_target_pairs={{0,1},{1,0},{2,3},{3,2},{4,5},{5,4},{6,7},{7,6},{8,9},{9,8},{10,11... | collective-permute-start | bytes 786440 | tf_op jit(solution)/shard_map/ppermute | solution.py:375
  96.8 5.9 %copy-start.2 = (bf16[512,256]{1,0:T(8,128)(2,1)S(1)}, bf16[512,256]{1,0:T(8,128)(2,1)}, u32[]{:S(2)}) copy-start(bf16[512,256]{1,0:T(8,128)(2,1)} %attend.2.own_ref) | copy-start | bytes 786436
  96.8 5.9 %collective-permute-start.9 = (bf16[512,256]{1,0:T(8,128)(2,1)}, bf16[512,256]{1,0:T(8,128)(2,1)S(1)}, u32[]{:S(2)}, u32[]{:S(2)}) collective-permute-start(bf16[512,256]{1,0:T(8,128)(2,1)} %attend.2.own_ref), channel_id=1, source_target_pairs={{0,1},{1,0},{2,3},{3,2},{4,5},{5,4},{6,7},{7,6},{8,9},{9,8},{10,11... | collective-permute-start | bytes 786440 | tf_op jit(solution)/shard_map/ppermute | solution.py:375
  98.4 11.7 %collective-permute-start.22 = (bf16[512,256]{1,0:T(8,128)(2,1)S(1)}, bf16[512,256]{1,0:T(8,128)(2,1)S(1)}, u32[]{:S(2)}, u32[]{:S(2)}) collective-permute-start(bf16[512,256]{1,0:T(8,128)(2,1)S(1)} %get-tuple-element.43), channel_id=1, source_target_pairs={{0,14},{2,0},{4,2},{6,4},{8,6},{10,8},{12,10},{14,12},{1,15},{3,1}... | collective-permute-start | bytes 786440 | tf_op jit(solution)/shard_map/ppermute | solution.py:283
  102.7 10.8 %collective-permute-start.19 = (bf16[512,256]{1,0:T(8,128)(2,1)S(1)}, bf16[512,256]{1,0:T(8,128)(2,1)S(1)}, u32[]{:S(2)}, u32[]{:S(2)}) collective-permute-start(bf16[512,256]{1,0:T(8,128)(2,1)S(1)} %get-tuple-element.40), channel_id=1, source_target_pairs={{0,2},{2,4},{4,6},{6,8},{8,10},{10,12},{12,14},{14,0},{1,3},{3,5},... | collective-permute-start | bytes 786440 | tf_op jit(solution)/shard_map/ppermute | solution.py:283
  103.7 11.3 %collective-permute-start.15 = (bf16[512,256]{1,0:T(8,128)(2,1)S(1)}, bf16[512,256]{1,0:T(8,128)(2,1)S(1)}, u32[]{:S(2)}, u32[]{:S(2)}) collective-permute-start(bf16[512,256]{1,0:T(8,128)(2,1)S(1)} %get-tuple-element.36), channel_id=1, source_target_pairs={{0,14},{2,0},{4,2},{6,4},{8,6},{10,8},{12,10},{14,12},{1,15},{3,1}... | collective-permute-start | bytes 786440 | tf_op jit(solution)/shard_map/ppermute | solution.py:283
  107.0 11.8 %collective-permute-start.11 = (bf16[512,256]{1,0:T(8,128)(2,1)S(1)}, bf16[512,256]{1,0:T(8,128)(2,1)S(1)}, u32[]{:S(2)}, u32[]{:S(2)}) collective-permute-start(bf16[512,256]{1,0:T(8,128)(2,1)S(1)} %get-tuple-element.32), channel_id=1, source_target_pairs={{0,2},{2,4},{4,6},{6,8},{8,10},{10,12},{12,14},{14,0},{1,3},{3,5},... | collective-permute-start | bytes 786440 | tf_op jit(solution)/shard_map/ppermute | solution.py:283
  110.1 10.5 %collective-permute-start.23 = (bf16[512,256]{1,0:T(8,128)(2,1)S(1)}, bf16[512,256]{1,0:T(8,128)(2,1)S(1)}, u32[]{:S(2)}, u32[]{:S(2)}) collective-permute-start(bf16[512,256]{1,0:T(8,128)(2,1)S(1)} %add_convert_fusion.3), channel_id=1, source_target_pairs={{0,14},{2,0},{4,2},{6,4},{8,6},{10,8},{12,10},{14,12},{1,15},{3,1}... | collective-permute-start | bytes 786440 | tf_op jit(solution)/shard_map/ppermute | solution.py:283
  113.5 11.1 %collective-permute-start.20 = (bf16[512,256]{1,0:T(8,128)(2,1)S(1)}, bf16[512,256]{1,0:T(8,128)(2,1)S(1)}, u32[]{:S(2)}, u32[]{:S(2)}) collective-permute-start(bf16[512,256]{1,0:T(8,128)(2,1)S(1)} %add_convert_fusion.5), channel_id=1, source_target_pairs={{0,2},{2,4},{4,6},{6,8},{8,10},{10,12},{12,14},{14,0},{1,3},{3,5},... | collective-permute-start | bytes 786440 | tf_op jit(solution)/shard_map/ppermute | solution.py:283
  115.0 19.7 %collective-permute-start.16 = (bf16[512,256]{1,0:T(8,128)(2,1)S(1)}, bf16[512,256]{1,0:T(8,128)(2,1)S(1)}, u32[]{:S(2)}, u32[]{:S(2)}) collective-permute-start(bf16[512,256]{1,0:T(8,128)(2,1)S(1)} %add_convert_fusion.8), channel_id=1, source_target_pairs={{0,14},{2,0},{4,2},{6,4},{8,6},{10,8},{12,10},{14,12},{1,15},{3,1}... | collective-permute-start | bytes 786440 | tf_op jit(solution)/shard_map/ppermute | solution.py:283
  118.9 11.1 %collective-permute-start.12 = (bf16[512,256]{1,0:T(8,128)(2,1)S(1)}, bf16[512,256]{1,0:T(8,128)(2,1)S(1)}, u32[]{:S(2)}, u32[]{:S(2)}) collective-permute-start(bf16[512,256]{1,0:T(8,128)(2,1)S(1)} %add_convert_fusion.11), channel_id=1, source_target_pairs={{0,2},{2,4},{4,6},{6,8},{8,10},{10,12},{12,14},{14,0},{1,3},{3,5},... | collective-permute-start | bytes 786440 | tf_op jit(solution)/shard_map/ppermute | solution.py:283
  120.7 10.2 %collective-permute-start.24 = (bf16[512,256]{1,0:T(8,128)(2,1)S(1)}, bf16[512,256]{1,0:T(8,128)(2,1)S(1)}, u32[]{:S(2)}, u32[]{:S(2)}) collective-permute-start(bf16[512,256]{1,0:T(8,128)(2,1)S(1)} %add_convert_fusion.2), channel_id=1, source_target_pairs={{0,14},{2,0},{4,2},{6,4},{8,6},{10,8},{12,10},{14,12},{1,15},{3,1}... | collective-permute-start | bytes 786440 | tf_op jit(solution)/shard_map/ppermute | solution.py:283
  124.7 15.4 %collective-permute-start.21 = (bf16[512,256]{1,0:T(8,128)(2,1)S(1)}, bf16[512,256]{1,0:T(8,128)(2,1)S(1)}, u32[]{:S(2)}, u32[]{:S(2)}) collective-permute-start(bf16[512,256]{1,0:T(8,128)(2,1)S(1)} %add_convert_fusion.4), channel_id=1, source_target_pairs={{0,2},{2,4},{4,6},{6,8},{8,10},{10,12},{12,14},{14,0},{1,3},{3,5},... | collective-permute-start | bytes 786440 | tf_op jit(solution)/shard_map/ppermute | solution.py:283
  130.0 9.9 %collective-permute-start.13 = (bf16[512,256]{1,0:T(8,128)(2,1)S(1)}, bf16[512,256]{1,0:T(8,128)(2,1)S(1)}, u32[]{:S(2)}, u32[]{:S(2)}) collective-permute-start(bf16[512,256]{1,0:T(8,128)(2,1)S(1)} %add_convert_fusion.10), channel_id=1, source_target_pairs={{0,2},{2,4},{4,6},{6,8},{8,10},{10,12},{12,14},{14,0},{1,3},{3,5},... | collective-permute-start | bytes 786440 | tf_op jit(solution)/shard_map/ppermute | solution.py:283
  131.0 10.5 %collective-permute-start.25 = (bf16[512,256]{1,0:T(8,128)(2,1)S(1)}, bf16[512,256]{1,0:T(8,128)(2,1)S(1)}, u32[]{:S(2)}, u32[]{:S(2)}) collective-permute-start(bf16[512,256]{1,0:T(8,128)(2,1)S(1)} %add_convert_fusion.1), channel_id=1, source_target_pairs={{0,14},{2,0},{4,2},{6,4},{8,6},{10,8},{12,10},{14,12},{1,15},{3,1}... | collective-permute-start | bytes 786440 | tf_op jit(solution)/shard_map/ppermute | solution.py:283
  134.8 10.5 %collective-permute-start.17 = (bf16[512,256]{1,0:T(8,128)(2,1)S(1)}, bf16[512,256]{1,0:T(8,128)(2,1)S(1)}, u32[]{:S(2)}, u32[]{:S(2)}) collective-permute-start(bf16[512,256]{1,0:T(8,128)(2,1)S(1)} %add_convert_fusion.7), channel_id=1, source_target_pairs={{0,14},{2,0},{4,2},{6,4},{8,6},{10,8},{12,10},{14,12},{1,15},{3,1}... | collective-permute-start | bytes 786440 | tf_op jit(solution)/shard_map/ppermute | solution.py:283
  140.0 8.4 %collective-permute-start.14 = (bf16[512,256]{1,0:T(8,128)(2,1)S(1)}, bf16[512,256]{1,0:T(8,128)(2,1)S(1)}, u32[]{:S(2)}, u32[]{:S(2)}) collective-permute-start(bf16[512,256]{1,0:T(8,128)(2,1)S(1)} %add_convert_fusion.9), channel_id=1, source_target_pairs={{0,2},{2,4},{4,6},{6,8},{8,10},{10,12},{12,14},{14,0},{1,3},{3,5},... | collective-permute-start | bytes 786440 | tf_op jit(solution)/shard_map/ppermute | solution.py:283

commit v9 on v8

--- a/solution.py
+++ b/solution.py
@@ -138,19 +138,22 @@
     )(place, *pieces, weight, partner_weight)
 
 
-def finish_kernel(own_ref, lent_ref, out_ref):
-    for h in range(out_ref.shape[1] // HD):
-        cols = slice(h * HD, (h + 1) * HD)
-        out_ref[:, cols] = unit(own_ref[:, cols] + lent_ref[:, cols]).astype(BF16)
-
-
-def finish_queries(own, lent):
+def finish_kernel(own_ref, lent_ref, *out_refs):
+    for i, out_ref in enumerate(out_refs):
+        rows = slice(i * out_ref.shape[0], (i + 1) * out_ref.shape[0])
+        for h in range(out_ref.shape[1] // HD):
+            cols = slice(h * HD, (h + 1) * HD)
+            out_ref[:, cols] = unit(own_ref[rows, cols] + lent_ref[rows, cols]).astype(BF16)
+
+
+def finish_queries(own, lent, parts):
+    rows, width = own.shape
     return pl.pallas_call(
         finish_kernel,
-        out_shape=jax.ShapeDtypeStruct(own.shape, BF16),
+        out_shape=[jax.ShapeDtypeStruct((rows // parts, width), BF16)] * parts,
         in_specs=[VMEM, VMEM],
-        out_specs=VMEM,
-        compiler_params=pltpu.CompilerParams(vmem_limit_bytes=8 << 20),
+        out_specs=[VMEM] * parts,
+        compiler_params=pltpu.CompilerParams(vmem_limit_bytes=56 << 20),
         cost_estimate=pl.CostEstimate(flops=1 << 20, bytes_accessed=3 << 20, transcendentals=0),
         name="finish_queries",
     )(own, lent)
@@ -162,9 +165,7 @@
     spans = slot_ref.shape[0] // NBRS
     count = sems.shape[0] // NBRS
     first = part * count
-    query_copy = pltpu.make_async_copy(
-        queries_ref.at[pl.ds(first * SPAN, count * SPAN)], query_ref, query_sem
-    )
+    query_copy = pltpu.make_async_copy(queries_ref, query_ref, query_sem)
     query_copy.start()
     width = out_ref.shape[1]
     keys = NBRS * NBR_LEN
@@ -208,8 +209,8 @@
             out_ref[c * SPAN : (c + 1) * SPAN, h * HD : (h + 1) * HD] = result.astype(BF16)
 
 
-def attend(part, parts, slot_index, lengths, queries, rows):
-    tokens, width = queries.shape[0] // parts, queries.shape[1]
+def attend(part, slot_index, lengths, queries, rows):
+    tokens, width = queries.shape
     requests = tokens // SPAN * NBRS
     return pl.pallas_call(
         functools.partial(attend_kernel, part),
@@ -222,7 +223,7 @@
             pltpu.SemaphoreType.DMA((requests,)),
             pltpu.SemaphoreType.DMA,
         ],
-        compiler_params=pltpu.CompilerParams(vmem_limit_bytes=56 << 20),
+        compiler_params=pltpu.CompilerParams(vmem_limit_bytes=24 << 20),
         cost_estimate=SMALL,
         name="attend",
     )(slot_index, lengths, queries, rows)
@@ -369,9 +370,8 @@
 
     own, lent = project_queries(place, [pieces[k] for k in range(ring)], by_core, partner_rows)
     lent = lax.ppermute(lent, "c", swap)
-    queries = finish_queries(own, lent)
-
-    attended = [attend(part, 2, slot_index, lengths, queries, rows) for part in range(2)]
+    queries = finish_queries(own, lent, 2)
+    attended = [attend(part, slot_index, lengths, queries[part], rows) for part in range(2)]
     partner_attended = [lax.ppermute(part, "c", swap) for part in attended]
     return reduce_ring(place, attended, partner_attended, out_weight, partner_weight, ring)
 

time: 150 us -> 148 us (0.987)
  waiting for transfers between devices: 55 us -> 57.2 us
    pallas_call x2, Pallas kernels: 8.51 us -> 6.19 us  [attend(): pl.pallas_call(functools.partial(attend_kernel, part), out_shape=jax.Shap...]
    all_to_all x1, waiting for transfers between devices: 1.66 us -> 3.72 us  [local(): rows = lax.all_to_all(sent, DB, split_axis=0, concat_axis=0, tiled=True)]
  transfers between devices with their start and end apart: 28 -> 28, of which waited for: 14 -> 14; matrix products, arithmetic and copies ran while one was open for 4% -> 3% of each run, Pallas kernels for 22% -> 21%
where the time goes in v9:
time: 148 us
  waiting for transfers between devices  57.2 us (39%)
  starting transfers between devices  51.9 us (35%)
  Pallas kernels  31.3 us (21%)
  local copies, waits for them, and re-layouts  3.98 us (3%)
  other arithmetic  3.27 us (2%)
    ppermute x14, starting transfers between devices, send(): return lax.ppermute(sums, 'z', up if way == 1 else down)  23.5 us
    ppermute x14, waiting for transfers between devices, send(): return lax.ppermute(sums, 'z', up if way == 1 else down)  21.7 us
    ppermute x2, waiting for transfers between devices, local(): pieces[ring - k] = lax.ppermute(pieces[ring - k + 1], 'z', down)  17.4 us
    ppermute x1, waiting for transfers between devices, local(): pieces[ring - 1] = lax.ppermute(tokens, 'z', down)  10.2 us
    ppermute x2, starting transfers between devices, local(): pieces[ring - k] = lax.ppermute(pieces[ring - k + 1], 'z', down)  7.38 us
    all_to_all x1, starting transfers between devices, local(): heard = lax.all_to_all(notes, DB, split_axis=0, concat_axis=0, tiled=True)  7.17 us
    pallas_call x1, Pallas kernels, project_queries(): pl.pallas_call(query_kernel, grid=(rows // tile,), out_shape=(out, out),...  6.96 us
    all_to_all x1, starting transfers between devices, local(): rows = lax.all_to_all(sent, DB, split_axis=0, concat_axis=0, tiled=True)  6.64 us
  transfers between devices with their start and end apart: 28, of which 14 were waited for; matrix products, arithmetic and copies ran while one was open for 3% of the time, Pallas kernels for 21%

profile of v9, /device:TPU:24, one launch (start us, length us, event | category | flops | bytes accessed | tf_op | source)
XLA Modules:
  0.0 147.9 jit_solution(5778173228046195202)
XLA Ops:
  0.0 1.9 %collective-permute-start = (bf16[1024,256]{1,0:T(8,128)(2,1)}, bf16[1024,256]{1,0:T(8,128)(2,1)}, u32[]{:S(2)}, u32[]{:S(2)}) collective-permute-start(bf16[1024,256]{1,0:T(8,128)(2,1)} %refs_0_.1), channel_id=1, source_target_pairs={{0,2},{2,4},{4,6},{6,8},{8,10},{10,12},{12,14},{14,0},{1,3},{3,5},... | collective-permute-start | bytes 1572872 | tf_op jit(solution)/shard_map/ppermute | solution.py:340
  1.9 0.7 pad_bitcast_fusion
  2.6 0.7 bitcast_add_fusion
  3.3 0.6 broadcast_in_dim.27
  3.9 7.2 %all-to-all-start = ((s32[16,3,16]{2,1,0:T(4,128)}), s32[16,3,16]{2,1,0:T(4,128)S(1)}, u32[]{:S(2)}, u32[]{:S(2)}) async-start(s32[16,3,16]{2,1,0:T(4,128)} %broadcast_in_dim.27), calls=%async_computation | async-start | bytes 65536 | tf_op jit(solution)/shard_map/all_to_all | solution.py:335
  11.1 4.9 %project_blocks.1.rows_ref = bf16[8,128,512]{2,1,0:T(8,128)(2,1)} custom-call(f32[8,7]{1,0:T(8,128)} %scales_ref.1, bf16[8,128,896]{2,1,0:T(8,128)(2,1)} %codes_ref.1, bf16[896,256]{1,0:T(8,128)(2,1)} %key_ref.1, bf16[896,256]{1,0:T(8,128)(2,1)} %value_ref.1), custom_call_target="tpu_custom_call" | custom-call | flops 939524096 | bytes 5242880 | tf_op jit(solution)/shard_map/project_blocks/pallas_call | solution.py:53
  16.0 0.7 all-to-all-done.heard_ref
  16.7 0.6 copy-done.5
  17.3 3.9 %select_blocks.1 = bf16[16,2,128,512]{3,2,1,0:T(8,128)(2,1)} custom-call(s32[1]{0:T(128)} %bitcast.5.place_ref, s32[16,3,16]{2,1,0:T(4,128)} %copy-done.5, bf16[8,128,512]{2,1,0:T(8,128)(2,1)} %project_blocks.1.rows_ref), custom_call_target="tpu_custom_call" | custom-call | bytes 9437184 | tf_op jit(solution)/shard_map/select_blocks/pallas_call | solution.py:92
  21.3 6.6 %all-to-all-start.1 = ((bf16[16,2,128,512]{3,2,1,0:T(8,128)(2,1)}), bf16[16,2,128,512]{3,2,1,0:T(8,128)(2,1)}, u32[]{:S(2)}, u32[]{:S(2)}) async-start(bf16[16,2,128,512]{3,2,1,0:T(8,128)(2,1)} %select_blocks.1), calls=%async_computation.1 | async-start | bytes 8388608 | tf_op jit(solution)/shard_map/all_to_all | solution.py:344
  27.9 3.9 %collective-permute-start.4 = (bf16[1024,256]{1,0:T(8,128)(2,1)}, bf16[1024,256]{1,0:T(8,128)(2,1)}, u32[]{:S(2)}, u32[]{:S(2)}) collective-permute-start(bf16[1024,256]{1,0:T(8,128)(2,1)} %refs_0_.1), channel_id=1, source_target_pairs={{0,14},{2,0},{4,2},{6,4},{8,6},{10,8},{12,10},{14,12},{1,15},{3,1}... | collective-permute-start | bytes 1572872 | tf_op jit(solution)/shard_map/ppermute | solution.py:341
  32.1 10.2 %collective-permute-done.4.refs_7_ = bf16[1024,256]{1,0:T(8,128)(2,1)} collective-permute-done((bf16[1024,256]{1,0:T(8,128)(2,1)}, bf16[1024,256]{1,0:T(8,128)(2,1)}, u32[]{:S(2)}, u32[]{:S(2)}) %collective-permute-start.4) | collective-permute-done | bytes 524320 | tf_op jit(solution)/shard_map/ppermute | solution.py:341
  42.2 3.7 %collective-permute-start.5 = (bf16[1024,256]{1,0:T(8,128)(2,1)}, bf16[1024,256]{1,0:T(8,128)(2,1)}, u32[]{:S(2)}, u32[]{:S(2)}) collective-permute-start(bf16[1024,256]{1,0:T(8,128)(2,1)} %collective-permute-done.4.refs_7_), channel_id=1, source_target_pairs={{0,14},{2,0},{4,2},{6,4},{8,6},{10,8},{12,10},{14,12},{1,15},{3,1}... | collective-permute-start | bytes 1572872 | tf_op jit(solution)/shard_map/ppermute | solution.py:364
  45.9 9.4 %collective-permute-done.5.refs_6_ = bf16[1024,256]{1,0:T(8,128)(2,1)} collective-permute-done((bf16[1024,256]{1,0:T(8,128)(2,1)}, bf16[1024,256]{1,0:T(8,128)(2,1)}, u32[]{:S(2)}, u32[]{:S(2)}) %collective-permute-start.5) | collective-permute-done | bytes 524320 | tf_op jit(solution)/shard_map/ppermute | solution.py:364
  55.4 3.7 %collective-permute-start.6 = (bf16[1024,256]{1,0:T(8,128)(2,1)}, bf16[1024,256]{1,0:T(8,128)(2,1)}, u32[]{:S(2)}, u32[]{:S(2)}) collective-permute-start(bf16[1024,256]{1,0:T(8,128)(2,1)} %collective-permute-done.5.refs_6_), channel_id=1, source_target_pairs={{0,14},{2,0},{4,2},{6,4},{8,6},{10,8},{12,10},{14,12},{1,15},{3,1}... | collective-permute-start | bytes 1572872 | tf_op jit(solution)/shard_map/ppermute | solution.py:364
  59.1 0.6 pad_add_fusion.1.place_ref
  59.7 7.9 %collective-permute-done.6.refs_5_ = bf16[1024,256]{1,0:T(8,128)(2,1)} collective-permute-done((bf16[1024,256]{1,0:T(8,128)(2,1)}, bf16[1024,256]{1,0:T(8,128)(2,1)}, u32[]{:S(2)}, u32[]{:S(2)}) %collective-permute-start.6) | collective-permute-done | bytes 524320 | tf_op jit(solution)/shard_map/ppermute | solution.py:364
  67.6 3.4 %collective-permute-done.3.refs_4_ = bf16[1024,256]{1,0:T(8,128)(2,1)} collective-permute-done((bf16[1024,256]{1,0:T(8,128)(2,1)}, bf16[1024,256]{1,0:T(8,128)(2,1)}, u32[]{:S(2)}, u32[]{:S(2)}) %collective-permute-start.3) | collective-permute-done | bytes 524320 | tf_op jit(solution)/shard_map/ppermute | solution.py:362
  71.0 7.0 %project_queries.1 = (f32[1024,256]{1,0:T(8,128)}, f32[1024,256]{1,0:T(8,128)}) custom-call(s32[2]{0:T(128)} %pad_add_fusion.1.place_ref, bf16[1024,256]{1,0:T(8,128)(2,1)} %refs_0_.1, bf16[1024,256]{1,0:T(8,128)(2,1)} %collective-permute-done.refs_1_, bf16[1024,256]{1,0:T(8,128)(2,1)} %collective-permute-done.1.refs_2_, ...), custom_call_target="tpu_custom_call" | custom-call | flops 2147483648 | bytes 9437184 | tf_op jit(solution)/shard_map/project_queries/pallas_call | solution.py:122
  78.1 1.7 %relay.1 = bf16[8,256,256]{2,1,0:T(8,128)(2,1)} custom-call(s32[2]{0:T(128)S(1)} %copy-done.3, bf16[256,4096]{1,0:T(8,128)(2,1)S(1)} %copy-done), custom_call_target="tpu_custom_call" | custom-call | bytes 3145728 | tf_op jit(solution)/shard_map/relay/pallas_call | solution.py:243
  79.8 0.5 collective-permute-start.10
  80.7 0.8 slice_reduce_fusion
  81.8 2.6 %finish_queries.1 = (bf16[512,256]{1,0:T(8,128)(2,1)}, bf16[512,256]{1,0:T(8,128)(2,1)}) custom-call(f32[1024,256]{1,0:T(8,128)} %get-tuple-element.31.own_ref, f32[1024,256]{1,0:T(8,128)} %collective-permute-done.8.lent_ref), custom_call_target="tpu_custom_call" | custom-call | flops 1048576 | bytes 3145728 | tf_op jit(solution)/shard_map/finish_queries/pallas_call | solution.py:151
  84.4 3.7 %all-to-all-done.1 = bf16[16,2,128,512]{3,2,1,0:T(8,128)(2,1)} async-done(((bf16[16,2,128,512]{3,2,1,0:T(8,128)(2,1)}), bf16[16,2,128,512]{3,2,1,0:T(8,128)(2,1)}, u32[]{:S(2)}, u32[]{:S(2)}) %all-to-all-start.1) | async-done | bytes 4194336 | tf_op jit(solution)/shard_map/all_to_all | solution.py:344
  88.1 0.9 copy-done.2
  89.1 3.1 %attend.3.own_ref = bf16[512,256]{1,0:T(8,128)(2,1)S(1)} custom-call(s32[32]{0:T(128)S(1)} %multiply_add_fusion.slot_ref, s32[32]{0:T(128)S(1)} %select_reduce_fusion.length_ref, bf16[512,256]{1,0:T(8,128)(2,1)S(1)} %copy-done.2, bf16[32,128,512]{2,1,0:T(8,128)(2,1)} %bitcast.8.rows_ref), custom_call_target="tpu_custom_call" | custom-call | flops 1024 | bytes 1024 | tf_op jit(solution)/shard_map/attend/pallas_call | solution.py:215
  92.3 3.1 %attend.2.own_ref = bf16[512,256]{1,0:T(8,128)(2,1)S(1)} custom-call(s32[32]{0:T(128)S(1)} %multiply_add_fusion.slot_ref, s32[32]{0:T(128)S(1)} %select_reduce_fusion.length_ref, bf16[512,256]{1,0:T(8,128)(2,1)S(1)} %copy-done.1, bf16[32,128,512]{2,1,0:T(8,128)(2,1)} %bitcast.8.rows_ref), custom_call_target="tpu_custom_call" | custom-call | flops 1024 | bytes 1024 | tf_op jit(solution)/shard_map/attend/pallas_call | solution.py:215
  95.4 0.6 collective-permute-start.9
  95.9 1.0 shares.7
  96.9 4.3 %collective-permute-start.22 = (bf16[512,256]{1,0:T(8,128)(2,1)S(1)}, bf16[512,256]{1,0:T(8,128)(2,1)S(1)}, u32[]{:S(2)}, u32[]{:S(2)}) collective-permute-start(bf16[512,256]{1,0:T(8,128)(2,1)S(1)} %get-tuple-element.47), channel_id=1, source_target_pairs={{0,14},{2,0},{4,2},{6,4},{8,6},{10,8},{12,10},{14,12},{1,15},{3,1}... | collective-permute-start | bytes 786440 | tf_op jit(solution)/shard_map/ppermute | solution.py:284
  101.3 1.0 shares.5
  102.3 3.3 %collective-permute-start.15 = (bf16[512,256]{1,0:T(8,128)(2,1)S(1)}, bf16[512,256]{1,0:T(8,128)(2,1)S(1)}, u32[]{:S(2)}, u32[]{:S(2)}) collective-permute-start(bf16[512,256]{1,0:T(8,128)(2,1)S(1)} %get-tuple-element.39), channel_id=1, source_target_pairs={{0,14},{2,0},{4,2},{6,4},{8,6},{10,8},{12,10},{14,12},{1,15},{3,1}... | collective-permute-start | bytes 786440 | tf_op jit(solution)/shard_map/ppermute | solution.py:284
  105.6 1.5 %shares.6 = (f32[512,256]{1,0:T(8,128)S(1)}, f32[512,256]{1,0:T(8,128)S(1)}, f32[512,256]{1,0:T(8,128)S(1)}, f32[512,256]{1,0:T(8,128)S(1)}, f32[512,256]{1,0:T(8,128)S(1)}, /*index=5*/f32[512,256]{1,0:T(8,128)S(1)}) custom-call(s32[2]{0:T(128)S(1)} %copy-done.3, bf16[512,256]{1,0:T(8,128)(2,1)S(1)} %attend.3.own_ref, ...), custom_call_target="tpu_custom_call" | custom-call | flops 1024 | bytes 1024 | tf_op jit(solution)/shard_map/shares/pallas_call | solution.py:268
  107.1 1.5 %shares.4 = (f32[512,256]{1,0:T(8,128)S(1)}, f32[512,256]{1,0:T(8,128)S(1)}, f32[512,256]{1,0:T(8,128)S(1)}, f32[512,256]{1,0:T(8,128)S(1)}, f32[512,256]{1,0:T(8,128)S(1)}, /*index=5*/f32[512,256]{1,0:T(8,128)S(1)}) custom-call(s32[2]{0:T(128)S(1)} %copy-done.3, bf16[512,256]{1,0:T(8,128)(2,1)S(1)} %attend.2.own_ref, ...), custom_call_target="tpu_custom_call" | custom-call | flops 1024 | bytes 1024 | tf_op jit(solution)/shard_map/shares/pallas_call | solution.py:268
  108.7 3.3 %collective-permute-start.23 = (bf16[512,256]{1,0:T(8,128)(2,1)S(1)}, bf16[512,256]{1,0:T(8,128)(2,1)S(1)}, u32[]{:S(2)}, u32[]{:S(2)}) collective-permute-start(bf16[512,256]{1,0:T(8,128)(2,1)S(1)} %add_convert_fusion.3), channel_id=1, source_target_pairs={{0,14},{2,0},{4,2},{6,4},{8,6},{10,8},{12,10},{14,12},{1,15},{3,1}... | collective-permute-start | bytes 786440 | tf_op jit(solution)/shard_map/ppermute | solution.py:284
  112.2 1.4 collective-permute-done.15
  113.6 3.8 %collective-permute-start.16 = (bf16[512,256]{1,0:T(8,128)(2,1)S(1)}, bf16[512,256]{1,0:T(8,128)(2,1)S(1)}, u32[]{:S(2)}, u32[]{:S(2)}) collective-permute-start(bf16[512,256]{1,0:T(8,128)(2,1)S(1)} %add_convert_fusion.8), channel_id=1, source_target_pairs={{0,14},{2,0},{4,2},{6,4},{8,6},{10,8},{12,10},{14,12},{1,15},{3,1}... | collective-permute-start | bytes 786440 | tf_op jit(solution)/shard_map/ppermute | solution.py:284
  117.6 1.6 %collective-permute-done.23 = bf16[512,256]{1,0:T(8,128)(2,1)S(1)} collective-permute-done((bf16[512,256]{1,0:T(8,128)(2,1)S(1)}, bf16[512,256]{1,0:T(8,128)(2,1)S(1)}, u32[]{:S(2)}, u32[]{:S(2)}) %collective-permute-start.23) | collective-permute-done | bytes 262176 | tf_op jit(solution)/shard_map/ppermute | solution.py:284
  119.2 4.0 %collective-permute-start.24 = (bf16[512,256]{1,0:T(8,128)(2,1)S(1)}, bf16[512,256]{1,0:T(8,128)(2,1)S(1)}, u32[]{:S(2)}, u32[]{:S(2)}) collective-permute-start(bf16[512,256]{1,0:T(8,128)(2,1)S(1)} %add_convert_fusion.2), channel_id=1, source_target_pairs={{0,14},{2,0},{4,2},{6,4},{8,6},{10,8},{12,10},{14,12},{1,15},{3,1}... | collective-permute-start | bytes 786440 | tf_op jit(solution)/shard_map/ppermute | solution.py:284
  123.4 5.1 %collective-permute-done.12 = bf16[512,256]{1,0:T(8,128)(2,1)S(1)} collective-permute-done((bf16[512,256]{1,0:T(8,128)(2,1)S(1)}, bf16[512,256]{1,0:T(8,128)(2,1)S(1)}, u32[]{:S(2)}, u32[]{:S(2)}) %collective-permute-start.12) | collective-permute-done | bytes 262176 | tf_op jit(solution)/shard_map/ppermute | solution.py:284
  128.7 0.8 collective-permute-done.24
  129.6 3.8 %collective-permute-start.25 = (bf16[512,256]{1,0:T(8,128)(2,1)S(1)}, bf16[512,256]{1,0:T(8,128)(2,1)S(1)}, u32[]{:S(2)}, u32[]{:S(2)}) collective-permute-start(bf16[512,256]{1,0:T(8,128)(2,1)S(1)} %add_convert_fusion.1), channel_id=1, source_target_pairs={{0,14},{2,0},{4,2},{6,4},{8,6},{10,8},{12,10},{14,12},{1,15},{3,1}... | collective-permute-start | bytes 786440 | tf_op jit(solution)/shard_map/ppermute | solution.py:284
  133.4 0.6 collective-permute-start.17
  134.0 4.6 %collective-permute-done.13 = bf16[512,256]{1,0:T(8,128)(2,1)S(1)} collective-permute-done((bf16[512,256]{1,0:T(8,128)(2,1)S(1)}, bf16[512,256]{1,0:T(8,128)(2,1)S(1)}, u32[]{:S(2)}, u32[]{:S(2)}) %collective-permute-start.13) | collective-permute-done | bytes 262176 | tf_op jit(solution)/shard_map/ppermute | solution.py:284
  138.7 1.4 collective-permute-done.25
  140.2 3.7 %collective-permute-done.17 = bf16[512,256]{1,0:T(8,128)(2,1)S(1)} collective-permute-done((bf16[512,256]{1,0:T(8,128)(2,1)S(1)}, bf16[512,256]{1,0:T(8,128)(2,1)S(1)}, u32[]{:S(2)}, u32[]{:S(2)}) %collective-permute-start.17) | collective-permute-done | bytes 262176 | tf_op jit(solution)/shard_map/ppermute | solution.py:284
  143.9 3.1 %collective-permute-done.14 = bf16[512,256]{1,0:T(8,128)(2,1)S(1)} collective-permute-done((bf16[512,256]{1,0:T(8,128)(2,1)S(1)}, bf16[512,256]{1,0:T(8,128)(2,1)S(1)}, u32[]{:S(2)}, u32[]{:S(2)}) %collective-permute-start.14) | collective-permute-done | bytes 262176 | tf_op jit(solution)/shard_map/ppermute | solution.py:284
  147.1 0.8 pad_maximum_fusion
  (59 shorter events, 2.2 us)
Async XLA Ops:
  0.0 21.3 %collective-permute-start = (bf16[1024,256]{1,0:T(8,128)(2,1)}, bf16[1024,256]{1,0:T(8,128)(2,1)}, u32[]{:S(2)}, u32[]{:S(2)}) collective-permute-start(bf16[1024,256]{1,0:T(8,128)(2,1)} %refs_0_.1), channel_id=1, source_target_pairs={{0,2},{2,4},{4,6},{6,8},{8,10},{10,12},{12,14},{14,0},{1,3},{3,5},... | collective-permute-start | bytes 1572872 | tf_op jit(solution)/shard_map/ppermute | solution.py:340
  3.9 12.8 %all-to-all-start = ((s32[16,3,16]{2,1,0:T(4,128)}), s32[16,3,16]{2,1,0:T(4,128)S(1)}, u32[]{:S(2)}, u32[]{:S(2)}) async-start(s32[16,3,16]{2,1,0:T(4,128)} %broadcast_in_dim.27), calls=%async_computation | async-start | bytes 65536 | tf_op jit(solution)/shard_map/all_to_all | solution.py:335
  16.7 0.6 copy-start.5
  21.3 10.6 %copy-start.4 = (bf16[4096,256]{1,0:T(8,128)(2,1)S(1)}, bf16[4096,256]{1,0:T(8,128)(2,1)}, u32[]{:S(2)}) copy-start(bf16[4096,256]{1,0:T(8,128)(2,1)} %param.11) | copy-start | bytes 6291460
  21.3 66.8 %all-to-all-start.1 = ((bf16[16,2,128,512]{3,2,1,0:T(8,128)(2,1)}), bf16[16,2,128,512]{3,2,1,0:T(8,128)(2,1)}, u32[]{:S(2)}, u32[]{:S(2)}) async-start(bf16[16,2,128,512]{3,2,1,0:T(8,128)(2,1)} %select_blocks.1), calls=%async_computation.1 | async-start | bytes 8388608 | tf_op jit(solution)/shard_map/all_to_all | solution.py:344
  27.9 14.3 %collective-permute-start.4 = (bf16[1024,256]{1,0:T(8,128)(2,1)}, bf16[1024,256]{1,0:T(8,128)(2,1)}, u32[]{:S(2)}, u32[]{:S(2)}) collective-permute-start(bf16[1024,256]{1,0:T(8,128)(2,1)} %refs_0_.1), channel_id=1, source_target_pairs={{0,14},{2,0},{4,2},{6,4},{8,6},{10,8},{12,10},{14,12},{1,15},{3,1}... | collective-permute-start | bytes 1572872 | tf_op jit(solution)/shard_map/ppermute | solution.py:341
  31.9 14.1 %collective-permute-start.1 = (bf16[1024,256]{1,0:T(8,128)(2,1)}, bf16[1024,256]{1,0:T(8,128)(2,1)}, u32[]{:S(2)}, u32[]{:S(2)}) collective-permute-start(bf16[1024,256]{1,0:T(8,128)(2,1)} %collective-permute-done.refs_1_), channel_id=1, source_target_pairs={{0,2},{2,4},{4,6},{6,8},{8,10},{10,12},{12,14},{14,0},{1,3},{3,5},... | collective-permute-start | bytes 1572872 | tf_op jit(solution)/shard_map/ppermute | solution.py:362
  32.0 27.7 %collective-permute-start.7 = (bf16[8,256,256]{2,1,0:T(8,128)(2,1)S(1)}, bf16[8,256,256]{2,1,0:T(8,128)(2,1)}, u32[]{:S(2)}, u32[]{:S(2)}) collective-permute-start(bf16[8,256,256]{2,1,0:T(8,128)(2,1)S(1)} %dynamic-slice_bitcast_fusion), channel_id=1, source_target_pairs={{0,1},{1,0},{2,3},{3,2},{4,5},{5,4},{6,7},{7,6},{8,9},{9,8},{10,11... | collective-permute-start | bytes 3145736 | tf_op jit(solution)/shard_map/ppermute | solution.py:367
  42.2 13.1 %collective-permute-start.5 = (bf16[1024,256]{1,0:T(8,128)(2,1)}, bf16[1024,256]{1,0:T(8,128)(2,1)}, u32[]{:S(2)}, u32[]{:S(2)}) collective-permute-start(bf16[1024,256]{1,0:T(8,128)(2,1)} %collective-permute-done.4.refs_7_), channel_id=1, source_target_pairs={{0,14},{2,0},{4,2},{6,4},{8,6},{10,8},{12,10},{14,12},{1,15},{3,1}... | collective-permute-start | bytes 1572872 | tf_op jit(solution)/shard_map/ppermute | solution.py:364
  45.9 13.1 %collective-permute-start.2 = (bf16[1024,256]{1,0:T(8,128)(2,1)}, bf16[1024,256]{1,0:T(8,128)(2,1)}, u32[]{:S(2)}, u32[]{:S(2)}) collective-permute-start(bf16[1024,256]{1,0:T(8,128)(2,1)} %collective-permute-done.1.refs_2_), channel_id=1, source_target_pairs={{0,2},{2,4},{4,6},{6,8},{8,10},{10,12},{12,14},{14,0},{1,3},{3,5},... | collective-permute-start | bytes 1572872 | tf_op jit(solution)/shard_map/ppermute | solution.py:362
  55.4 12.2 %collective-permute-start.6 = (bf16[1024,256]{1,0:T(8,128)(2,1)}, bf16[1024,256]{1,0:T(8,128)(2,1)}, u32[]{:S(2)}, u32[]{:S(2)}) collective-permute-start(bf16[1024,256]{1,0:T(8,128)(2,1)} %collective-permute-done.5.refs_6_), channel_id=1, source_target_pairs={{0,14},{2,0},{4,2},{6,4},{8,6},{10,8},{12,10},{14,12},{1,15},{3,1}... | collective-permute-start | bytes 1572872 | tf_op jit(solution)/shard_map/ppermute | solution.py:364
  59.1 11.9 %collective-permute-start.3 = (bf16[1024,256]{1,0:T(8,128)(2,1)}, bf16[1024,256]{1,0:T(8,128)(2,1)}, u32[]{:S(2)}, u32[]{:S(2)}) collective-permute-start(bf16[1024,256]{1,0:T(8,128)(2,1)} %collective-permute-done.2.refs_3_), channel_id=1, source_target_pairs={{0,2},{2,4},{4,6},{6,8},{8,10},{10,12},{12,14},{14,0},{1,3},{3,5},... | collective-permute-start | bytes 1572872 | tf_op jit(solution)/shard_map/ppermute | solution.py:362
  59.7 18.4 %copy-start = (bf16[256,4096]{1,0:T(8,128)(2,1)S(1)}, bf16[256,4096]{1,0:T(8,128)(2,1)}, u32[]{:S(2)}) copy-start(bf16[256,4096]{1,0:T(8,128)(2,1)} %weight_ref.9) | copy-start | bytes 6291460
  59.7 18.4 %copy-start.3 = (s32[2]{0:T(128)S(1)}, s32[2]{0:T(128)}, u32[]{:S(2)}) copy-start(s32[2]{0:T(128)} %pad_add_fusion.1.place_ref) | copy-start | bytes 28
  78.0 2.4 %copy-start.6 = (s32[16,2]{0,1:T(2,128)S(1)}, s32[16,2]{0,1:T(2,128)}, u32[]{:S(2)}) copy-start(s32[16,2]{0,1:T(2,128)} %param.18) | copy-start | bytes 388
  78.0 3.7 %collective-permute-start.8 = (f32[1024,256]{1,0:T(8,128)}, f32[1024,256]{1,0:T(8,128)}, u32[]{:S(2)}, u32[]{:S(2)}) collective-permute-start(f32[1024,256]{1,0:T(8,128)} %get-tuple-element.32), channel_id=1, source_target_pairs={{0,1},{1,0},{2,3},{3,2},{4,5},{5,4},{6,7},{7,6},{8,9},{9,8},{10,11... | collective-permute-start | bytes 3145736 | tf_op jit(solution)/shard_map/ppermute | solution.py:372
  79.8 16.1 %collective-permute-start.10 = (bf16[8,256,256]{2,1,0:T(8,128)(2,1)}, bf16[8,256,256]{2,1,0:T(8,128)(2,1)S(1)}, u32[]{:S(2)}, u32[]{:S(2)}) collective-permute-start(bf16[8,256,256]{2,1,0:T(8,128)(2,1)} %relay.1), channel_id=1, source_target_pairs={{0,1},{1,0},{2,3},{3,2},{4,5},{5,4},{6,7},{7,6},{8,9},{9,8},{10,11... | collective-permute-start | bytes 3145736 | tf_op jit(solution)/shard_map/ppermute | solution.py:369
  88.1 1.0 copy-start.2
  89.1 3.2 %copy-start.1 = (bf16[512,256]{1,0:T(8,128)(2,1)S(1)}, bf16[512,256]{1,0:T(8,128)(2,1)}, u32[]{:S(2)}) copy-start(bf16[512,256]{1,0:T(8,128)(2,1)} %get-tuple-element.33.queries_ref) | copy-start | bytes 786436
  92.2 3.8 %collective-permute-start.18 = (bf16[512,256]{1,0:T(8,128)(2,1)S(1)}, bf16[512,256]{1,0:T(8,128)(2,1)S(1)}, u32[]{:S(2)}, u32[]{:S(2)}) collective-permute-start(bf16[512,256]{1,0:T(8,128)(2,1)S(1)} %attend.3.own_ref), channel_id=1, source_target_pairs={{0,1},{1,0},{2,3},{3,2},{4,5},{5,4},{6,7},{7,6},{8,9},{9,8},{10,11... | collective-permute-start | bytes 786440 | tf_op jit(solution)/shard_map/ppermute | solution.py:375
  95.4 5.9 %collective-permute-start.9 = (bf16[512,256]{1,0:T(8,128)(2,1)S(1)}, bf16[512,256]{1,0:T(8,128)(2,1)S(1)}, u32[]{:S(2)}, u32[]{:S(2)}) collective-permute-start(bf16[512,256]{1,0:T(8,128)(2,1)S(1)} %attend.2.own_ref), channel_id=1, source_target_pairs={{0,1},{1,0},{2,3},{3,2},{4,5},{5,4},{6,7},{7,6},{8,9},{9,8},{10,11... | collective-permute-start | bytes 786440 | tf_op jit(solution)/shard_map/ppermute | solution.py:375
  96.9 11.7 %collective-permute-start.22 = (bf16[512,256]{1,0:T(8,128)(2,1)S(1)}, bf16[512,256]{1,0:T(8,128)(2,1)S(1)}, u32[]{:S(2)}, u32[]{:S(2)}) collective-permute-start(bf16[512,256]{1,0:T(8,128)(2,1)S(1)} %get-tuple-element.47), channel_id=1, source_target_pairs={{0,14},{2,0},{4,2},{6,4},{8,6},{10,8},{12,10},{14,12},{1,15},{3,1}... | collective-permute-start | bytes 786440 | tf_op jit(solution)/shard_map/ppermute | solution.py:284
  101.3 10.8 %collective-permute-start.19 = (bf16[512,256]{1,0:T(8,128)(2,1)S(1)}, bf16[512,256]{1,0:T(8,128)(2,1)S(1)}, u32[]{:S(2)}, u32[]{:S(2)}) collective-permute-start(bf16[512,256]{1,0:T(8,128)(2,1)S(1)} %get-tuple-element.44), channel_id=1, source_target_pairs={{0,2},{2,4},{4,6},{6,8},{8,10},{10,12},{12,14},{14,0},{1,3},{3,5},... | collective-permute-start | bytes 786440 | tf_op jit(solution)/shard_map/ppermute | solution.py:284
  102.3 11.3 %collective-permute-start.15 = (bf16[512,256]{1,0:T(8,128)(2,1)S(1)}, bf16[512,256]{1,0:T(8,128)(2,1)S(1)}, u32[]{:S(2)}, u32[]{:S(2)}) collective-permute-start(bf16[512,256]{1,0:T(8,128)(2,1)S(1)} %get-tuple-element.39), channel_id=1, source_target_pairs={{0,14},{2,0},{4,2},{6,4},{8,6},{10,8},{12,10},{14,12},{1,15},{3,1}... | collective-permute-start | bytes 786440 | tf_op jit(solution)/shard_map/ppermute | solution.py:284
  105.6 11.8 %collective-permute-start.11 = (bf16[512,256]{1,0:T(8,128)(2,1)S(1)}, bf16[512,256]{1,0:T(8,128)(2,1)S(1)}, u32[]{:S(2)}, u32[]{:S(2)}) collective-permute-start(bf16[512,256]{1,0:T(8,128)(2,1)S(1)} %get-tuple-element.35), channel_id=1, source_target_pairs={{0,2},{2,4},{4,6},{6,8},{8,10},{10,12},{12,14},{14,0},{1,3},{3,5},... | collective-permute-start | bytes 786440 | tf_op jit(solution)/shard_map/ppermute | solution.py:284
  108.7 10.5 %collective-permute-start.23 = (bf16[512,256]{1,0:T(8,128)(2,1)S(1)}, bf16[512,256]{1,0:T(8,128)(2,1)S(1)}, u32[]{:S(2)}, u32[]{:S(2)}) collective-permute-start(bf16[512,256]{1,0:T(8,128)(2,1)S(1)} %add_convert_fusion.3), channel_id=1, source_target_pairs={{0,14},{2,0},{4,2},{6,4},{8,6},{10,8},{12,10},{14,12},{1,15},{3,1}... | collective-permute-start | bytes 786440 | tf_op jit(solution)/shard_map/ppermute | solution.py:284
  112.1 11.2 %collective-permute-start.20 = (bf16[512,256]{1,0:T(8,128)(2,1)S(1)}, bf16[512,256]{1,0:T(8,128)(2,1)S(1)}, u32[]{:S(2)}, u32[]{:S(2)}) collective-permute-start(bf16[512,256]{1,0:T(8,128)(2,1)S(1)} %add_convert_fusion.5), channel_id=1, source_target_pairs={{0,2},{2,4},{4,6},{6,8},{8,10},{10,12},{12,14},{14,0},{1,3},{3,5},... | collective-permute-start | bytes 786440 | tf_op jit(solution)/shard_map/ppermute | solution.py:284
  113.6 19.7 %collective-permute-start.16 = (bf16[512,256]{1,0:T(8,128)(2,1)S(1)}, bf16[512,256]{1,0:T(8,128)(2,1)S(1)}, u32[]{:S(2)}, u32[]{:S(2)}) collective-permute-start(bf16[512,256]{1,0:T(8,128)(2,1)S(1)} %add_convert_fusion.8), channel_id=1, source_target_pairs={{0,14},{2,0},{4,2},{6,4},{8,6},{10,8},{12,10},{14,12},{1,15},{3,1}... | collective-permute-start | bytes 786440 | tf_op jit(solution)/shard_map/ppermute | solution.py:284
  117.5 11.1 %collective-permute-start.12 = (bf16[512,256]{1,0:T(8,128)(2,1)S(1)}, bf16[512,256]{1,0:T(8,128)(2,1)S(1)}, u32[]{:S(2)}, u32[]{:S(2)}) collective-permute-start(bf16[512,256]{1,0:T(8,128)(2,1)S(1)} %add_convert_fusion.11), channel_id=1, source_target_pairs={{0,2},{2,4},{4,6},{6,8},{8,10},{10,12},{12,14},{14,0},{1,3},{3,5},... | collective-permute-start | bytes 786440 | tf_op jit(solution)/shard_map/ppermute | solution.py:284
  119.2 10.2 %collective-permute-start.24 = (bf16[512,256]{1,0:T(8,128)(2,1)S(1)}, bf16[512,256]{1,0:T(8,128)(2,1)S(1)}, u32[]{:S(2)}, u32[]{:S(2)}) collective-permute-start(bf16[512,256]{1,0:T(8,128)(2,1)S(1)} %add_convert_fusion.2), channel_id=1, source_target_pairs={{0,14},{2,0},{4,2},{6,4},{8,6},{10,8},{12,10},{14,12},{1,15},{3,1}... | collective-permute-start | bytes 786440 | tf_op jit(solution)/shard_map/ppermute | solution.py:284
  123.3 15.4 %collective-permute-start.21 = (bf16[512,256]{1,0:T(8,128)(2,1)S(1)}, bf16[512,256]{1,0:T(8,128)(2,1)S(1)}, u32[]{:S(2)}, u32[]{:S(2)}) collective-permute-start(bf16[512,256]{1,0:T(8,128)(2,1)S(1)} %add_convert_fusion.4), channel_id=1, source_target_pairs={{0,2},{2,4},{4,6},{6,8},{8,10},{10,12},{12,14},{14,0},{1,3},{3,5},... | collective-permute-start | bytes 786440 | tf_op jit(solution)/shard_map/ppermute | solution.py:284
  128.6 9.9 %collective-permute-start.13 = (bf16[512,256]{1,0:T(8,128)(2,1)S(1)}, bf16[512,256]{1,0:T(8,128)(2,1)S(1)}, u32[]{:S(2)}, u32[]{:S(2)}) collective-permute-start(bf16[512,256]{1,0:T(8,128)(2,1)S(1)} %add_convert_fusion.10), channel_id=1, source_target_pairs={{0,2},{2,4},{4,6},{6,8},{8,10},{10,12},{12,14},{14,0},{1,3},{3,5},... | collective-permute-start | bytes 786440 | tf_op jit(solution)/shard_map/ppermute | solution.py:284
  129.6 10.5 %collective-permute-start.25 = (bf16[512,256]{1,0:T(8,128)(2,1)S(1)}, bf16[512,256]{1,0:T(8,128)(2,1)S(1)}, u32[]{:S(2)}, u32[]{:S(2)}) collective-permute-start(bf16[512,256]{1,0:T(8,128)(2,1)S(1)} %add_convert_fusion.1), channel_id=1, source_target_pairs={{0,14},{2,0},{4,2},{6,4},{8,6},{10,8},{12,10},{14,12},{1,15},{3,1}... | collective-permute-start | bytes 786440 | tf_op jit(solution)/shard_map/ppermute | solution.py:284
  133.4 10.5 %collective-permute-start.17 = (bf16[512,256]{1,0:T(8,128)(2,1)S(1)}, bf16[512,256]{1,0:T(8,128)(2,1)S(1)}, u32[]{:S(2)}, u32[]{:S(2)}) collective-permute-start(bf16[512,256]{1,0:T(8,128)(2,1)S(1)} %add_convert_fusion.7), channel_id=1, source_target_pairs={{0,14},{2,0},{4,2},{6,4},{8,6},{10,8},{12,10},{14,12},{1,15},{3,1}... | collective-permute-start | bytes 786440 | tf_op jit(solution)/shard_map/ppermute | solution.py:284
  138.6 8.4 %collective-permute-start.14 = (bf16[512,256]{1,0:T(8,128)(2,1)S(1)}, bf16[512,256]{1,0:T(8,128)(2,1)S(1)}, u32[]{:S(2)}, u32[]{:S(2)}) collective-permute-start(bf16[512,256]{1,0:T(8,128)(2,1)S(1)} %add_convert_fusion.9), channel_id=1, source_target_pairs={{0,2},{2,4},{4,6},{6,8},{8,10},{10,12},{12,14},{14,0},{1,3},{3,5},... | collective-permute-start | bytes 786440 | tf_op jit(solution)/shard_map/ppermute | solution.py:284

commit v10 on v8

--- a/solution.py
+++ b/solution.py
@@ -150,30 +150,26 @@
         out_shape=jax.ShapeDtypeStruct(own.shape, BF16),
         in_specs=[VMEM, VMEM],
         out_specs=VMEM,
-        compiler_params=pltpu.CompilerParams(vmem_limit_bytes=8 << 20),
+        compiler_params=pltpu.CompilerParams(vmem_limit_bytes=56 << 20),
         cost_estimate=pl.CostEstimate(flops=1 << 20, bytes_accessed=3 << 20, transcendentals=0),
         name="finish_queries",
     )(own, lent)
 
 
 def attend_kernel(
-    part, slot_ref, length_ref, queries_ref, rows_ref, out_ref, query_ref, held_ref, sems, query_sem
+    slot_ref, length_ref, queries_ref, rows_ref, out_ref, query_ref, held_ref, sems, query_sem
 ):
     spans = slot_ref.shape[0] // NBRS
-    count = sems.shape[0] // NBRS
-    first = part * count
-    query_copy = pltpu.make_async_copy(
-        queries_ref.at[pl.ds(first * SPAN, count * SPAN)], query_ref, query_sem
-    )
+    query_copy = pltpu.make_async_copy(queries_ref, query_ref, query_sem)
     query_copy.start()
     width = out_ref.shape[1]
     keys = NBRS * NBR_LEN
     factor = 2.0 / math.sqrt(HD)
     copies = []
-    for c in range(count):
+    for c in range(spans):
         for n in range(NBRS):
             copy = pltpu.make_async_copy(
-                rows_ref.at[slot_ref[n * spans + first + c]],
+                rows_ref.at[slot_ref[n * spans + c]],
                 held_ref.at[pl.ds((c * NBRS + n) * NBR_LEN, NBR_LEN)],
                 sems.at[c * NBRS + n],
             )
@@ -182,7 +178,7 @@
     query_copy.wait()
     places = lax.broadcasted_iota(jnp.int32, (SPAN, keys), 1)
     group = 4
-    for start in range(0, count, group):
+    for start in range(0, spans, group):
         members = [(c, h) for c in range(start, start + group) for h in range(width // HD)]
         for copy in copies[start * NBRS : (start + group) * NBRS]:
             copy.wait()
@@ -194,7 +190,7 @@
                 (((1,), (1,)), ((), ())),
                 preferred_element_type=F32,
             )
-            ends = [length_ref[n * spans + first + c] + n * NBR_LEN for n in range(NBRS)]
+            ends = [length_ref[n * spans + c] + n * NBR_LEN for n in range(NBRS)]
             valid = (places < ends[0]) | ((places >= NBR_LEN) & (places < ends[1]))
             raised.append(jnp.where(valid, jnp.exp(scores * factor), 0.0))
         weights = [
@@ -208,11 +204,11 @@
             out_ref[c * SPAN : (c + 1) * SPAN, h * HD : (h + 1) * HD] = result.astype(BF16)
 
 
-def attend(part, parts, slot_index, lengths, queries, rows):
-    tokens, width = queries.shape[0] // parts, queries.shape[1]
+def attend(slot_index, lengths, queries, rows):
+    tokens, width = queries.shape
     requests = tokens // SPAN * NBRS
     return pl.pallas_call(
-        functools.partial(attend_kernel, part),
+        attend_kernel,
         out_shape=jax.ShapeDtypeStruct((tokens, width), BF16),
         in_specs=[SMEM, SMEM, ANY, ANY],
         out_specs=VMEM,
@@ -222,7 +218,7 @@
             pltpu.SemaphoreType.DMA((requests,)),
             pltpu.SemaphoreType.DMA,
         ],
-        compiler_params=pltpu.CompilerParams(vmem_limit_bytes=56 << 20),
+        compiler_params=pltpu.CompilerParams(vmem_limit_bytes=24 << 20),
         cost_estimate=SMALL,
         name="attend",
     )(slot_index, lengths, queries, rows)
@@ -250,60 +246,77 @@
     )(place, weight)
 
 
-def share_kernel(steps, place_ref, own_ref, partner_ref, weight_ref, partner_w_ref, *out_refs):
+def share_kernel(parts, place_ref, own_ref, partner_ref, weight_ref, partner_w_ref, *out_refs):
     here, core = place_ref[0], place_ref[1]
     ring, _, width = partner_w_ref.shape
-    for step, ref in zip(steps, out_refs):
+    for (half, step), ref in zip(parts, out_refs):
         chip = lax.rem(here + step, ring)
         cols = pl.ds(pl.multiple_of((chip * 2 + core) * width, width), width)
+        rows = slice(half * ref.shape[0], (half + 1) * ref.shape[0])
         ref[...] = (
-            jnp.dot(own_ref[...], weight_ref[:, cols], preferred_element_type=F32)
-            + jnp.dot(partner_ref[...], partner_w_ref[step], preferred_element_type=F32)
+            jnp.dot(own_ref[rows], weight_ref[:, cols], preferred_element_type=F32)
+            + jnp.dot(partner_ref[rows], partner_w_ref[step], preferred_element_type=F32)
         ).astype(ref.dtype)
 
 
-def shares(place, steps, dtype, own, partner, weight, partner_weight):
-    rows, width = own.shape
-    return pl.pallas_call(
-        functools.partial(share_kernel, steps),
-        out_shape=[jax.ShapeDtypeStruct((rows, width), dtype)] * len(steps),
+def shares(place, parts, dtype, own, partner, weight, partner_weight):
+    rows, width = own.shape[0] // 2, own.shape[1]
+    made = pl.pallas_call(
+        functools.partial(share_kernel, parts),
+        out_shape=[jax.ShapeDtypeStruct((rows, width), dtype)] * len(parts),
         in_specs=[SMEM] + [VMEM] * 4,
-        out_specs=[VMEM] * len(steps),
+        out_specs=[VMEM] * len(parts),
         compiler_params=pltpu.CompilerParams(vmem_limit_bytes=12 << 20),
         cost_estimate=SMALL,
         name="shares",
     )(place, own, partner, weight, partner_weight)
+    return dict(zip(parts, made))
+
+
+def total_kernel(*refs):
+    *in_refs, out_ref = refs
+    rows = in_refs[0].shape[0]
+    for half in range(2):
+        part_ref, one_ref, other_ref = in_refs[half], in_refs[2 + half], in_refs[4 + half]
+        total = part_ref[...] + one_ref[...].astype(F32) + other_ref[...].astype(F32)
+        out_ref[half * rows : (half + 1) * rows] = total.astype(BF16)
+
+
+def total_rows(parts, sums):
+    rows, width = parts[0].shape
+    return pl.pallas_call(
+        total_kernel,
+        out_shape=jax.ShapeDtypeStruct((2 * rows, width), BF16),
+        in_specs=[VMEM] * 6,
+        out_specs=VMEM,
+        compiler_params=pltpu.CompilerParams(vmem_limit_bytes=8 << 20),
+        cost_estimate=SMALL,
+        name="total_rows",
+    )(*parts, *sums)
 
 
 def reduce_ring(place, attended, partner_attended, weight, partner_weight, ring):
     up = [(i, (i + 1) % ring) for i in range(ring)]
     down = [(i, (i - 1) % ring) for i in range(ring)]
-
-    def send(sums, way):
-        return lax.ppermute(sums, "z", up if way == 1 else down)
-
+    operands = (attended, partner_attended, weight, partner_weight)
     far = ring // 2
     chains = [(0, 1, far), (1, -1, far), (0, -1, far - 1), (1, 1, far - 1)]
-    held, part = {}, {}
+    begun, held = {}, {}
+    for pair in (chains[:2], chains[2:]):
+        begun.update(shares(place, [(h, w * d % ring) for h, w, d in pair], BF16, *operands))
+        for half, way, first in pair:
+            sums = begun[half, way * first % ring]
+            held[half, way] = lax.ppermute(sums, "z", up if way == 1 else down)
+    part = {}
     for half in range(2):
-        mine = [(way, first) for rows, way, first in chains if rows == half]
-        starts = [way * first % ring for way, first in mine]
-        rest = [k for k in range(ring) if k not in starts]
-        operands = (attended[half], partner_attended[half], weight, partner_weight)
-        begun = shares(place, starts, BF16, *operands)
-        held.update({(half, way): send(begun[i], way) for i, (way, _) in enumerate(mine)})
-        others = shares(place, rest, F32, *operands)
-        part.update({(half, k): others[i] for i, k in enumerate(rest)})
-    for distance in range(far, 0, -1):
+        rest = [(half, k) for k in range(ring) if (half, k) not in begun]
+        part.update(shares(place, rest, F32, *operands))
+    for distance in range(far - 1, 0, -1):
         for half, way, first in chains:
             if distance < first:
                 total = held[half, way].astype(F32) + part[half, way * distance % ring]
-                held[half, way] = send(total.astype(BF16), way)
-    out = [
-        (part[half, 0] + held[half, 1].astype(F32) + held[half, -1].astype(F32)).astype(BF16)
-        for half in range(2)
-    ]
-    return jnp.concatenate(out, axis=0)
+                held[half, way] = lax.ppermute(total.astype(BF16), "z", up if way == 1 else down)
+    return total_rows([part[half, 0] for half in range(2)], list(held.values()))
 
 
 def local(
@@ -369,10 +382,8 @@
 
     own, lent = project_queries(place, [pieces[k] for k in range(ring)], by_core, partner_rows)
     lent = lax.ppermute(lent, "c", swap)
-    queries = finish_queries(own, lent)
-
-    attended = [attend(part, 2, slot_index, lengths, queries, rows) for part in range(2)]
-    partner_attended = [lax.ppermute(part, "c", swap) for part in attended]
+    attended = attend(slot_index, lengths, finish_queries(own, lent), rows)
+    partner_attended = lax.ppermute(attended, "c", swap)
     return reduce_ring(place, attended, partner_attended, out_weight, partner_weight, ring)
 
 

time: 150 us -> 144 us (0.960)
  other arithmetic: 4.55 us -> 2.26 us
  waiting for transfers between devices: 55 us -> 52.8 us
  Pallas kernels: 32.5 us -> 30.5 us
    ppermute x16 -> x15, waiting for transfers between devices: 21.7 us -> 17.4 us  [the longest x10 13 us: reduce_ring(): lax.ppermute(total.astype(BF16), 'z', up if way == 1 else down)]
    pallas_call x6, Pallas kernels: 13.5 us -> 10.3 us  [the longest x4 5.01 us: shares(): pl.pallas_call(functools.partial(share_kernel, parts), out_shape=[jax.Sha...]
    all_to_all x1, waiting for transfers between devices: 1.66 us -> 3.67 us  [local(): rows = lax.all_to_all(sent, DB, split_axis=0, concat_axis=0, tiled=True)]
    ppermute x16 -> x15, starting transfers between devices: 24.2 us -> 25.1 us  [the longest x10 18.5 us: reduce_ring(): lax.ppermute(total.astype(BF16), 'z', up if way == 1 else down)]
  transfers between devices with their start and end apart: 28 -> 27, of which waited for: 14 -> 16; matrix products, arithmetic and copies ran while one was open for 4% -> 3% of each run, Pallas kernels for 22% -> 20%
where the time goes in v10:
time: 144 us; the launch traced here: 143 us
  starting transfers between devices  52.8 us (37%)
  waiting for transfers between devices  52.8 us (37%)
  Pallas kernels  30.5 us (21%)
  local copies, waits for them, and re-layouts  4.06 us (3%)
  other arithmetic  2.26 us (2%)
    ppermute x10, starting transfers between devices, reduce_ring(): lax.ppermute(total.astype(BF16), 'z', up if way == 1 else down)  18.5 us
    ppermute x2, waiting for transfers between devices, local(): pieces[ring - k] = lax.ppermute(pieces[ring - k + 1], 'z', down)  17.4 us
    ppermute x10, waiting for transfers between devices, reduce_ring(): lax.ppermute(total.astype(BF16), 'z', up if way == 1 else down)  13 us
    ppermute x1, waiting for transfers between devices, local(): pieces[ring - 1] = lax.ppermute(tokens, 'z', down)  10.2 us
    ppermute x2, starting transfers between devices, local(): pieces[ring - k] = lax.ppermute(pieces[ring - k + 1], 'z', down)  7.38 us
    all_to_all x1, starting transfers between devices, local(): heard = lax.all_to_all(notes, DB, split_axis=0, concat_axis=0, tiled=True)  7.17 us
    pallas_call x1, Pallas kernels, project_queries(): pl.pallas_call(query_kernel, grid=(rows // tile,), out_shape=(out, out),...  6.93 us
    all_to_all x1, starting transfers between devices, local(): rows = lax.all_to_all(sent, DB, split_axis=0, concat_axis=0, tiled=True)  6.63 us
  transfers between devices with their start and end apart: 27, of which 16 were waited for; matrix products, arithmetic and copies ran while one was open for 3% of the time, Pallas kernels for 20%

profile of v10, /device:TPU:24, one launch (start us, length us, event | category | flops | bytes accessed | tf_op | source)
XLA Modules:
  0.0 142.6 jit_solution(5607992004079801038)
XLA Ops:
  0.0 1.9 %collective-permute-start = (bf16[1024,256]{1,0:T(8,128)(2,1)}, bf16[1024,256]{1,0:T(8,128)(2,1)}, u32[]{:S(2)}, u32[]{:S(2)}) collective-permute-start(bf16[1024,256]{1,0:T(8,128)(2,1)} %refs_0_.1), channel_id=1, source_target_pairs={{0,2},{2,4},{4,6},{6,8},{8,10},{10,12},{12,14},{14,0},{1,3},{3,5},... | collective-permute-start | bytes 1572872 | tf_op jit(solution)/shard_map/ppermute | solution.py:352
  1.9 0.7 pad_bitcast_fusion
  2.6 0.7 bitcast_add_fusion
  3.3 0.6 broadcast_in_dim.27
  3.9 7.2 %all-to-all-start = ((s32[16,3,16]{2,1,0:T(4,128)}), s32[16,3,16]{2,1,0:T(4,128)S(1)}, u32[]{:S(2)}, u32[]{:S(2)}) async-start(s32[16,3,16]{2,1,0:T(4,128)} %broadcast_in_dim.27), calls=%async_computation | async-start | bytes 65536 | tf_op jit(solution)/shard_map/all_to_all | solution.py:347
  11.1 4.9 %project_blocks.1.rows_ref = bf16[8,128,512]{2,1,0:T(8,128)(2,1)} custom-call(f32[8,7]{1,0:T(8,128)} %scales_ref.1, bf16[8,128,896]{2,1,0:T(8,128)(2,1)} %codes_ref.1, bf16[896,256]{1,0:T(8,128)(2,1)} %key_ref.1, bf16[896,256]{1,0:T(8,128)(2,1)} %value_ref.1), custom_call_target="tpu_custom_call" | custom-call | flops 939524096 | bytes 5242880 | tf_op jit(solution)/shard_map/project_blocks/pallas_call | solution.py:53
  16.0 0.7 all-to-all-done.heard_ref
  16.7 0.6 copy-done.4
  17.3 3.9 %select_blocks.1 = bf16[16,2,128,512]{3,2,1,0:T(8,128)(2,1)} custom-call(s32[1]{0:T(128)} %bitcast.5.place_ref, s32[16,3,16]{2,1,0:T(4,128)} %copy-done.4, bf16[8,128,512]{2,1,0:T(8,128)(2,1)} %project_blocks.1.rows_ref), custom_call_target="tpu_custom_call" | custom-call | bytes 9437184 | tf_op jit(solution)/shard_map/select_blocks/pallas_call | solution.py:92
  21.3 6.6 %all-to-all-start.1 = ((bf16[16,2,128,512]{3,2,1,0:T(8,128)(2,1)}), bf16[16,2,128,512]{3,2,1,0:T(8,128)(2,1)}, u32[]{:S(2)}, u32[]{:S(2)}) async-start(bf16[16,2,128,512]{3,2,1,0:T(8,128)(2,1)} %select_blocks.1), calls=%async_computation.1 | async-start | bytes 8388608 | tf_op jit(solution)/shard_map/all_to_all | solution.py:356
  27.9 3.9 %collective-permute-start.4 = (bf16[1024,256]{1,0:T(8,128)(2,1)}, bf16[1024,256]{1,0:T(8,128)(2,1)}, u32[]{:S(2)}, u32[]{:S(2)}) collective-permute-start(bf16[1024,256]{1,0:T(8,128)(2,1)} %refs_0_.1), channel_id=1, source_target_pairs={{0,14},{2,0},{4,2},{6,4},{8,6},{10,8},{12,10},{14,12},{1,15},{3,1}... | collective-permute-start | bytes 1572872 | tf_op jit(solution)/shard_map/ppermute | solution.py:353
  32.0 10.2 %collective-permute-done.4.refs_7_ = bf16[1024,256]{1,0:T(8,128)(2,1)} collective-permute-done((bf16[1024,256]{1,0:T(8,128)(2,1)}, bf16[1024,256]{1,0:T(8,128)(2,1)}, u32[]{:S(2)}, u32[]{:S(2)}) %collective-permute-start.4) | collective-permute-done | bytes 524320 | tf_op jit(solution)/shard_map/ppermute | solution.py:353
  42.2 3.7 %collective-permute-start.5 = (bf16[1024,256]{1,0:T(8,128)(2,1)}, bf16[1024,256]{1,0:T(8,128)(2,1)}, u32[]{:S(2)}, u32[]{:S(2)}) collective-permute-start(bf16[1024,256]{1,0:T(8,128)(2,1)} %collective-permute-done.4.refs_7_), channel_id=1, source_target_pairs={{0,14},{2,0},{4,2},{6,4},{8,6},{10,8},{12,10},{14,12},{1,15},{3,1}... | collective-permute-start | bytes 1572872 | tf_op jit(solution)/shard_map/ppermute | solution.py:376
  45.9 9.5 %collective-permute-done.5.refs_6_ = bf16[1024,256]{1,0:T(8,128)(2,1)} collective-permute-done((bf16[1024,256]{1,0:T(8,128)(2,1)}, bf16[1024,256]{1,0:T(8,128)(2,1)}, u32[]{:S(2)}, u32[]{:S(2)}) %collective-permute-start.5) | collective-permute-done | bytes 524320 | tf_op jit(solution)/shard_map/ppermute | solution.py:376
  55.4 3.7 %collective-permute-start.6 = (bf16[1024,256]{1,0:T(8,128)(2,1)}, bf16[1024,256]{1,0:T(8,128)(2,1)}, u32[]{:S(2)}, u32[]{:S(2)}) collective-permute-start(bf16[1024,256]{1,0:T(8,128)(2,1)} %collective-permute-done.5.refs_6_), channel_id=1, source_target_pairs={{0,14},{2,0},{4,2},{6,4},{8,6},{10,8},{12,10},{14,12},{1,15},{3,1}... | collective-permute-start | bytes 1572872 | tf_op jit(solution)/shard_map/ppermute | solution.py:376
  59.1 0.6 pad_add_fusion.1.place_ref
  59.7 7.9 %collective-permute-done.6.refs_5_ = bf16[1024,256]{1,0:T(8,128)(2,1)} collective-permute-done((bf16[1024,256]{1,0:T(8,128)(2,1)}, bf16[1024,256]{1,0:T(8,128)(2,1)}, u32[]{:S(2)}, u32[]{:S(2)}) %collective-permute-start.6) | collective-permute-done | bytes 524320 | tf_op jit(solution)/shard_map/ppermute | solution.py:376
  67.6 3.4 %collective-permute-done.3.refs_4_ = bf16[1024,256]{1,0:T(8,128)(2,1)} collective-permute-done((bf16[1024,256]{1,0:T(8,128)(2,1)}, bf16[1024,256]{1,0:T(8,128)(2,1)}, u32[]{:S(2)}, u32[]{:S(2)}) %collective-permute-start.3) | collective-permute-done | bytes 524320 | tf_op jit(solution)/shard_map/ppermute | solution.py:374
  71.0 6.9 %project_queries.1 = (f32[1024,256]{1,0:T(8,128)}, f32[1024,256]{1,0:T(8,128)}) custom-call(s32[2]{0:T(128)} %pad_add_fusion.1.place_ref, bf16[1024,256]{1,0:T(8,128)(2,1)} %refs_0_.1, bf16[1024,256]{1,0:T(8,128)(2,1)} %collective-permute-done.refs_1_, bf16[1024,256]{1,0:T(8,128)(2,1)} %collective-permute-done.1.refs_2_, ...), custom_call_target="tpu_custom_call" | custom-call | flops 2147483648 | bytes 9437184 | tf_op jit(solution)/shard_map/project_queries/pallas_call | solution.py:122
  78.1 1.7 %relay.1 = bf16[8,256,256]{2,1,0:T(8,128)(2,1)} custom-call(s32[2]{0:T(128)S(1)} %copy-done.2, bf16[256,4096]{1,0:T(8,128)(2,1)S(1)} %copy-done), custom_call_target="tpu_custom_call" | custom-call | bytes 3145728 | tf_op jit(solution)/shard_map/relay/pallas_call | solution.py:238
  79.8 0.5 collective-permute-start.10
  80.7 0.8 slice_reduce_fusion
  81.7 2.7 %finish_queries.1.queries_ref = bf16[1024,256]{1,0:T(8,128)(2,1)} custom-call(f32[1024,256]{1,0:T(8,128)} %get-tuple-element.29.own_ref, f32[1024,256]{1,0:T(8,128)} %collective-permute-done.8.lent_ref), custom_call_target="tpu_custom_call" | custom-call | flops 1048576 | bytes 3145728 | tf_op jit(solution)/shard_map/finish_queries/pallas_call | solution.py:148
  84.4 3.7 %all-to-all-done.1 = bf16[16,2,128,512]{3,2,1,0:T(8,128)(2,1)} async-done(((bf16[16,2,128,512]{3,2,1,0:T(8,128)(2,1)}), bf16[16,2,128,512]{3,2,1,0:T(8,128)(2,1)}, u32[]{:S(2)}, u32[]{:S(2)}) %all-to-all-start.1) | async-done | bytes 4194336 | tf_op jit(solution)/shard_map/all_to_all | solution.py:356
  88.1 1.0 copy-done.1
  89.1 4.4 %attend.1.own_ref = bf16[1024,256]{1,0:T(8,128)(2,1)S(1)} custom-call(s32[32]{0:T(128)S(1)} %multiply_add_fusion.slot_ref, s32[32]{0:T(128)S(1)} %select_reduce_fusion.length_ref, bf16[1024,256]{1,0:T(8,128)(2,1)S(1)} %copy-done.1, bf16[32,128,512]{2,1,0:T(8,128)(2,1)} %bitcast.8.rows_ref), custom_call_target="tpu_custom_call" | custom-call | flops 1024 | bytes 1024 | tf_op jit(solution)/shard_map/attend/pallas_call | solution.py:210
  93.6 1.9 %collective-permute-done.9.partner_ref = bf16[1024,256]{1,0:T(8,128)(2,1)S(1)} collective-permute-done((bf16[1024,256]{1,0:T(8,128)(2,1)S(1)}, bf16[1024,256]{1,0:T(8,128)(2,1)S(1)}, u32[]{:S(2)}, u32[]{:S(2)}) %collective-permute-start.9) | collective-permute-done | bytes 524320 | tf_op jit(solution)/shard_map/ppermute | solution.py:386
  95.5 1.0 shares.6
  96.5 2.0 %collective-permute-start.11 = (bf16[512,256]{1,0:T(8,128)(2,1)S(1)}, bf16[512,256]{1,0:T(8,128)(2,1)S(1)}, u32[]{:S(2)}, u32[]{:S(2)}) collective-permute-start(bf16[512,256]{1,0:T(8,128)(2,1)S(1)} %get-tuple-element.33), channel_id=1, source_target_pairs={{0,2},{2,4},{4,6},{6,8},{8,10},{10,12},{12,14},{14,0},{1,3},{3,5},... | collective-permute-start | bytes 786440 | tf_op jit(solution)/shard_map/ppermute | solution.py:309
  98.5 2.4 %collective-permute-start.15 = (bf16[512,256]{1,0:T(8,128)(2,1)S(1)}, bf16[512,256]{1,0:T(8,128)(2,1)S(1)}, u32[]{:S(2)}, u32[]{:S(2)}) collective-permute-start(bf16[512,256]{1,0:T(8,128)(2,1)S(1)} %get-tuple-element.37), channel_id=1, source_target_pairs={{0,14},{2,0},{4,2},{6,4},{8,6},{10,8},{12,10},{14,12},{1,15},{3,1}... | collective-permute-start | bytes 786440 | tf_op jit(solution)/shard_map/ppermute | solution.py:309
  100.9 1.0 shares.7
  101.9 2.0 %collective-permute-start.19 = (bf16[512,256]{1,0:T(8,128)(2,1)S(1)}, bf16[512,256]{1,0:T(8,128)(2,1)S(1)}, u32[]{:S(2)}, u32[]{:S(2)}) collective-permute-start(bf16[512,256]{1,0:T(8,128)(2,1)S(1)} %get-tuple-element.41), channel_id=1, source_target_pairs={{0,14},{2,0},{4,2},{6,4},{8,6},{10,8},{12,10},{14,12},{1,15},{3,1}... | collective-permute-start | bytes 786440 | tf_op jit(solution)/shard_map/ppermute | solution.py:309
  104.0 1.5 %shares.4 = (f32[512,256]{1,0:T(8,128)S(1)}, f32[512,256]{1,0:T(8,128)S(1)}, f32[512,256]{1,0:T(8,128)S(1)}, f32[512,256]{1,0:T(8,128)S(1)}, f32[512,256]{1,0:T(8,128)S(1)}, /*index=5*/f32[512,256]{1,0:T(8,128)S(1)}) custom-call(s32[2]{0:T(128)S(1)} %copy-done.2, bf16[1024,256]{1,0:T(8,128)(2,1)S(1)} %attend.1.own_ref, ...), custom_call_target="tpu_custom_call" | custom-call | flops 1024 | bytes 1024 | tf_op jit(solution)/shard_map/shares/pallas_call | solution.py:264
  105.5 1.5 %shares.5 = (f32[512,256]{1,0:T(8,128)S(1)}, f32[512,256]{1,0:T(8,128)S(1)}, f32[512,256]{1,0:T(8,128)S(1)}, f32[512,256]{1,0:T(8,128)S(1)}, f32[512,256]{1,0:T(8,128)S(1)}, /*index=5*/f32[512,256]{1,0:T(8,128)S(1)}) custom-call(s32[2]{0:T(128)S(1)} %copy-done.2, bf16[1024,256]{1,0:T(8,128)(2,1)S(1)} %attend.1.own_ref, ...), custom_call_target="tpu_custom_call" | custom-call | flops 1024 | bytes 1024 | tf_op jit(solution)/shard_map/shares/pallas_call | solution.py:264
  107.1 0.7 collective-permute-done.11
  108.0 3.4 %collective-permute-start.16 = (bf16[512,256]{1,0:T(8,128)(2,1)S(1)}, bf16[512,256]{1,0:T(8,128)(2,1)S(1)}, u32[]{:S(2)}, u32[]{:S(2)}) collective-permute-start(bf16[512,256]{1,0:T(8,128)(2,1)S(1)} %add_convert_fusion.6), channel_id=1, source_target_pairs={{0,14},{2,0},{4,2},{6,4},{8,6},{10,8},{12,10},{14,12},{1,15},{3,1}... | collective-permute-start | bytes 786440 | tf_op jit(solution)/shard_map/ppermute | solution.py:318
  111.4 1.9 %collective-permute-done.19 = bf16[512,256]{1,0:T(8,128)(2,1)S(1)} collective-permute-done((bf16[512,256]{1,0:T(8,128)(2,1)S(1)}, bf16[512,256]{1,0:T(8,128)(2,1)S(1)}, u32[]{:S(2)}, u32[]{:S(2)}) %collective-permute-start.19) | collective-permute-done | bytes 262176 | tf_op jit(solution)/shard_map/ppermute | solution.py:309
  113.3 3.7 %collective-permute-start.20 = (bf16[512,256]{1,0:T(8,128)(2,1)S(1)}, bf16[512,256]{1,0:T(8,128)(2,1)S(1)}, u32[]{:S(2)}, u32[]{:S(2)}) collective-permute-start(bf16[512,256]{1,0:T(8,128)(2,1)S(1)} %add_convert_fusion.3), channel_id=1, source_target_pairs={{0,14},{2,0},{4,2},{6,4},{8,6},{10,8},{12,10},{14,12},{1,15},{3,1}... | collective-permute-start | bytes 786440 | tf_op jit(solution)/shard_map/ppermute | solution.py:318
  117.2 1.5 %collective-permute-done.12 = bf16[512,256]{1,0:T(8,128)(2,1)S(1)} collective-permute-done((bf16[512,256]{1,0:T(8,128)(2,1)S(1)}, bf16[512,256]{1,0:T(8,128)(2,1)S(1)}, u32[]{:S(2)}, u32[]{:S(2)}) %collective-permute-start.12) | collective-permute-done | bytes 262176 | tf_op jit(solution)/shard_map/ppermute | solution.py:318
  118.9 3.9 %collective-permute-start.17 = (bf16[512,256]{1,0:T(8,128)(2,1)S(1)}, bf16[512,256]{1,0:T(8,128)(2,1)S(1)}, u32[]{:S(2)}, u32[]{:S(2)}) collective-permute-start(bf16[512,256]{1,0:T(8,128)(2,1)S(1)} %add_convert_fusion.5), channel_id=1, source_target_pairs={{0,14},{2,0},{4,2},{6,4},{8,6},{10,8},{12,10},{14,12},{1,15},{3,1}... | collective-permute-start | bytes 786440 | tf_op jit(solution)/shard_map/ppermute | solution.py:318
  122.9 1.6 %collective-permute-done.20 = bf16[512,256]{1,0:T(8,128)(2,1)S(1)} collective-permute-done((bf16[512,256]{1,0:T(8,128)(2,1)S(1)}, bf16[512,256]{1,0:T(8,128)(2,1)S(1)}, u32[]{:S(2)}, u32[]{:S(2)}) %collective-permute-start.20) | collective-permute-done | bytes 262176 | tf_op jit(solution)/shard_map/ppermute | solution.py:318
  124.6 3.7 %collective-permute-start.21 = (bf16[512,256]{1,0:T(8,128)(2,1)S(1)}, bf16[512,256]{1,0:T(8,128)(2,1)S(1)}, u32[]{:S(2)}, u32[]{:S(2)}) collective-permute-start(bf16[512,256]{1,0:T(8,128)(2,1)S(1)} %add_convert_fusion.2), channel_id=1, source_target_pairs={{0,14},{2,0},{4,2},{6,4},{8,6},{10,8},{12,10},{14,12},{1,15},{3,1}... | collective-permute-start | bytes 786440 | tf_op jit(solution)/shard_map/ppermute | solution.py:318
  128.4 2.0 %collective-permute-done.13 = bf16[512,256]{1,0:T(8,128)(2,1)S(1)} collective-permute-done((bf16[512,256]{1,0:T(8,128)(2,1)S(1)}, bf16[512,256]{1,0:T(8,128)(2,1)S(1)}, u32[]{:S(2)}, u32[]{:S(2)}) %collective-permute-start.13) | collective-permute-done | bytes 262176 | tf_op jit(solution)/shard_map/ppermute | solution.py:318
  130.7 3.3 %collective-permute-start.18 = (bf16[512,256]{1,0:T(8,128)(2,1)S(1)}, bf16[512,256]{1,0:T(8,128)(2,1)S(1)}, u32[]{:S(2)}, u32[]{:S(2)}) collective-permute-start(bf16[512,256]{1,0:T(8,128)(2,1)S(1)} %add_convert_fusion.4), channel_id=1, source_target_pairs={{0,14},{2,0},{4,2},{6,4},{8,6},{10,8},{12,10},{14,12},{1,15},{3,1}... | collective-permute-start | bytes 786440 | tf_op jit(solution)/shard_map/ppermute | solution.py:318
  133.9 1.8 %collective-permute-done.21.refs_4_ = bf16[512,256]{1,0:T(8,128)(2,1)S(1)} collective-permute-done((bf16[512,256]{1,0:T(8,128)(2,1)S(1)}, bf16[512,256]{1,0:T(8,128)(2,1)S(1)}, u32[]{:S(2)}, u32[]{:S(2)}) %collective-permute-start.21) | collective-permute-done | bytes 262176 | tf_op jit(solution)/shard_map/ppermute | solution.py:318
  135.7 3.1 %collective-permute-done.24.refs_5_ = bf16[512,256]{1,0:T(8,128)(2,1)S(1)} collective-permute-done((bf16[512,256]{1,0:T(8,128)(2,1)S(1)}, bf16[512,256]{1,0:T(8,128)(2,1)S(1)}, u32[]{:S(2)}, u32[]{:S(2)}) %collective-permute-start.24) | collective-permute-done | bytes 262176 | tf_op jit(solution)/shard_map/ppermute | solution.py:318
  138.9 2.8 %collective-permute-done.14.refs_2_ = bf16[512,256]{1,0:T(8,128)(2,1)S(1)} collective-permute-done((bf16[512,256]{1,0:T(8,128)(2,1)S(1)}, bf16[512,256]{1,0:T(8,128)(2,1)S(1)}, u32[]{:S(2)}, u32[]{:S(2)}) %collective-permute-start.14) | collective-permute-done | bytes 262176 | tf_op jit(solution)/shard_map/ppermute | solution.py:318
  141.7 0.9 total_rows.1
  (52 shorter events, 2.2 us)
Async XLA Ops:
  0.0 21.3 %collective-permute-start = (bf16[1024,256]{1,0:T(8,128)(2,1)}, bf16[1024,256]{1,0:T(8,128)(2,1)}, u32[]{:S(2)}, u32[]{:S(2)}) collective-permute-start(bf16[1024,256]{1,0:T(8,128)(2,1)} %refs_0_.1), channel_id=1, source_target_pairs={{0,2},{2,4},{4,6},{6,8},{8,10},{10,12},{12,14},{14,0},{1,3},{3,5},... | collective-permute-start | bytes 1572872 | tf_op jit(solution)/shard_map/ppermute | solution.py:352
  3.9 12.8 %all-to-all-start = ((s32[16,3,16]{2,1,0:T(4,128)}), s32[16,3,16]{2,1,0:T(4,128)S(1)}, u32[]{:S(2)}, u32[]{:S(2)}) async-start(s32[16,3,16]{2,1,0:T(4,128)} %broadcast_in_dim.27), calls=%async_computation | async-start | bytes 65536 | tf_op jit(solution)/shard_map/all_to_all | solution.py:347
  16.7 0.6 copy-start.4
  21.3 10.6 %copy-start.3 = (bf16[4096,256]{1,0:T(8,128)(2,1)S(1)}, bf16[4096,256]{1,0:T(8,128)(2,1)}, u32[]{:S(2)}) copy-start(bf16[4096,256]{1,0:T(8,128)(2,1)} %param.11) | copy-start | bytes 6291460
  21.3 66.8 %all-to-all-start.1 = ((bf16[16,2,128,512]{3,2,1,0:T(8,128)(2,1)}), bf16[16,2,128,512]{3,2,1,0:T(8,128)(2,1)}, u32[]{:S(2)}, u32[]{:S(2)}) async-start(bf16[16,2,128,512]{3,2,1,0:T(8,128)(2,1)} %select_blocks.1), calls=%async_computation.1 | async-start | bytes 8388608 | tf_op jit(solution)/shard_map/all_to_all | solution.py:356
  27.9 14.3 %collective-permute-start.4 = (bf16[1024,256]{1,0:T(8,128)(2,1)}, bf16[1024,256]{1,0:T(8,128)(2,1)}, u32[]{:S(2)}, u32[]{:S(2)}) collective-permute-start(bf16[1024,256]{1,0:T(8,128)(2,1)} %refs_0_.1), channel_id=1, source_target_pairs={{0,14},{2,0},{4,2},{6,4},{8,6},{10,8},{12,10},{14,12},{1,15},{3,1}... | collective-permute-start | bytes 1572872 | tf_op jit(solution)/shard_map/ppermute | solution.py:353
  31.9 14.1 %collective-permute-start.1 = (bf16[1024,256]{1,0:T(8,128)(2,1)}, bf16[1024,256]{1,0:T(8,128)(2,1)}, u32[]{:S(2)}, u32[]{:S(2)}) collective-permute-start(bf16[1024,256]{1,0:T(8,128)(2,1)} %collective-permute-done.refs_1_), channel_id=1, source_target_pairs={{0,2},{2,4},{4,6},{6,8},{8,10},{10,12},{12,14},{14,0},{1,3},{3,5},... | collective-permute-start | bytes 1572872 | tf_op jit(solution)/shard_map/ppermute | solution.py:374
  31.9 27.8 %collective-permute-start.7 = (bf16[8,256,256]{2,1,0:T(8,128)(2,1)S(1)}, bf16[8,256,256]{2,1,0:T(8,128)(2,1)}, u32[]{:S(2)}, u32[]{:S(2)}) collective-permute-start(bf16[8,256,256]{2,1,0:T(8,128)(2,1)S(1)} %dynamic-slice_bitcast_fusion), channel_id=1, source_target_pairs={{0,1},{1,0},{2,3},{3,2},{4,5},{5,4},{6,7},{7,6},{8,9},{9,8},{10,11... | collective-permute-start | bytes 3145736 | tf_op jit(solution)/shard_map/ppermute | solution.py:379
  42.2 13.2 %collective-permute-start.5 = (bf16[1024,256]{1,0:T(8,128)(2,1)}, bf16[1024,256]{1,0:T(8,128)(2,1)}, u32[]{:S(2)}, u32[]{:S(2)}) collective-permute-start(bf16[1024,256]{1,0:T(8,128)(2,1)} %collective-permute-done.4.refs_7_), channel_id=1, source_target_pairs={{0,14},{2,0},{4,2},{6,4},{8,6},{10,8},{12,10},{14,12},{1,15},{3,1}... | collective-permute-start | bytes 1572872 | tf_op jit(solution)/shard_map/ppermute | solution.py:376
  45.9 13.2 %collective-permute-start.2 = (bf16[1024,256]{1,0:T(8,128)(2,1)}, bf16[1024,256]{1,0:T(8,128)(2,1)}, u32[]{:S(2)}, u32[]{:S(2)}) collective-permute-start(bf16[1024,256]{1,0:T(8,128)(2,1)} %collective-permute-done.1.refs_2_), channel_id=1, source_target_pairs={{0,2},{2,4},{4,6},{6,8},{8,10},{10,12},{12,14},{14,0},{1,3},{3,5},... | collective-permute-start | bytes 1572872 | tf_op jit(solution)/shard_map/ppermute | solution.py:374
  55.4 12.2 %collective-permute-start.6 = (bf16[1024,256]{1,0:T(8,128)(2,1)}, bf16[1024,256]{1,0:T(8,128)(2,1)}, u32[]{:S(2)}, u32[]{:S(2)}) collective-permute-start(bf16[1024,256]{1,0:T(8,128)(2,1)} %collective-permute-done.5.refs_6_), channel_id=1, source_target_pairs={{0,14},{2,0},{4,2},{6,4},{8,6},{10,8},{12,10},{14,12},{1,15},{3,1}... | collective-permute-start | bytes 1572872 | tf_op jit(solution)/shard_map/ppermute | solution.py:376
  59.1 11.9 %collective-permute-start.3 = (bf16[1024,256]{1,0:T(8,128)(2,1)}, bf16[1024,256]{1,0:T(8,128)(2,1)}, u32[]{:S(2)}, u32[]{:S(2)}) collective-permute-start(bf16[1024,256]{1,0:T(8,128)(2,1)} %collective-permute-done.2.refs_3_), channel_id=1, source_target_pairs={{0,2},{2,4},{4,6},{6,8},{8,10},{10,12},{12,14},{14,0},{1,3},{3,5},... | collective-permute-start | bytes 1572872 | tf_op jit(solution)/shard_map/ppermute | solution.py:374
  59.7 18.4 %copy-start = (bf16[256,4096]{1,0:T(8,128)(2,1)S(1)}, bf16[256,4096]{1,0:T(8,128)(2,1)}, u32[]{:S(2)}) copy-start(bf16[256,4096]{1,0:T(8,128)(2,1)} %weight_ref.9) | copy-start | bytes 6291460
  59.7 18.4 %copy-start.2 = (s32[2]{0:T(128)S(1)}, s32[2]{0:T(128)}, u32[]{:S(2)}) copy-start(s32[2]{0:T(128)} %pad_add_fusion.1.place_ref) | copy-start | bytes 28
  78.0 2.4 %copy-start.5 = (s32[16,2]{0,1:T(2,128)S(1)}, s32[16,2]{0,1:T(2,128)}, u32[]{:S(2)}) copy-start(s32[16,2]{0,1:T(2,128)} %param.18) | copy-start | bytes 388
  78.0 3.7 %collective-permute-start.8 = (f32[1024,256]{1,0:T(8,128)}, f32[1024,256]{1,0:T(8,128)}, u32[]{:S(2)}, u32[]{:S(2)}) collective-permute-start(f32[1024,256]{1,0:T(8,128)} %get-tuple-element.30), channel_id=1, source_target_pairs={{0,1},{1,0},{2,3},{3,2},{4,5},{5,4},{6,7},{7,6},{8,9},{9,8},{10,11... | collective-permute-start | bytes 3145736 | tf_op jit(solution)/shard_map/ppermute | solution.py:384
  79.8 13.8 %collective-permute-start.10 = (bf16[8,256,256]{2,1,0:T(8,128)(2,1)}, bf16[8,256,256]{2,1,0:T(8,128)(2,1)S(1)}, u32[]{:S(2)}, u32[]{:S(2)}) collective-permute-start(bf16[8,256,256]{2,1,0:T(8,128)(2,1)} %relay.1), channel_id=1, source_target_pairs={{0,1},{1,0},{2,3},{3,2},{4,5},{5,4},{6,7},{7,6},{8,9},{9,8},{10,11... | collective-permute-start | bytes 3145736 | tf_op jit(solution)/shard_map/ppermute | solution.py:381
  88.1 1.0 copy-start.1
  93.5 2.0 %collective-permute-start.9 = (bf16[1024,256]{1,0:T(8,128)(2,1)S(1)}, bf16[1024,256]{1,0:T(8,128)(2,1)S(1)}, u32[]{:S(2)}, u32[]{:S(2)}) collective-permute-start(bf16[1024,256]{1,0:T(8,128)(2,1)S(1)} %attend.1.own_ref), channel_id=1, source_target_pairs={{0,1},{1,0},{2,3},{3,2},{4,5},{5,4},{6,7},{7,6},{8,9},{9,8},{10,11... | collective-permute-start | bytes 1572872 | tf_op jit(solution)/shard_map/ppermute | solution.py:386
  96.5 11.2 %collective-permute-start.11 = (bf16[512,256]{1,0:T(8,128)(2,1)S(1)}, bf16[512,256]{1,0:T(8,128)(2,1)S(1)}, u32[]{:S(2)}, u32[]{:S(2)}) collective-permute-start(bf16[512,256]{1,0:T(8,128)(2,1)S(1)} %get-tuple-element.33), channel_id=1, source_target_pairs={{0,2},{2,4},{4,6},{6,8},{8,10},{10,12},{12,14},{14,0},{1,3},{3,5},... | collective-permute-start | bytes 786440 | tf_op jit(solution)/shard_map/ppermute | solution.py:309
  98.5 9.4 %collective-permute-start.15 = (bf16[512,256]{1,0:T(8,128)(2,1)S(1)}, bf16[512,256]{1,0:T(8,128)(2,1)S(1)}, u32[]{:S(2)}, u32[]{:S(2)}) collective-permute-start(bf16[512,256]{1,0:T(8,128)(2,1)S(1)} %get-tuple-element.37), channel_id=1, source_target_pairs={{0,14},{2,0},{4,2},{6,4},{8,6},{10,8},{12,10},{14,12},{1,15},{3,1}... | collective-permute-start | bytes 786440 | tf_op jit(solution)/shard_map/ppermute | solution.py:309
  101.9 11.4 %collective-permute-start.19 = (bf16[512,256]{1,0:T(8,128)(2,1)S(1)}, bf16[512,256]{1,0:T(8,128)(2,1)S(1)}, u32[]{:S(2)}, u32[]{:S(2)}) collective-permute-start(bf16[512,256]{1,0:T(8,128)(2,1)S(1)} %get-tuple-element.41), channel_id=1, source_target_pairs={{0,14},{2,0},{4,2},{6,4},{8,6},{10,8},{12,10},{14,12},{1,15},{3,1}... | collective-permute-start | bytes 786440 | tf_op jit(solution)/shard_map/ppermute | solution.py:309
  103.9 13.1 %collective-permute-start.22 = (bf16[512,256]{1,0:T(8,128)(2,1)S(1)}, bf16[512,256]{1,0:T(8,128)(2,1)S(1)}, u32[]{:S(2)}, u32[]{:S(2)}) collective-permute-start(bf16[512,256]{1,0:T(8,128)(2,1)S(1)} %get-tuple-element.44), channel_id=1, source_target_pairs={{0,2},{2,4},{4,6},{6,8},{8,10},{10,12},{12,14},{14,0},{1,3},{3,5},... | collective-permute-start | bytes 786440 | tf_op jit(solution)/shard_map/ppermute | solution.py:309
  107.8 10.9 %collective-permute-start.12 = (bf16[512,256]{1,0:T(8,128)(2,1)S(1)}, bf16[512,256]{1,0:T(8,128)(2,1)S(1)}, u32[]{:S(2)}, u32[]{:S(2)}) collective-permute-start(bf16[512,256]{1,0:T(8,128)(2,1)S(1)} %add_convert_fusion.9), channel_id=1, source_target_pairs={{0,2},{2,4},{4,6},{6,8},{8,10},{10,12},{12,14},{14,0},{1,3},{3,5},... | collective-permute-start | bytes 786440 | tf_op jit(solution)/shard_map/ppermute | solution.py:318
  108.0 10.9 %collective-permute-start.16 = (bf16[512,256]{1,0:T(8,128)(2,1)S(1)}, bf16[512,256]{1,0:T(8,128)(2,1)S(1)}, u32[]{:S(2)}, u32[]{:S(2)}) collective-permute-start(bf16[512,256]{1,0:T(8,128)(2,1)S(1)} %add_convert_fusion.6), channel_id=1, source_target_pairs={{0,14},{2,0},{4,2},{6,4},{8,6},{10,8},{12,10},{14,12},{1,15},{3,1}... | collective-permute-start | bytes 786440 | tf_op jit(solution)/shard_map/ppermute | solution.py:318
  113.3 11.2 %collective-permute-start.20 = (bf16[512,256]{1,0:T(8,128)(2,1)S(1)}, bf16[512,256]{1,0:T(8,128)(2,1)S(1)}, u32[]{:S(2)}, u32[]{:S(2)}) collective-permute-start(bf16[512,256]{1,0:T(8,128)(2,1)S(1)} %add_convert_fusion.3), channel_id=1, source_target_pairs={{0,14},{2,0},{4,2},{6,4},{8,6},{10,8},{12,10},{14,12},{1,15},{3,1}... | collective-permute-start | bytes 786440 | tf_op jit(solution)/shard_map/ppermute | solution.py:318
  117.1 11.2 %collective-permute-start.23 = (bf16[512,256]{1,0:T(8,128)(2,1)S(1)}, bf16[512,256]{1,0:T(8,128)(2,1)S(1)}, u32[]{:S(2)}, u32[]{:S(2)}) collective-permute-start(bf16[512,256]{1,0:T(8,128)(2,1)S(1)} %add_convert_fusion.1), channel_id=1, source_target_pairs={{0,2},{2,4},{4,6},{6,8},{8,10},{10,12},{12,14},{14,0},{1,3},{3,5},... | collective-permute-start | bytes 786440 | tf_op jit(solution)/shard_map/ppermute | solution.py:318
  118.7 11.7 %collective-permute-start.13 = (bf16[512,256]{1,0:T(8,128)(2,1)S(1)}, bf16[512,256]{1,0:T(8,128)(2,1)S(1)}, u32[]{:S(2)}, u32[]{:S(2)}) collective-permute-start(bf16[512,256]{1,0:T(8,128)(2,1)S(1)} %add_convert_fusion.8), channel_id=1, source_target_pairs={{0,2},{2,4},{4,6},{6,8},{8,10},{10,12},{12,14},{14,0},{1,3},{3,5},... | collective-permute-start | bytes 786440 | tf_op jit(solution)/shard_map/ppermute | solution.py:318
  118.9 11.6 %collective-permute-start.17 = (bf16[512,256]{1,0:T(8,128)(2,1)S(1)}, bf16[512,256]{1,0:T(8,128)(2,1)S(1)}, u32[]{:S(2)}, u32[]{:S(2)}) collective-permute-start(bf16[512,256]{1,0:T(8,128)(2,1)S(1)} %add_convert_fusion.5), channel_id=1, source_target_pairs={{0,14},{2,0},{4,2},{6,4},{8,6},{10,8},{12,10},{14,12},{1,15},{3,1}... | collective-permute-start | bytes 786440 | tf_op jit(solution)/shard_map/ppermute | solution.py:318
  124.6 11.2 %collective-permute-start.21 = (bf16[512,256]{1,0:T(8,128)(2,1)S(1)}, bf16[512,256]{1,0:T(8,128)(2,1)S(1)}, u32[]{:S(2)}, u32[]{:S(2)}) collective-permute-start(bf16[512,256]{1,0:T(8,128)(2,1)S(1)} %add_convert_fusion.2), channel_id=1, source_target_pairs={{0,14},{2,0},{4,2},{6,4},{8,6},{10,8},{12,10},{14,12},{1,15},{3,1}... | collective-permute-start | bytes 786440 | tf_op jit(solution)/shard_map/ppermute | solution.py:318
  128.3 10.5 %collective-permute-start.24 = (bf16[512,256]{1,0:T(8,128)(2,1)S(1)}, bf16[512,256]{1,0:T(8,128)(2,1)S(1)}, u32[]{:S(2)}, u32[]{:S(2)}) collective-permute-start(bf16[512,256]{1,0:T(8,128)(2,1)S(1)} %add_convert_fusion), channel_id=1, source_target_pairs={{0,2},{2,4},{4,6},{6,8},{8,10},{10,12},{12,14},{14,0},{1,3},{3,5},... | collective-permute-start | bytes 786440 | tf_op jit(solution)/shard_map/ppermute | solution.py:318
  130.5 11.2 %collective-permute-start.14 = (bf16[512,256]{1,0:T(8,128)(2,1)S(1)}, bf16[512,256]{1,0:T(8,128)(2,1)S(1)}, u32[]{:S(2)}, u32[]{:S(2)}) collective-permute-start(bf16[512,256]{1,0:T(8,128)(2,1)S(1)} %add_convert_fusion.7), channel_id=1, source_target_pairs={{0,2},{2,4},{4,6},{6,8},{8,10},{10,12},{12,14},{14,0},{1,3},{3,5},... | collective-permute-start | bytes 786440 | tf_op jit(solution)/shard_map/ppermute | solution.py:318
  130.7 11.0 %collective-permute-start.18 = (bf16[512,256]{1,0:T(8,128)(2,1)S(1)}, bf16[512,256]{1,0:T(8,128)(2,1)S(1)}, u32[]{:S(2)}, u32[]{:S(2)}) collective-permute-start(bf16[512,256]{1,0:T(8,128)(2,1)S(1)} %add_convert_fusion.4), channel_id=1, source_target_pairs={{0,14},{2,0},{4,2},{6,4},{8,6},{10,8},{12,10},{14,12},{1,15},{3,1}... | collective-permute-start | bytes 786440 | tf_op jit(solution)/shard_map/ppermute | solution.py:318

commit v11 on v10

--- a/solution.py
+++ b/solution.py
@@ -16,6 +16,7 @@
 NBR_LEN = 128
 NBRS = 2
 DB = ("y", "x")
+LENGTH = 1024
 F32 = jnp.float32
 BF16 = jnp.bfloat16
 VMEM = pl.BlockSpec(memory_space=pltpu.VMEM)
@@ -74,7 +75,12 @@
     lowest = place_ref[0] * blocks
     copies = []
     for e in range(shards):
-        named = [heard_ref[e, n, c] - lowest for n in range(NBRS) for c in range(spans)]
+        named = [
+            (heard_ref[e, n, c] & (LENGTH - 1) if n == 0 and c < blocks else heard_ref[e, n, c])
+            - lowest
+            for n in range(NBRS)
+            for c in range(spans)
+        ]
         first, last = jnp.int32(0), jnp.int32(0)
         for up, down in zip(named, reversed(named)):
             last = jnp.where((up >= 0) & (up < blocks), up, last)
@@ -308,10 +314,12 @@
             sums = begun[half, way * first % ring]
             held[half, way] = lax.ppermute(sums, "z", up if way == 1 else down)
     part = {}
-    for half in range(2):
-        rest = [(half, k) for k in range(ring) if (half, k) not in begun]
+    for distance in range(far - 1, 0, -1):
+        rest = [(h, w * distance % ring) for h, w, first in chains if distance < first]
+        rest += [(0, 0), (1, 0)] if distance == 1 else []
         part.update(shares(place, rest, F32, *operands))
-    for distance in range(far - 1, 0, -1):
+        own, _ = lax.optimization_barrier((attended, held[0, 1]))
+        operands = (own, *operands[1:])
         for half, way, first in chains:
             if distance < first:
                 total = held[half, way].astype(F32) + part[half, way * distance % ring]
@@ -342,8 +350,9 @@
     spans, blocks = nbr_owner.shape[0], block_len.shape[0]
 
     block_ids = nbr_owner.T * blocks + nbr_block.T
-    notes = jnp.concatenate([block_ids, jnp.pad(block_len, (0, spans - blocks))[None, :]], axis=0)
-    notes = jnp.broadcast_to(notes[None], (shards,) + notes.shape)
+    assert shards * blocks <= LENGTH and blocks <= spans
+    lengths_here = jnp.pad(block_len[None, :] * LENGTH, ((0, NBRS - 1), (0, spans - blocks)))
+    notes = jnp.broadcast_to((block_ids + lengths_here)[None], (shards, NBRS, spans))
     heard = lax.all_to_all(notes, DB, split_axis=0, concat_axis=0, tiled=True)
     projected = project_blocks(codes, scales, key_weight, value_weight)
     sent = select_blocks(lax.axis_index(DB).astype(jnp.int32).reshape(1), heard, projected)
@@ -364,7 +373,7 @@
         axis=1,
     )
     slot_index = owners * NBRS + earlier
-    all_lengths = heard[:, NBRS, :blocks].reshape(-1)
+    all_lengths = (heard[:, 0, :blocks] // LENGTH).reshape(-1)
     ids = jnp.arange(all_lengths.shape[0], dtype=jnp.int32)
     lengths = jnp.sum(
         jnp.where(block_ids[:, None] == ids[None, :], all_lengths[None, :], 0), axis=1

time: 144 us -> 144 us (level)
    ppermute x10, waiting for transfers between devices: 13 us -> 11.4 us  [reduce_ring(): lax.ppermute(total.astype(BF16), 'z', up if way == 1 else down)]
    pallas_call x4 -> x5, Pallas kernels: 5.01 us -> 5.71 us  [shares(): pl.pallas_call(functools.partial(share_kernel, parts), out_shape=[jax.Sha...]
  transfers between devices with their start and end apart: 27 -> 27, of which waited for: 16 -> 17; matrix products, arithmetic and copies ran while one was open for 3% -> 3% of each run, Pallas kernels for 20% -> 21%
where the time goes in v11:
time: 144 us; the launch traced here: 143 us
  starting transfers between devices  52.8 us (37%)
  waiting for transfers between devices  52.8 us (37%)
  Pallas kernels  31.2 us (22%)
  other arithmetic  2.9 us (2%)
  local copies, waits for them, and re-layouts  2.63 us (2%)
    ppermute x10, starting transfers between devices, reduce_ring(): lax.ppermute(total.astype(BF16), 'z', up if way == 1 else down)  18.5 us
    ppermute x2, waiting for transfers between devices, local(): pieces[ring - k] = lax.ppermute(pieces[ring - k + 1], 'z', down)  17.4 us
    ppermute x10, waiting for transfers between devices, reduce_ring(): lax.ppermute(total.astype(BF16), 'z', up if way == 1 else down)  11.4 us
    ppermute x1, waiting for transfers between devices, local(): pieces[ring - 1] = lax.ppermute(tokens, 'z', down)  10.2 us
    ppermute x2, starting transfers between devices, local(): pieces[ring - k] = lax.ppermute(pieces[ring - k + 1], 'z', down)  7.38 us
    all_to_all x1, starting transfers between devices, local(): heard = lax.all_to_all(notes, DB, split_axis=0, concat_axis=0, tiled=True)  7.17 us
    pallas_call x1, Pallas kernels, project_queries(): pl.pallas_call(query_kernel, grid=(rows // tile,), out_shape=(out, out),...  6.96 us
    all_to_all x1, starting transfers between devices, local(): rows = lax.all_to_all(sent, DB, split_axis=0, concat_axis=0, tiled=True)  6.65 us
  transfers between devices with their start and end apart: 27, of which 17 were waited for; matrix products, arithmetic and copies ran while one was open for 3% of the time, Pallas kernels for 21%

profile of v11, /device:TPU:24, one launch (start us, length us, event | category | flops | bytes accessed | tf_op | source)
XLA Modules:
  0.0 142.6 jit_solution(8900655588843110438)
XLA Ops:
  0.0 1.9 %collective-permute-start = (bf16[1024,256]{1,0:T(8,128)(2,1)}, bf16[1024,256]{1,0:T(8,128)(2,1)}, u32[]{:S(2)}, u32[]{:S(2)}) collective-permute-start(bf16[1024,256]{1,0:T(8,128)(2,1)} %refs_0_.1), channel_id=1, source_target_pairs={{0,2},{2,4},{4,6},{6,8},{8,10},{10,12},{12,14},{14,0},{1,3},{3,5},... | collective-permute-start | bytes 1572872 | tf_op jit(solution)/shard_map/ppermute | solution.py:361
  1.9 0.7 multiply_bitcast_fusion
  2.6 0.7 pad_add_fusion
  3.3 0.6 broadcast_in_dim.10
  3.9 7.2 %all-to-all-start = ((s32[16,2,16]{2,1,0:T(2,128)}), s32[16,2,16]{2,1,0:T(2,128)S(1)}, u32[]{:S(2)}, u32[]{:S(2)}) async-start(s32[16,2,16]{2,1,0:T(2,128)} %broadcast_in_dim.10), calls=%async_computation | async-start | bytes 32768 | tf_op jit(solution)/shard_map/all_to_all | solution.py:356
  11.1 4.9 %project_blocks.1.rows_ref = bf16[8,128,512]{2,1,0:T(8,128)(2,1)} custom-call(f32[8,7]{1,0:T(8,128)} %scales_ref.1, bf16[8,128,896]{2,1,0:T(8,128)(2,1)} %codes_ref.1, bf16[896,256]{1,0:T(8,128)(2,1)} %key_ref.1, bf16[896,256]{1,0:T(8,128)(2,1)} %value_ref.1), custom_call_target="tpu_custom_call" | custom-call | flops 939524096 | bytes 5242880 | tf_op jit(solution)/shard_map/project_blocks/pallas_call | solution.py:54
  15.9 0.7 all-to-all-done.heard_ref
  16.7 0.6 copy-done.4
  17.3 4.0 %select_blocks.1 = bf16[16,2,128,512]{3,2,1,0:T(8,128)(2,1)} custom-call(s32[1]{0:T(128)} %bitcast.5.place_ref, s32[16,2,16]{2,1,0:T(2,128)} %copy-done.4, bf16[8,128,512]{2,1,0:T(8,128)(2,1)} %project_blocks.1.rows_ref), custom_call_target="tpu_custom_call" | custom-call | bytes 9437184 | tf_op jit(solution)/shard_map/select_blocks/pallas_call | solution.py:98
  21.3 6.7 %all-to-all-start.1 = ((bf16[16,2,128,512]{3,2,1,0:T(8,128)(2,1)}), bf16[16,2,128,512]{3,2,1,0:T(8,128)(2,1)}, u32[]{:S(2)}, u32[]{:S(2)}) async-start(bf16[16,2,128,512]{3,2,1,0:T(8,128)(2,1)} %select_blocks.1), calls=%async_computation.1 | async-start | bytes 8388608 | tf_op jit(solution)/shard_map/all_to_all | solution.py:365
  27.9 3.9 %collective-permute-start.4 = (bf16[1024,256]{1,0:T(8,128)(2,1)}, bf16[1024,256]{1,0:T(8,128)(2,1)}, u32[]{:S(2)}, u32[]{:S(2)}) collective-permute-start(bf16[1024,256]{1,0:T(8,128)(2,1)} %refs_0_.1), channel_id=1, source_target_pairs={{0,14},{2,0},{4,2},{6,4},{8,6},{10,8},{12,10},{14,12},{1,15},{3,1}... | collective-permute-start | bytes 1572872 | tf_op jit(solution)/shard_map/ppermute | solution.py:362
  32.0 10.2 %collective-permute-done.4.refs_7_ = bf16[1024,256]{1,0:T(8,128)(2,1)} collective-permute-done((bf16[1024,256]{1,0:T(8,128)(2,1)}, bf16[1024,256]{1,0:T(8,128)(2,1)}, u32[]{:S(2)}, u32[]{:S(2)}) %collective-permute-start.4) | collective-permute-done | bytes 524320 | tf_op jit(solution)/shard_map/ppermute | solution.py:362
  42.2 3.7 %collective-permute-start.5 = (bf16[1024,256]{1,0:T(8,128)(2,1)}, bf16[1024,256]{1,0:T(8,128)(2,1)}, u32[]{:S(2)}, u32[]{:S(2)}) collective-permute-start(bf16[1024,256]{1,0:T(8,128)(2,1)} %collective-permute-done.4.refs_7_), channel_id=1, source_target_pairs={{0,14},{2,0},{4,2},{6,4},{8,6},{10,8},{12,10},{14,12},{1,15},{3,1}... | collective-permute-start | bytes 1572872 | tf_op jit(solution)/shard_map/ppermute | solution.py:385
  45.9 9.4 %collective-permute-done.5.refs_6_ = bf16[1024,256]{1,0:T(8,128)(2,1)} collective-permute-done((bf16[1024,256]{1,0:T(8,128)(2,1)}, bf16[1024,256]{1,0:T(8,128)(2,1)}, u32[]{:S(2)}, u32[]{:S(2)}) %collective-permute-start.5) | collective-permute-done | bytes 524320 | tf_op jit(solution)/shard_map/ppermute | solution.py:385
  55.4 3.7 %collective-permute-start.6 = (bf16[1024,256]{1,0:T(8,128)(2,1)}, bf16[1024,256]{1,0:T(8,128)(2,1)}, u32[]{:S(2)}, u32[]{:S(2)}) collective-permute-start(bf16[1024,256]{1,0:T(8,128)(2,1)} %collective-permute-done.5.refs_6_), channel_id=1, source_target_pairs={{0,14},{2,0},{4,2},{6,4},{8,6},{10,8},{12,10},{14,12},{1,15},{3,1}... | collective-permute-start | bytes 1572872 | tf_op jit(solution)/shard_map/ppermute | solution.py:385
  59.1 0.6 pad_add_fusion.1.place_ref
  59.7 7.9 %collective-permute-done.6.refs_5_ = bf16[1024,256]{1,0:T(8,128)(2,1)} collective-permute-done((bf16[1024,256]{1,0:T(8,128)(2,1)}, bf16[1024,256]{1,0:T(8,128)(2,1)}, u32[]{:S(2)}, u32[]{:S(2)}) %collective-permute-start.6) | collective-permute-done | bytes 524320 | tf_op jit(solution)/shard_map/ppermute | solution.py:385
  67.6 3.4 %collective-permute-done.3.refs_4_ = bf16[1024,256]{1,0:T(8,128)(2,1)} collective-permute-done((bf16[1024,256]{1,0:T(8,128)(2,1)}, bf16[1024,256]{1,0:T(8,128)(2,1)}, u32[]{:S(2)}, u32[]{:S(2)}) %collective-permute-start.3) | collective-permute-done | bytes 524320 | tf_op jit(solution)/shard_map/ppermute | solution.py:383
  71.0 7.0 %project_queries.1 = (f32[1024,256]{1,0:T(8,128)}, f32[1024,256]{1,0:T(8,128)}) custom-call(s32[2]{0:T(128)} %pad_add_fusion.1.place_ref, bf16[1024,256]{1,0:T(8,128)(2,1)} %refs_0_.1, bf16[1024,256]{1,0:T(8,128)(2,1)} %collective-permute-done.refs_1_, bf16[1024,256]{1,0:T(8,128)(2,1)} %collective-permute-done.1.refs_2_, ...), custom_call_target="tpu_custom_call" | custom-call | flops 2147483648 | bytes 9437184 | tf_op jit(solution)/shard_map/project_queries/pallas_call | solution.py:128
  78.1 1.7 %relay.1 = bf16[8,256,256]{2,1,0:T(8,128)(2,1)} custom-call(s32[2]{0:T(128)S(1)} %copy-done.2, bf16[256,4096]{1,0:T(8,128)(2,1)S(1)} %copy-done), custom_call_target="tpu_custom_call" | custom-call | bytes 3145728 | tf_op jit(solution)/shard_map/relay/pallas_call | solution.py:244
  79.8 0.5 collective-permute-start.10
  80.4 0.2 convert_reduce_fusion
  81.1 2.7 %finish_queries.1.queries_ref = bf16[1024,256]{1,0:T(8,128)(2,1)} custom-call(f32[1024,256]{1,0:T(8,128)} %get-tuple-element.31.own_ref, f32[1024,256]{1,0:T(8,128)} %collective-permute-done.8.lent_ref), custom_call_target="tpu_custom_call" | custom-call | flops 1048576 | bytes 3145728 | tf_op jit(solution)/shard_map/finish_queries/pallas_call | solution.py:154
  83.8 4.3 %all-to-all-done.1 = bf16[16,2,128,512]{3,2,1,0:T(8,128)(2,1)} async-done(((bf16[16,2,128,512]{3,2,1,0:T(8,128)(2,1)}), bf16[16,2,128,512]{3,2,1,0:T(8,128)(2,1)}, u32[]{:S(2)}, u32[]{:S(2)}) %all-to-all-start.1) | async-done | bytes 4194336 | tf_op jit(solution)/shard_map/all_to_all | solution.py:365
  88.1 1.0 copy-done.1
  89.1 4.4 %attend.1.own_ref = bf16[1024,256]{1,0:T(8,128)(2,1)S(1)} custom-call(s32[32]{0:T(128)S(1)} %multiply_add_fusion.slot_ref, s32[32]{0:T(128)S(1)} %select_reduce_fusion.length_ref, bf16[1024,256]{1,0:T(8,128)(2,1)S(1)} %copy-done.1, bf16[32,128,512]{2,1,0:T(8,128)(2,1)} %bitcast.8.rows_ref), custom_call_target="tpu_custom_call" | custom-call | flops 1024 | bytes 1024 | tf_op jit(solution)/shard_map/attend/pallas_call | solution.py:216
  93.6 1.9 %collective-permute-done.9.partner_ref = bf16[1024,256]{1,0:T(8,128)(2,1)S(1)} collective-permute-done((bf16[1024,256]{1,0:T(8,128)(2,1)S(1)}, bf16[1024,256]{1,0:T(8,128)(2,1)S(1)}, u32[]{:S(2)}, u32[]{:S(2)}) %collective-permute-start.9) | collective-permute-done | bytes 524320 | tf_op jit(solution)/shard_map/ppermute | solution.py:395
  95.5 1.0 shares.5
  96.5 2.0 %collective-permute-start.11 = (bf16[512,256]{1,0:T(8,128)(2,1)S(1)}, bf16[512,256]{1,0:T(8,128)(2,1)S(1)}, u32[]{:S(2)}, u32[]{:S(2)}) collective-permute-start(bf16[512,256]{1,0:T(8,128)(2,1)S(1)} %get-tuple-element.33), channel_id=1, source_target_pairs={{0,2},{2,4},{4,6},{6,8},{8,10},{10,12},{12,14},{14,0},{1,3},{3,5},... | collective-permute-start | bytes 786440 | tf_op jit(solution)/shard_map/ppermute | solution.py:315
  98.5 2.4 %collective-permute-start.15 = (bf16[512,256]{1,0:T(8,128)(2,1)S(1)}, bf16[512,256]{1,0:T(8,128)(2,1)S(1)}, u32[]{:S(2)}, u32[]{:S(2)}) collective-permute-start(bf16[512,256]{1,0:T(8,128)(2,1)S(1)} %get-tuple-element.41), channel_id=1, source_target_pairs={{0,14},{2,0},{4,2},{6,4},{8,6},{10,8},{12,10},{14,12},{1,15},{3,1}... | collective-permute-start | bytes 786440 | tf_op jit(solution)/shard_map/ppermute | solution.py:315
  100.9 1.0 shares.9
  101.9 2.0 %collective-permute-start.19 = (bf16[512,256]{1,0:T(8,128)(2,1)S(1)}, bf16[512,256]{1,0:T(8,128)(2,1)S(1)}, u32[]{:S(2)}, u32[]{:S(2)}) collective-permute-start(bf16[512,256]{1,0:T(8,128)(2,1)S(1)} %get-tuple-element.45), channel_id=1, source_target_pairs={{0,14},{2,0},{4,2},{6,4},{8,6},{10,8},{12,10},{14,12},{1,15},{3,1}... | collective-permute-start | bytes 786440 | tf_op jit(solution)/shard_map/ppermute | solution.py:315
  104.0 1.0 shares.6
  105.0 2.8 %collective-permute-done.11 = bf16[512,256]{1,0:T(8,128)(2,1)S(1)} collective-permute-done((bf16[512,256]{1,0:T(8,128)(2,1)S(1)}, bf16[512,256]{1,0:T(8,128)(2,1)S(1)}, u32[]{:S(2)}, u32[]{:S(2)}) %collective-permute-start.11) | collective-permute-done | bytes 262176 | tf_op jit(solution)/shard_map/ppermute | solution.py:315
  107.9 3.5 %collective-permute-start.16 = (bf16[512,256]{1,0:T(8,128)(2,1)S(1)}, bf16[512,256]{1,0:T(8,128)(2,1)S(1)}, u32[]{:S(2)}, u32[]{:S(2)}) collective-permute-start(bf16[512,256]{1,0:T(8,128)(2,1)S(1)} %add_convert_fusion.6), channel_id=1, source_target_pairs={{0,14},{2,0},{4,2},{6,4},{8,6},{10,8},{12,10},{14,12},{1,15},{3,1}... | collective-permute-start | bytes 786440 | tf_op jit(solution)/shard_map/ppermute | solution.py:326
  111.4 1.3 shares.8
  112.7 0.6 collective-permute-done.19
  113.3 3.7 %collective-permute-start.20 = (bf16[512,256]{1,0:T(8,128)(2,1)S(1)}, bf16[512,256]{1,0:T(8,128)(2,1)S(1)}, u32[]{:S(2)}, u32[]{:S(2)}) collective-permute-start(bf16[512,256]{1,0:T(8,128)(2,1)S(1)} %add_convert_fusion.3), channel_id=1, source_target_pairs={{0,14},{2,0},{4,2},{6,4},{8,6},{10,8},{12,10},{14,12},{1,15},{3,1}... | collective-permute-start | bytes 786440 | tf_op jit(solution)/shard_map/ppermute | solution.py:326
  117.2 1.5 %collective-permute-done.12 = bf16[512,256]{1,0:T(8,128)(2,1)S(1)} collective-permute-done((bf16[512,256]{1,0:T(8,128)(2,1)S(1)}, bf16[512,256]{1,0:T(8,128)(2,1)S(1)}, u32[]{:S(2)}, u32[]{:S(2)}) %collective-permute-start.12) | collective-permute-done | bytes 262176 | tf_op jit(solution)/shard_map/ppermute | solution.py:326
  118.9 3.9 %collective-permute-start.17 = (bf16[512,256]{1,0:T(8,128)(2,1)S(1)}, bf16[512,256]{1,0:T(8,128)(2,1)S(1)}, u32[]{:S(2)}, u32[]{:S(2)}) collective-permute-start(bf16[512,256]{1,0:T(8,128)(2,1)S(1)} %add_convert_fusion.5), channel_id=1, source_target_pairs={{0,14},{2,0},{4,2},{6,4},{8,6},{10,8},{12,10},{14,12},{1,15},{3,1}... | collective-permute-start | bytes 786440 | tf_op jit(solution)/shard_map/ppermute | solution.py:326
  122.9 1.5 %shares.7 = (f32[512,256]{1,0:T(8,128)S(1)}, f32[512,256]{1,0:T(8,128)S(1)}, f32[512,256]{1,0:T(8,128)S(1)}, f32[512,256]{1,0:T(8,128)S(1)}, f32[512,256]{1,0:T(8,128)S(1)}, /*index=5*/f32[512,256]{1,0:T(8,128)S(1)}) custom-call(s32[2]{0:T(128)S(1)} %copy-done.2, bf16[1024,256]{1,0:T(8,128)(2,1)S(1)} %attend.1.own_ref, ...), custom_call_target="tpu_custom_call" | custom-call | flops 1024 | bytes 1024 | tf_op jit(solution)/shard_map/shares/pallas_call | solution.py:270
  124.6 3.7 %collective-permute-start.21 = (bf16[512,256]{1,0:T(8,128)(2,1)S(1)}, bf16[512,256]{1,0:T(8,128)(2,1)S(1)}, u32[]{:S(2)}, u32[]{:S(2)}) collective-permute-start(bf16[512,256]{1,0:T(8,128)(2,1)S(1)} %add_convert_fusion.2), channel_id=1, source_target_pairs={{0,14},{2,0},{4,2},{6,4},{8,6},{10,8},{12,10},{14,12},{1,15},{3,1}... | collective-permute-start | bytes 786440 | tf_op jit(solution)/shard_map/ppermute | solution.py:326
  128.4 2.0 %collective-permute-done.13 = bf16[512,256]{1,0:T(8,128)(2,1)S(1)} collective-permute-done((bf16[512,256]{1,0:T(8,128)(2,1)S(1)}, bf16[512,256]{1,0:T(8,128)(2,1)S(1)}, u32[]{:S(2)}, u32[]{:S(2)}) %collective-permute-start.13) | collective-permute-done | bytes 262176 | tf_op jit(solution)/shard_map/ppermute | solution.py:326
  130.7 3.3 %collective-permute-start.18 = (bf16[512,256]{1,0:T(8,128)(2,1)S(1)}, bf16[512,256]{1,0:T(8,128)(2,1)S(1)}, u32[]{:S(2)}, u32[]{:S(2)}) collective-permute-start(bf16[512,256]{1,0:T(8,128)(2,1)S(1)} %add_convert_fusion.4), channel_id=1, source_target_pairs={{0,14},{2,0},{4,2},{6,4},{8,6},{10,8},{12,10},{14,12},{1,15},{3,1}... | collective-permute-start | bytes 786440 | tf_op jit(solution)/shard_map/ppermute | solution.py:326
  133.9 1.8 %collective-permute-done.21.refs_4_ = bf16[512,256]{1,0:T(8,128)(2,1)S(1)} collective-permute-done((bf16[512,256]{1,0:T(8,128)(2,1)S(1)}, bf16[512,256]{1,0:T(8,128)(2,1)S(1)}, u32[]{:S(2)}, u32[]{:S(2)}) %collective-permute-start.21) | collective-permute-done | bytes 262176 | tf_op jit(solution)/shard_map/ppermute | solution.py:326
  135.7 3.1 %collective-permute-done.24.refs_5_ = bf16[512,256]{1,0:T(8,128)(2,1)S(1)} collective-permute-done((bf16[512,256]{1,0:T(8,128)(2,1)S(1)}, bf16[512,256]{1,0:T(8,128)(2,1)S(1)}, u32[]{:S(2)}, u32[]{:S(2)}) %collective-permute-start.24) | collective-permute-done | bytes 262176 | tf_op jit(solution)/shard_map/ppermute | solution.py:326
  138.9 2.8 %collective-permute-done.14.refs_2_ = bf16[512,256]{1,0:T(8,128)(2,1)S(1)} collective-permute-done((bf16[512,256]{1,0:T(8,128)(2,1)S(1)}, bf16[512,256]{1,0:T(8,128)(2,1)S(1)}, u32[]{:S(2)}, u32[]{:S(2)}) %collective-permute-start.14) | collective-permute-done | bytes 262176 | tf_op jit(solution)/shard_map/ppermute | solution.py:326
  141.7 0.9 total_rows.1
  (55 shorter events, 2.2 us)
Async XLA Ops:
  0.0 21.3 %collective-permute-start = (bf16[1024,256]{1,0:T(8,128)(2,1)}, bf16[1024,256]{1,0:T(8,128)(2,1)}, u32[]{:S(2)}, u32[]{:S(2)}) collective-permute-start(bf16[1024,256]{1,0:T(8,128)(2,1)} %refs_0_.1), channel_id=1, source_target_pairs={{0,2},{2,4},{4,6},{6,8},{8,10},{10,12},{12,14},{14,0},{1,3},{3,5},... | collective-permute-start | bytes 1572872 | tf_op jit(solution)/shard_map/ppermute | solution.py:361
  3.9 12.8 %all-to-all-start = ((s32[16,2,16]{2,1,0:T(2,128)}), s32[16,2,16]{2,1,0:T(2,128)S(1)}, u32[]{:S(2)}, u32[]{:S(2)}) async-start(s32[16,2,16]{2,1,0:T(2,128)} %broadcast_in_dim.10), calls=%async_computation | async-start | bytes 32768 | tf_op jit(solution)/shard_map/all_to_all | solution.py:356
  16.7 0.6 copy-start.4
  21.2 10.6 %copy-start.3 = (bf16[4096,256]{1,0:T(8,128)(2,1)S(1)}, bf16[4096,256]{1,0:T(8,128)(2,1)}, u32[]{:S(2)}) copy-start(bf16[4096,256]{1,0:T(8,128)(2,1)} %param.11) | copy-start | bytes 6291460
  21.3 66.8 %all-to-all-start.1 = ((bf16[16,2,128,512]{3,2,1,0:T(8,128)(2,1)}), bf16[16,2,128,512]{3,2,1,0:T(8,128)(2,1)}, u32[]{:S(2)}, u32[]{:S(2)}) async-start(bf16[16,2,128,512]{3,2,1,0:T(8,128)(2,1)} %select_blocks.1), calls=%async_computation.1 | async-start | bytes 8388608 | tf_op jit(solution)/shard_map/all_to_all | solution.py:365
  27.9 14.3 %collective-permute-start.4 = (bf16[1024,256]{1,0:T(8,128)(2,1)}, bf16[1024,256]{1,0:T(8,128)(2,1)}, u32[]{:S(2)}, u32[]{:S(2)}) collective-permute-start(bf16[1024,256]{1,0:T(8,128)(2,1)} %refs_0_.1), channel_id=1, source_target_pairs={{0,14},{2,0},{4,2},{6,4},{8,6},{10,8},{12,10},{14,12},{1,15},{3,1}... | collective-permute-start | bytes 1572872 | tf_op jit(solution)/shard_map/ppermute | solution.py:362
  31.9 14.1 %collective-permute-start.1 = (bf16[1024,256]{1,0:T(8,128)(2,1)}, bf16[1024,256]{1,0:T(8,128)(2,1)}, u32[]{:S(2)}, u32[]{:S(2)}) collective-permute-start(bf16[1024,256]{1,0:T(8,128)(2,1)} %collective-permute-done.refs_1_), channel_id=1, source_target_pairs={{0,2},{2,4},{4,6},{6,8},{8,10},{10,12},{12,14},{14,0},{1,3},{3,5},... | collective-permute-start | bytes 1572872 | tf_op jit(solution)/shard_map/ppermute | solution.py:383
  31.9 27.7 %collective-permute-start.7 = (bf16[8,256,256]{2,1,0:T(8,128)(2,1)S(1)}, bf16[8,256,256]{2,1,0:T(8,128)(2,1)}, u32[]{:S(2)}, u32[]{:S(2)}) collective-permute-start(bf16[8,256,256]{2,1,0:T(8,128)(2,1)S(1)} %dynamic-slice_bitcast_fusion), channel_id=1, source_target_pairs={{0,1},{1,0},{2,3},{3,2},{4,5},{5,4},{6,7},{7,6},{8,9},{9,8},{10,11... | collective-permute-start | bytes 3145736 | tf_op jit(solution)/shard_map/ppermute | solution.py:388
  42.2 13.1 %collective-permute-start.5 = (bf16[1024,256]{1,0:T(8,128)(2,1)}, bf16[1024,256]{1,0:T(8,128)(2,1)}, u32[]{:S(2)}, u32[]{:S(2)}) collective-permute-start(bf16[1024,256]{1,0:T(8,128)(2,1)} %collective-permute-done.4.refs_7_), channel_id=1, source_target_pairs={{0,14},{2,0},{4,2},{6,4},{8,6},{10,8},{12,10},{14,12},{1,15},{3,1}... | collective-permute-start | bytes 1572872 | tf_op jit(solution)/shard_map/ppermute | solution.py:385
  45.9 13.1 %collective-permute-start.2 = (bf16[1024,256]{1,0:T(8,128)(2,1)}, bf16[1024,256]{1,0:T(8,128)(2,1)}, u32[]{:S(2)}, u32[]{:S(2)}) collective-permute-start(bf16[1024,256]{1,0:T(8,128)(2,1)} %collective-permute-done.1.refs_2_), channel_id=1, source_target_pairs={{0,2},{2,4},{4,6},{6,8},{8,10},{10,12},{12,14},{14,0},{1,3},{3,5},... | collective-permute-start | bytes 1572872 | tf_op jit(solution)/shard_map/ppermute | solution.py:383
  55.4 12.2 %collective-permute-start.6 = (bf16[1024,256]{1,0:T(8,128)(2,1)}, bf16[1024,256]{1,0:T(8,128)(2,1)}, u32[]{:S(2)}, u32[]{:S(2)}) collective-permute-start(bf16[1024,256]{1,0:T(8,128)(2,1)} %collective-permute-done.5.refs_6_), channel_id=1, source_target_pairs={{0,14},{2,0},{4,2},{6,4},{8,6},{10,8},{12,10},{14,12},{1,15},{3,1}... | collective-permute-start | bytes 1572872 | tf_op jit(solution)/shard_map/ppermute | solution.py:385
  59.1 11.9 %collective-permute-start.3 = (bf16[1024,256]{1,0:T(8,128)(2,1)}, bf16[1024,256]{1,0:T(8,128)(2,1)}, u32[]{:S(2)}, u32[]{:S(2)}) collective-permute-start(bf16[1024,256]{1,0:T(8,128)(2,1)} %collective-permute-done.2.refs_3_), channel_id=1, source_target_pairs={{0,2},{2,4},{4,6},{6,8},{8,10},{10,12},{12,14},{14,0},{1,3},{3,5},... | collective-permute-start | bytes 1572872 | tf_op jit(solution)/shard_map/ppermute | solution.py:383
  59.7 18.4 %copy-start = (bf16[256,4096]{1,0:T(8,128)(2,1)S(1)}, bf16[256,4096]{1,0:T(8,128)(2,1)}, u32[]{:S(2)}) copy-start(bf16[256,4096]{1,0:T(8,128)(2,1)} %weight_ref.11) | copy-start | bytes 6291460
  59.7 18.4 %copy-start.2 = (s32[2]{0:T(128)S(1)}, s32[2]{0:T(128)}, u32[]{:S(2)}) copy-start(s32[2]{0:T(128)} %pad_add_fusion.1.place_ref) | copy-start | bytes 28
  78.0 2.3 %copy-start.6 = (s32[16,2]{0,1:T(2,128)S(1)}, s32[16,2]{0,1:T(2,128)}, u32[]{:S(2)}) copy-start(s32[16,2]{0,1:T(2,128)} %param.18) | copy-start | bytes 388
  78.0 2.7 %copy-start.5 = (s32[16,2,16]{2,1,0:T(2,128)S(1)}, s32[16,2,16]{2,1,0:T(2,128)}, u32[]{:S(2)}) copy-start(s32[16,2,16]{2,1,0:T(2,128)} %copy-done.4) | copy-start | bytes 6148
  78.0 3.1 %collective-permute-start.8 = (f32[1024,256]{1,0:T(8,128)}, f32[1024,256]{1,0:T(8,128)}, u32[]{:S(2)}, u32[]{:S(2)}) collective-permute-start(f32[1024,256]{1,0:T(8,128)} %get-tuple-element.32), channel_id=1, source_target_pairs={{0,1},{1,0},{2,3},{3,2},{4,5},{5,4},{6,7},{7,6},{8,9},{9,8},{10,11... | collective-permute-start | bytes 3145736 | tf_op jit(solution)/shard_map/ppermute | solution.py:393
  79.8 13.8 %collective-permute-start.10 = (bf16[8,256,256]{2,1,0:T(8,128)(2,1)}, bf16[8,256,256]{2,1,0:T(8,128)(2,1)S(1)}, u32[]{:S(2)}, u32[]{:S(2)}) collective-permute-start(bf16[8,256,256]{2,1,0:T(8,128)(2,1)} %relay.1), channel_id=1, source_target_pairs={{0,1},{1,0},{2,3},{3,2},{4,5},{5,4},{6,7},{7,6},{8,9},{9,8},{10,11... | collective-permute-start | bytes 3145736 | tf_op jit(solution)/shard_map/ppermute | solution.py:390
  88.1 1.0 copy-start.1
  93.5 2.0 %collective-permute-start.9 = (bf16[1024,256]{1,0:T(8,128)(2,1)S(1)}, bf16[1024,256]{1,0:T(8,128)(2,1)S(1)}, u32[]{:S(2)}, u32[]{:S(2)}) collective-permute-start(bf16[1024,256]{1,0:T(8,128)(2,1)S(1)} %attend.1.own_ref), channel_id=1, source_target_pairs={{0,1},{1,0},{2,3},{3,2},{4,5},{5,4},{6,7},{7,6},{8,9},{9,8},{10,11... | collective-permute-start | bytes 1572872 | tf_op jit(solution)/shard_map/ppermute | solution.py:395
  96.5 11.2 %collective-permute-start.11 = (bf16[512,256]{1,0:T(8,128)(2,1)S(1)}, bf16[512,256]{1,0:T(8,128)(2,1)S(1)}, u32[]{:S(2)}, u32[]{:S(2)}) collective-permute-start(bf16[512,256]{1,0:T(8,128)(2,1)S(1)} %get-tuple-element.33), channel_id=1, source_target_pairs={{0,2},{2,4},{4,6},{6,8},{8,10},{10,12},{12,14},{14,0},{1,3},{3,5},... | collective-permute-start | bytes 786440 | tf_op jit(solution)/shard_map/ppermute | solution.py:315
  98.5 9.4 %collective-permute-start.15 = (bf16[512,256]{1,0:T(8,128)(2,1)S(1)}, bf16[512,256]{1,0:T(8,128)(2,1)S(1)}, u32[]{:S(2)}, u32[]{:S(2)}) collective-permute-start(bf16[512,256]{1,0:T(8,128)(2,1)S(1)} %get-tuple-element.41), channel_id=1, source_target_pairs={{0,14},{2,0},{4,2},{6,4},{8,6},{10,8},{12,10},{14,12},{1,15},{3,1}... | collective-permute-start | bytes 786440 | tf_op jit(solution)/shard_map/ppermute | solution.py:315
  101.9 11.4 %collective-permute-start.19 = (bf16[512,256]{1,0:T(8,128)(2,1)S(1)}, bf16[512,256]{1,0:T(8,128)(2,1)S(1)}, u32[]{:S(2)}, u32[]{:S(2)}) collective-permute-start(bf16[512,256]{1,0:T(8,128)(2,1)S(1)} %get-tuple-element.45), channel_id=1, source_target_pairs={{0,14},{2,0},{4,2},{6,4},{8,6},{10,8},{12,10},{14,12},{1,15},{3,1}... | collective-permute-start | bytes 786440 | tf_op jit(solution)/shard_map/ppermute | solution.py:315
  103.9 13.1 %collective-permute-start.22 = (bf16[512,256]{1,0:T(8,128)(2,1)S(1)}, bf16[512,256]{1,0:T(8,128)(2,1)S(1)}, u32[]{:S(2)}, u32[]{:S(2)}) collective-permute-start(bf16[512,256]{1,0:T(8,128)(2,1)S(1)} %get-tuple-element.48), channel_id=1, source_target_pairs={{0,2},{2,4},{4,6},{6,8},{8,10},{10,12},{12,14},{14,0},{1,3},{3,5},... | collective-permute-start | bytes 786440 | tf_op jit(solution)/shard_map/ppermute | solution.py:315
  107.8 10.9 %collective-permute-start.12 = (bf16[512,256]{1,0:T(8,128)(2,1)S(1)}, bf16[512,256]{1,0:T(8,128)(2,1)S(1)}, u32[]{:S(2)}, u32[]{:S(2)}) collective-permute-start(bf16[512,256]{1,0:T(8,128)(2,1)S(1)} %add_convert_fusion.9), channel_id=1, source_target_pairs={{0,2},{2,4},{4,6},{6,8},{8,10},{10,12},{12,14},{14,0},{1,3},{3,5},... | collective-permute-start | bytes 786440 | tf_op jit(solution)/shard_map/ppermute | solution.py:326
  107.9 10.9 %collective-permute-start.16 = (bf16[512,256]{1,0:T(8,128)(2,1)S(1)}, bf16[512,256]{1,0:T(8,128)(2,1)S(1)}, u32[]{:S(2)}, u32[]{:S(2)}) collective-permute-start(bf16[512,256]{1,0:T(8,128)(2,1)S(1)} %add_convert_fusion.6), channel_id=1, source_target_pairs={{0,14},{2,0},{4,2},{6,4},{8,6},{10,8},{12,10},{14,12},{1,15},{3,1}... | collective-permute-start | bytes 786440 | tf_op jit(solution)/shard_map/ppermute | solution.py:326
  113.3 11.2 %collective-permute-start.20 = (bf16[512,256]{1,0:T(8,128)(2,1)S(1)}, bf16[512,256]{1,0:T(8,128)(2,1)S(1)}, u32[]{:S(2)}, u32[]{:S(2)}) collective-permute-start(bf16[512,256]{1,0:T(8,128)(2,1)S(1)} %add_convert_fusion.3), channel_id=1, source_target_pairs={{0,14},{2,0},{4,2},{6,4},{8,6},{10,8},{12,10},{14,12},{1,15},{3,1}... | collective-permute-start | bytes 786440 | tf_op jit(solution)/shard_map/ppermute | solution.py:326
  117.1 11.2 %collective-permute-start.23 = (bf16[512,256]{1,0:T(8,128)(2,1)S(1)}, bf16[512,256]{1,0:T(8,128)(2,1)S(1)}, u32[]{:S(2)}, u32[]{:S(2)}) collective-permute-start(bf16[512,256]{1,0:T(8,128)(2,1)S(1)} %add_convert_fusion.1), channel_id=1, source_target_pairs={{0,2},{2,4},{4,6},{6,8},{8,10},{10,12},{12,14},{14,0},{1,3},{3,5},... | collective-permute-start | bytes 786440 | tf_op jit(solution)/shard_map/ppermute | solution.py:326
  118.7 11.7 %collective-permute-start.13 = (bf16[512,256]{1,0:T(8,128)(2,1)S(1)}, bf16[512,256]{1,0:T(8,128)(2,1)S(1)}, u32[]{:S(2)}, u32[]{:S(2)}) collective-permute-start(bf16[512,256]{1,0:T(8,128)(2,1)S(1)} %add_convert_fusion.8), channel_id=1, source_target_pairs={{0,2},{2,4},{4,6},{6,8},{8,10},{10,12},{12,14},{14,0},{1,3},{3,5},... | collective-permute-start | bytes 786440 | tf_op jit(solution)/shard_map/ppermute | solution.py:326
  118.9 11.6 %collective-permute-start.17 = (bf16[512,256]{1,0:T(8,128)(2,1)S(1)}, bf16[512,256]{1,0:T(8,128)(2,1)S(1)}, u32[]{:S(2)}, u32[]{:S(2)}) collective-permute-start(bf16[512,256]{1,0:T(8,128)(2,1)S(1)} %add_convert_fusion.5), channel_id=1, source_target_pairs={{0,14},{2,0},{4,2},{6,4},{8,6},{10,8},{12,10},{14,12},{1,15},{3,1}... | collective-permute-start | bytes 786440 | tf_op jit(solution)/shard_map/ppermute | solution.py:326
  124.6 11.2 %collective-permute-start.21 = (bf16[512,256]{1,0:T(8,128)(2,1)S(1)}, bf16[512,256]{1,0:T(8,128)(2,1)S(1)}, u32[]{:S(2)}, u32[]{:S(2)}) collective-permute-start(bf16[512,256]{1,0:T(8,128)(2,1)S(1)} %add_convert_fusion.2), channel_id=1, source_target_pairs={{0,14},{2,0},{4,2},{6,4},{8,6},{10,8},{12,10},{14,12},{1,15},{3,1}... | collective-permute-start | bytes 786440 | tf_op jit(solution)/shard_map/ppermute | solution.py:326
  128.3 10.5 %collective-permute-start.24 = (bf16[512,256]{1,0:T(8,128)(2,1)S(1)}, bf16[512,256]{1,0:T(8,128)(2,1)S(1)}, u32[]{:S(2)}, u32[]{:S(2)}) collective-permute-start(bf16[512,256]{1,0:T(8,128)(2,1)S(1)} %add_convert_fusion), channel_id=1, source_target_pairs={{0,2},{2,4},{4,6},{6,8},{8,10},{10,12},{12,14},{14,0},{1,3},{3,5},... | collective-permute-start | bytes 786440 | tf_op jit(solution)/shard_map/ppermute | solution.py:326
  130.5 11.2 %collective-permute-start.14 = (bf16[512,256]{1,0:T(8,128)(2,1)S(1)}, bf16[512,256]{1,0:T(8,128)(2,1)S(1)}, u32[]{:S(2)}, u32[]{:S(2)}) collective-permute-start(bf16[512,256]{1,0:T(8,128)(2,1)S(1)} %add_convert_fusion.7), channel_id=1, source_target_pairs={{0,2},{2,4},{4,6},{6,8},{8,10},{10,12},{12,14},{14,0},{1,3},{3,5},... | collective-permute-start | bytes 786440 | tf_op jit(solution)/shard_map/ppermute | solution.py:326
  130.7 11.0 %collective-permute-start.18 = (bf16[512,256]{1,0:T(8,128)(2,1)S(1)}, bf16[512,256]{1,0:T(8,128)(2,1)S(1)}, u32[]{:S(2)}, u32[]{:S(2)}) collective-permute-start(bf16[512,256]{1,0:T(8,128)(2,1)S(1)} %add_convert_fusion.4), channel_id=1, source_target_pairs={{0,14},{2,0},{4,2},{6,4},{8,6},{10,8},{12,10},{14,12},{1,15},{3,1}... | collective-permute-start | bytes 786440 | tf_op jit(solution)/shard_map/ppermute | solution.py:326

commit v12 on v10

--- a/solution.py
+++ b/solution.py
@@ -177,7 +177,7 @@
             copies.append(copy)
     query_copy.wait()
     places = lax.broadcasted_iota(jnp.int32, (SPAN, keys), 1)
-    group = 4
+    group = 8
     for start in range(0, spans, group):
         members = [(c, h) for c in range(start, start + group) for h in range(width // HD)]
         for copy in copies[start * NBRS : (start + group) * NBRS]:

time: 144 us -> 143 us (level)
  no operation moved by 1% of the time
where the time goes in v12:
time: 143 us; the launch traced here: 142 us
  starting transfers between devices  52.8 us (37%)
  waiting for transfers between devices  52.8 us (37%)
  Pallas kernels  30.1 us (21%)
  local copies, waits for them, and re-layouts  4.06 us (3%)
  other arithmetic  2.26 us (2%)
    ppermute x10, starting transfers between devices, reduce_ring(): lax.ppermute(total.astype(BF16), 'z', up if way == 1 else down)  18.5 us
    ppermute x2, waiting for transfers between devices, local(): pieces[ring - k] = lax.ppermute(pieces[ring - k + 1], 'z', down)  17.4 us
    ppermute x10, waiting for transfers between devices, reduce_ring(): lax.ppermute(total.astype(BF16), 'z', up if way == 1 else down)  12.9 us
    ppermute x1, waiting for transfers between devices, local(): pieces[ring - 1] = lax.ppermute(tokens, 'z', down)  10.2 us
    ppermute x2, starting transfers between devices, local(): pieces[ring - k] = lax.ppermute(pieces[ring - k + 1], 'z', down)  7.38 us
    all_to_all x1, starting transfers between devices, local(): heard = lax.all_to_all(notes, DB, split_axis=0, concat_axis=0, tiled=True)  7.17 us
    pallas_call x1, Pallas kernels, project_queries(): pl.pallas_call(query_kernel, grid=(rows // tile,), out_shape=(out, out),...  6.93 us
    all_to_all x1, starting transfers between devices, local(): rows = lax.all_to_all(sent, DB, split_axis=0, concat_axis=0, tiled=True)  6.63 us
  transfers between devices with their start and end apart: 27, of which 16 were waited for; matrix products, arithmetic and copies ran while one was open for 3% of the time, Pallas kernels for 20%

profile of v12, /device:TPU:24, one launch (start us, length us, event | category | flops | bytes accessed | tf_op | source)
XLA Modules:
  0.0 142.3 jit_solution(16805196041323480838)
XLA Ops:
  0.0 1.9 %collective-permute-start = (bf16[1024,256]{1,0:T(8,128)(2,1)}, bf16[1024,256]{1,0:T(8,128)(2,1)}, u32[]{:S(2)}, u32[]{:S(2)}) collective-permute-start(bf16[1024,256]{1,0:T(8,128)(2,1)} %refs_0_.1), channel_id=1, source_target_pairs={{0,2},{2,4},{4,6},{6,8},{8,10},{10,12},{12,14},{14,0},{1,3},{3,5},... | collective-permute-start | bytes 1572872 | tf_op jit(solution)/shard_map/ppermute | solution.py:352
  1.9 0.7 pad_bitcast_fusion
  2.6 0.7 bitcast_add_fusion
  3.3 0.6 broadcast_in_dim.27
  3.9 7.2 %all-to-all-start = ((s32[16,3,16]{2,1,0:T(4,128)}), s32[16,3,16]{2,1,0:T(4,128)S(1)}, u32[]{:S(2)}, u32[]{:S(2)}) async-start(s32[16,3,16]{2,1,0:T(4,128)} %broadcast_in_dim.27), calls=%async_computation | async-start | bytes 65536 | tf_op jit(solution)/shard_map/all_to_all | solution.py:347
  11.1 4.9 %project_blocks.1.rows_ref = bf16[8,128,512]{2,1,0:T(8,128)(2,1)} custom-call(f32[8,7]{1,0:T(8,128)} %scales_ref.1, bf16[8,128,896]{2,1,0:T(8,128)(2,1)} %codes_ref.1, bf16[896,256]{1,0:T(8,128)(2,1)} %key_ref.1, bf16[896,256]{1,0:T(8,128)(2,1)} %value_ref.1), custom_call_target="tpu_custom_call" | custom-call | flops 939524096 | bytes 5242880 | tf_op jit(solution)/shard_map/project_blocks/pallas_call | solution.py:53
  16.0 0.7 all-to-all-done.heard_ref
  16.7 0.6 copy-done.4
  17.3 3.9 %select_blocks.1 = bf16[16,2,128,512]{3,2,1,0:T(8,128)(2,1)} custom-call(s32[1]{0:T(128)} %bitcast.5.place_ref, s32[16,3,16]{2,1,0:T(4,128)} %copy-done.4, bf16[8,128,512]{2,1,0:T(8,128)(2,1)} %project_blocks.1.rows_ref), custom_call_target="tpu_custom_call" | custom-call | bytes 9437184 | tf_op jit(solution)/shard_map/select_blocks/pallas_call | solution.py:92
  21.3 6.6 %all-to-all-start.1 = ((bf16[16,2,128,512]{3,2,1,0:T(8,128)(2,1)}), bf16[16,2,128,512]{3,2,1,0:T(8,128)(2,1)}, u32[]{:S(2)}, u32[]{:S(2)}) async-start(bf16[16,2,128,512]{3,2,1,0:T(8,128)(2,1)} %select_blocks.1), calls=%async_computation.1 | async-start | bytes 8388608 | tf_op jit(solution)/shard_map/all_to_all | solution.py:356
  27.9 3.9 %collective-permute-start.4 = (bf16[1024,256]{1,0:T(8,128)(2,1)}, bf16[1024,256]{1,0:T(8,128)(2,1)}, u32[]{:S(2)}, u32[]{:S(2)}) collective-permute-start(bf16[1024,256]{1,0:T(8,128)(2,1)} %refs_0_.1), channel_id=1, source_target_pairs={{0,14},{2,0},{4,2},{6,4},{8,6},{10,8},{12,10},{14,12},{1,15},{3,1}... | collective-permute-start | bytes 1572872 | tf_op jit(solution)/shard_map/ppermute | solution.py:353
  32.0 10.2 %collective-permute-done.4.refs_7_ = bf16[1024,256]{1,0:T(8,128)(2,1)} collective-permute-done((bf16[1024,256]{1,0:T(8,128)(2,1)}, bf16[1024,256]{1,0:T(8,128)(2,1)}, u32[]{:S(2)}, u32[]{:S(2)}) %collective-permute-start.4) | collective-permute-done | bytes 524320 | tf_op jit(solution)/shard_map/ppermute | solution.py:353
  42.2 3.7 %collective-permute-start.5 = (bf16[1024,256]{1,0:T(8,128)(2,1)}, bf16[1024,256]{1,0:T(8,128)(2,1)}, u32[]{:S(2)}, u32[]{:S(2)}) collective-permute-start(bf16[1024,256]{1,0:T(8,128)(2,1)} %collective-permute-done.4.refs_7_), channel_id=1, source_target_pairs={{0,14},{2,0},{4,2},{6,4},{8,6},{10,8},{12,10},{14,12},{1,15},{3,1}... | collective-permute-start | bytes 1572872 | tf_op jit(solution)/shard_map/ppermute | solution.py:376
  45.9 9.5 %collective-permute-done.5.refs_6_ = bf16[1024,256]{1,0:T(8,128)(2,1)} collective-permute-done((bf16[1024,256]{1,0:T(8,128)(2,1)}, bf16[1024,256]{1,0:T(8,128)(2,1)}, u32[]{:S(2)}, u32[]{:S(2)}) %collective-permute-start.5) | collective-permute-done | bytes 524320 | tf_op jit(solution)/shard_map/ppermute | solution.py:376
  55.4 3.7 %collective-permute-start.6 = (bf16[1024,256]{1,0:T(8,128)(2,1)}, bf16[1024,256]{1,0:T(8,128)(2,1)}, u32[]{:S(2)}, u32[]{:S(2)}) collective-permute-start(bf16[1024,256]{1,0:T(8,128)(2,1)} %collective-permute-done.5.refs_6_), channel_id=1, source_target_pairs={{0,14},{2,0},{4,2},{6,4},{8,6},{10,8},{12,10},{14,12},{1,15},{3,1}... | collective-permute-start | bytes 1572872 | tf_op jit(solution)/shard_map/ppermute | solution.py:376
  59.1 0.6 pad_add_fusion.1.place_ref
  59.7 7.9 %collective-permute-done.6.refs_5_ = bf16[1024,256]{1,0:T(8,128)(2,1)} collective-permute-done((bf16[1024,256]{1,0:T(8,128)(2,1)}, bf16[1024,256]{1,0:T(8,128)(2,1)}, u32[]{:S(2)}, u32[]{:S(2)}) %collective-permute-start.6) | collective-permute-done | bytes 524320 | tf_op jit(solution)/shard_map/ppermute | solution.py:376
  67.6 3.4 %collective-permute-done.3.refs_4_ = bf16[1024,256]{1,0:T(8,128)(2,1)} collective-permute-done((bf16[1024,256]{1,0:T(8,128)(2,1)}, bf16[1024,256]{1,0:T(8,128)(2,1)}, u32[]{:S(2)}, u32[]{:S(2)}) %collective-permute-start.3) | collective-permute-done | bytes 524320 | tf_op jit(solution)/shard_map/ppermute | solution.py:374
  71.0 6.9 %project_queries.1 = (f32[1024,256]{1,0:T(8,128)}, f32[1024,256]{1,0:T(8,128)}) custom-call(s32[2]{0:T(128)} %pad_add_fusion.1.place_ref, bf16[1024,256]{1,0:T(8,128)(2,1)} %refs_0_.1, bf16[1024,256]{1,0:T(8,128)(2,1)} %collective-permute-done.refs_1_, bf16[1024,256]{1,0:T(8,128)(2,1)} %collective-permute-done.1.refs_2_, ...), custom_call_target="tpu_custom_call" | custom-call | flops 2147483648 | bytes 9437184 | tf_op jit(solution)/shard_map/project_queries/pallas_call | solution.py:122
  78.1 1.7 %relay.1 = bf16[8,256,256]{2,1,0:T(8,128)(2,1)} custom-call(s32[2]{0:T(128)S(1)} %copy-done.2, bf16[256,4096]{1,0:T(8,128)(2,1)S(1)} %copy-done), custom_call_target="tpu_custom_call" | custom-call | bytes 3145728 | tf_op jit(solution)/shard_map/relay/pallas_call | solution.py:238
  79.8 0.5 collective-permute-start.10
  80.7 0.8 slice_reduce_fusion
  81.7 2.7 %finish_queries.1.queries_ref = bf16[1024,256]{1,0:T(8,128)(2,1)} custom-call(f32[1024,256]{1,0:T(8,128)} %get-tuple-element.29.own_ref, f32[1024,256]{1,0:T(8,128)} %collective-permute-done.8.lent_ref), custom_call_target="tpu_custom_call" | custom-call | flops 1048576 | bytes 3145728 | tf_op jit(solution)/shard_map/finish_queries/pallas_call | solution.py:148
  84.4 3.7 %all-to-all-done.1 = bf16[16,2,128,512]{3,2,1,0:T(8,128)(2,1)} async-done(((bf16[16,2,128,512]{3,2,1,0:T(8,128)(2,1)}), bf16[16,2,128,512]{3,2,1,0:T(8,128)(2,1)}, u32[]{:S(2)}, u32[]{:S(2)}) %all-to-all-start.1) | async-done | bytes 4194336 | tf_op jit(solution)/shard_map/all_to_all | solution.py:356
  88.1 1.0 copy-done.1
  89.1 4.0 %attend.1.own_ref = bf16[1024,256]{1,0:T(8,128)(2,1)S(1)} custom-call(s32[32]{0:T(128)S(1)} %multiply_add_fusion.slot_ref, s32[32]{0:T(128)S(1)} %select_reduce_fusion.length_ref, bf16[1024,256]{1,0:T(8,128)(2,1)S(1)} %copy-done.1, bf16[32,128,512]{2,1,0:T(8,128)(2,1)} %bitcast.8.rows_ref), custom_call_target="tpu_custom_call" | custom-call | flops 1024 | bytes 1024 | tf_op jit(solution)/shard_map/attend/pallas_call | solution.py:210
  93.3 1.9 %collective-permute-done.9.partner_ref = bf16[1024,256]{1,0:T(8,128)(2,1)S(1)} collective-permute-done((bf16[1024,256]{1,0:T(8,128)(2,1)S(1)}, bf16[1024,256]{1,0:T(8,128)(2,1)S(1)}, u32[]{:S(2)}, u32[]{:S(2)}) %collective-permute-start.9) | collective-permute-done | bytes 524320 | tf_op jit(solution)/shard_map/ppermute | solution.py:386
  95.2 1.0 shares.6
  96.1 2.0 %collective-permute-start.11 = (bf16[512,256]{1,0:T(8,128)(2,1)S(1)}, bf16[512,256]{1,0:T(8,128)(2,1)S(1)}, u32[]{:S(2)}, u32[]{:S(2)}) collective-permute-start(bf16[512,256]{1,0:T(8,128)(2,1)S(1)} %get-tuple-element.33), channel_id=1, source_target_pairs={{0,2},{2,4},{4,6},{6,8},{8,10},{10,12},{12,14},{14,0},{1,3},{3,5},... | collective-permute-start | bytes 786440 | tf_op jit(solution)/shard_map/ppermute | solution.py:309
  98.1 2.4 %collective-permute-start.15 = (bf16[512,256]{1,0:T(8,128)(2,1)S(1)}, bf16[512,256]{1,0:T(8,128)(2,1)S(1)}, u32[]{:S(2)}, u32[]{:S(2)}) collective-permute-start(bf16[512,256]{1,0:T(8,128)(2,1)S(1)} %get-tuple-element.37), channel_id=1, source_target_pairs={{0,14},{2,0},{4,2},{6,4},{8,6},{10,8},{12,10},{14,12},{1,15},{3,1}... | collective-permute-start | bytes 786440 | tf_op jit(solution)/shard_map/ppermute | solution.py:309
  100.6 1.0 shares.7
  101.5 2.0 %collective-permute-start.19 = (bf16[512,256]{1,0:T(8,128)(2,1)S(1)}, bf16[512,256]{1,0:T(8,128)(2,1)S(1)}, u32[]{:S(2)}, u32[]{:S(2)}) collective-permute-start(bf16[512,256]{1,0:T(8,128)(2,1)S(1)} %get-tuple-element.41), channel_id=1, source_target_pairs={{0,14},{2,0},{4,2},{6,4},{8,6},{10,8},{12,10},{14,12},{1,15},{3,1}... | collective-permute-start | bytes 786440 | tf_op jit(solution)/shard_map/ppermute | solution.py:309
  103.6 1.5 %shares.4 = (f32[512,256]{1,0:T(8,128)S(1)}, f32[512,256]{1,0:T(8,128)S(1)}, f32[512,256]{1,0:T(8,128)S(1)}, f32[512,256]{1,0:T(8,128)S(1)}, f32[512,256]{1,0:T(8,128)S(1)}, /*index=5*/f32[512,256]{1,0:T(8,128)S(1)}) custom-call(s32[2]{0:T(128)S(1)} %copy-done.2, bf16[1024,256]{1,0:T(8,128)(2,1)S(1)} %attend.1.own_ref, ...), custom_call_target="tpu_custom_call" | custom-call | flops 1024 | bytes 1024 | tf_op jit(solution)/shard_map/shares/pallas_call | solution.py:264
  105.2 1.5 %shares.5 = (f32[512,256]{1,0:T(8,128)S(1)}, f32[512,256]{1,0:T(8,128)S(1)}, f32[512,256]{1,0:T(8,128)S(1)}, f32[512,256]{1,0:T(8,128)S(1)}, f32[512,256]{1,0:T(8,128)S(1)}, /*index=5*/f32[512,256]{1,0:T(8,128)S(1)}) custom-call(s32[2]{0:T(128)S(1)} %copy-done.2, bf16[1024,256]{1,0:T(8,128)(2,1)S(1)} %attend.1.own_ref, ...), custom_call_target="tpu_custom_call" | custom-call | flops 1024 | bytes 1024 | tf_op jit(solution)/shard_map/shares/pallas_call | solution.py:264
  106.7 0.7 collective-permute-done.11
  107.6 3.4 %collective-permute-start.16 = (bf16[512,256]{1,0:T(8,128)(2,1)S(1)}, bf16[512,256]{1,0:T(8,128)(2,1)S(1)}, u32[]{:S(2)}, u32[]{:S(2)}) collective-permute-start(bf16[512,256]{1,0:T(8,128)(2,1)S(1)} %add_convert_fusion.6), channel_id=1, source_target_pairs={{0,14},{2,0},{4,2},{6,4},{8,6},{10,8},{12,10},{14,12},{1,15},{3,1}... | collective-permute-start | bytes 786440 | tf_op jit(solution)/shard_map/ppermute | solution.py:318
  111.1 1.9 %collective-permute-done.19 = bf16[512,256]{1,0:T(8,128)(2,1)S(1)} collective-permute-done((bf16[512,256]{1,0:T(8,128)(2,1)S(1)}, bf16[512,256]{1,0:T(8,128)(2,1)S(1)}, u32[]{:S(2)}, u32[]{:S(2)}) %collective-permute-start.19) | collective-permute-done | bytes 262176 | tf_op jit(solution)/shard_map/ppermute | solution.py:309
  113.0 3.7 %collective-permute-start.20 = (bf16[512,256]{1,0:T(8,128)(2,1)S(1)}, bf16[512,256]{1,0:T(8,128)(2,1)S(1)}, u32[]{:S(2)}, u32[]{:S(2)}) collective-permute-start(bf16[512,256]{1,0:T(8,128)(2,1)S(1)} %add_convert_fusion.3), channel_id=1, source_target_pairs={{0,14},{2,0},{4,2},{6,4},{8,6},{10,8},{12,10},{14,12},{1,15},{3,1}... | collective-permute-start | bytes 786440 | tf_op jit(solution)/shard_map/ppermute | solution.py:318
  116.8 1.5 %collective-permute-done.12 = bf16[512,256]{1,0:T(8,128)(2,1)S(1)} collective-permute-done((bf16[512,256]{1,0:T(8,128)(2,1)S(1)}, bf16[512,256]{1,0:T(8,128)(2,1)S(1)}, u32[]{:S(2)}, u32[]{:S(2)}) %collective-permute-start.12) | collective-permute-done | bytes 262176 | tf_op jit(solution)/shard_map/ppermute | solution.py:318
  118.6 3.9 %collective-permute-start.17 = (bf16[512,256]{1,0:T(8,128)(2,1)S(1)}, bf16[512,256]{1,0:T(8,128)(2,1)S(1)}, u32[]{:S(2)}, u32[]{:S(2)}) collective-permute-start(bf16[512,256]{1,0:T(8,128)(2,1)S(1)} %add_convert_fusion.5), channel_id=1, source_target_pairs={{0,14},{2,0},{4,2},{6,4},{8,6},{10,8},{12,10},{14,12},{1,15},{3,1}... | collective-permute-start | bytes 786440 | tf_op jit(solution)/shard_map/ppermute | solution.py:318
  122.5 1.6 %collective-permute-done.20 = bf16[512,256]{1,0:T(8,128)(2,1)S(1)} collective-permute-done((bf16[512,256]{1,0:T(8,128)(2,1)S(1)}, bf16[512,256]{1,0:T(8,128)(2,1)S(1)}, u32[]{:S(2)}, u32[]{:S(2)}) %collective-permute-start.20) | collective-permute-done | bytes 262176 | tf_op jit(solution)/shard_map/ppermute | solution.py:318
  124.2 3.7 %collective-permute-start.21 = (bf16[512,256]{1,0:T(8,128)(2,1)S(1)}, bf16[512,256]{1,0:T(8,128)(2,1)S(1)}, u32[]{:S(2)}, u32[]{:S(2)}) collective-permute-start(bf16[512,256]{1,0:T(8,128)(2,1)S(1)} %add_convert_fusion.2), channel_id=1, source_target_pairs={{0,14},{2,0},{4,2},{6,4},{8,6},{10,8},{12,10},{14,12},{1,15},{3,1}... | collective-permute-start | bytes 786440 | tf_op jit(solution)/shard_map/ppermute | solution.py:318
  128.1 2.0 %collective-permute-done.13 = bf16[512,256]{1,0:T(8,128)(2,1)S(1)} collective-permute-done((bf16[512,256]{1,0:T(8,128)(2,1)S(1)}, bf16[512,256]{1,0:T(8,128)(2,1)S(1)}, u32[]{:S(2)}, u32[]{:S(2)}) %collective-permute-start.13) | collective-permute-done | bytes 262176 | tf_op jit(solution)/shard_map/ppermute | solution.py:318
  130.3 3.3 %collective-permute-start.18 = (bf16[512,256]{1,0:T(8,128)(2,1)S(1)}, bf16[512,256]{1,0:T(8,128)(2,1)S(1)}, u32[]{:S(2)}, u32[]{:S(2)}) collective-permute-start(bf16[512,256]{1,0:T(8,128)(2,1)S(1)} %add_convert_fusion.4), channel_id=1, source_target_pairs={{0,14},{2,0},{4,2},{6,4},{8,6},{10,8},{12,10},{14,12},{1,15},{3,1}... | collective-permute-start | bytes 786440 | tf_op jit(solution)/shard_map/ppermute | solution.py:318
  133.6 1.8 %collective-permute-done.21.refs_4_ = bf16[512,256]{1,0:T(8,128)(2,1)S(1)} collective-permute-done((bf16[512,256]{1,0:T(8,128)(2,1)S(1)}, bf16[512,256]{1,0:T(8,128)(2,1)S(1)}, u32[]{:S(2)}, u32[]{:S(2)}) %collective-permute-start.21) | collective-permute-done | bytes 262176 | tf_op jit(solution)/shard_map/ppermute | solution.py:318
  135.4 3.1 %collective-permute-done.24.refs_5_ = bf16[512,256]{1,0:T(8,128)(2,1)S(1)} collective-permute-done((bf16[512,256]{1,0:T(8,128)(2,1)S(1)}, bf16[512,256]{1,0:T(8,128)(2,1)S(1)}, u32[]{:S(2)}, u32[]{:S(2)}) %collective-permute-start.24) | collective-permute-done | bytes 262176 | tf_op jit(solution)/shard_map/ppermute | solution.py:318
  138.5 2.8 %collective-permute-done.14.refs_2_ = bf16[512,256]{1,0:T(8,128)(2,1)S(1)} collective-permute-done((bf16[512,256]{1,0:T(8,128)(2,1)S(1)}, bf16[512,256]{1,0:T(8,128)(2,1)S(1)}, u32[]{:S(2)}, u32[]{:S(2)}) %collective-permute-start.14) | collective-permute-done | bytes 262176 | tf_op jit(solution)/shard_map/ppermute | solution.py:318
  141.3 0.9 total_rows.1
  (52 shorter events, 2.2 us)
Async XLA Ops:
  0.0 21.3 %collective-permute-start = (bf16[1024,256]{1,0:T(8,128)(2,1)}, bf16[1024,256]{1,0:T(8,128)(2,1)}, u32[]{:S(2)}, u32[]{:S(2)}) collective-permute-start(bf16[1024,256]{1,0:T(8,128)(2,1)} %refs_0_.1), channel_id=1, source_target_pairs={{0,2},{2,4},{4,6},{6,8},{8,10},{10,12},{12,14},{14,0},{1,3},{3,5},... | collective-permute-start | bytes 1572872 | tf_op jit(solution)/shard_map/ppermute | solution.py:352
  3.9 12.8 %all-to-all-start = ((s32[16,3,16]{2,1,0:T(4,128)}), s32[16,3,16]{2,1,0:T(4,128)S(1)}, u32[]{:S(2)}, u32[]{:S(2)}) async-start(s32[16,3,16]{2,1,0:T(4,128)} %broadcast_in_dim.27), calls=%async_computation | async-start | bytes 65536 | tf_op jit(solution)/shard_map/all_to_all | solution.py:347
  16.7 0.6 copy-start.4
  21.3 10.6 %copy-start.3 = (bf16[4096,256]{1,0:T(8,128)(2,1)S(1)}, bf16[4096,256]{1,0:T(8,128)(2,1)}, u32[]{:S(2)}) copy-start(bf16[4096,256]{1,0:T(8,128)(2,1)} %param.11) | copy-start | bytes 6291460
  21.3 66.8 %all-to-all-start.1 = ((bf16[16,2,128,512]{3,2,1,0:T(8,128)(2,1)}), bf16[16,2,128,512]{3,2,1,0:T(8,128)(2,1)}, u32[]{:S(2)}, u32[]{:S(2)}) async-start(bf16[16,2,128,512]{3,2,1,0:T(8,128)(2,1)} %select_blocks.1), calls=%async_computation.1 | async-start | bytes 8388608 | tf_op jit(solution)/shard_map/all_to_all | solution.py:356
  27.9 14.3 %collective-permute-start.4 = (bf16[1024,256]{1,0:T(8,128)(2,1)}, bf16[1024,256]{1,0:T(8,128)(2,1)}, u32[]{:S(2)}, u32[]{:S(2)}) collective-permute-start(bf16[1024,256]{1,0:T(8,128)(2,1)} %refs_0_.1), channel_id=1, source_target_pairs={{0,14},{2,0},{4,2},{6,4},{8,6},{10,8},{12,10},{14,12},{1,15},{3,1}... | collective-permute-start | bytes 1572872 | tf_op jit(solution)/shard_map/ppermute | solution.py:353
  31.9 14.1 %collective-permute-start.1 = (bf16[1024,256]{1,0:T(8,128)(2,1)}, bf16[1024,256]{1,0:T(8,128)(2,1)}, u32[]{:S(2)}, u32[]{:S(2)}) collective-permute-start(bf16[1024,256]{1,0:T(8,128)(2,1)} %collective-permute-done.refs_1_), channel_id=1, source_target_pairs={{0,2},{2,4},{4,6},{6,8},{8,10},{10,12},{12,14},{14,0},{1,3},{3,5},... | collective-permute-start | bytes 1572872 | tf_op jit(solution)/shard_map/ppermute | solution.py:374
  31.9 27.8 %collective-permute-start.7 = (bf16[8,256,256]{2,1,0:T(8,128)(2,1)S(1)}, bf16[8,256,256]{2,1,0:T(8,128)(2,1)}, u32[]{:S(2)}, u32[]{:S(2)}) collective-permute-start(bf16[8,256,256]{2,1,0:T(8,128)(2,1)S(1)} %dynamic-slice_bitcast_fusion), channel_id=1, source_target_pairs={{0,1},{1,0},{2,3},{3,2},{4,5},{5,4},{6,7},{7,6},{8,9},{9,8},{10,11... | collective-permute-start | bytes 3145736 | tf_op jit(solution)/shard_map/ppermute | solution.py:379
  42.2 13.2 %collective-permute-start.5 = (bf16[1024,256]{1,0:T(8,128)(2,1)}, bf16[1024,256]{1,0:T(8,128)(2,1)}, u32[]{:S(2)}, u32[]{:S(2)}) collective-permute-start(bf16[1024,256]{1,0:T(8,128)(2,1)} %collective-permute-done.4.refs_7_), channel_id=1, source_target_pairs={{0,14},{2,0},{4,2},{6,4},{8,6},{10,8},{12,10},{14,12},{1,15},{3,1}... | collective-permute-start | bytes 1572872 | tf_op jit(solution)/shard_map/ppermute | solution.py:376
  45.9 13.2 %collective-permute-start.2 = (bf16[1024,256]{1,0:T(8,128)(2,1)}, bf16[1024,256]{1,0:T(8,128)(2,1)}, u32[]{:S(2)}, u32[]{:S(2)}) collective-permute-start(bf16[1024,256]{1,0:T(8,128)(2,1)} %collective-permute-done.1.refs_2_), channel_id=1, source_target_pairs={{0,2},{2,4},{4,6},{6,8},{8,10},{10,12},{12,14},{14,0},{1,3},{3,5},... | collective-permute-start | bytes 1572872 | tf_op jit(solution)/shard_map/ppermute | solution.py:374
  55.4 12.2 %collective-permute-start.6 = (bf16[1024,256]{1,0:T(8,128)(2,1)}, bf16[1024,256]{1,0:T(8,128)(2,1)}, u32[]{:S(2)}, u32[]{:S(2)}) collective-permute-start(bf16[1024,256]{1,0:T(8,128)(2,1)} %collective-permute-done.5.refs_6_), channel_id=1, source_target_pairs={{0,14},{2,0},{4,2},{6,4},{8,6},{10,8},{12,10},{14,12},{1,15},{3,1}... | collective-permute-start | bytes 1572872 | tf_op jit(solution)/shard_map/ppermute | solution.py:376
  59.1 11.9 %collective-permute-start.3 = (bf16[1024,256]{1,0:T(8,128)(2,1)}, bf16[1024,256]{1,0:T(8,128)(2,1)}, u32[]{:S(2)}, u32[]{:S(2)}) collective-permute-start(bf16[1024,256]{1,0:T(8,128)(2,1)} %collective-permute-done.2.refs_3_), channel_id=1, source_target_pairs={{0,2},{2,4},{4,6},{6,8},{8,10},{10,12},{12,14},{14,0},{1,3},{3,5},... | collective-permute-start | bytes 1572872 | tf_op jit(solution)/shard_map/ppermute | solution.py:374
  59.7 18.4 %copy-start = (bf16[256,4096]{1,0:T(8,128)(2,1)S(1)}, bf16[256,4096]{1,0:T(8,128)(2,1)}, u32[]{:S(2)}) copy-start(bf16[256,4096]{1,0:T(8,128)(2,1)} %weight_ref.9) | copy-start | bytes 6291460
  59.7 18.4 %copy-start.2 = (s32[2]{0:T(128)S(1)}, s32[2]{0:T(128)}, u32[]{:S(2)}) copy-start(s32[2]{0:T(128)} %pad_add_fusion.1.place_ref) | copy-start | bytes 28
  78.0 2.4 %copy-start.5 = (s32[16,2]{0,1:T(2,128)S(1)}, s32[16,2]{0,1:T(2,128)}, u32[]{:S(2)}) copy-start(s32[16,2]{0,1:T(2,128)} %param.18) | copy-start | bytes 388
  78.0 3.7 %collective-permute-start.8 = (f32[1024,256]{1,0:T(8,128)}, f32[1024,256]{1,0:T(8,128)}, u32[]{:S(2)}, u32[]{:S(2)}) collective-permute-start(f32[1024,256]{1,0:T(8,128)} %get-tuple-element.30), channel_id=1, source_target_pairs={{0,1},{1,0},{2,3},{3,2},{4,5},{5,4},{6,7},{7,6},{8,9},{9,8},{10,11... | collective-permute-start | bytes 3145736 | tf_op jit(solution)/shard_map/ppermute | solution.py:384
  79.8 13.4 %collective-permute-start.10 = (bf16[8,256,256]{2,1,0:T(8,128)(2,1)}, bf16[8,256,256]{2,1,0:T(8,128)(2,1)S(1)}, u32[]{:S(2)}, u32[]{:S(2)}) collective-permute-start(bf16[8,256,256]{2,1,0:T(8,128)(2,1)} %relay.1), channel_id=1, source_target_pairs={{0,1},{1,0},{2,3},{3,2},{4,5},{5,4},{6,7},{7,6},{8,9},{9,8},{10,11... | collective-permute-start | bytes 3145736 | tf_op jit(solution)/shard_map/ppermute | solution.py:381
  88.1 1.0 copy-start.1
  93.2 2.0 %collective-permute-start.9 = (bf16[1024,256]{1,0:T(8,128)(2,1)S(1)}, bf16[1024,256]{1,0:T(8,128)(2,1)S(1)}, u32[]{:S(2)}, u32[]{:S(2)}) collective-permute-start(bf16[1024,256]{1,0:T(8,128)(2,1)S(1)} %attend.1.own_ref), channel_id=1, source_target_pairs={{0,1},{1,0},{2,3},{3,2},{4,5},{5,4},{6,7},{7,6},{8,9},{9,8},{10,11... | collective-permute-start | bytes 1572872 | tf_op jit(solution)/shard_map/ppermute | solution.py:386
  96.1 11.2 %collective-permute-start.11 = (bf16[512,256]{1,0:T(8,128)(2,1)S(1)}, bf16[512,256]{1,0:T(8,128)(2,1)S(1)}, u32[]{:S(2)}, u32[]{:S(2)}) collective-permute-start(bf16[512,256]{1,0:T(8,128)(2,1)S(1)} %get-tuple-element.33), channel_id=1, source_target_pairs={{0,2},{2,4},{4,6},{6,8},{8,10},{10,12},{12,14},{14,0},{1,3},{3,5},... | collective-permute-start | bytes 786440 | tf_op jit(solution)/shard_map/ppermute | solution.py:309
  98.1 9.4 %collective-permute-start.15 = (bf16[512,256]{1,0:T(8,128)(2,1)S(1)}, bf16[512,256]{1,0:T(8,128)(2,1)S(1)}, u32[]{:S(2)}, u32[]{:S(2)}) collective-permute-start(bf16[512,256]{1,0:T(8,128)(2,1)S(1)} %get-tuple-element.37), channel_id=1, source_target_pairs={{0,14},{2,0},{4,2},{6,4},{8,6},{10,8},{12,10},{14,12},{1,15},{3,1}... | collective-permute-start | bytes 786440 | tf_op jit(solution)/shard_map/ppermute | solution.py:309
  101.5 11.4 %collective-permute-start.19 = (bf16[512,256]{1,0:T(8,128)(2,1)S(1)}, bf16[512,256]{1,0:T(8,128)(2,1)S(1)}, u32[]{:S(2)}, u32[]{:S(2)}) collective-permute-start(bf16[512,256]{1,0:T(8,128)(2,1)S(1)} %get-tuple-element.41), channel_id=1, source_target_pairs={{0,14},{2,0},{4,2},{6,4},{8,6},{10,8},{12,10},{14,12},{1,15},{3,1}... | collective-permute-start | bytes 786440 | tf_op jit(solution)/shard_map/ppermute | solution.py:309
  103.6 13.1 %collective-permute-start.22 = (bf16[512,256]{1,0:T(8,128)(2,1)S(1)}, bf16[512,256]{1,0:T(8,128)(2,1)S(1)}, u32[]{:S(2)}, u32[]{:S(2)}) collective-permute-start(bf16[512,256]{1,0:T(8,128)(2,1)S(1)} %get-tuple-element.44), channel_id=1, source_target_pairs={{0,2},{2,4},{4,6},{6,8},{8,10},{10,12},{12,14},{14,0},{1,3},{3,5},... | collective-permute-start | bytes 786440 | tf_op jit(solution)/shard_map/ppermute | solution.py:309
  107.4 10.9 %collective-permute-start.12 = (bf16[512,256]{1,0:T(8,128)(2,1)S(1)}, bf16[512,256]{1,0:T(8,128)(2,1)S(1)}, u32[]{:S(2)}, u32[]{:S(2)}) collective-permute-start(bf16[512,256]{1,0:T(8,128)(2,1)S(1)} %add_convert_fusion.9), channel_id=1, source_target_pairs={{0,2},{2,4},{4,6},{6,8},{8,10},{10,12},{12,14},{14,0},{1,3},{3,5},... | collective-permute-start | bytes 786440 | tf_op jit(solution)/shard_map/ppermute | solution.py:318
  107.6 10.9 %collective-permute-start.16 = (bf16[512,256]{1,0:T(8,128)(2,1)S(1)}, bf16[512,256]{1,0:T(8,128)(2,1)S(1)}, u32[]{:S(2)}, u32[]{:S(2)}) collective-permute-start(bf16[512,256]{1,0:T(8,128)(2,1)S(1)} %add_convert_fusion.6), channel_id=1, source_target_pairs={{0,14},{2,0},{4,2},{6,4},{8,6},{10,8},{12,10},{14,12},{1,15},{3,1}... | collective-permute-start | bytes 786440 | tf_op jit(solution)/shard_map/ppermute | solution.py:318
  113.0 11.2 %collective-permute-start.20 = (bf16[512,256]{1,0:T(8,128)(2,1)S(1)}, bf16[512,256]{1,0:T(8,128)(2,1)S(1)}, u32[]{:S(2)}, u32[]{:S(2)}) collective-permute-start(bf16[512,256]{1,0:T(8,128)(2,1)S(1)} %add_convert_fusion.3), channel_id=1, source_target_pairs={{0,14},{2,0},{4,2},{6,4},{8,6},{10,8},{12,10},{14,12},{1,15},{3,1}... | collective-permute-start | bytes 786440 | tf_op jit(solution)/shard_map/ppermute | solution.py:318
  116.7 11.2 %collective-permute-start.23 = (bf16[512,256]{1,0:T(8,128)(2,1)S(1)}, bf16[512,256]{1,0:T(8,128)(2,1)S(1)}, u32[]{:S(2)}, u32[]{:S(2)}) collective-permute-start(bf16[512,256]{1,0:T(8,128)(2,1)S(1)} %add_convert_fusion.1), channel_id=1, source_target_pairs={{0,2},{2,4},{4,6},{6,8},{8,10},{10,12},{12,14},{14,0},{1,3},{3,5},... | collective-permute-start | bytes 786440 | tf_op jit(solution)/shard_map/ppermute | solution.py:318
  118.4 11.7 %collective-permute-start.13 = (bf16[512,256]{1,0:T(8,128)(2,1)S(1)}, bf16[512,256]{1,0:T(8,128)(2,1)S(1)}, u32[]{:S(2)}, u32[]{:S(2)}) collective-permute-start(bf16[512,256]{1,0:T(8,128)(2,1)S(1)} %add_convert_fusion.8), channel_id=1, source_target_pairs={{0,2},{2,4},{4,6},{6,8},{8,10},{10,12},{12,14},{14,0},{1,3},{3,5},... | collective-permute-start | bytes 786440 | tf_op jit(solution)/shard_map/ppermute | solution.py:318
  118.6 11.6 %collective-permute-start.17 = (bf16[512,256]{1,0:T(8,128)(2,1)S(1)}, bf16[512,256]{1,0:T(8,128)(2,1)S(1)}, u32[]{:S(2)}, u32[]{:S(2)}) collective-permute-start(bf16[512,256]{1,0:T(8,128)(2,1)S(1)} %add_convert_fusion.5), channel_id=1, source_target_pairs={{0,14},{2,0},{4,2},{6,4},{8,6},{10,8},{12,10},{14,12},{1,15},{3,1}... | collective-permute-start | bytes 786440 | tf_op jit(solution)/shard_map/ppermute | solution.py:318
  124.2 11.2 %collective-permute-start.21 = (bf16[512,256]{1,0:T(8,128)(2,1)S(1)}, bf16[512,256]{1,0:T(8,128)(2,1)S(1)}, u32[]{:S(2)}, u32[]{:S(2)}) collective-permute-start(bf16[512,256]{1,0:T(8,128)(2,1)S(1)} %add_convert_fusion.2), channel_id=1, source_target_pairs={{0,14},{2,0},{4,2},{6,4},{8,6},{10,8},{12,10},{14,12},{1,15},{3,1}... | collective-permute-start | bytes 786440 | tf_op jit(solution)/shard_map/ppermute | solution.py:318
  128.0 10.5 %collective-permute-start.24 = (bf16[512,256]{1,0:T(8,128)(2,1)S(1)}, bf16[512,256]{1,0:T(8,128)(2,1)S(1)}, u32[]{:S(2)}, u32[]{:S(2)}) collective-permute-start(bf16[512,256]{1,0:T(8,128)(2,1)S(1)} %add_convert_fusion), channel_id=1, source_target_pairs={{0,2},{2,4},{4,6},{6,8},{8,10},{10,12},{12,14},{14,0},{1,3},{3,5},... | collective-permute-start | bytes 786440 | tf_op jit(solution)/shard_map/ppermute | solution.py:318
  130.1 11.2 %collective-permute-start.14 = (bf16[512,256]{1,0:T(8,128)(2,1)S(1)}, bf16[512,256]{1,0:T(8,128)(2,1)S(1)}, u32[]{:S(2)}, u32[]{:S(2)}) collective-permute-start(bf16[512,256]{1,0:T(8,128)(2,1)S(1)} %add_convert_fusion.7), channel_id=1, source_target_pairs={{0,2},{2,4},{4,6},{6,8},{8,10},{10,12},{12,14},{14,0},{1,3},{3,5},... | collective-permute-start | bytes 786440 | tf_op jit(solution)/shard_map/ppermute | solution.py:318
  130.3 11.0 %collective-permute-start.18 = (bf16[512,256]{1,0:T(8,128)(2,1)S(1)}, bf16[512,256]{1,0:T(8,128)(2,1)S(1)}, u32[]{:S(2)}, u32[]{:S(2)}) collective-permute-start(bf16[512,256]{1,0:T(8,128)(2,1)S(1)} %add_convert_fusion.4), channel_id=1, source_target_pairs={{0,14},{2,0},{4,2},{6,4},{8,6},{10,8},{12,10},{14,12},{1,15},{3,1}... | collective-permute-start | bytes 786440 | tf_op jit(solution)/shard_map/ppermute | solution.py:318

commit v13 on v11

--- a/solution.py
+++ b/solution.py
@@ -183,7 +183,7 @@
             copies.append(copy)
     query_copy.wait()
     places = lax.broadcasted_iota(jnp.int32, (SPAN, keys), 1)
-    group = 4
+    group = 8
     for start in range(0, spans, group):
         members = [(c, h) for c in range(start, start + group) for h in range(width // HD)]
         for copy in copies[start * NBRS : (start + group) * NBRS]:

time: 144 us -> 143 us (level)
  transfers between devices with their start and end apart: 27 -> 27, of which waited for: 17 -> 17; matrix products, arithmetic and copies ran while one was open for 3% -> 3% of each run, Pallas kernels for 21% -> 20%
where the time goes in v13:
time: 143 us; the launch traced here: 142 us
  starting transfers between devices  52.8 us (37%)
  waiting for transfers between devices  52.7 us (37%)
  Pallas kernels  30.9 us (22%)
  other arithmetic  2.9 us (2%)
  local copies, waits for them, and re-layouts  2.63 us (2%)
    ppermute x10, starting transfers between devices, reduce_ring(): lax.ppermute(total.astype(BF16), 'z', up if way == 1 else down)  18.5 us
    ppermute x2, waiting for transfers between devices, local(): pieces[ring - k] = lax.ppermute(pieces[ring - k + 1], 'z', down)  17.4 us
    ppermute x10, waiting for transfers between devices, reduce_ring(): lax.ppermute(total.astype(BF16), 'z', up if way == 1 else down)  11.4 us
    ppermute x1, waiting for transfers between devices, local(): pieces[ring - 1] = lax.ppermute(tokens, 'z', down)  10.2 us
    ppermute x2, starting transfers between devices, local(): pieces[ring - k] = lax.ppermute(pieces[ring - k + 1], 'z', down)  7.38 us
    all_to_all x1, starting transfers between devices, local(): heard = lax.all_to_all(notes, DB, split_axis=0, concat_axis=0, tiled=True)  7.17 us
    pallas_call x1, Pallas kernels, project_queries(): pl.pallas_call(query_kernel, grid=(rows // tile,), out_shape=(out, out),...  6.96 us
    all_to_all x1, starting transfers between devices, local(): rows = lax.all_to_all(sent, DB, split_axis=0, concat_axis=0, tiled=True)  6.65 us
  transfers between devices with their start and end apart: 27, of which 17 were waited for; matrix products, arithmetic and copies ran while one was open for 3% of the time, Pallas kernels for 20%

profile of v13, /device:TPU:24, one launch (start us, length us, event | category | flops | bytes accessed | tf_op | source)
XLA Modules:
  0.0 142.3 jit_solution(9536819693608458610)
XLA Ops:
  0.0 1.9 %collective-permute-start = (bf16[1024,256]{1,0:T(8,128)(2,1)}, bf16[1024,256]{1,0:T(8,128)(2,1)}, u32[]{:S(2)}, u32[]{:S(2)}) collective-permute-start(bf16[1024,256]{1,0:T(8,128)(2,1)} %refs_0_.1), channel_id=1, source_target_pairs={{0,2},{2,4},{4,6},{6,8},{8,10},{10,12},{12,14},{14,0},{1,3},{3,5},... | collective-permute-start | bytes 1572872 | tf_op jit(solution)/shard_map/ppermute | solution.py:361
  1.9 0.7 multiply_bitcast_fusion
  2.6 0.7 pad_add_fusion
  3.3 0.6 broadcast_in_dim.10
  3.9 7.2 %all-to-all-start = ((s32[16,2,16]{2,1,0:T(2,128)}), s32[16,2,16]{2,1,0:T(2,128)S(1)}, u32[]{:S(2)}, u32[]{:S(2)}) async-start(s32[16,2,16]{2,1,0:T(2,128)} %broadcast_in_dim.10), calls=%async_computation | async-start | bytes 32768 | tf_op jit(solution)/shard_map/all_to_all | solution.py:356
  11.1 4.9 %project_blocks.1.rows_ref = bf16[8,128,512]{2,1,0:T(8,128)(2,1)} custom-call(f32[8,7]{1,0:T(8,128)} %scales_ref.1, bf16[8,128,896]{2,1,0:T(8,128)(2,1)} %codes_ref.1, bf16[896,256]{1,0:T(8,128)(2,1)} %key_ref.1, bf16[896,256]{1,0:T(8,128)(2,1)} %value_ref.1), custom_call_target="tpu_custom_call" | custom-call | flops 939524096 | bytes 5242880 | tf_op jit(solution)/shard_map/project_blocks/pallas_call | solution.py:54
  15.9 0.7 all-to-all-done.heard_ref
  16.7 0.6 copy-done.4
  17.3 4.0 %select_blocks.1 = bf16[16,2,128,512]{3,2,1,0:T(8,128)(2,1)} custom-call(s32[1]{0:T(128)} %bitcast.5.place_ref, s32[16,2,16]{2,1,0:T(2,128)} %copy-done.4, bf16[8,128,512]{2,1,0:T(8,128)(2,1)} %project_blocks.1.rows_ref), custom_call_target="tpu_custom_call" | custom-call | bytes 9437184 | tf_op jit(solution)/shard_map/select_blocks/pallas_call | solution.py:98
  21.3 6.7 %all-to-all-start.1 = ((bf16[16,2,128,512]{3,2,1,0:T(8,128)(2,1)}), bf16[16,2,128,512]{3,2,1,0:T(8,128)(2,1)}, u32[]{:S(2)}, u32[]{:S(2)}) async-start(bf16[16,2,128,512]{3,2,1,0:T(8,128)(2,1)} %select_blocks.1), calls=%async_computation.1 | async-start | bytes 8388608 | tf_op jit(solution)/shard_map/all_to_all | solution.py:365
  27.9 3.9 %collective-permute-start.4 = (bf16[1024,256]{1,0:T(8,128)(2,1)}, bf16[1024,256]{1,0:T(8,128)(2,1)}, u32[]{:S(2)}, u32[]{:S(2)}) collective-permute-start(bf16[1024,256]{1,0:T(8,128)(2,1)} %refs_0_.1), channel_id=1, source_target_pairs={{0,14},{2,0},{4,2},{6,4},{8,6},{10,8},{12,10},{14,12},{1,15},{3,1}... | collective-permute-start | bytes 1572872 | tf_op jit(solution)/shard_map/ppermute | solution.py:362
  32.0 10.2 %collective-permute-done.4.refs_7_ = bf16[1024,256]{1,0:T(8,128)(2,1)} collective-permute-done((bf16[1024,256]{1,0:T(8,128)(2,1)}, bf16[1024,256]{1,0:T(8,128)(2,1)}, u32[]{:S(2)}, u32[]{:S(2)}) %collective-permute-start.4) | collective-permute-done | bytes 524320 | tf_op jit(solution)/shard_map/ppermute | solution.py:362
  42.2 3.7 %collective-permute-start.5 = (bf16[1024,256]{1,0:T(8,128)(2,1)}, bf16[1024,256]{1,0:T(8,128)(2,1)}, u32[]{:S(2)}, u32[]{:S(2)}) collective-permute-start(bf16[1024,256]{1,0:T(8,128)(2,1)} %collective-permute-done.4.refs_7_), channel_id=1, source_target_pairs={{0,14},{2,0},{4,2},{6,4},{8,6},{10,8},{12,10},{14,12},{1,15},{3,1}... | collective-permute-start | bytes 1572872 | tf_op jit(solution)/shard_map/ppermute | solution.py:385
  45.9 9.4 %collective-permute-done.5.refs_6_ = bf16[1024,256]{1,0:T(8,128)(2,1)} collective-permute-done((bf16[1024,256]{1,0:T(8,128)(2,1)}, bf16[1024,256]{1,0:T(8,128)(2,1)}, u32[]{:S(2)}, u32[]{:S(2)}) %collective-permute-start.5) | collective-permute-done | bytes 524320 | tf_op jit(solution)/shard_map/ppermute | solution.py:385
  55.4 3.7 %collective-permute-start.6 = (bf16[1024,256]{1,0:T(8,128)(2,1)}, bf16[1024,256]{1,0:T(8,128)(2,1)}, u32[]{:S(2)}, u32[]{:S(2)}) collective-permute-start(bf16[1024,256]{1,0:T(8,128)(2,1)} %collective-permute-done.5.refs_6_), channel_id=1, source_target_pairs={{0,14},{2,0},{4,2},{6,4},{8,6},{10,8},{12,10},{14,12},{1,15},{3,1}... | collective-permute-start | bytes 1572872 | tf_op jit(solution)/shard_map/ppermute | solution.py:385
  59.1 0.6 pad_add_fusion.1.place_ref
  59.7 7.9 %collective-permute-done.6.refs_5_ = bf16[1024,256]{1,0:T(8,128)(2,1)} collective-permute-done((bf16[1024,256]{1,0:T(8,128)(2,1)}, bf16[1024,256]{1,0:T(8,128)(2,1)}, u32[]{:S(2)}, u32[]{:S(2)}) %collective-permute-start.6) | collective-permute-done | bytes 524320 | tf_op jit(solution)/shard_map/ppermute | solution.py:385
  67.6 3.4 %collective-permute-done.3.refs_4_ = bf16[1024,256]{1,0:T(8,128)(2,1)} collective-permute-done((bf16[1024,256]{1,0:T(8,128)(2,1)}, bf16[1024,256]{1,0:T(8,128)(2,1)}, u32[]{:S(2)}, u32[]{:S(2)}) %collective-permute-start.3) | collective-permute-done | bytes 524320 | tf_op jit(solution)/shard_map/ppermute | solution.py:383
  71.0 7.0 %project_queries.1 = (f32[1024,256]{1,0:T(8,128)}, f32[1024,256]{1,0:T(8,128)}) custom-call(s32[2]{0:T(128)} %pad_add_fusion.1.place_ref, bf16[1024,256]{1,0:T(8,128)(2,1)} %refs_0_.1, bf16[1024,256]{1,0:T(8,128)(2,1)} %collective-permute-done.refs_1_, bf16[1024,256]{1,0:T(8,128)(2,1)} %collective-permute-done.1.refs_2_, ...), custom_call_target="tpu_custom_call" | custom-call | flops 2147483648 | bytes 9437184 | tf_op jit(solution)/shard_map/project_queries/pallas_call | solution.py:128
  78.1 1.7 %relay.1 = bf16[8,256,256]{2,1,0:T(8,128)(2,1)} custom-call(s32[2]{0:T(128)S(1)} %copy-done.2, bf16[256,4096]{1,0:T(8,128)(2,1)S(1)} %copy-done), custom_call_target="tpu_custom_call" | custom-call | bytes 3145728 | tf_op jit(solution)/shard_map/relay/pallas_call | solution.py:244
  79.8 0.5 collective-permute-start.10
  80.4 0.2 convert_reduce_fusion
  81.1 2.7 %finish_queries.1.queries_ref = bf16[1024,256]{1,0:T(8,128)(2,1)} custom-call(f32[1024,256]{1,0:T(8,128)} %get-tuple-element.31.own_ref, f32[1024,256]{1,0:T(8,128)} %collective-permute-done.8.lent_ref), custom_call_target="tpu_custom_call" | custom-call | flops 1048576 | bytes 3145728 | tf_op jit(solution)/shard_map/finish_queries/pallas_call | solution.py:154
  83.8 4.3 %all-to-all-done.1 = bf16[16,2,128,512]{3,2,1,0:T(8,128)(2,1)} async-done(((bf16[16,2,128,512]{3,2,1,0:T(8,128)(2,1)}), bf16[16,2,128,512]{3,2,1,0:T(8,128)(2,1)}, u32[]{:S(2)}, u32[]{:S(2)}) %all-to-all-start.1) | async-done | bytes 4194336 | tf_op jit(solution)/shard_map/all_to_all | solution.py:365
  88.1 1.0 copy-done.1
  89.1 4.0 %attend.1.own_ref = bf16[1024,256]{1,0:T(8,128)(2,1)S(1)} custom-call(s32[32]{0:T(128)S(1)} %multiply_add_fusion.slot_ref, s32[32]{0:T(128)S(1)} %select_reduce_fusion.length_ref, bf16[1024,256]{1,0:T(8,128)(2,1)S(1)} %copy-done.1, bf16[32,128,512]{2,1,0:T(8,128)(2,1)} %bitcast.8.rows_ref), custom_call_target="tpu_custom_call" | custom-call | flops 1024 | bytes 1024 | tf_op jit(solution)/shard_map/attend/pallas_call | solution.py:216
  93.3 1.9 %collective-permute-done.9.partner_ref = bf16[1024,256]{1,0:T(8,128)(2,1)S(1)} collective-permute-done((bf16[1024,256]{1,0:T(8,128)(2,1)S(1)}, bf16[1024,256]{1,0:T(8,128)(2,1)S(1)}, u32[]{:S(2)}, u32[]{:S(2)}) %collective-permute-start.9) | collective-permute-done | bytes 524320 | tf_op jit(solution)/shard_map/ppermute | solution.py:395
  95.2 1.0 shares.5
  96.1 2.0 %collective-permute-start.11 = (bf16[512,256]{1,0:T(8,128)(2,1)S(1)}, bf16[512,256]{1,0:T(8,128)(2,1)S(1)}, u32[]{:S(2)}, u32[]{:S(2)}) collective-permute-start(bf16[512,256]{1,0:T(8,128)(2,1)S(1)} %get-tuple-element.33), channel_id=1, source_target_pairs={{0,2},{2,4},{4,6},{6,8},{8,10},{10,12},{12,14},{14,0},{1,3},{3,5},... | collective-permute-start | bytes 786440 | tf_op jit(solution)/shard_map/ppermute | solution.py:315
  98.1 2.4 %collective-permute-start.15 = (bf16[512,256]{1,0:T(8,128)(2,1)S(1)}, bf16[512,256]{1,0:T(8,128)(2,1)S(1)}, u32[]{:S(2)}, u32[]{:S(2)}) collective-permute-start(bf16[512,256]{1,0:T(8,128)(2,1)S(1)} %get-tuple-element.41), channel_id=1, source_target_pairs={{0,14},{2,0},{4,2},{6,4},{8,6},{10,8},{12,10},{14,12},{1,15},{3,1}... | collective-permute-start | bytes 786440 | tf_op jit(solution)/shard_map/ppermute | solution.py:315
  100.6 1.0 shares.9
  101.5 2.0 %collective-permute-start.19 = (bf16[512,256]{1,0:T(8,128)(2,1)S(1)}, bf16[512,256]{1,0:T(8,128)(2,1)S(1)}, u32[]{:S(2)}, u32[]{:S(2)}) collective-permute-start(bf16[512,256]{1,0:T(8,128)(2,1)S(1)} %get-tuple-element.45), channel_id=1, source_target_pairs={{0,14},{2,0},{4,2},{6,4},{8,6},{10,8},{12,10},{14,12},{1,15},{3,1}... | collective-permute-start | bytes 786440 | tf_op jit(solution)/shard_map/ppermute | solution.py:315
  103.6 1.0 shares.6
  104.6 2.8 %collective-permute-done.11 = bf16[512,256]{1,0:T(8,128)(2,1)S(1)} collective-permute-done((bf16[512,256]{1,0:T(8,128)(2,1)S(1)}, bf16[512,256]{1,0:T(8,128)(2,1)S(1)}, u32[]{:S(2)}, u32[]{:S(2)}) %collective-permute-start.11) | collective-permute-done | bytes 262176 | tf_op jit(solution)/shard_map/ppermute | solution.py:315
  107.6 3.5 %collective-permute-start.16 = (bf16[512,256]{1,0:T(8,128)(2,1)S(1)}, bf16[512,256]{1,0:T(8,128)(2,1)S(1)}, u32[]{:S(2)}, u32[]{:S(2)}) collective-permute-start(bf16[512,256]{1,0:T(8,128)(2,1)S(1)} %add_convert_fusion.6), channel_id=1, source_target_pairs={{0,14},{2,0},{4,2},{6,4},{8,6},{10,8},{12,10},{14,12},{1,15},{3,1}... | collective-permute-start | bytes 786440 | tf_op jit(solution)/shard_map/ppermute | solution.py:326
  111.1 1.3 shares.8
  112.3 0.6 collective-permute-done.19
  113.0 3.7 %collective-permute-start.20 = (bf16[512,256]{1,0:T(8,128)(2,1)S(1)}, bf16[512,256]{1,0:T(8,128)(2,1)S(1)}, u32[]{:S(2)}, u32[]{:S(2)}) collective-permute-start(bf16[512,256]{1,0:T(8,128)(2,1)S(1)} %add_convert_fusion.3), channel_id=1, source_target_pairs={{0,14},{2,0},{4,2},{6,4},{8,6},{10,8},{12,10},{14,12},{1,15},{3,1}... | collective-permute-start | bytes 786440 | tf_op jit(solution)/shard_map/ppermute | solution.py:326
  116.8 1.5 %collective-permute-done.12 = bf16[512,256]{1,0:T(8,128)(2,1)S(1)} collective-permute-done((bf16[512,256]{1,0:T(8,128)(2,1)S(1)}, bf16[512,256]{1,0:T(8,128)(2,1)S(1)}, u32[]{:S(2)}, u32[]{:S(2)}) %collective-permute-start.12) | collective-permute-done | bytes 262176 | tf_op jit(solution)/shard_map/ppermute | solution.py:326
  118.6 3.9 %collective-permute-start.17 = (bf16[512,256]{1,0:T(8,128)(2,1)S(1)}, bf16[512,256]{1,0:T(8,128)(2,1)S(1)}, u32[]{:S(2)}, u32[]{:S(2)}) collective-permute-start(bf16[512,256]{1,0:T(8,128)(2,1)S(1)} %add_convert_fusion.5), channel_id=1, source_target_pairs={{0,14},{2,0},{4,2},{6,4},{8,6},{10,8},{12,10},{14,12},{1,15},{3,1}... | collective-permute-start | bytes 786440 | tf_op jit(solution)/shard_map/ppermute | solution.py:326
  122.5 1.5 %shares.7 = (f32[512,256]{1,0:T(8,128)S(1)}, f32[512,256]{1,0:T(8,128)S(1)}, f32[512,256]{1,0:T(8,128)S(1)}, f32[512,256]{1,0:T(8,128)S(1)}, f32[512,256]{1,0:T(8,128)S(1)}, /*index=5*/f32[512,256]{1,0:T(8,128)S(1)}) custom-call(s32[2]{0:T(128)S(1)} %copy-done.2, bf16[1024,256]{1,0:T(8,128)(2,1)S(1)} %attend.1.own_ref, ...), custom_call_target="tpu_custom_call" | custom-call | flops 1024 | bytes 1024 | tf_op jit(solution)/shard_map/shares/pallas_call | solution.py:270
  124.2 3.7 %collective-permute-start.21 = (bf16[512,256]{1,0:T(8,128)(2,1)S(1)}, bf16[512,256]{1,0:T(8,128)(2,1)S(1)}, u32[]{:S(2)}, u32[]{:S(2)}) collective-permute-start(bf16[512,256]{1,0:T(8,128)(2,1)S(1)} %add_convert_fusion.2), channel_id=1, source_target_pairs={{0,14},{2,0},{4,2},{6,4},{8,6},{10,8},{12,10},{14,12},{1,15},{3,1}... | collective-permute-start | bytes 786440 | tf_op jit(solution)/shard_map/ppermute | solution.py:326
  128.1 2.0 %collective-permute-done.13 = bf16[512,256]{1,0:T(8,128)(2,1)S(1)} collective-permute-done((bf16[512,256]{1,0:T(8,128)(2,1)S(1)}, bf16[512,256]{1,0:T(8,128)(2,1)S(1)}, u32[]{:S(2)}, u32[]{:S(2)}) %collective-permute-start.13) | collective-permute-done | bytes 262176 | tf_op jit(solution)/shard_map/ppermute | solution.py:326
  130.3 3.3 %collective-permute-start.18 = (bf16[512,256]{1,0:T(8,128)(2,1)S(1)}, bf16[512,256]{1,0:T(8,128)(2,1)S(1)}, u32[]{:S(2)}, u32[]{:S(2)}) collective-permute-start(bf16[512,256]{1,0:T(8,128)(2,1)S(1)} %add_convert_fusion.4), channel_id=1, source_target_pairs={{0,14},{2,0},{4,2},{6,4},{8,6},{10,8},{12,10},{14,12},{1,15},{3,1}... | collective-permute-start | bytes 786440 | tf_op jit(solution)/shard_map/ppermute | solution.py:326
  133.6 1.8 %collective-permute-done.21.refs_4_ = bf16[512,256]{1,0:T(8,128)(2,1)S(1)} collective-permute-done((bf16[512,256]{1,0:T(8,128)(2,1)S(1)}, bf16[512,256]{1,0:T(8,128)(2,1)S(1)}, u32[]{:S(2)}, u32[]{:S(2)}) %collective-permute-start.21) | collective-permute-done | bytes 262176 | tf_op jit(solution)/shard_map/ppermute | solution.py:326
  135.4 3.1 %collective-permute-done.24.refs_5_ = bf16[512,256]{1,0:T(8,128)(2,1)S(1)} collective-permute-done((bf16[512,256]{1,0:T(8,128)(2,1)S(1)}, bf16[512,256]{1,0:T(8,128)(2,1)S(1)}, u32[]{:S(2)}, u32[]{:S(2)}) %collective-permute-start.24) | collective-permute-done | bytes 262176 | tf_op jit(solution)/shard_map/ppermute | solution.py:326
  138.5 2.8 %collective-permute-done.14.refs_2_ = bf16[512,256]{1,0:T(8,128)(2,1)S(1)} collective-permute-done((bf16[512,256]{1,0:T(8,128)(2,1)S(1)}, bf16[512,256]{1,0:T(8,128)(2,1)S(1)}, u32[]{:S(2)}, u32[]{:S(2)}) %collective-permute-start.14) | collective-permute-done | bytes 262176 | tf_op jit(solution)/shard_map/ppermute | solution.py:326
  141.3 0.9 total_rows.1
  (55 shorter events, 2.2 us)
Async XLA Ops:
  0.0 21.3 %collective-permute-start = (bf16[1024,256]{1,0:T(8,128)(2,1)}, bf16[1024,256]{1,0:T(8,128)(2,1)}, u32[]{:S(2)}, u32[]{:S(2)}) collective-permute-start(bf16[1024,256]{1,0:T(8,128)(2,1)} %refs_0_.1), channel_id=1, source_target_pairs={{0,2},{2,4},{4,6},{6,8},{8,10},{10,12},{12,14},{14,0},{1,3},{3,5},... | collective-permute-start | bytes 1572872 | tf_op jit(solution)/shard_map/ppermute | solution.py:361
  3.9 12.8 %all-to-all-start = ((s32[16,2,16]{2,1,0:T(2,128)}), s32[16,2,16]{2,1,0:T(2,128)S(1)}, u32[]{:S(2)}, u32[]{:S(2)}) async-start(s32[16,2,16]{2,1,0:T(2,128)} %broadcast_in_dim.10), calls=%async_computation | async-start | bytes 32768 | tf_op jit(solution)/shard_map/all_to_all | solution.py:356
  16.7 0.6 copy-start.4
  21.2 10.6 %copy-start.3 = (bf16[4096,256]{1,0:T(8,128)(2,1)S(1)}, bf16[4096,256]{1,0:T(8,128)(2,1)}, u32[]{:S(2)}) copy-start(bf16[4096,256]{1,0:T(8,128)(2,1)} %param.11) | copy-start | bytes 6291460
  21.3 66.8 %all-to-all-start.1 = ((bf16[16,2,128,512]{3,2,1,0:T(8,128)(2,1)}), bf16[16,2,128,512]{3,2,1,0:T(8,128)(2,1)}, u32[]{:S(2)}, u32[]{:S(2)}) async-start(bf16[16,2,128,512]{3,2,1,0:T(8,128)(2,1)} %select_blocks.1), calls=%async_computation.1 | async-start | bytes 8388608 | tf_op jit(solution)/shard_map/all_to_all | solution.py:365
  27.9 14.3 %collective-permute-start.4 = (bf16[1024,256]{1,0:T(8,128)(2,1)}, bf16[1024,256]{1,0:T(8,128)(2,1)}, u32[]{:S(2)}, u32[]{:S(2)}) collective-permute-start(bf16[1024,256]{1,0:T(8,128)(2,1)} %refs_0_.1), channel_id=1, source_target_pairs={{0,14},{2,0},{4,2},{6,4},{8,6},{10,8},{12,10},{14,12},{1,15},{3,1}... | collective-permute-start | bytes 1572872 | tf_op jit(solution)/shard_map/ppermute | solution.py:362
  31.9 14.1 %collective-permute-start.1 = (bf16[1024,256]{1,0:T(8,128)(2,1)}, bf16[1024,256]{1,0:T(8,128)(2,1)}, u32[]{:S(2)}, u32[]{:S(2)}) collective-permute-start(bf16[1024,256]{1,0:T(8,128)(2,1)} %collective-permute-done.refs_1_), channel_id=1, source_target_pairs={{0,2},{2,4},{4,6},{6,8},{8,10},{10,12},{12,14},{14,0},{1,3},{3,5},... | collective-permute-start | bytes 1572872 | tf_op jit(solution)/shard_map/ppermute | solution.py:383
  31.9 27.7 %collective-permute-start.7 = (bf16[8,256,256]{2,1,0:T(8,128)(2,1)S(1)}, bf16[8,256,256]{2,1,0:T(8,128)(2,1)}, u32[]{:S(2)}, u32[]{:S(2)}) collective-permute-start(bf16[8,256,256]{2,1,0:T(8,128)(2,1)S(1)} %dynamic-slice_bitcast_fusion), channel_id=1, source_target_pairs={{0,1},{1,0},{2,3},{3,2},{4,5},{5,4},{6,7},{7,6},{8,9},{9,8},{10,11... | collective-permute-start | bytes 3145736 | tf_op jit(solution)/shard_map/ppermute | solution.py:388
  42.2 13.1 %collective-permute-start.5 = (bf16[1024,256]{1,0:T(8,128)(2,1)}, bf16[1024,256]{1,0:T(8,128)(2,1)}, u32[]{:S(2)}, u32[]{:S(2)}) collective-permute-start(bf16[1024,256]{1,0:T(8,128)(2,1)} %collective-permute-done.4.refs_7_), channel_id=1, source_target_pairs={{0,14},{2,0},{4,2},{6,4},{8,6},{10,8},{12,10},{14,12},{1,15},{3,1}... | collective-permute-start | bytes 1572872 | tf_op jit(solution)/shard_map/ppermute | solution.py:385
  45.9 13.1 %collective-permute-start.2 = (bf16[1024,256]{1,0:T(8,128)(2,1)}, bf16[1024,256]{1,0:T(8,128)(2,1)}, u32[]{:S(2)}, u32[]{:S(2)}) collective-permute-start(bf16[1024,256]{1,0:T(8,128)(2,1)} %collective-permute-done.1.refs_2_), channel_id=1, source_target_pairs={{0,2},{2,4},{4,6},{6,8},{8,10},{10,12},{12,14},{14,0},{1,3},{3,5},... | collective-permute-start | bytes 1572872 | tf_op jit(solution)/shard_map/ppermute | solution.py:383
  55.4 12.2 %collective-permute-start.6 = (bf16[1024,256]{1,0:T(8,128)(2,1)}, bf16[1024,256]{1,0:T(8,128)(2,1)}, u32[]{:S(2)}, u32[]{:S(2)}) collective-permute-start(bf16[1024,256]{1,0:T(8,128)(2,1)} %collective-permute-done.5.refs_6_), channel_id=1, source_target_pairs={{0,14},{2,0},{4,2},{6,4},{8,6},{10,8},{12,10},{14,12},{1,15},{3,1}... | collective-permute-start | bytes 1572872 | tf_op jit(solution)/shard_map/ppermute | solution.py:385
  59.1 11.9 %collective-permute-start.3 = (bf16[1024,256]{1,0:T(8,128)(2,1)}, bf16[1024,256]{1,0:T(8,128)(2,1)}, u32[]{:S(2)}, u32[]{:S(2)}) collective-permute-start(bf16[1024,256]{1,0:T(8,128)(2,1)} %collective-permute-done.2.refs_3_), channel_id=1, source_target_pairs={{0,2},{2,4},{4,6},{6,8},{8,10},{10,12},{12,14},{14,0},{1,3},{3,5},... | collective-permute-start | bytes 1572872 | tf_op jit(solution)/shard_map/ppermute | solution.py:383
  59.7 18.4 %copy-start = (bf16[256,4096]{1,0:T(8,128)(2,1)S(1)}, bf16[256,4096]{1,0:T(8,128)(2,1)}, u32[]{:S(2)}) copy-start(bf16[256,4096]{1,0:T(8,128)(2,1)} %weight_ref.11) | copy-start | bytes 6291460
  59.7 18.4 %copy-start.2 = (s32[2]{0:T(128)S(1)}, s32[2]{0:T(128)}, u32[]{:S(2)}) copy-start(s32[2]{0:T(128)} %pad_add_fusion.1.place_ref) | copy-start | bytes 28
  78.0 2.3 %copy-start.6 = (s32[16,2]{0,1:T(2,128)S(1)}, s32[16,2]{0,1:T(2,128)}, u32[]{:S(2)}) copy-start(s32[16,2]{0,1:T(2,128)} %param.18) | copy-start | bytes 388
  78.0 2.7 %copy-start.5 = (s32[16,2,16]{2,1,0:T(2,128)S(1)}, s32[16,2,16]{2,1,0:T(2,128)}, u32[]{:S(2)}) copy-start(s32[16,2,16]{2,1,0:T(2,128)} %copy-done.4) | copy-start | bytes 6148
  78.0 3.1 %collective-permute-start.8 = (f32[1024,256]{1,0:T(8,128)}, f32[1024,256]{1,0:T(8,128)}, u32[]{:S(2)}, u32[]{:S(2)}) collective-permute-start(f32[1024,256]{1,0:T(8,128)} %get-tuple-element.32), channel_id=1, source_target_pairs={{0,1},{1,0},{2,3},{3,2},{4,5},{5,4},{6,7},{7,6},{8,9},{9,8},{10,11... | collective-permute-start | bytes 3145736 | tf_op jit(solution)/shard_map/ppermute | solution.py:393
  79.8 13.4 %collective-permute-start.10 = (bf16[8,256,256]{2,1,0:T(8,128)(2,1)}, bf16[8,256,256]{2,1,0:T(8,128)(2,1)S(1)}, u32[]{:S(2)}, u32[]{:S(2)}) collective-permute-start(bf16[8,256,256]{2,1,0:T(8,128)(2,1)} %relay.1), channel_id=1, source_target_pairs={{0,1},{1,0},{2,3},{3,2},{4,5},{5,4},{6,7},{7,6},{8,9},{9,8},{10,11... | collective-permute-start | bytes 3145736 | tf_op jit(solution)/shard_map/ppermute | solution.py:390
  88.1 1.0 copy-start.1
  93.2 2.0 %collective-permute-start.9 = (bf16[1024,256]{1,0:T(8,128)(2,1)S(1)}, bf16[1024,256]{1,0:T(8,128)(2,1)S(1)}, u32[]{:S(2)}, u32[]{:S(2)}) collective-permute-start(bf16[1024,256]{1,0:T(8,128)(2,1)S(1)} %attend.1.own_ref), channel_id=1, source_target_pairs={{0,1},{1,0},{2,3},{3,2},{4,5},{5,4},{6,7},{7,6},{8,9},{9,8},{10,11... | collective-permute-start | bytes 1572872 | tf_op jit(solution)/shard_map/ppermute | solution.py:395
  96.1 11.2 %collective-permute-start.11 = (bf16[512,256]{1,0:T(8,128)(2,1)S(1)}, bf16[512,256]{1,0:T(8,128)(2,1)S(1)}, u32[]{:S(2)}, u32[]{:S(2)}) collective-permute-start(bf16[512,256]{1,0:T(8,128)(2,1)S(1)} %get-tuple-element.33), channel_id=1, source_target_pairs={{0,2},{2,4},{4,6},{6,8},{8,10},{10,12},{12,14},{14,0},{1,3},{3,5},... | collective-permute-start | bytes 786440 | tf_op jit(solution)/shard_map/ppermute | solution.py:315
  98.1 9.4 %collective-permute-start.15 = (bf16[512,256]{1,0:T(8,128)(2,1)S(1)}, bf16[512,256]{1,0:T(8,128)(2,1)S(1)}, u32[]{:S(2)}, u32[]{:S(2)}) collective-permute-start(bf16[512,256]{1,0:T(8,128)(2,1)S(1)} %get-tuple-element.41), channel_id=1, source_target_pairs={{0,14},{2,0},{4,2},{6,4},{8,6},{10,8},{12,10},{14,12},{1,15},{3,1}... | collective-permute-start | bytes 786440 | tf_op jit(solution)/shard_map/ppermute | solution.py:315
  101.5 11.4 %collective-permute-start.19 = (bf16[512,256]{1,0:T(8,128)(2,1)S(1)}, bf16[512,256]{1,0:T(8,128)(2,1)S(1)}, u32[]{:S(2)}, u32[]{:S(2)}) collective-permute-start(bf16[512,256]{1,0:T(8,128)(2,1)S(1)} %get-tuple-element.45), channel_id=1, source_target_pairs={{0,14},{2,0},{4,2},{6,4},{8,6},{10,8},{12,10},{14,12},{1,15},{3,1}... | collective-permute-start | bytes 786440 | tf_op jit(solution)/shard_map/ppermute | solution.py:315
  103.6 13.1 %collective-permute-start.22 = (bf16[512,256]{1,0:T(8,128)(2,1)S(1)}, bf16[512,256]{1,0:T(8,128)(2,1)S(1)}, u32[]{:S(2)}, u32[]{:S(2)}) collective-permute-start(bf16[512,256]{1,0:T(8,128)(2,1)S(1)} %get-tuple-element.48), channel_id=1, source_target_pairs={{0,2},{2,4},{4,6},{6,8},{8,10},{10,12},{12,14},{14,0},{1,3},{3,5},... | collective-permute-start | bytes 786440 | tf_op jit(solution)/shard_map/ppermute | solution.py:315
  107.4 10.9 %collective-permute-start.12 = (bf16[512,256]{1,0:T(8,128)(2,1)S(1)}, bf16[512,256]{1,0:T(8,128)(2,1)S(1)}, u32[]{:S(2)}, u32[]{:S(2)}) collective-permute-start(bf16[512,256]{1,0:T(8,128)(2,1)S(1)} %add_convert_fusion.9), channel_id=1, source_target_pairs={{0,2},{2,4},{4,6},{6,8},{8,10},{10,12},{12,14},{14,0},{1,3},{3,5},... | collective-permute-start | bytes 786440 | tf_op jit(solution)/shard_map/ppermute | solution.py:326
  107.6 10.9 %collective-permute-start.16 = (bf16[512,256]{1,0:T(8,128)(2,1)S(1)}, bf16[512,256]{1,0:T(8,128)(2,1)S(1)}, u32[]{:S(2)}, u32[]{:S(2)}) collective-permute-start(bf16[512,256]{1,0:T(8,128)(2,1)S(1)} %add_convert_fusion.6), channel_id=1, source_target_pairs={{0,14},{2,0},{4,2},{6,4},{8,6},{10,8},{12,10},{14,12},{1,15},{3,1}... | collective-permute-start | bytes 786440 | tf_op jit(solution)/shard_map/ppermute | solution.py:326
  113.0 11.2 %collective-permute-start.20 = (bf16[512,256]{1,0:T(8,128)(2,1)S(1)}, bf16[512,256]{1,0:T(8,128)(2,1)S(1)}, u32[]{:S(2)}, u32[]{:S(2)}) collective-permute-start(bf16[512,256]{1,0:T(8,128)(2,1)S(1)} %add_convert_fusion.3), channel_id=1, source_target_pairs={{0,14},{2,0},{4,2},{6,4},{8,6},{10,8},{12,10},{14,12},{1,15},{3,1}... | collective-permute-start | bytes 786440 | tf_op jit(solution)/shard_map/ppermute | solution.py:326
  116.7 11.2 %collective-permute-start.23 = (bf16[512,256]{1,0:T(8,128)(2,1)S(1)}, bf16[512,256]{1,0:T(8,128)(2,1)S(1)}, u32[]{:S(2)}, u32[]{:S(2)}) collective-permute-start(bf16[512,256]{1,0:T(8,128)(2,1)S(1)} %add_convert_fusion.1), channel_id=1, source_target_pairs={{0,2},{2,4},{4,6},{6,8},{8,10},{10,12},{12,14},{14,0},{1,3},{3,5},... | collective-permute-start | bytes 786440 | tf_op jit(solution)/shard_map/ppermute | solution.py:326
  118.4 11.7 %collective-permute-start.13 = (bf16[512,256]{1,0:T(8,128)(2,1)S(1)}, bf16[512,256]{1,0:T(8,128)(2,1)S(1)}, u32[]{:S(2)}, u32[]{:S(2)}) collective-permute-start(bf16[512,256]{1,0:T(8,128)(2,1)S(1)} %add_convert_fusion.8), channel_id=1, source_target_pairs={{0,2},{2,4},{4,6},{6,8},{8,10},{10,12},{12,14},{14,0},{1,3},{3,5},... | collective-permute-start | bytes 786440 | tf_op jit(solution)/shard_map/ppermute | solution.py:326
  118.6 11.6 %collective-permute-start.17 = (bf16[512,256]{1,0:T(8,128)(2,1)S(1)}, bf16[512,256]{1,0:T(8,128)(2,1)S(1)}, u32[]{:S(2)}, u32[]{:S(2)}) collective-permute-start(bf16[512,256]{1,0:T(8,128)(2,1)S(1)} %add_convert_fusion.5), channel_id=1, source_target_pairs={{0,14},{2,0},{4,2},{6,4},{8,6},{10,8},{12,10},{14,12},{1,15},{3,1}... | collective-permute-start | bytes 786440 | tf_op jit(solution)/shard_map/ppermute | solution.py:326
  124.2 11.2 %collective-permute-start.21 = (bf16[512,256]{1,0:T(8,128)(2,1)S(1)}, bf16[512,256]{1,0:T(8,128)(2,1)S(1)}, u32[]{:S(2)}, u32[]{:S(2)}) collective-permute-start(bf16[512,256]{1,0:T(8,128)(2,1)S(1)} %add_convert_fusion.2), channel_id=1, source_target_pairs={{0,14},{2,0},{4,2},{6,4},{8,6},{10,8},{12,10},{14,12},{1,15},{3,1}... | collective-permute-start | bytes 786440 | tf_op jit(solution)/shard_map/ppermute | solution.py:326
  128.0 10.5 %collective-permute-start.24 = (bf16[512,256]{1,0:T(8,128)(2,1)S(1)}, bf16[512,256]{1,0:T(8,128)(2,1)S(1)}, u32[]{:S(2)}, u32[]{:S(2)}) collective-permute-start(bf16[512,256]{1,0:T(8,128)(2,1)S(1)} %add_convert_fusion), channel_id=1, source_target_pairs={{0,2},{2,4},{4,6},{6,8},{8,10},{10,12},{12,14},{14,0},{1,3},{3,5},... | collective-permute-start | bytes 786440 | tf_op jit(solution)/shard_map/ppermute | solution.py:326
  130.1 11.2 %collective-permute-start.14 = (bf16[512,256]{1,0:T(8,128)(2,1)S(1)}, bf16[512,256]{1,0:T(8,128)(2,1)S(1)}, u32[]{:S(2)}, u32[]{:S(2)}) collective-permute-start(bf16[512,256]{1,0:T(8,128)(2,1)S(1)} %add_convert_fusion.7), channel_id=1, source_target_pairs={{0,2},{2,4},{4,6},{6,8},{8,10},{10,12},{12,14},{14,0},{1,3},{3,5},... | collective-permute-start | bytes 786440 | tf_op jit(solution)/shard_map/ppermute | solution.py:326
  130.3 11.0 %collective-permute-start.18 = (bf16[512,256]{1,0:T(8,128)(2,1)S(1)}, bf16[512,256]{1,0:T(8,128)(2,1)S(1)}, u32[]{:S(2)}, u32[]{:S(2)}) collective-permute-start(bf16[512,256]{1,0:T(8,128)(2,1)S(1)} %add_convert_fusion.4), channel_id=1, source_target_pairs={{0,14},{2,0},{4,2},{6,4},{8,6},{10,8},{12,10},{14,12},{1,15},{3,1}... | collective-permute-start | bytes 786440 | tf_op jit(solution)/shard_map/ppermute | solution.py:326
